TPU v7x, 256 devices: a whole 4x4x8 slice. The times are simulated.
256 devices in a mesh: rows: 32 (over x, z), cols: 8 (over y, core).
Axes of the slice: x: 4, y: 4, z: 8, core: 2. Of those that a mesh axis runs over, the one named last changes fastest.
Arguments:
- cost: bfloat16 [32768, 8192], P('rows', 'cols'), may hold values from -12 to 12.45
- src_label: int32 [32768], P('rows'), may hold values from 0 to 63
- tgt_label: int32 [8192], P('cols'), may hold values from 0 to 63
- class_mask: int32 [64, 64], replicated, may hold values from 0 to 1, as said below
- g_start: float32 [8192], P('cols'), may hold values from -1.5 to 1.5
- f_bar: float32 [32768], P('rows'), may hold values from -6 to 6
- g_bar: float32 [8192], P('cols'), may hold values from -6 to 6
- src_emb: bfloat16 [32768, 1024], P('rows'), may hold values from -6 to 6
- tgt_emb: bfloat16 [8192, 1024], P('cols'), may hold values from -6 to 6
Outputs:
- g_start_bar: float32 [8192], P('cols')
- grad_x: float32 [1024, 32768], P('cols', 'rows')
- grad_y: float32 [1024, 8192], P('rows', 'cols')
Inputs may be any that keep to these rules, and one draw needn't show every extreme that they name: Every class may be matched with itself: class_mask[c, c] = 1; other entries are 0 or 1.
All inputs are finite; a program needn't handle non-finite values.
Results may differ from a plain program's by a relative error of at most 0.003.
Values sent between devices are 32-bit elements; how exact they have to be, the bound alone decides.
No kernel may reach another device: no remote copies, remote signals or barrier semaphores. Data moves between devices by JAX's collectives and lax.ppermute only.
A program may use at most 64 MiB of HBM per device.

v0:
```python
import functools
import math

import jax
import jax.numpy as jnp
from jax import lax
from jax.experimental import pallas as pl
from jax.experimental.pallas import tpu as pltpu
from jax.sharding import PartitionSpec as P

K = 3


EPSILON = 0.05
PENALTY = 1.0
SCALE = 1.0 / (EPSILON * math.log(2.0))
LANES = 128
STRIP = 32
REACH = 40.0
FIRST_REACH = 75.0
VMEM_BYTES = 16 * 2**20
F32 = jnp.float32


def eye():
    return lax.broadcasted_iota(jnp.int32, (LANES, LANES), 0) == lax.broadcasted_iota(
        jnp.int32, (LANES, LANES), 1
    )


def to_column(row):
    return jnp.sum(jnp.where(eye(), row, 0.0), axis=1, keepdims=True)


def to_row(column):
    return jnp.sum(jnp.where(eye(), column, 0.0), axis=0, keepdims=True)


def log_combined(parts):
    top = jnp.max(parts, axis=0)
    return top + jnp.log2(jnp.sum(jnp.exp2(parts - top[None]), axis=0))


def spread(copies_ref, value):
    copies_ref[...] = jnp.broadcast_to(value[None], copies_ref.shape)


def groups_of(ref):
    return ref.shape[0]


def row_sums(base_ref, weight_ref, out_ref):
    for s in range(groups_of(out_ref)):
        held = None
        for c in range(groups_of(weight_ref)):
            tile = base_ref[s * LANES : (s + 1) * LANES, c * LANES : (c + 1) * LANES]
            term = tile * weight_ref[c : c + 1, :]
            held = term if held is None else held + term
        out_ref[s : s + 1, :] = to_row(jnp.sum(held, axis=1, keepdims=True))


def col_sums(base_ref, weight_ref, out_ref):
    held = [None] * groups_of(out_ref)
    for s in range(groups_of(weight_ref)):
        column = jnp.broadcast_to(to_column(weight_ref[s : s + 1, :]), (LANES, LANES))
        for c in range(len(held)):
            tile = base_ref[s * LANES : (s + 1) * LANES, c * LANES : (c + 1) * LANES]
            term = jnp.sum((tile * column).reshape(LANES // 8, 8, LANES), axis=0)
            held[c] = term if held[c] is None else held[c] + term
    for c, term in enumerate(held):
        out_ref[c : c + 1, :] = jnp.sum(term, axis=0, keepdims=True)


def strip_logs(scores):
    highest = jnp.max(scores, axis=1, keepdims=True)
    powers = jnp.exp2(scores - highest)
    return highest, powers, highest + jnp.log2(jnp.sum(powers, axis=1, keepdims=True))


def wide(ref):
    return jnp.concatenate([ref[c : c + 1, :] for c in range(groups_of(ref))], axis=1)


def load_rows(score_hbm, tile_ref, sem, group):
    copy = pltpu.make_async_copy(
        score_hbm.at[pl.ds(pl.multiple_of(group * LANES, LANES), LANES), :], tile_ref, sem
    )
    copy.start()
    copy.wait()


def slow_row_logs(score_hbm, tile_ref, sem, col_ref, out_ref):
    @pl.loop(0, groups_of(out_ref))
    def _(group):
        load_rows(score_hbm, tile_ref, sem, group)
        logs = []
        for q in range(LANES // STRIP):
            logs.append(strip_logs(tile_ref[q * STRIP : (q + 1) * STRIP, :] + wide(col_ref))[2])
        out_ref[pl.ds(group, 1), :] = to_row(jnp.concatenate(logs, axis=0))


def slow_col_logs(score_hbm, tile_ref, sem, row_ref, out_ref):
    count = groups_of(out_ref)
    tops = tuple(jnp.full((1, LANES), -1e30, F32) for _ in range(count))

    def highest(group, tops):
        load_rows(score_hbm, tile_ref, sem, group)
        column = to_column(row_ref[pl.ds(group, 1), :])
        return tuple(
            jnp.maximum(
                tops[c],
                jnp.max(
                    tile_ref[:, c * LANES : (c + 1) * LANES] + column, axis=0, keepdims=True
                ),
            )
            for c in range(count)
        )

    tops = lax.fori_loop(0, groups_of(row_ref), highest, tops)
    sums = tuple(jnp.zeros((1, LANES), F32) for _ in range(count))

    def summed(group, sums):
        load_rows(score_hbm, tile_ref, sem, group)
        column = to_column(row_ref[pl.ds(group, 1), :])
        return tuple(
            sums[c]
            + jnp.sum(
                jnp.exp2(tile_ref[:, c * LANES : (c + 1) * LANES] + column - tops[c]),
                axis=0,
                keepdims=True,
            )
            for c in range(count)
        )

    sums = lax.fori_loop(0, groups_of(row_ref), summed, sums)
    for c in range(count):
        out_ref[c : c + 1, :] = tops[c] + jnp.log2(sums[c])


def slow_row_weighted(score_hbm, tile_ref, sem, row_ref, col_ref, weight_ref, out_ref):
    @pl.loop(0, groups_of(out_ref))
    def _(group):
        load_rows(score_hbm, tile_ref, sem, group)
        column = to_column(row_ref[pl.ds(group, 1), :])
        sums = []
        for q in range(LANES // STRIP):
            part = slice(q * STRIP, (q + 1) * STRIP)
            plan = jnp.exp2(tile_ref[part, :] + column[part] + wide(col_ref))
            sums.append(jnp.sum(plan * wide(weight_ref), axis=1, keepdims=True))
        out_ref[pl.ds(group, 1), :] = to_row(jnp.concatenate(sums, axis=0))


def slow_col_weighted(score_hbm, tile_ref, sem, row_ref, col_ref, weight_ref, out_ref):
    count = groups_of(out_ref)
    sums = tuple(jnp.zeros((1, LANES), F32) for _ in range(count))

    def summed(group, sums):
        load_rows(score_hbm, tile_ref, sem, group)
        column = to_column(row_ref[pl.ds(group, 1), :])
        weight = to_column(weight_ref[pl.ds(group, 1), :])
        return tuple(
            sums[c]
            + jnp.sum(
                weight
                * jnp.exp2(
                    tile_ref[:, c * LANES : (c + 1) * LANES] + column + col_ref[c : c + 1, :]
                ),
                axis=0,
                keepdims=True,
            )
            for c in range(count)
        )

    sums = lax.fori_loop(0, groups_of(row_ref), summed, sums)
    for c in range(count):
        out_ref[c : c + 1, :] = sums[c]


def first_kernel(
    cost_hbm, src_hbm, tgt_hbm, mask_hbm, dual_hbm, score_hbm, base_ref, top_ref, copies_ref,
    cost_ref, src_ref, tgt_ref, mask_ref, dual_ref, allowed_ref, log_ref, score_ref,
    small_sem, cost_sem, score_sem,
):
    small = [
        pltpu.make_async_copy(source, target, small_sem.at[at])
        for at, (source, target) in enumerate(
            ((tgt_hbm, tgt_ref), (mask_hbm, mask_ref), (src_hbm, src_ref), (dual_hbm, dual_ref))
        )
    ]
    for copy in small:
        copy.start()
    blocks = []
    for s in range(groups_of(log_ref)):
        rows = pl.ds(s * LANES, LANES)
        blocks.append(
            pltpu.make_async_copy(cost_hbm.at[rows, :], cost_ref.at[rows, :], cost_sem.at[s])
        )
        blocks[-1].start()
    for copy in small:
        copy.wait()
    classes = mask_ref.shape[0]
    mask = mask_ref[...].astype(F32).astype(jnp.bfloat16)
    ids = lax.broadcasted_iota(jnp.int32, (classes, LANES), 0)
    hot = jnp.concatenate(
        [
            jnp.where(tgt_ref[c : c + 1, :] == ids, 1.0, 0.0).astype(jnp.bfloat16)
            for c in range(groups_of(tgt_ref))
        ],
        axis=1,
    )
    allowed_of = jnp.dot(mask, hot, preferred_element_type=F32).astype(jnp.bfloat16)
    lane_ids = lax.broadcasted_iota(jnp.int32, (LANES, classes), 1).astype(F32)
    dual = wide(dual_ref) * SCALE - PENALTY * SCALE
    for s in range(groups_of(log_ref)):
        label = to_column(src_ref[s : s + 1, :].astype(F32))
        src_hot = jnp.where(label == lane_ids, 1.0, 0.0).astype(jnp.bfloat16)
        allowed_ref[...] = jnp.dot(src_hot, allowed_of, preferred_element_type=F32)
        blocks[s].wait()
        tops, logs = [], []
        for q in range(LANES // STRIP):
            rows = slice(s * LANES + q * STRIP, s * LANES + (q + 1) * STRIP)
            shifted = cost_ref[rows, :].astype(F32) - PENALTY * allowed_ref[
                q * STRIP : (q + 1) * STRIP, :
            ]
            scores = dual - shifted * SCALE
            highest, powers, log = strip_logs(scores)
            score_ref[rows, :] = scores
            base_ref[rows, :] = powers
            tops.append(highest)
            logs.append(log)
        top_ref[s : s + 1, :] = to_row(jnp.concatenate(tops, axis=0))
        log_ref[s : s + 1, :] = to_row(jnp.concatenate(logs, axis=0))
        rows = pl.ds(s * LANES, LANES)
        blocks[s] = pltpu.make_async_copy(
            score_ref.at[rows, :], score_hbm.at[rows, :], score_sem.at[s]
        )
        blocks[s].start()
    spread(copies_ref, log_ref[...])
    for copy in blocks:
        copy.wait()


def rebase_kernel(
    log_target, parts_ref, score_hbm, base_ref, top_ref, dual_ref, copies_ref, log_ref, score_ref,
    score_sem,
):
    blocks = []
    for s in range(groups_of(log_ref)):
        rows = pl.ds(s * LANES, LANES)
        blocks.append(
            pltpu.make_async_copy(score_hbm.at[rows, :], score_ref.at[rows, :], score_sem.at[s])
        )
        blocks[-1].start()
    dual_ref[...] = log_target - log_combined(parts_ref[...])
    dual = wide(dual_ref)
    for s in range(groups_of(log_ref)):
        blocks[s].wait()
        tops, logs = [], []
        for q in range(LANES // STRIP):
            rows = slice(s * LANES + q * STRIP, s * LANES + (q + 1) * STRIP)
            highest, powers, log = strip_logs(score_ref[rows, :] + dual)
            base_ref[rows, :] = powers
            tops.append(highest)
            logs.append(log)
        top_ref[s : s + 1, :] = to_row(jnp.concatenate(tops, axis=0))
        log_ref[s : s + 1, :] = to_row(jnp.concatenate(logs, axis=0))
    spread(copies_ref, log_ref[...])


def row_log_kernel(
    log_target, parts_ref, top_ref, base_dual_ref, base_ref, score_hbm, dual_ref, copies_ref,
    weight_ref, sum_ref, tile_ref, sem,
):
    dual_ref[...] = log_target - log_combined(parts_ref[...])
    lead = dual_ref[...] - base_dual_ref[...]
    near = jnp.max(jnp.abs(lead)) <= REACH

    @pl.when(near)
    def _():
        weight_ref[...] = jnp.exp2(lead)
        row_sums(base_ref, weight_ref, sum_ref)
        sum_ref[...] = top_ref[...] + jnp.log2(sum_ref[...])

    @pl.when(jnp.logical_not(near))
    def _():
        slow_row_logs(score_hbm, tile_ref, sem, dual_ref, sum_ref)

    spread(copies_ref, sum_ref[...])


def col_log_kernel(
    log_source, parts_ref, top_ref, base_dual_ref, base_ref, score_hbm, dual_ref, copies_ref,
    weight_ref, sum_ref, tile_ref, sem,
):
    dual_ref[...] = log_source - log_combined(parts_ref[...])
    lead = dual_ref[...] + top_ref[...]
    weight_ref[...] = jnp.exp2(jnp.minimum(lead, 100.0))
    col_sums(base_ref, weight_ref, sum_ref)
    most = jnp.max(lead)
    near = jnp.logical_and(
        most <= 60.0,
        jnp.min(jnp.log2(jnp.maximum(sum_ref[...], 1e-37))) >= jnp.maximum(most, -15.0) - 85.0,
    )

    @pl.when(near)
    def _():
        sum_ref[...] = jnp.log2(sum_ref[...]) - base_dual_ref[...]

    @pl.when(jnp.logical_not(near))
    def _():
        slow_col_logs(score_hbm, tile_ref, sem, dual_ref, sum_ref)

    spread(copies_ref, sum_ref[...])


def row_plan_kernel(
    log_target, first, parts_ref, grad_ref, dual_in_ref, row_dual_ref, top_ref, base_dual_ref,
    base_ref, score_hbm, out_ref, copies_ref, weight_ref, col_ref, sum_ref, tile_ref, sem,
):
    if first:
        dual = log_target - log_combined(parts_ref[...])
        grad = grad_ref[...]
        out_ref[...] = dual
    else:
        dual = dual_in_ref[...]
        grad = -jnp.sum(parts_ref[...], axis=0)
        out_ref[...] = grad
    lead = dual - base_dual_ref[...]
    row_lead = row_dual_ref[...] + top_ref[...]
    near = jnp.logical_and(jnp.max(jnp.abs(lead)) <= REACH, jnp.max(row_lead) <= 60.0)

    @pl.when(near)
    def _():
        weight_ref[...] = jnp.exp2(lead - log_target) * grad
        row_sums(base_ref, weight_ref, sum_ref)
        sum_ref[...] = sum_ref[...] * jnp.exp2(row_lead)

    @pl.when(jnp.logical_not(near))
    def _():
        col_ref[...] = dual - log_target
        weight_ref[...] = grad
        slow_row_weighted(score_hbm, tile_ref, sem, row_dual_ref, col_ref, weight_ref, sum_ref)

    spread(copies_ref, sum_ref[...])


def col_plan_kernel(
    log_source, reach, parts_ref, outer_ref, dual_ref, row_dual_ref, top_ref, base_dual_ref, base_ref,
    score_hbm, out_ref, copies_ref, weight_ref, col_ref, sum_ref, tile_ref, sem,
):
    grad = outer_ref[...] - jnp.sum(parts_ref[...], axis=0)
    out_ref[...] = grad
    lead = dual_ref[...] - base_dual_ref[...]
    row_lead = row_dual_ref[...] + top_ref[...]
    near = jnp.logical_and(jnp.max(jnp.abs(lead)) <= reach, jnp.max(row_lead) <= 60.0)

    @pl.when(near)
    def _():
        weight_ref[...] = jnp.exp2(row_lead) * grad
        col_sums(base_ref, weight_ref, sum_ref)
        sum_ref[...] = sum_ref[...] * jnp.exp2(lead - log_source)

    @pl.when(jnp.logical_not(near))
    def _():
        col_ref[...] = dual_ref[...] - log_source
        weight_ref[...] = grad
        slow_col_weighted(score_hbm, tile_ref, sem, row_dual_ref, col_ref, weight_ref, sum_ref)

    spread(copies_ref, sum_ref[...])


def is_near(dual_refs, row_refs, top_ref, base_dual_ref):
    near = None
    for ref in dual_refs:
        test = jnp.max(jnp.abs(ref[...] - base_dual_ref[...])) <= REACH
        near = test if near is None else jnp.logical_and(near, test)
    for ref in row_refs:
        near = jnp.logical_and(near, jnp.max(ref[...] + top_ref[...]) <= 60.0)
    return near


def most_grad_kernel(
    log_source, log_target,
    row1, row2, row3, col1, col2, col3, fbar2, fbar3, gbar1, gbar2, gbar3, top_ref, base_ref,
    score_hbm, out_ref, rows_ref, cols_ref, tile_ref, sem,
):
    near = is_near((col2, col3), (row1, row2, row3), top_ref, col1)
    count = groups_of(col1)

    @pl.when(near)
    def _():
        for k, row in enumerate((row1, row2, row3)):
            rows_ref[k] = -jnp.exp2(row[...] + top_ref[...])
        rows_ref[3] = rows_ref[1] * fbar2[...]
        rows_ref[4] = rows_ref[2] * fbar3[...]
        leads = [jnp.zeros_like(col1), col2[...] - col1[...], col3[...] - col1[...]]
        for k, grad in enumerate((gbar1, gbar2, gbar3)):
            cols_ref[k] = jnp.exp2(leads[k] - log_target) * grad[...]
        for k in range(2):
            cols_ref[3 + k] = jnp.exp2(leads[k] - log_source)
        for s in range(groups_of(row1)):
            columns = [to_column(rows_ref[k, s : s + 1, :]) for k in range(5)]
            for q in range(LANES // STRIP):
                rows = slice(s * LANES + q * STRIP, s * LANES + (q + 1) * STRIP)
                strips = [
                    jnp.broadcast_to(part[q * STRIP : (q + 1) * STRIP], (STRIP, LANES))
                    for part in columns
                ]
                for c in range(count):
                    lanes = slice(c * LANES, (c + 1) * LANES)
                    weight = strips[0] * cols_ref[0, c : c + 1, :]
                    for k in range(1, 5):
                        weight = weight + strips[k] * cols_ref[k, c : c + 1, :]
                    out_ref[rows, lanes] = base_ref[rows, lanes] * weight

    @pl.when(jnp.logical_not(near))
    def _():
        for k, row in enumerate((row1, row2, row3)):
            rows_ref[k] = row[...]
        rows_ref[3] = fbar2[...]
        rows_ref[4] = fbar3[...]
        for k, col in enumerate((col1, col2, col3)):
            cols_ref[k] = col[...]
        for k, grad in enumerate((gbar1, gbar2, gbar3)):
            cols_ref[3 + k] = grad[...]

        @pl.loop(0, groups_of(row1))
        def _(group):
            load_rows(score_hbm, tile_ref, sem, group)
            columns = [to_column(rows_ref[k, pl.ds(group, 1), :]) for k in range(5)]
            for c in range(count):
                lanes = slice(c * LANES, (c + 1) * LANES)
                value = jnp.zeros((LANES, LANES), F32)
                for k in reversed(range(3)):
                    scores = tile_ref[:, lanes] + columns[k]
                    plan_q = jnp.exp2(scores + (cols_ref[k, c : c + 1, :] - log_target))
                    value = value + plan_q * cols_ref[3 + k, c : c + 1, :]
                    if k:
                        plan_r = jnp.exp2(scores + (cols_ref[k - 1, c : c + 1, :] - log_source))
                        value = value + plan_r * columns[2 + k]
                start = pl.multiple_of(group * LANES, LANES)
                out_ref[pl.ds(start, LANES), lanes] = -value


def direction(place_ref):
    return 1 - 2 * place_ref[3]


def ring_place(place_ref, axis, offset, count):
    return lax.rem(place_ref[axis] + direction(place_ref) * offset + count, count)


def z_block(place_ref, src_ref, grad_ref, offset, counts):
    x_count, z_count = counts
    width, half = src_ref.shape[0], grad_ref.shape[1] // 2
    owned = width // (x_count * z_count)
    at = ring_place(place_ref, 2, offset, z_count)
    rows = [
        src_ref[pl.ds(pl.multiple_of((x * z_count + at) * owned, owned), owned), :]
        for x in range(x_count)
    ]
    return jnp.dot(
        jnp.concatenate(rows, axis=0), grad_ref[:, half:], preferred_element_type=F32
    )


def x_block(place_ref, src_ref, grad_ref, offset, counts):
    x_count = counts[0]
    width, half = src_ref.shape[0], grad_ref.shape[1] // 2
    owned = width // x_count
    at = ring_place(place_ref, 0, offset, x_count)
    rows = src_ref[pl.ds(pl.multiple_of(at * owned, owned), owned), :]
    return jnp.dot(rows, grad_ref[:, :half], preferred_element_type=F32)


def grad_kernel(
    log_source, counts, place_ref, parts_ref, row1, col1, top_ref, base_ref, most_ref, src_ref,
    score_hbm, out_ref, z_far_ref, x_far_ref, rows_ref, cols_ref, tile_ref, sem,
):
    fbar1 = -jnp.sum(parts_ref[...], axis=0)
    row_lead = row1[...] + top_ref[...]
    near = jnp.logical_and(jnp.max(jnp.abs(col1[...])) <= FIRST_REACH, jnp.max(row_lead) <= 60.0)

    @pl.when(near)
    def _():
        rows_ref[...] = -jnp.exp2(row_lead) * fbar1
        cols_ref[...] = jnp.exp2(-col1[...] - log_source)
        for s in range(groups_of(row1)):
            column = jnp.broadcast_to(to_column(rows_ref[s : s + 1, :]), (LANES, LANES))
            rows = slice(s * LANES, (s + 1) * LANES)
            for c in range(groups_of(col1)):
                lanes = slice(c * LANES, (c + 1) * LANES)
                term = base_ref[rows, lanes] * (column * cols_ref[c : c + 1, :])
                out_ref[rows, lanes] = (most_ref[rows, lanes] + term).astype(jnp.bfloat16)

    @pl.when(jnp.logical_not(near))
    def _():
        rows_ref[...] = -fbar1

        @pl.loop(0, groups_of(row1))
        def _(group):
            load_rows(score_hbm, tile_ref, sem, group)
            column = to_column(row1[pl.ds(group, 1), :]) - log_source
            weight = to_column(rows_ref[pl.ds(group, 1), :])
            rows = pl.ds(pl.multiple_of(group * LANES, LANES), LANES)
            term = jnp.exp2(tile_ref[...] + column) * weight
            out_ref[rows, :] = (most_ref[rows, :] + term).astype(jnp.bfloat16)

    z_far_ref[...] = z_block(place_ref, src_ref, out_ref, counts[1] // 2, counts)
    x_far_ref[...] = x_block(place_ref, src_ref, out_ref, counts[0] // 2, counts)


def x_part_kernel(y_count, place_ref, grad_ref, tgt_ref, sent_ref, kept_ref, order_ref):
    block = tgt_ref.shape[0] // (2 * y_count)
    core, turn = place_ref[3], direction(place_ref)
    for side, out_ref in ((0, sent_ref), (1, kept_ref)):
        for k, offset in enumerate((2, 1, -1, 0)):
            step = offset * (2 * side - 1)
            at = lax.rem(place_ref[1] + turn * step + y_count, y_count)
            owner = at * 2 + (core if side else 1 - core)
            order_ref[k * block : (k + 1) * block, :] = tgt_ref[
                pl.ds(pl.multiple_of(owner * block, block), block), :
            ]
        product = lax.dot_general(
            order_ref[...], grad_ref[...], (((1,), (1,)), ((), ())), preferred_element_type=F32
        )
        out_ref[...] = product.reshape(out_ref.shape)


def y_parts_kernel(counts, place_ref, grad_ref, src_ref, after_ref, *outs):
    reach = counts[1] // 2
    offsets = [*range(reach - 1, 0, -1), *range(1 - reach, 1)]
    for out_ref, offset in zip(outs, offsets):
        out_ref[...] = z_block(place_ref, src_ref, grad_ref, offset, counts)
    for out_ref, offset in zip(outs[len(offsets) :], (1, -1, 0)):
        out_ref[...] = x_block(place_ref, src_ref, grad_ref, offset, counts)


def add_kernel(count, *refs):
    value = refs[0][...]
    for ref in refs[1:count]:
        value = value + ref[...]
    refs[-1][...] = value


def split_kernel(x_count, place_ref, own_ref, up_ref, down_ref, *outs):
    block = own_ref.shape[0] // x_count
    for out_ref, offset in zip(outs, (2, 1, -1, 0)):
        at = ring_place(place_ref, 0, offset, x_count)
        rows = pl.ds(pl.multiple_of(at * block, block), block)
        out_ref[...] = own_ref[rows, :] + up_ref[rows, :] + down_ref[rows, :]


def join_kernel(parts_ref, own_ref, up_ref, down_ref, out_ref):
    half = own_ref.shape[1]
    out_ref[:, :half] = jnp.sum(parts_ref[...], axis=0)
    out_ref[:, half:] = own_ref[...] + up_ref[...] + down_ref[...]


def call(
    kernel, arguments, outs, scratch=(), in_hbm=(), loose=(), in_smem=(), out_hbm=(), name=None
):
    specs = [
        pl.BlockSpec(
            memory_space=pltpu.HBM
            if at in in_hbm
            else pl.ANY
            if at in loose
            else pltpu.SMEM
            if at in in_smem
            else pltpu.VMEM
        )
        for at in range(len(arguments))
    ]
    arguments = [
        pltpu.with_memory_space_constraint(value, pltpu.HBM) if at in in_hbm else value
        for at, value in enumerate(arguments)
    ]
    outs = [
        pltpu.HBM(out.shape, out.dtype) if at in out_hbm else out for at, out in enumerate(outs)
    ]
    return pl.pallas_call(
        kernel,
        out_shape=outs,
        in_specs=specs,
        out_specs=[
            pl.BlockSpec(memory_space=pltpu.HBM if at in out_hbm else pltpu.VMEM)
            for at in range(len(outs))
        ],
        scratch_shapes=list(scratch),
        compiler_params=pltpu.CompilerParams(vmem_limit_bytes=VMEM_BYTES),
        name=name,
    )(*arguments)


def exchanged(copies, axis):
    return lax.all_to_all(copies, axis, 0, 0, tiled=True)


def added(values, after=()):
    return call(
        functools.partial(add_kernel, len(values)),
        (*values, *after),
        [jax.ShapeDtypeStruct(values[0].shape, F32)],
        loose=range(len(values), len(values) + len(after)),
        name="added",
    )[0]


def body(cost, src_label, tgt_label, class_mask, g_start, f_bar, g_bar, src_emb, tgt_emb):
    row_count = lax.axis_size("rows")
    col_count = lax.axis_size("cols")
    src_rows, tgt_cols = cost.shape
    width = src_emb.shape[1]
    log_source = -math.log2(src_rows * row_count)
    log_target = -math.log2(tgt_cols * col_count)
    row_shape = (src_rows // LANES, LANES)
    col_shape = (tgt_cols // LANES, LANES)
    src_label, f_bar = src_label.reshape(row_shape), f_bar.reshape(row_shape)
    tgt_label, g_bar = tgt_label.reshape(col_shape), g_bar.reshape(col_shape)
    g_start = g_start.reshape(col_shape)

    def array(shape, dtype=F32):
        return jax.ShapeDtypeStruct(shape, dtype)

    matrix = array(cost.shape)
    row_vector, col_vector = array(row_shape), array(col_shape)
    row_copies = array((col_count,) + row_shape)
    col_copies = array((row_count,) + col_shape)
    row_held, col_held = pltpu.VMEM(row_shape, F32), pltpu.VMEM(col_shape, F32)
    slow = [pltpu.VMEM((LANES, tgt_cols), F32), pltpu.SemaphoreType.DMA]

    score, start_base, start_top, copies = call(
        first_kernel,
        (cost, src_label, tgt_label, class_mask, g_start),
        [matrix, matrix, row_vector, row_copies],
        [
            pltpu.VMEM(cost.shape, cost.dtype),
            pltpu.VMEM(row_shape, jnp.int32),
            pltpu.VMEM(col_shape, jnp.int32),
            pltpu.VMEM(class_mask.shape, jnp.int32),
            col_held,
            pltpu.VMEM((LANES, tgt_cols), F32),
            row_held,
            pltpu.VMEM(cost.shape, F32),
            pltpu.SemaphoreType.DMA((4,)),
            pltpu.SemaphoreType.DMA(row_shape[:1]),
            pltpu.SemaphoreType.DMA(row_shape[:1]),
        ],
        in_hbm=range(5),
        out_hbm=(0,),
        name="first_row_logs",
    )

    def col_logs(parts, top, base_dual, base):
        return call(
            functools.partial(col_log_kernel, log_source),
            (parts, top, base_dual, base, score),
            [row_vector, col_copies],
            [row_held, col_held] + slow,
            in_hbm=(4,),
            name="col_logs",
        )

    zero = jnp.zeros(col_shape, F32)
    row1, copies = col_logs(exchanged(copies, "cols"), start_top, zero, start_base)
    base, top, col1, copies = call(
        functools.partial(rebase_kernel, log_target),
        (exchanged(copies, "rows"), score),
        [matrix, row_vector, col_vector, row_copies],
        [row_held, pltpu.VMEM(cost.shape, F32), pltpu.SemaphoreType.DMA(row_shape[:1])],
        in_hbm=(1,),
        name="second_row_logs",
    )
    row2, copies = col_logs(exchanged(copies, "cols"), top, col1, base)
    col2, copies = call(
        functools.partial(row_log_kernel, log_target),
        (exchanged(copies, "rows"), top, col1, base, score),
        [col_vector, row_copies],
        [col_held, row_held] + slow,
        in_hbm=(4,),
        name="third_row_logs",
    )
    row3, copies = col_logs(exchanged(copies, "cols"), top, col1, base)

    def row_plan(first, parts, grad, dual, row):
        return call(
            functools.partial(row_plan_kernel, log_target, first),
            (parts, grad, dual, row, top, col1, base, score),
            [col_vector, row_copies],
            [col_held, col_held, row_held] + slow,
            in_hbm=(7,),
            name="row_plan",
        )

    def col_plan(parts, outer, dual, row, top, base_dual, base, reach=REACH):
        return call(
            functools.partial(col_plan_kernel, log_source, reach),
            (parts, outer, dual, row, top, base_dual, base, score),
            [row_vector, col_copies],
            [row_held, col_held, col_held] + slow,
            in_hbm=(7,),
            name="col_plan",
        )

    none = jnp.zeros(row_shape, F32)
    src_turned, tgt_turned = src_emb.T, tgt_emb.T
    col3, copies = row_plan(True, exchanged(copies, "rows"), g_bar, col2, row3)
    fbar3, copies = col_plan(exchanged(copies, "cols"), f_bar, col2, row3, top, col1, base)
    gbar2, copies = row_plan(False, exchanged(copies, "rows"), g_bar, col2, row2)
    fbar2, copies = col_plan(exchanged(copies, "cols"), none, col1, row2, top, col1, base)
    gbar1, copies = row_plan(False, exchanged(copies, "rows"), g_bar, col1, row1)
    parts = exchanged(copies, "cols")
    (most,) = call(
        functools.partial(most_grad_kernel, log_source, log_target),
        (
            row1, row2, row3, col1, col2, col3, fbar2, fbar3, gbar1, gbar2, g_bar, top, base, score,
        ),
        [matrix],
        [pltpu.VMEM((5,) + row_shape, F32), pltpu.VMEM((6,) + col_shape, F32)] + slow,
        in_hbm=(13,),
        name="most_cost_grad",
    )
    x_count, z_count, y_count = 4, row_count // 4, col_count // 2
    counts = (x_count, z_count)
    owned = width // row_count
    row_at, col_at = lax.axis_index("rows"), lax.axis_index("cols")
    place = jnp.stack(
        [row_at // z_count, col_at // 2, row_at % z_count, col_at % 2]
    ).astype(jnp.int32)
    devices = [
        (x, y, z, core)
        for x in range(x_count)
        for y in range(y_count)
        for z in range(z_count)
        for core in range(2)
    ]

    def number(x, y, z, core):
        spot = (x % x_count * z_count + z % z_count) * y_count + y % y_count
        return spot * 2 + core

    def turn(value, axis, step):
        moves = []
        for device in devices:
            ahead = list(device)
            ahead[axis] += step * (1 - 2 * device[3])
            moves.append((number(*device), number(*ahead)))
        return lax.ppermute(value, ("rows", "cols"), moves)

    half = tgt_cols // 2
    z_shape = array((x_count * owned, half))
    x_shape = array((z_count * owned, half))
    rounded, z_far, x_far = call(
        functools.partial(grad_kernel, log_source, counts),
        (place, parts, row1, col1, top, base, most, src_turned, score),
        [array(cost.shape, jnp.bfloat16), z_shape, x_shape],
        [row_held, col_held] + slow,
        in_smem=(0,),
        in_hbm=(8,),
        name="cost_grad",
    )
    z_long = turn(z_far, 2, 1)
    x_long = turn(x_far, 0, 1)
    chip_part = array((y_count, width // col_count, src_rows))
    sent, kept = call(
        functools.partial(x_part_kernel, y_count),
        (place, rounded, tgt_turned),
        [chip_part, chip_part],
        [pltpu.VMEM((width // 2, tgt_cols), jnp.bfloat16)],
        in_smem=(0,),
        name="grad_x_parts",
    )
    arrived = lax.ppermute(sent, "cols", [(at, at ^ 1) for at in range(col_count)])
    outs = call(
        functools.partial(y_parts_kernel, counts),
        (place, rounded, src_turned, kept),
        [z_shape] * (z_count - 1) + [x_shape] * 3,
        in_smem=(0,),
        loose=(3,),
        name="grad_y_parts",
    )
    z_longs, z_shorts, z_own = outs[:3], outs[3:6], outs[6]
    x_one, x_back, x_own = outs[7:]
    x_short = turn(x_back, 0, -1)
    z_short = turn(z_shorts[0], 2, -1)
    fbar1, copies = col_plan(
        parts, none, zero, row1, top, col1, base, FIRST_REACH
    )
    start_parts = exchanged(copies, "rows")
    z_long = turn(added((z_longs[0], z_long)), 2, 1)
    chip = added((kept, arrived), (z_long,))
    y_long = turn(chip[0], 1, 1)
    x_long = turn(added((x_one, x_long)), 0, 1)
    y_short = turn(chip[2], 1, -1)
    z_short = turn(added((z_shorts[1], z_short)), 2, -1)
    z_long = turn(added((z_longs[1], z_long)), 2, 1)
    y_long = turn(added((chip[1], y_long)), 1, 1)
    z_short = turn(added((z_shorts[2], z_short)), 2, -1)
    z_long = turn(added((z_longs[2], z_long)), 2, 1)
    first = added((x_own, x_long, x_short))
    along_z = [[x * z_count + z for z in range(z_count)] for x in range(x_count)]
    first = lax.all_to_all(
        first.reshape(z_count, owned, half), "rows", 0, 0, tiled=True, axis_index_groups=along_z
    )
    last = array((owned, half))
    far, one, back, own = call(
        functools.partial(split_kernel, x_count),
        (place, z_own, z_long, z_short),
        [last] * 4,
        in_smem=(0,),
        name="second_half",
    )
    x_long = turn(far, 0, 1)
    x_short = turn(back, 0, -1)
    x_long = turn(added((one, x_long)), 0, 1)
    grad_x = added((chip[3], y_long, y_short))
    (grad_y,) = call(
        join_kernel, (first, own, x_long, x_short), [array((owned, tgt_cols))], name="grad_y"
    )
    g_start_bar = -jnp.sum(start_parts, axis=0).reshape(tgt_cols)
    return (g_start_bar, grad_x, grad_y)


def solution(mesh):
    placed = (
        P("rows", "cols"),
        P("rows"),
        P("cols"),
        P(),
        P("cols"),
        P("rows"),
        P("cols"),
        P("rows", None),
        P("cols", None),
    )
    return jax.shard_map(
        body,
        mesh=mesh,
        in_specs=placed,
        out_specs=(P("cols"), P("cols", "rows"), P("rows", "cols")),
        check_vma=False,
    )
```

profile of v0, /device:TPU:8, one launch (start us, length us, event | category | flops | bytes accessed | tf_op | source)
XLA Modules:
  0.0 275.4 jit_solution(16163565709969731129)
XLA Ops:
  0.6 5.5 %first_row_logs.1 = (f32[1024,1024]{1,0:T(8,128)}, f32[1024,1024]{1,0:T(8,128)S(1)}, f32[8,128]{1,0:T(8,128)S(1)}, f32[8,8,128]{2,1,0:T(8,128)S(1)}) custom-call(bf16[1024,1024]{1,0:T(8,128)(2,1)} %cost_hbm.1, s32[8,128]{1,0:T(8,128)} %bitcast.30, s32[8,128]{1,0:T(8,128)} %bitcast.31, s32[64,64]{1,0:T(8,128)} %mask_hbm.1, f32[8,128]{1,0:T(8,128)} %bitcast.32), custom_call_target="tpu_custom_call" | custom-call | tf_op jit(solution)/shard_map/first_row_logs/pallas_call | solution.py:582
  6.2 8.7 %all_to_all.65.parts_ref = f32[8,8,128]{2,1,0:T(8,128)S(1)} all-to-all(f32[8,8,128]{2,1,0:T(8,128)S(1)} %get-tuple-element.49), channel_id=1, replica_groups=mesh['rows'=32,'cols'=8] {'cols'}, dimensions={0} | all-to-all | bytes 65536 | tf_op jit(solution)/shard_map/all_to_all | solution.py:597
  14.9 19.5 %col_logs.3 = (f32[8,128]{1,0:T(8,128)S(1)}, f32[32,8,128]{2,1,0:T(8,128)S(1)}) custom-call(f32[8,8,128]{2,1,0:T(8,128)S(1)} %all_to_all.65.parts_ref, f32[8,128]{1,0:T(8,128)S(1)} %get-tuple-element.50.top_ref, f32[8,128]{1,0:T(8,128)S(1)} %broadcast_1_base_dual_ref_outer_ref_dual_ref.2.base_dual_ref.outer_ref.dual_ref, ...), custom_call_target="tpu_custom_call" | custom-call | tf_op jit(solution)/shard_map/col_logs/pallas_call | solution.py:582
  34.3 21.4 %all_to_all.66.parts_ref = f32[32,8,128]{2,1,0:T(8,128)S(1)} all-to-all(f32[32,8,128]{2,1,0:T(8,128)S(1)} %get-tuple-element.53), channel_id=1, replica_groups=mesh['rows'=32,'cols'=8] {'rows'}, dimensions={0} | all-to-all | bytes 262144 | tf_op jit(solution)/shard_map/all_to_all | solution.py:597
  55.8 4.0 %second_row_logs.1 = (f32[1024,1024]{1,0:T(8,128)S(1)}, f32[8,128]{1,0:T(8,128)S(1)}, f32[8,128]{1,0:T(8,128)S(1)}, f32[8,8,128]{2,1,0:T(8,128)S(1)}) custom-call(f32[32,8,128]{2,1,0:T(8,128)S(1)} %all_to_all.66.parts_ref, f32[1024,1024]{1,0:T(8,128)} %get-tuple-element.52.score_hbm), custom_call_target="tpu_custom_call" | custom-call | tf_op jit(solution)/shard_map/second_row_logs/pallas_call | solution.py:582
  59.8 7.8 %all_to_all.67.parts_ref = f32[8,8,128]{2,1,0:T(8,128)S(1)} all-to-all(f32[8,8,128]{2,1,0:T(8,128)S(1)} %get-tuple-element.54), channel_id=1, replica_groups=mesh['rows'=32,'cols'=8] {'cols'}, dimensions={0} | all-to-all | bytes 65536 | tf_op jit(solution)/shard_map/all_to_all | solution.py:597
  67.6 0.6 col_logs.4
  68.2 13.9 %all_to_all.68.parts_ref = f32[32,8,128]{2,1,0:T(8,128)S(1)} all-to-all(f32[32,8,128]{2,1,0:T(8,128)S(1)} %get-tuple-element.58), channel_id=1, replica_groups=mesh['rows'=32,'cols'=8] {'rows'}, dimensions={0} | all-to-all | bytes 262144 | tf_op jit(solution)/shard_map/all_to_all | solution.py:597
  82.1 0.6 third_row_logs.1
  82.7 7.8 %all_to_all.69.parts_ref = f32[8,8,128]{2,1,0:T(8,128)S(1)} all-to-all(f32[8,8,128]{2,1,0:T(8,128)S(1)} %get-tuple-element.59), channel_id=1, replica_groups=mesh['rows'=32,'cols'=8] {'cols'}, dimensions={0} | all-to-all | bytes 65536 | tf_op jit(solution)/shard_map/all_to_all | solution.py:597
  90.5 0.6 col_logs.5
  91.2 13.9 %all_to_all.70.parts_ref = f32[32,8,128]{2,1,0:T(8,128)S(1)} all-to-all(f32[32,8,128]{2,1,0:T(8,128)S(1)} %get-tuple-element.60), channel_id=1, replica_groups=mesh['rows'=32,'cols'=8] {'rows'}, dimensions={0} | all-to-all | bytes 262144 | tf_op jit(solution)/shard_map/all_to_all | solution.py:597
  105.0 0.6 row_plan.3
  105.6 7.8 %all_to_all.71.parts_ref = f32[8,8,128]{2,1,0:T(8,128)S(1)} all-to-all(f32[8,8,128]{2,1,0:T(8,128)S(1)} %get-tuple-element.63), channel_id=1, replica_groups=mesh['rows'=32,'cols'=8] {'cols'}, dimensions={0} | all-to-all | bytes 65536 | tf_op jit(solution)/shard_map/all_to_all | solution.py:597
  114.0 13.9 %all_to_all.72.parts_ref = f32[32,8,128]{2,1,0:T(8,128)S(1)} all-to-all(f32[32,8,128]{2,1,0:T(8,128)S(1)} %get-tuple-element.64), channel_id=1, replica_groups=mesh['rows'=32,'cols'=8] {'rows'}, dimensions={0} | all-to-all | bytes 262144 | tf_op jit(solution)/shard_map/all_to_all | solution.py:597
  128.4 7.8 %all_to_all.73.parts_ref = f32[8,8,128]{2,1,0:T(8,128)S(1)} all-to-all(f32[8,8,128]{2,1,0:T(8,128)S(1)} %get-tuple-element.66), channel_id=1, replica_groups=mesh['rows'=32,'cols'=8] {'cols'}, dimensions={0} | all-to-all | bytes 65536 | tf_op jit(solution)/shard_map/all_to_all | solution.py:597
  136.2 1.2 col_plan.4
  137.4 4.1 %all-to-all-start.9 = ((f32[32,8,128]{2,1,0:T(8,128)}), f32[32,8,128]{2,1,0:T(8,128)S(1)}, u32[]{:S(2)}, u32[]{:S(2)}) async-start(f32[32,8,128]{2,1,0:T(8,128)} %get-tuple-element.67), calls=%async_computation.9 | async-start | bytes 262144 | tf_op jit(solution)/shard_map/all_to_all | solution.py:597
  141.5 10.4 %all-to-all-done.9.parts_ref = f32[32,8,128]{2,1,0:T(8,128)S(1)} async-done(((f32[32,8,128]{2,1,0:T(8,128)}), f32[32,8,128]{2,1,0:T(8,128)S(1)}, u32[]{:S(2)}, u32[]{:S(2)}) %all-to-all-start.9) | async-done | bytes 131104 | tf_op jit(solution)/shard_map/all_to_all | solution.py:597
  152.0 2.2 copy-done.1
  154.2 1.2 row_plan.5
  155.3 4.7 %all-to-all-start.10 = ((f32[8,8,128]{2,1,0:T(8,128)}), f32[8,8,128]{2,1,0:T(8,128)S(1)}, u32[]{:S(2)}, u32[]{:S(2)}) async-start(f32[8,8,128]{2,1,0:T(8,128)} %get-tuple-element.69), calls=%async_computation.10 | async-start | bytes 65536 | tf_op jit(solution)/shard_map/all_to_all | solution.py:597
  160.1 2.9 %copy.12 = bf16[1024,1024]{0,1:T(8,128)(2,1)S(1)} copy(bf16[1024,1024]{1,0:T(8,128)(2,1)} %param.16) | data formatting | bytes 4194304 | tf_op args[7]
  163.0 4.0 %copy.13 = bf16[1024,1024]{0,1:T(8,128)(2,1)} copy(bf16[1024,1024]{1,0:T(8,128)(2,1)} %param.17) | data formatting | bytes 4194304 | tf_op args[8]
  167.0 2.2 copy-done.2
  169.1 2.2 most_cost_grad.1.most_ref
  171.4 2.1 copy-done.5
  173.4 2.2 copy-done.3
  175.6 2.2 copy-done.6
  177.8 11.1 %cost_grad.1 = (bf16[1024,1024]{1,0:T(8,128)(2,1)S(1)}, f32[128,512]{1,0:T(8,128)S(1)}, f32[256,512]{1,0:T(8,128)S(1)}) custom-call(s32[4]{0:T(128)S(1)} %pad_add_fusion.place_ref, f32[8,8,128]{2,1,0:T(8,128)S(1)} %all-to-all-done.10.parts_ref, f32[8,128]{1,0:T(8,128)S(1)} %get-tuple-element.68.row_dual_ref.row1, ...), custom_call_target="tpu_custom_call" | custom-call | tf_op jit(solution)/shard_map/cost_grad/pallas_call | solution.py:582
  188.9 3.1 %grad_x_parts.1 = (f32[4,128,1024]{2,1,0:T(8,128)}, f32[4,128,1024]{2,1,0:T(8,128)S(1)}) custom-call(s32[4]{0:T(128)S(1)} %pad_add_fusion.place_ref, bf16[1024,1024]{1,0:T(8,128)(2,1)S(1)} %get-tuple-element.76.grad_ref, bf16[1024,1024]{1,0:T(8,128)(2,1)S(1)} %bitcast.24), custom_call_target="tpu_custom_call" | custom-call | tf_op jit(solution)/shard_map/grad_x_parts/pallas_call | solution.py:582
  192.0 0.6 collective-permute-start.6
  192.6 1.2 collective-permute-start.1
  193.9 3.1 %grad_y_parts.1 = (f32[128,512]{1,0:T(8,128)S(1)}, f32[128,512]{1,0:T(8,128)S(1)}, f32[128,512]{1,0:T(8,128)S(1)}, f32[128,512]{1,0:T(8,128)S(1)}, f32[128,512]{...) custom-call(s32[4]{0:T(128)S(1)} %pad_add_fusion.place_ref, ...), custom_call_target="tpu_custom_call" | custom-call | tf_op jit(solution)/shard_map/grad_y_parts/pallas_call | solution.py:582
  197.0 3.2 %collective-permute-done.1.refs_1_ = f32[128,512]{1,0:T(8,128)S(1)} collective-permute-done((f32[128,512]{1,0:T(8,128)S(1)}, f32[128,512]{1,0:T(8,128)S(1)}, u32[]{:S(2)}, u32[]{:S(2)}) %collective-permute-start.1) | collective-permute-done | bytes 262176 | tf_op jit(solution)/shard_map/ppermute | solution.py:749
  200.2 0.7 added.11
  201.0 2.6 collective-permute-start.8
  203.8 10.6 %col_plan.5 = (f32[8,128]{1,0:T(8,128)}, f32[32,8,128]{2,1,0:T(8,128)S(1)}) custom-call(f32[8,8,128]{2,1,0:T(8,128)S(1)} %all-to-all-done.10.parts_ref, f32[8,128]{1,0:T(8,128)S(1)} %broadcast_1_base_dual_ref_outer_ref_dual_ref.2.base_dual_ref.outer_ref.dual_ref, f32[8,128]{1,0:T(8,128)S(1)} %broadcast_1_base_dual_ref_outer_ref_dual_ref.2.base_dual_ref.outer_ref.dual_ref, ...), custom_call_target="tpu_custom_call" | custom-call | tf_op jit(solution)/shard_map/col_plan/pallas_call | solution.py:582
  214.4 0.6 copy-done.20
  215.1 7.5 %all-to-all-start.11 = ((f32[32,8,128]{2,1,0:T(8,128)}), f32[32,8,128]{2,1,0:T(8,128)}, u32[]{:S(2)}, u32[]{:S(2)}) async-start(f32[32,8,128]{2,1,0:T(8,128)} %copy-done.20), calls=%async_computation.11 | async-start | bytes 262144 | tf_op jit(solution)/shard_map/all_to_all | solution.py:597
  222.6 3.0 %collective-permute-start.11 = (f32[128,512]{1,0:T(8,128)}, f32[128,512]{1,0:T(8,128)}, u32[]{:S(2)}, u32[]{:S(2)}) collective-permute-start(f32[128,512]{1,0:T(8,128)} %copy-done.23), channel_id=1, source_target_pairs={{0,56},{1,9},{8,0},{9,17},{16,8},{17,25},{24,16},{25,33},{32,24},{... | collective-permute-start | bytes 786440 | tf_op jit(solution)/shard_map/ppermute | solution.py:749
  225.6 1.8 added.12
  227.4 1.2 slice_bitcast_fusion
  228.7 1.6 collective-permute-start.3
  230.3 2.1 added.16
  232.9 4.2 %all-to-all-start.12 = ((f32[8,32,512]{2,1,0:T(8,128)}), f32[8,32,512]{2,1,0:T(8,128)S(1)}, u32[]{:S(2)}, u32[]{:S(2)}) async-start(f32[8,32,512]{2,1,0:T(8,128)} %bitcast.16), calls=%async_computation.12 | async-start | bytes 1048576 | tf_op jit(solution)/shard_map/all_to_all | solution.py:803
  237.1 0.9 copy-done.17
  238.1 1.0 added.19
  239.1 3.3 %collective-permute-start.12 = (f32[128,512]{1,0:T(8,128)S(1)}, f32[128,512]{1,0:T(8,128)S(1)}, u32[]{:S(2)}, u32[]{:S(2)}) collective-permute-start(f32[128,512]{1,0:T(8,128)S(1)} %added.19), channel_id=1, source_target_pairs={{0,56},{1,9},{8,0},{9,17},{16,8},{17,25},{24,16},{25,33},{32,24},{... | collective-permute-start | bytes 786440 | tf_op jit(solution)/shard_map/ppermute | solution.py:749
  242.4 0.9 copy-done.15
  243.5 8.7 %collective-permute-done.12.refs_1_ = f32[128,512]{1,0:T(8,128)S(1)} collective-permute-done((f32[128,512]{1,0:T(8,128)S(1)}, f32[128,512]{1,0:T(8,128)S(1)}, u32[]{:S(2)}, u32[]{:S(2)}) %collective-permute-start.12) | collective-permute-done | bytes 262176 | tf_op jit(solution)/shard_map/ppermute | solution.py:749
  252.2 2.2 collective-permute-start.13
  254.5 0.9 collective-permute-start.5
  255.5 1.3 collective-permute-start.4
  256.8 1.9 collective-permute-done.13.down_ref
  258.6 3.5 %collective-permute-done.10.up_ref = f32[128,512]{1,0:T(8,128)S(1)} collective-permute-done((f32[128,512]{1,0:T(8,128)S(1)}, f32[128,512]{1,0:T(8,128)S(1)}, u32[]{:S(2)}, u32[]{:S(2)}) %collective-permute-start.10) | collective-permute-done | bytes 262176 | tf_op jit(solution)/shard_map/ppermute | solution.py:749
  262.7 1.5 collective-permute-start.14
  264.2 0.9 reduce_sum.9
  265.2 1.8 collective-permute-start.16
  267.0 1.2 collective-permute-done.14.refs_1_
  268.6 0.6 negate_bitcast_fusion
  269.5 4.3 %collective-permute-done.15.up_ref = f32[32,512]{1,0:T(8,128)S(1)} collective-permute-done((f32[32,512]{1,0:T(8,128)S(1)}, f32[32,512]{1,0:T(8,128)S(1)}, u32[]{:S(2)}, u32[]{:S(2)}) %collective-permute-start.15) | collective-permute-done | bytes 65568 | tf_op jit(solution)/shard_map/ppermute | solution.py:749
  273.8 0.7 grad_y.1
  274.5 0.9 added.14
  (71 shorter events, 3.5 us)
Async XLA Ops:
  59.8 76.5 %copy-start = (f32[1024,1024]{1,0:T(8,128)}, f32[1024,1024]{1,0:T(8,128)S(1)}, u32[]{:S(2)}) copy-start(f32[1024,1024]{1,0:T(8,128)S(1)} %get-tuple-element.57.base_ref) | copy-start | bytes 12582916
  90.5 14.5 %copy-start.21 = (f32[1024]{0:T(1024)S(1)}, f32[1024]{0:T(1024)}, u32[]{:S(2)}) copy-start(f32[1024]{0:T(1024)} %param.15) | copy-start | bytes 12292
  105.0 8.4 %copy-start.22 = (f32[1024]{0:T(1024)S(1)}, f32[1024]{0:T(1024)}, u32[]{:S(2)}) copy-start(f32[1024]{0:T(1024)} %param.14) | copy-start | bytes 12292
  137.4 14.5 %all-to-all-start.9 = ((f32[32,8,128]{2,1,0:T(8,128)}), f32[32,8,128]{2,1,0:T(8,128)S(1)}, u32[]{:S(2)}, u32[]{:S(2)}) async-start(f32[32,8,128]{2,1,0:T(8,128)} %get-tuple-element.67), calls=%async_computation.9 | async-start | bytes 262144 | tf_op jit(solution)/shard_map/all_to_all | solution.py:597
  152.0 2.2 copy-start.1
  155.3 18.1 %all-to-all-start.10 = ((f32[8,8,128]{2,1,0:T(8,128)}), f32[8,8,128]{2,1,0:T(8,128)S(1)}, u32[]{:S(2)}, u32[]{:S(2)}) async-start(f32[8,8,128]{2,1,0:T(8,128)} %get-tuple-element.69), calls=%async_computation.10 | async-start | bytes 65536 | tf_op jit(solution)/shard_map/all_to_all | solution.py:597
  167.0 2.2 copy-start.2
  171.3 2.1 copy-start.5
  173.4 2.2 copy-start.3
  175.6 2.2 copy-start.6
  177.8 11.1 %copy-start.9 = (bf16[1024,1024]{0,1:T(8,128)(2,1)S(1)}, bf16[1024,1024]{0,1:T(8,128)(2,1)}, u32[]{:S(2)}) copy-start(bf16[1024,1024]{0,1:T(8,128)(2,1)} %copy.13) | copy-start | bytes 6291460
  192.0 5.0 %copy-start.7 = (f32[4,128,1024]{2,1,0:T(8,128)}, f32[4,128,1024]{2,1,0:T(8,128)S(1)}, u32[]{:S(2)}) copy-start(f32[4,128,1024]{2,1,0:T(8,128)S(1)} %get-tuple-element.77.after_ref.refs_0_) | copy-start | bytes 6291460
  192.0 33.6 %collective-permute-start = (f32[4,128,1024]{2,1,0:T(8,128)}, f32[4,128,1024]{2,1,0:T(8,128)}, u32[]{:S(2)}, u32[]{:S(2)}) collective-permute-start(f32[4,128,1024]{2,1,0:T(8,128)} %get-tuple-element.78), channel_id=1, source_target_pairs={{0,1},{1,0},{2,3},{3,2},{4,5},{5,4},{6,7},{7,6},{8,9},{9,8},{10,11... | collective-permute-start | bytes 6291464 | tf_op jit(solution)/shard_map/ppermute | solution.py:774
  192.0 11.6 %collective-permute-start.6 = (f32[256,512]{1,0:T(8,128)S(1)}, f32[256,512]{1,0:T(8,128)S(1)}, u32[]{:S(2)}, u32[]{:S(2)}) collective-permute-start(f32[256,512]{1,0:T(8,128)S(1)} %get-tuple-element.83), channel_id=1, source_target_pairs={{0,64},{1,193},{8,72},{9,201},{16,80},{17,209},{24,88},{25,217},{3... | collective-permute-start | bytes 1572872 | tf_op jit(solution)/shard_map/ppermute | solution.py:749
  192.6 7.6 %collective-permute-start.1 = (f32[128,512]{1,0:T(8,128)S(1)}, f32[128,512]{1,0:T(8,128)S(1)}, u32[]{:S(2)}, u32[]{:S(2)}) collective-permute-start(f32[128,512]{1,0:T(8,128)S(1)} %get-tuple-element.80), channel_id=1, source_target_pairs={{0,8},{1,57},{8,16},{9,1},{16,24},{17,9},{24,32},{25,17},{32,40},{... | collective-permute-start | bytes 786440 | tf_op jit(solution)/shard_map/ppermute | solution.py:749
  193.9 9.9 %copy-start.4 = (f32[1024,1024]{1,0:T(8,128)S(1)}, f32[1024,1024]{1,0:T(8,128)}, u32[]{:S(2)}) copy-start(f32[1024,1024]{1,0:T(8,128)} %copy-done) | copy-start | bytes 12582916
  197.0 6.7 %copy-start.23 = (f32[128,512]{1,0:T(8,128)}, f32[128,512]{1,0:T(8,128)S(1)}, u32[]{:S(2)}) copy-start(f32[128,512]{1,0:T(8,128)S(1)} %get-tuple-element.90) | copy-start | bytes 786436
  197.0 17.4 %copy-start.10 = (f32[128,512]{1,0:T(8,128)}, f32[128,512]{1,0:T(8,128)S(1)}, u32[]{:S(2)}) copy-start(f32[128,512]{1,0:T(8,128)S(1)} %get-tuple-element.86.refs_0_) | copy-start | bytes 786436
  197.0 17.4 %copy-start.12 = (f32[128,512]{1,0:T(8,128)}, f32[128,512]{1,0:T(8,128)S(1)}, u32[]{:S(2)}) copy-start(f32[128,512]{1,0:T(8,128)S(1)} %get-tuple-element.88.refs_0_) | copy-start | bytes 786436
  197.0 17.4 %copy-start.14 = (f32[128,512]{1,0:T(8,128)}, f32[128,512]{1,0:T(8,128)S(1)}, u32[]{:S(2)}) copy-start(f32[128,512]{1,0:T(8,128)S(1)} %get-tuple-element.87.refs_0_) | copy-start | bytes 786436
  197.0 17.4 %copy-start.16 = (f32[128,512]{1,0:T(8,128)}, f32[128,512]{1,0:T(8,128)S(1)}, u32[]{:S(2)}) copy-start(f32[128,512]{1,0:T(8,128)S(1)} %get-tuple-element.89.refs_0_) | copy-start | bytes 786436
  197.0 17.4 %copy-start.18 = (f32[128,512]{1,0:T(8,128)}, f32[128,512]{1,0:T(8,128)S(1)}, u32[]{:S(2)}) copy-start(f32[128,512]{1,0:T(8,128)S(1)} %get-tuple-element.85.own_ref) | copy-start | bytes 786436
  201.0 24.7 %collective-permute-start.2 = (f32[128,512]{1,0:T(8,128)}, f32[128,512]{1,0:T(8,128)S(1)}, u32[]{:S(2)}, u32[]{:S(2)}) collective-permute-start(f32[128,512]{1,0:T(8,128)} %added.11), channel_id=1, source_target_pairs={{0,8},{1,57},{8,16},{9,1},{16,24},{17,9},{24,32},{25,17},{32,40},{... | collective-permute-start | bytes 786440 | tf_op jit(solution)/shard_map/ppermute | solution.py:749
  201.0 29.3 %collective-permute-start.8 = (f32[256,512]{1,0:T(8,128)}, f32[256,512]{1,0:T(8,128)}, u32[]{:S(2)}, u32[]{:S(2)}) collective-permute-start(f32[256,512]{1,0:T(8,128)} %get-tuple-element.84), channel_id=1, source_target_pairs={{0,192},{1,65},{8,200},{9,73},{16,208},{17,81},{24,216},{25,89},{3... | collective-permute-start | bytes 1572872 | tf_op jit(solution)/shard_map/ppermute | solution.py:749
  203.7 22.0 %copy-start.8 = (f32[4,128,1024]{2,1,0:T(8,128)S(1)}, f32[4,128,1024]{2,1,0:T(8,128)}, u32[]{:S(2)}) copy-start(f32[4,128,1024]{2,1,0:T(8,128)} %copy-done.7) | copy-start | bytes 6291460
  203.7 26.6 %collective-permute-start.7 = (f32[256,512]{1,0:T(8,128)S(1)}, f32[256,512]{1,0:T(8,128)}, u32[]{:S(2)}, u32[]{:S(2)}) collective-permute-start(f32[256,512]{1,0:T(8,128)S(1)} %added.15), channel_id=1, source_target_pairs={{0,64},{1,193},{8,72},{9,201},{16,80},{17,209},{24,88},{25,217},{3... | collective-permute-start | bytes 1572872 | tf_op jit(solution)/shard_map/ppermute | solution.py:749
  214.4 0.7 copy-start.20
  215.1 17.8 %all-to-all-start.11 = ((f32[32,8,128]{2,1,0:T(8,128)}), f32[32,8,128]{2,1,0:T(8,128)}, u32[]{:S(2)}, u32[]{:S(2)}) async-start(f32[32,8,128]{2,1,0:T(8,128)} %copy-done.20), calls=%async_computation.11 | async-start | bytes 262144 | tf_op jit(solution)/shard_map/all_to_all | solution.py:597
  222.6 14.5 %collective-permute-start.11 = (f32[128,512]{1,0:T(8,128)}, f32[128,512]{1,0:T(8,128)}, u32[]{:S(2)}, u32[]{:S(2)}) collective-permute-start(f32[128,512]{1,0:T(8,128)} %copy-done.23), channel_id=1, source_target_pairs={{0,56},{1,9},{8,0},{9,17},{16,8},{17,25},{24,16},{25,33},{32,24},{... | collective-permute-start | bytes 786440 | tf_op jit(solution)/shard_map/ppermute | solution.py:749
  228.7 26.7 %collective-permute-start.3 = (f32[128,1024]{1,0:T(8,128)}, f32[128,1024]{1,0:T(8,128)S(1)}, u32[]{:S(2)}, u32[]{:S(2)}) collective-permute-start(f32[128,1024]{1,0:T(8,128)} %get-tuple-element.96), channel_id=1, source_target_pairs={{0,2},{1,7},{8,10},{9,15},{16,18},{17,23},{24,26},{25,31},{32,34},... | collective-permute-start | bytes 1572872 | tf_op jit(solution)/shard_map/ppermute | solution.py:749
  230.3 21.9 %copy-start.13 = (f32[128,512]{1,0:T(8,128)S(1)}, f32[128,512]{1,0:T(8,128)}, u32[]{:S(2)}) copy-start(f32[128,512]{1,0:T(8,128)} %copy-done.12) | copy-start | bytes 786436
  232.4 22.0 %copy-start.11 = (f32[128,512]{1,0:T(8,128)S(1)}, f32[128,512]{1,0:T(8,128)}, u32[]{:S(2)}) copy-start(f32[128,512]{1,0:T(8,128)} %copy-done.10) | copy-start | bytes 786436
  232.9 40.9 %all-to-all-start.12 = ((f32[8,32,512]{2,1,0:T(8,128)}), f32[8,32,512]{2,1,0:T(8,128)S(1)}, u32[]{:S(2)}, u32[]{:S(2)}) async-start(f32[8,32,512]{2,1,0:T(8,128)} %bitcast.16), calls=%async_computation.12 | async-start | bytes 1048576 | tf_op jit(solution)/shard_map/all_to_all | solution.py:803
  237.1 1.0 copy-start.17
  238.1 24.0 %copy-start.19 = (f32[128,512]{1,0:T(8,128)S(1)}, f32[128,512]{1,0:T(8,128)}, u32[]{:S(2)}) copy-start(f32[128,512]{1,0:T(8,128)} %copy-done.18) | copy-start | bytes 786436
  239.1 13.1 %collective-permute-start.12 = (f32[128,512]{1,0:T(8,128)S(1)}, f32[128,512]{1,0:T(8,128)S(1)}, u32[]{:S(2)}, u32[]{:S(2)}) collective-permute-start(f32[128,512]{1,0:T(8,128)S(1)} %added.19), channel_id=1, source_target_pairs={{0,56},{1,9},{8,0},{9,17},{16,8},{17,25},{24,16},{25,33},{32,24},{... | collective-permute-start | bytes 786440 | tf_op jit(solution)/shard_map/ppermute | solution.py:749
  242.4 0.9 copy-start.15
  243.4 11.0 %collective-permute-start.9 = (f32[128,512]{1,0:T(8,128)S(1)}, f32[128,512]{1,0:T(8,128)S(1)}, u32[]{:S(2)}, u32[]{:S(2)}) collective-permute-start(f32[128,512]{1,0:T(8,128)S(1)} %added.17), channel_id=1, source_target_pairs={{0,8},{1,57},{8,16},{9,1},{16,24},{17,9},{24,32},{25,17},{32,40},{... | collective-permute-start | bytes 786440 | tf_op jit(solution)/shard_map/ppermute | solution.py:749
  252.2 6.5 %collective-permute-start.13 = (f32[128,512]{1,0:T(8,128)S(1)}, f32[128,512]{1,0:T(8,128)S(1)}, u32[]{:S(2)}, u32[]{:S(2)}) collective-permute-start(f32[128,512]{1,0:T(8,128)S(1)} %added.20), channel_id=1, source_target_pairs={{0,56},{1,9},{8,0},{9,17},{16,8},{17,25},{24,16},{25,33},{32,24},{... | collective-permute-start | bytes 786440 | tf_op jit(solution)/shard_map/ppermute | solution.py:749
  254.4 7.7 %collective-permute-start.10 = (f32[128,512]{1,0:T(8,128)S(1)}, f32[128,512]{1,0:T(8,128)S(1)}, u32[]{:S(2)}, u32[]{:S(2)}) collective-permute-start(f32[128,512]{1,0:T(8,128)S(1)} %added.18), channel_id=1, source_target_pairs={{0,8},{1,57},{8,16},{9,1},{16,24},{17,9},{24,32},{25,17},{32,40},{... | collective-permute-start | bytes 786440 | tf_op jit(solution)/shard_map/ppermute | solution.py:749
  254.5 20.0 %collective-permute-start.5 = (f32[128,1024]{1,0:T(8,128)}, f32[128,1024]{1,0:T(8,128)S(1)}, u32[]{:S(2)}, u32[]{:S(2)}) collective-permute-start(f32[128,1024]{1,0:T(8,128)} %get-tuple-element.95), channel_id=1, source_target_pairs={{0,6},{1,3},{8,14},{9,11},{16,22},{17,19},{24,30},{25,27},{32,38},... | collective-permute-start | bytes 1572872 | tf_op jit(solution)/shard_map/ppermute | solution.py:749
  255.5 19.0 %collective-permute-start.4 = (f32[128,1024]{1,0:T(8,128)S(1)}, f32[128,1024]{1,0:T(8,128)S(1)}, u32[]{:S(2)}, u32[]{:S(2)}) collective-permute-start(f32[128,1024]{1,0:T(8,128)S(1)} %added.13), channel_id=1, source_target_pairs={{0,2},{1,7},{8,10},{9,15},{16,18},{17,23},{24,26},{25,31},{32,34},... | collective-permute-start | bytes 1572872 | tf_op jit(solution)/shard_map/ppermute | solution.py:749
  262.7 5.6 %collective-permute-start.14 = (f32[32,512]{1,0:T(8,128)S(1)}, f32[32,512]{1,0:T(8,128)S(1)}, u32[]{:S(2)}, u32[]{:S(2)}) collective-permute-start(f32[32,512]{1,0:T(8,128)S(1)} %get-tuple-element.93), channel_id=1, source_target_pairs={{0,64},{1,193},{8,72},{9,201},{16,80},{17,209},{24,88},{25,217},{3... | collective-permute-start | bytes 196616 | tf_op jit(solution)/shard_map/ppermute | solution.py:749
  265.2 4.3 %collective-permute-start.16 = (f32[32,512]{1,0:T(8,128)S(1)}, f32[32,512]{1,0:T(8,128)S(1)}, u32[]{:S(2)}, u32[]{:S(2)}) collective-permute-start(f32[32,512]{1,0:T(8,128)S(1)} %get-tuple-element.94), channel_id=1, source_target_pairs={{0,192},{1,65},{8,200},{9,73},{16,208},{17,81},{24,216},{25,89},{3... | collective-permute-start | bytes 196616 | tf_op jit(solution)/shard_map/ppermute | solution.py:749
  268.3 5.6 %collective-permute-start.15 = (f32[32,512]{1,0:T(8,128)S(1)}, f32[32,512]{1,0:T(8,128)S(1)}, u32[]{:S(2)}, u32[]{:S(2)}) collective-permute-start(f32[32,512]{1,0:T(8,128)S(1)} %added.21), channel_id=1, source_target_pairs={{0,64},{1,193},{8,72},{9,201},{16,80},{17,209},{24,88},{25,217},{3... | collective-permute-start | bytes 196616 | tf_op jit(solution)/shard_map/ppermute | solution.py:749
where the time goes:
time: 279 us; the launch traced here: 275 us
  blocking collectives  103 us (37%)
  Pallas kernels  73.1 us (26%)
  starting transfers between devices  41.3 us (15%)
  waiting for transfers between devices  34 us (12%)
  local copies, waits for them, and re-layouts  21.5 us (8%)
    all_to_all x9, blocking collectives, exchanged(): return lax.all_to_all(copies, axis, 0, 0, tiled=True)  103 us
    pallas_call x29, Pallas kernels, call(): pl.pallas_call(kernel, out_shape=outs, in_specs=specs, out_specs=[pl.Bloc...  73.1 us
    ppermute x16, waiting for transfers between devices, turn(): return lax.ppermute(value, ('rows', 'cols'), moves)  23.1 us
    ppermute x16, starting transfers between devices, turn(): return lax.ppermute(value, ('rows', 'cols'), moves)  20.8 us
    unnamed x50, local copies, waits for them, and re-layouts  20.2 us
    all_to_all x3, starting transfers between devices, exchanged(): return lax.all_to_all(copies, axis, 0, 0, tiled=True)  16.3 us
    all_to_all x3, waiting for transfers between devices, exchanged(): return lax.all_to_all(copies, axis, 0, 0, tiled=True)  10.9 us
  transfers between devices with their start and end apart: 21, of which 9 were waited for; matrix products, arithmetic and copies ran while one was open for 4% of the time, Pallas kernels for 8%

commit v1 on v0

--- a/solution.py
+++ b/solution.py
@@ -19,6 +19,7 @@
 REACH = 40.0
 FIRST_REACH = 75.0
 VMEM_BYTES = 16 * 2**20
+PINNED = 2**16
 F32 = jnp.float32
 
 
@@ -81,30 +82,26 @@
     return jnp.concatenate([ref[c : c + 1, :] for c in range(groups_of(ref))], axis=1)
 
 
-def load_rows(score_hbm, tile_ref, sem, group):
-    copy = pltpu.make_async_copy(
-        score_hbm.at[pl.ds(pl.multiple_of(group * LANES, LANES), LANES), :], tile_ref, sem
-    )
-    copy.start()
-    copy.wait()
-
-
-def slow_row_logs(score_hbm, tile_ref, sem, col_ref, out_ref):
+def load_rows(score_ref, tile_ref, group):
+    tile_ref[...] = score_ref[pl.ds(pl.multiple_of(group * LANES, LANES), LANES), :]
+
+
+def slow_row_logs(score_ref, tile_ref, col_ref, out_ref):
     @pl.loop(0, groups_of(out_ref))
     def _(group):
-        load_rows(score_hbm, tile_ref, sem, group)
+        load_rows(score_ref, tile_ref, group)
         logs = []
         for q in range(LANES // STRIP):
             logs.append(strip_logs(tile_ref[q * STRIP : (q + 1) * STRIP, :] + wide(col_ref))[2])
         out_ref[pl.ds(group, 1), :] = to_row(jnp.concatenate(logs, axis=0))
 
 
-def slow_col_logs(score_hbm, tile_ref, sem, row_ref, out_ref):
+def slow_col_logs(score_ref, tile_ref, row_ref, out_ref):
     count = groups_of(out_ref)
     tops = tuple(jnp.full((1, LANES), -1e30, F32) for _ in range(count))
 
     def highest(group, tops):
-        load_rows(score_hbm, tile_ref, sem, group)
+        load_rows(score_ref, tile_ref, group)
         column = to_column(row_ref[pl.ds(group, 1), :])
         return tuple(
             jnp.maximum(
@@ -120,7 +117,7 @@
     sums = tuple(jnp.zeros((1, LANES), F32) for _ in range(count))
 
     def summed(group, sums):
-        load_rows(score_hbm, tile_ref, sem, group)
+        load_rows(score_ref, tile_ref, group)
         column = to_column(row_ref[pl.ds(group, 1), :])
         return tuple(
             sums[c]
@@ -137,10 +134,10 @@
         out_ref[c : c + 1, :] = tops[c] + jnp.log2(sums[c])
 
 
-def slow_row_weighted(score_hbm, tile_ref, sem, row_ref, col_ref, weight_ref, out_ref):
+def slow_row_weighted(score_ref, tile_ref, row_ref, col_ref, weight_ref, out_ref):
     @pl.loop(0, groups_of(out_ref))
     def _(group):
-        load_rows(score_hbm, tile_ref, sem, group)
+        load_rows(score_ref, tile_ref, group)
         column = to_column(row_ref[pl.ds(group, 1), :])
         sums = []
         for q in range(LANES // STRIP):
@@ -150,12 +147,12 @@
         out_ref[pl.ds(group, 1), :] = to_row(jnp.concatenate(sums, axis=0))
 
 
-def slow_col_weighted(score_hbm, tile_ref, sem, row_ref, col_ref, weight_ref, out_ref):
+def slow_col_weighted(score_ref, tile_ref, row_ref, col_ref, weight_ref, out_ref):
     count = groups_of(out_ref)
     sums = tuple(jnp.zeros((1, LANES), F32) for _ in range(count))
 
     def summed(group, sums):
-        load_rows(score_hbm, tile_ref, sem, group)
+        load_rows(score_ref, tile_ref, group)
         column = to_column(row_ref[pl.ds(group, 1), :])
         weight = to_column(weight_ref[pl.ds(group, 1), :])
         return tuple(
@@ -177,9 +174,8 @@
 
 
 def first_kernel(
-    cost_hbm, src_hbm, tgt_hbm, mask_hbm, dual_hbm, score_hbm, base_ref, top_ref, copies_ref,
-    cost_ref, src_ref, tgt_ref, mask_ref, dual_ref, allowed_ref, log_ref, score_ref,
-    small_sem, cost_sem, score_sem,
+    cost_hbm, src_hbm, tgt_hbm, mask_hbm, dual_hbm, score_ref, base_ref, top_ref, copies_ref,
+    cost_ref, src_ref, tgt_ref, mask_ref, dual_ref, allowed_ref, log_ref, small_sem, cost_sem,
 ):
     small = [
         pltpu.make_async_copy(source, target, small_sem.at[at])
@@ -230,31 +226,15 @@
             logs.append(log)
         top_ref[s : s + 1, :] = to_row(jnp.concatenate(tops, axis=0))
         log_ref[s : s + 1, :] = to_row(jnp.concatenate(logs, axis=0))
-        rows = pl.ds(s * LANES, LANES)
-        blocks[s] = pltpu.make_async_copy(
-            score_ref.at[rows, :], score_hbm.at[rows, :], score_sem.at[s]
-        )
-        blocks[s].start()
     spread(copies_ref, log_ref[...])
-    for copy in blocks:
-        copy.wait()
 
 
 def rebase_kernel(
-    log_target, parts_ref, score_hbm, base_ref, top_ref, dual_ref, copies_ref, log_ref, score_ref,
-    score_sem,
+    log_target, parts_ref, score_ref, base_ref, top_ref, dual_ref, copies_ref, log_ref
 ):
-    blocks = []
-    for s in range(groups_of(log_ref)):
-        rows = pl.ds(s * LANES, LANES)
-        blocks.append(
-            pltpu.make_async_copy(score_hbm.at[rows, :], score_ref.at[rows, :], score_sem.at[s])
-        )
-        blocks[-1].start()
     dual_ref[...] = log_target - log_combined(parts_ref[...])
     dual = wide(dual_ref)
     for s in range(groups_of(log_ref)):
-        blocks[s].wait()
         tops, logs = [], []
         for q in range(LANES // STRIP):
             rows = slice(s * LANES + q * STRIP, s * LANES + (q + 1) * STRIP)
@@ -268,8 +248,8 @@
 
 
 def row_log_kernel(
-    log_target, parts_ref, top_ref, base_dual_ref, base_ref, score_hbm, dual_ref, copies_ref,
-    weight_ref, sum_ref, tile_ref, sem,
+    log_target, parts_ref, top_ref, base_dual_ref, base_ref, score_ref, dual_ref, copies_ref,
+    weight_ref, sum_ref, tile_ref,
 ):
     dual_ref[...] = log_target - log_combined(parts_ref[...])
     lead = dual_ref[...] - base_dual_ref[...]
@@ -283,14 +263,14 @@
 
     @pl.when(jnp.logical_not(near))
     def _():
-        slow_row_logs(score_hbm, tile_ref, sem, dual_ref, sum_ref)
+        slow_row_logs(score_ref, tile_ref, dual_ref, sum_ref)
 
     spread(copies_ref, sum_ref[...])
 
 
 def col_log_kernel(
-    log_source, parts_ref, top_ref, base_dual_ref, base_ref, score_hbm, dual_ref, copies_ref,
-    weight_ref, sum_ref, tile_ref, sem,
+    log_source, parts_ref, top_ref, base_dual_ref, base_ref, score_ref, dual_ref, copies_ref,
+    weight_ref, sum_ref, tile_ref,
 ):
     dual_ref[...] = log_source - log_combined(parts_ref[...])
     lead = dual_ref[...] + top_ref[...]
@@ -308,14 +288,14 @@
 
     @pl.when(jnp.logical_not(near))
     def _():
-        slow_col_logs(score_hbm, tile_ref, sem, dual_ref, sum_ref)
+        slow_col_logs(score_ref, tile_ref, dual_ref, sum_ref)
 
     spread(copies_ref, sum_ref[...])
 
 
 def row_plan_kernel(
     log_target, first, parts_ref, grad_ref, dual_in_ref, row_dual_ref, top_ref, base_dual_ref,
-    base_ref, score_hbm, out_ref, copies_ref, weight_ref, col_ref, sum_ref, tile_ref, sem,
+    base_ref, score_ref, after_ref, out_ref, copies_ref, weight_ref, col_ref, sum_ref, tile_ref,
 ):
     if first:
         dual = log_target - log_combined(parts_ref[...])
@@ -339,20 +319,20 @@
     def _():
         col_ref[...] = dual - log_target
         weight_ref[...] = grad
-        slow_row_weighted(score_hbm, tile_ref, sem, row_dual_ref, col_ref, weight_ref, sum_ref)
+        slow_row_weighted(score_ref, tile_ref, row_dual_ref, col_ref, weight_ref, sum_ref)
 
     spread(copies_ref, sum_ref[...])
 
 
 def col_plan_kernel(
-    log_source, reach, parts_ref, outer_ref, dual_ref, row_dual_ref, top_ref, base_dual_ref, base_ref,
-    score_hbm, out_ref, copies_ref, weight_ref, col_ref, sum_ref, tile_ref, sem,
+    log_source, parts_ref, outer_ref, dual_ref, row_dual_ref, top_ref, base_dual_ref, base_ref,
+    score_ref, out_ref, copies_ref, weight_ref, col_ref, sum_ref, tile_ref,
 ):
     grad = outer_ref[...] - jnp.sum(parts_ref[...], axis=0)
     out_ref[...] = grad
     lead = dual_ref[...] - base_dual_ref[...]
     row_lead = row_dual_ref[...] + top_ref[...]
-    near = jnp.logical_and(jnp.max(jnp.abs(lead)) <= reach, jnp.max(row_lead) <= 60.0)
+    near = jnp.logical_and(jnp.max(jnp.abs(lead)) <= REACH, jnp.max(row_lead) <= 60.0)
 
     @pl.when(near)
     def _():
@@ -364,9 +344,24 @@
     def _():
         col_ref[...] = dual_ref[...] - log_source
         weight_ref[...] = grad
-        slow_col_weighted(score_hbm, tile_ref, sem, row_dual_ref, col_ref, weight_ref, sum_ref)
+        slow_col_weighted(score_ref, tile_ref, row_dual_ref, col_ref, weight_ref, sum_ref)
 
     spread(copies_ref, sum_ref[...])
+
+
+def turn_kernel(emb_hbm, after_ref, out_ref, emb_ref, sem):
+    strips = [slice(at, at + LANES) for at in range(0, emb_ref.shape[0], LANES)]
+    copies = [
+        pltpu.make_async_copy(
+            emb_hbm.at[pl.ds(at * LANES, LANES), :], emb_ref.at[pl.ds(at * LANES, LANES), :], sem.at[at]
+        )
+        for at in range(len(strips))
+    ]
+    for copy in copies:
+        copy.start()
+    for copy, strip in zip(copies, strips):
+        copy.wait()
+        out_ref[:, strip] = emb_ref[strip, :].T
 
 
 def is_near(dual_refs, row_refs, top_ref, base_dual_ref):
@@ -382,7 +377,7 @@
 def most_grad_kernel(
     log_source, log_target,
     row1, row2, row3, col1, col2, col3, fbar2, fbar3, gbar1, gbar2, gbar3, top_ref, base_ref,
-    score_hbm, out_ref, rows_ref, cols_ref, tile_ref, sem,
+    score_ref, out_ref, rows_ref, cols_ref, tile_ref,
 ):
     near = is_near((col2, col3), (row1, row2, row3), top_ref, col1)
     count = groups_of(col1)
@@ -426,7 +421,7 @@
 
         @pl.loop(0, groups_of(row1))
         def _(group):
-            load_rows(score_hbm, tile_ref, sem, group)
+            load_rows(score_ref, tile_ref, group)
             columns = [to_column(rows_ref[k, pl.ds(group, 1), :]) for k in range(5)]
             for c in range(count):
                 lanes = slice(c * LANES, (c + 1) * LANES)
@@ -475,39 +470,60 @@
 
 def grad_kernel(
     log_source, counts, place_ref, parts_ref, row1, col1, top_ref, base_ref, most_ref, src_ref,
-    score_hbm, out_ref, z_far_ref, x_far_ref, rows_ref, cols_ref, tile_ref, sem,
+    score_ref, out_ref, start_ref, z_far_ref, x_far_ref, rows_ref, cols_ref, tile_ref,
 ):
     fbar1 = -jnp.sum(parts_ref[...], axis=0)
     row_lead = row1[...] + top_ref[...]
     near = jnp.logical_and(jnp.max(jnp.abs(col1[...])) <= FIRST_REACH, jnp.max(row_lead) <= 60.0)
+    count = groups_of(col1)
 
     @pl.when(near)
     def _():
         rows_ref[...] = -jnp.exp2(row_lead) * fbar1
         cols_ref[...] = jnp.exp2(-col1[...] - log_source)
+        held = [None] * count
         for s in range(groups_of(row1)):
             column = jnp.broadcast_to(to_column(rows_ref[s : s + 1, :]), (LANES, LANES))
             rows = slice(s * LANES, (s + 1) * LANES)
-            for c in range(groups_of(col1)):
+            for c in range(count):
                 lanes = slice(c * LANES, (c + 1) * LANES)
-                term = base_ref[rows, lanes] * (column * cols_ref[c : c + 1, :])
+                term = base_ref[rows, lanes] * column * cols_ref[c : c + 1, :]
                 out_ref[rows, lanes] = (most_ref[rows, lanes] + term).astype(jnp.bfloat16)
+                term = jnp.sum(term.reshape(LANES // 8, 8, LANES), axis=0)
+                held[c] = term if held[c] is None else held[c] + term
+        for c, term in enumerate(held):
+            start_ref[c : c + 1, :] = jnp.sum(term, axis=0, keepdims=True)
 
     @pl.when(jnp.logical_not(near))
     def _():
         rows_ref[...] = -fbar1
+        start_ref[...] = jnp.zeros_like(start_ref)
 
         @pl.loop(0, groups_of(row1))
         def _(group):
-            load_rows(score_hbm, tile_ref, sem, group)
+            load_rows(score_ref, tile_ref, group)
             column = to_column(row1[pl.ds(group, 1), :]) - log_source
             weight = to_column(rows_ref[pl.ds(group, 1), :])
             rows = pl.ds(pl.multiple_of(group * LANES, LANES), LANES)
-            term = jnp.exp2(tile_ref[...] + column) * weight
-            out_ref[rows, :] = (most_ref[rows, :] + term).astype(jnp.bfloat16)
-
-    z_far_ref[...] = z_block(place_ref, src_ref, out_ref, counts[1] // 2, counts)
+            for c in range(count):
+                lanes = slice(c * LANES, (c + 1) * LANES)
+                term = jnp.exp2(tile_ref[:, lanes] + column) * weight
+                out_ref[rows, lanes] = (most_ref[rows, lanes] + term).astype(jnp.bfloat16)
+                start_ref[c : c + 1, :] += jnp.sum(term, axis=0, keepdims=True)
+
     x_far_ref[...] = x_block(place_ref, src_ref, out_ref, counts[0] // 2, counts)
+    put(z_far_ref, z_block(place_ref, src_ref, out_ref, counts[1] // 2, counts), start_ref[...])
+
+
+def put(out_ref, block, rider):
+    rows = block.shape[0]
+    out_ref[:rows, :] = block
+    out_ref[rows:, :] = jnp.zeros_like(out_ref[rows:, :])
+    out_ref[rows:, :LANES] = rider
+
+
+def rider(ref):
+    return ref[ref.shape[0] - 8 :, :LANES]
 
 
 def x_part_kernel(y_count, place_ref, grad_ref, tgt_ref, sent_ref, kept_ref, order_ref):
@@ -527,84 +543,137 @@
         out_ref[...] = product.reshape(out_ref.shape)
 
 
-def y_parts_kernel(counts, place_ref, grad_ref, src_ref, after_ref, *outs):
+def y_parts_kernel(counts, place_ref, grad_ref, src_ref, start_ref, after_ref, *outs):
+    x_outs, z_outs = outs[:3], outs[3:]
+    for out_ref, offset in zip(x_outs, (-1, 1, 0)):
+        out_ref[...] = x_block(place_ref, src_ref, grad_ref, offset, counts)
     reach = counts[1] // 2
-    offsets = [*range(reach - 1, 0, -1), *range(1 - reach, 1)]
-    for out_ref, offset in zip(outs, offsets):
-        out_ref[...] = z_block(place_ref, src_ref, grad_ref, offset, counts)
-    for out_ref, offset in zip(outs[len(offsets) :], (1, -1, 0)):
-        out_ref[...] = x_block(place_ref, src_ref, grad_ref, offset, counts)
+    offsets = [1 - reach, *range(reach - 1, 0, -1), *range(2 - reach, 1)]
+    for out_ref, offset in zip(z_outs, offsets):
+        block = z_block(place_ref, src_ref, grad_ref, offset, counts)
+        if offset == 1 - reach:
+            put(out_ref, block, start_ref[...])
+        else:
+            out_ref[...] = block
 
 
 def add_kernel(count, *refs):
     value = refs[0][...]
     for ref in refs[1:count]:
         value = value + ref[...]
-    refs[-1][...] = value
-
-
-def split_kernel(x_count, place_ref, own_ref, up_ref, down_ref, *outs):
+    out_ref, token_ref = refs[-2:]
+    out_ref[...] = value
+    token_ref[...] = jnp.zeros_like(token_ref)
+
+
+def pair_kernel(one_ref, up_ref, own_ref, down_ref, after_ref, pay_ref, sum_ref, token_ref):
+    pay_ref[...] = one_ref[...] + up_ref[...]
+    sum_ref[...] = own_ref[...] + down_ref[...]
+    token_ref[...] = jnp.zeros_like(token_ref)
+
+
+def pass_kernel(block_ref, arrived_ref, held_ref, after_ref, out_ref, sum_ref):
+    rows = block_ref.shape[0]
+    out_ref[:rows, :] = block_ref[...] + arrived_ref[:rows, :]
+    out_ref[rows:, :] = arrived_ref[rows:, :]
+    sum_ref[...] = held_ref[...] + rider(arrived_ref)
+
+
+def chip_kernel(kept_ref, arrived_ref, after_ref, *outs):
+    for k, out_ref in enumerate(outs[:-1]):
+        out_ref[...] = kept_ref[k] + arrived_ref[k]
+    outs[-1][...] = jnp.zeros_like(outs[-1])
+
+
+def split_kernel(
+    x_count, place_ref, own_ref, up_ref, down_ref, held_up_ref, held_down_ref, after_ref, far_ref,
+    back_ref, one_ref, last_ref, start_ref,
+):
+    start_ref[...] = (
+        held_up_ref[...] + held_down_ref[...] + rider(up_ref) + rider(down_ref)
+    )
     block = own_ref.shape[0] // x_count
-    for out_ref, offset in zip(outs, (2, 1, -1, 0)):
+    for out_ref, offset in ((far_ref, 2), (back_ref, -1), (one_ref, 1), (last_ref, 0)):
         at = ring_place(place_ref, 0, offset, x_count)
         rows = pl.ds(pl.multiple_of(at * block, block), block)
-        out_ref[...] = own_ref[rows, :] + up_ref[rows, :] + down_ref[rows, :]
-
-
-def join_kernel(parts_ref, own_ref, up_ref, down_ref, out_ref):
-    half = own_ref.shape[1]
+        value = own_ref[rows, :] + up_ref[rows, :] + down_ref[rows, :]
+        if offset in (2, -1):
+            put(out_ref, value, start_ref[...])
+        else:
+            out_ref[...] = value
+
+
+def join_kernel(parts_ref, own_ref, up_ref, down_ref, held_ref, out_ref, start_ref):
+    rows, half = own_ref.shape
     out_ref[:, :half] = jnp.sum(parts_ref[...], axis=0)
-    out_ref[:, half:] = own_ref[...] + up_ref[...] + down_ref[...]
+    out_ref[:, half:] = own_ref[...] + up_ref[:rows, :] + down_ref[:rows, :]
+    start_ref[...] = held_ref[...] + rider(up_ref) + rider(down_ref)
 
 
 def call(
-    kernel, arguments, outs, scratch=(), in_hbm=(), loose=(), in_smem=(), out_hbm=(), name=None
+    kernel, arguments, outs, scratch=(), in_hbm=(), loose=(), in_smem=(), last=False, name=None
 ):
-    specs = [
-        pl.BlockSpec(
-            memory_space=pltpu.HBM
-            if at in in_hbm
-            else pl.ANY
-            if at in loose
-            else pltpu.SMEM
-            if at in in_smem
-            else pltpu.VMEM
-        )
-        for at in range(len(arguments))
-    ]
-    arguments = [
-        pltpu.with_memory_space_constraint(value, pltpu.HBM) if at in in_hbm else value
-        for at, value in enumerate(arguments)
-    ]
-    outs = [
-        pltpu.HBM(out.shape, out.dtype) if at in out_hbm else out for at, out in enumerate(outs)
-    ]
+    spaces, values = [], []
+    for at, value in enumerate(arguments):
+        space = pltpu.VMEM
+        if at in in_hbm:
+            space = pltpu.HBM
+        elif at in loose:
+            space = pl.ANY
+        elif at in in_smem:
+            space = pltpu.SMEM
+        if at in in_hbm or (space is pltpu.VMEM and value.size >= PINNED):
+            value = pltpu.with_memory_space_constraint(value, space)
+        spaces.append(space)
+        values.append(value)
     return pl.pallas_call(
         kernel,
-        out_shape=outs,
-        in_specs=specs,
-        out_specs=[
-            pl.BlockSpec(memory_space=pltpu.HBM if at in out_hbm else pltpu.VMEM)
-            for at in range(len(outs))
+        out_shape=[
+            pltpu.VMEM(out.shape, out.dtype) if math.prod(out.shape) >= PINNED and not last else out
+            for out in outs
         ],
+        in_specs=[pl.BlockSpec(memory_space=space) for space in spaces],
+        out_specs=[pl.BlockSpec(memory_space=pltpu.VMEM)] * len(outs),
         scratch_shapes=list(scratch),
         compiler_params=pltpu.CompilerParams(vmem_limit_bytes=VMEM_BYTES),
         name=name,
-    )(*arguments)
+    )(*values)
 
 
 def exchanged(copies, axis):
     return lax.all_to_all(copies, axis, 0, 0, tiled=True)
 
 
-def added(values, after=()):
+def token():
+    return jax.ShapeDtypeStruct((8, LANES), F32)
+
+
+def added(values, after, last=False):
     return call(
         functools.partial(add_kernel, len(values)),
-        (*values, *after),
-        [jax.ShapeDtypeStruct(values[0].shape, F32)],
-        loose=range(len(values), len(values) + len(after)),
+        (*values, after),
+        [jax.ShapeDtypeStruct(values[0].shape, F32), token()],
+        loose=(len(values),),
+        last=last,
         name="added",
-    )[0]
+    )
+
+
+def paired(one, up, own, down, after):
+    shape = jax.ShapeDtypeStruct(one.shape, F32)
+    return call(
+        pair_kernel, (one, up, own, down, after), [shape, shape, token()], loose=(4,), name="paired"
+    )
+
+
+def passed(block, arrived, held, after):
+    return call(
+        pass_kernel,
+        (block, arrived, held, after),
+        [jax.ShapeDtypeStruct(arrived.shape, F32), token()],
+        loose=(3,),
+        name="passed",
+    )
 
 
 def body(cost, src_label, tgt_label, class_mask, g_start, f_bar, g_bar, src_emb, tgt_emb):
@@ -628,7 +697,7 @@
     row_copies = array((col_count,) + row_shape)
     col_copies = array((row_count,) + col_shape)
     row_held, col_held = pltpu.VMEM(row_shape, F32), pltpu.VMEM(col_shape, F32)
-    slow = [pltpu.VMEM((LANES, tgt_cols), F32), pltpu.SemaphoreType.DMA]
+    slow = [pltpu.VMEM((LANES, tgt_cols), F32)]
 
     score, start_base, start_top, copies = call(
         first_kernel,
@@ -642,13 +711,10 @@
             col_held,
             pltpu.VMEM((LANES, tgt_cols), F32),
             row_held,
-            pltpu.VMEM(cost.shape, F32),
             pltpu.SemaphoreType.DMA((4,)),
-            pltpu.SemaphoreType.DMA(row_shape[:1]),
             pltpu.SemaphoreType.DMA(row_shape[:1]),
         ],
         in_hbm=range(5),
-        out_hbm=(0,),
         name="first_row_logs",
     )
 
@@ -658,8 +724,7 @@
             (parts, top, base_dual, base, score),
             [row_vector, col_copies],
             [row_held, col_held] + slow,
-            in_hbm=(4,),
-            name="col_logs",
+                name="col_logs",
         )
 
     zero = jnp.zeros(col_shape, F32)
@@ -668,8 +733,7 @@
         functools.partial(rebase_kernel, log_target),
         (exchanged(copies, "rows"), score),
         [matrix, row_vector, col_vector, row_copies],
-        [row_held, pltpu.VMEM(cost.shape, F32), pltpu.SemaphoreType.DMA(row_shape[:1])],
-        in_hbm=(1,),
+        [row_held],
         name="second_row_logs",
     )
     row2, copies = col_logs(exchanged(copies, "cols"), top, col1, base)
@@ -678,38 +742,49 @@
         (exchanged(copies, "rows"), top, col1, base, score),
         [col_vector, row_copies],
         [col_held, row_held] + slow,
-        in_hbm=(4,),
         name="third_row_logs",
     )
     row3, copies = col_logs(exchanged(copies, "cols"), top, col1, base)
 
-    def row_plan(first, parts, grad, dual, row):
+    def row_plan(first, parts, grad, dual, row, after):
         return call(
             functools.partial(row_plan_kernel, log_target, first),
-            (parts, grad, dual, row, top, col1, base, score),
+            (parts, grad, dual, row, top, col1, base, score, after),
             [col_vector, row_copies],
             [col_held, col_held, row_held] + slow,
-            in_hbm=(7,),
-            name="row_plan",
+            loose=(8,),
+                name="row_plan",
         )
 
-    def col_plan(parts, outer, dual, row, top, base_dual, base, reach=REACH):
+    def col_plan(parts, outer, dual, row):
         return call(
-            functools.partial(col_plan_kernel, log_source, reach),
-            (parts, outer, dual, row, top, base_dual, base, score),
+            functools.partial(col_plan_kernel, log_source),
+            (parts, outer, dual, row, top, col1, base, score),
             [row_vector, col_copies],
             [row_held, col_held, col_held] + slow,
-            in_hbm=(7,),
-            name="col_plan",
+                name="col_plan",
         )
 
     none = jnp.zeros(row_shape, F32)
-    src_turned, tgt_turned = src_emb.T, tgt_emb.T
-    col3, copies = row_plan(True, exchanged(copies, "rows"), g_bar, col2, row3)
-    fbar3, copies = col_plan(exchanged(copies, "cols"), f_bar, col2, row3, top, col1, base)
-    gbar2, copies = row_plan(False, exchanged(copies, "rows"), g_bar, col2, row2)
-    fbar2, copies = col_plan(exchanged(copies, "cols"), none, col1, row2, top, col1, base)
-    gbar1, copies = row_plan(False, exchanged(copies, "rows"), g_bar, col1, row1)
+
+    def turned(emb, after):
+        return call(
+            turn_kernel,
+            (emb, after),
+            [array(emb.shape[::-1], emb.dtype)],
+            [pltpu.VMEM(emb.shape, emb.dtype), pltpu.SemaphoreType.DMA((emb.shape[0] // LANES,))],
+            in_hbm=(0,),
+            loose=(1,),
+            name="turned",
+        )[0]
+
+    col3, copies = row_plan(True, exchanged(copies, "rows"), g_bar, col2, row3, g_bar)
+    fbar3, copies = col_plan(exchanged(copies, "cols"), f_bar, col2, row3)
+    src_turned = turned(src_emb, copies)
+    gbar2, copies = row_plan(False, exchanged(copies, "rows"), g_bar, col2, row2, src_turned)
+    fbar2, copies = col_plan(exchanged(copies, "cols"), none, col1, row2)
+    tgt_turned = turned(tgt_emb, copies)
+    gbar1, copies = row_plan(False, exchanged(copies, "rows"), g_bar, col1, row1, tgt_turned)
     parts = exchanged(copies, "cols")
     (most,) = call(
         functools.partial(most_grad_kernel, log_source, log_target),
@@ -718,7 +793,6 @@
         ),
         [matrix],
         [pltpu.VMEM((5,) + row_shape, F32), pltpu.VMEM((6,) + col_shape, F32)] + slow,
-        in_hbm=(13,),
         name="most_cost_grad",
     )
     x_count, z_count, y_count = 4, row_count // 4, col_count // 2
@@ -749,19 +823,19 @@
         return lax.ppermute(value, ("rows", "cols"), moves)
 
     half = tgt_cols // 2
-    z_shape = array((x_count * owned, half))
-    x_shape = array((z_count * owned, half))
-    rounded, z_far, x_far = call(
+    z_rows, x_rows = x_count * owned, z_count * owned
+    z_shape, z_riding = array((z_rows, half)), array((z_rows + 8, half))
+    x_shape = array((x_rows, half))
+    rounded, start, z_far, x_far = call(
         functools.partial(grad_kernel, log_source, counts),
         (place, parts, row1, col1, top, base, most, src_turned, score),
-        [array(cost.shape, jnp.bfloat16), z_shape, x_shape],
+        [array(cost.shape, jnp.bfloat16), col_vector, z_riding, x_shape],
         [row_held, col_held] + slow,
         in_smem=(0,),
-        in_hbm=(8,),
         name="cost_grad",
     )
-    z_long = turn(z_far, 2, 1)
-    x_long = turn(x_far, 0, 1)
+    z_up = turn(z_far, 2, 1)
+    x_up = turn(x_far, 0, 1)
     chip_part = array((y_count, width // col_count, src_rows))
     sent, kept = call(
         functools.partial(x_part_kernel, y_count),
@@ -774,51 +848,63 @@
     arrived = lax.ppermute(sent, "cols", [(at, at ^ 1) for at in range(col_count)])
     outs = call(
         functools.partial(y_parts_kernel, counts),
-        (place, rounded, src_turned, kept),
-        [z_shape] * (z_count - 1) + [x_shape] * 3,
+        (place, rounded, src_turned, start, kept),
+        [x_shape] * 3 + [z_riding] + [z_shape] * (z_count - 2),
         in_smem=(0,),
-        loose=(3,),
+        loose=(4,),
         name="grad_y_parts",
     )
-    z_longs, z_shorts, z_own = outs[:3], outs[3:6], outs[6]
-    x_one, x_back, x_own = outs[7:]
-    x_short = turn(x_back, 0, -1)
-    z_short = turn(z_shorts[0], 2, -1)
-    fbar1, copies = col_plan(
-        parts, none, zero, row1, top, col1, base, FIRST_REACH
-    )
-    start_parts = exchanged(copies, "rows")
-    z_long = turn(added((z_longs[0], z_long)), 2, 1)
-    chip = added((kept, arrived), (z_long,))
-    y_long = turn(chip[0], 1, 1)
-    x_long = turn(added((x_one, x_long)), 0, 1)
-    y_short = turn(chip[2], 1, -1)
-    z_short = turn(added((z_shorts[1], z_short)), 2, -1)
-    z_long = turn(added((z_longs[1], z_long)), 2, 1)
-    y_long = turn(added((chip[1], y_long)), 1, 1)
-    z_short = turn(added((z_shorts[2], z_short)), 2, -1)
-    z_long = turn(added((z_longs[2], z_long)), 2, 1)
-    first = added((x_own, x_long, x_short))
+    x_back, x_one, x_own, z_back, z_3, z_2, z_1, z_back2, z_back1, z_own = outs
+    x_down = turn(x_back, 0, -1)
+    z_down = turn(z_back, 2, -1)
+    z_pay, up_held = passed(z_3, z_up, start, start)
+    z_up = turn(z_pay, 2, 1)
+    far, one, back, own = (array((width // col_count, src_rows)) for _ in range(4))
+    far, one, back, own, mark = call(
+        chip_kernel,
+        (kept, arrived, up_held),
+        [far, one, back, own, token()],
+        loose=(2,),
+        name="chip_sums",
+    )
+    y_up, y_down = turn(far, 1, 1), turn(back, 1, -1)
+    z_pay, down_held = passed(z_back2, z_down, jnp.zeros_like(start), mark)
+    z_down = turn(z_pay, 2, -1)
+    x_pay, x_sum, mark = paired(x_one, x_up, x_own, x_down, down_held)
+    x_up = turn(x_pay, 0, 1)
+    z_pay, up_held = passed(z_2, z_up, up_held, mark)
+    z_up = turn(z_pay, 2, 1)
+    z_pay, down_held = passed(z_back1, z_down, down_held, up_held)
+    z_down = turn(z_pay, 2, -1)
+    y_pay, y_sum, mark = paired(one, y_up, own, y_down, down_held)
+    y_up = turn(y_pay, 1, 1)
+    first, mark = added((x_sum, x_up), mark)
     along_z = [[x * z_count + z for z in range(z_count)] for x in range(x_count)]
     first = lax.all_to_all(
         first.reshape(z_count, owned, half), "rows", 0, 0, tiled=True, axis_index_groups=along_z
     )
-    last = array((owned, half))
-    far, one, back, own = call(
+    z_pay, up_held = passed(z_1, z_up, up_held, mark)
+    z_up = turn(z_pay, 2, 1)
+    grad_x, mark = added((y_sum, y_up), up_held, last=True)
+    last, riding = array((owned, half)), array((owned + 8, half))
+    x_far, x_back, x_one, x_own, start = call(
         functools.partial(split_kernel, x_count),
-        (place, z_own, z_long, z_short),
-        [last] * 4,
+        (place, z_own, z_up, z_down, up_held, down_held, mark),
+        [riding, riding, last, last, col_vector],
         in_smem=(0,),
+        loose=(6,),
         name="second_half",
     )
-    x_long = turn(far, 0, 1)
-    x_short = turn(back, 0, -1)
-    x_long = turn(added((one, x_long)), 0, 1)
-    grad_x = added((chip[3], y_long, y_short))
-    (grad_y,) = call(
-        join_kernel, (first, own, x_long, x_short), [array((owned, tgt_cols))], name="grad_y"
-    )
-    g_start_bar = -jnp.sum(start_parts, axis=0).reshape(tgt_cols)
+    x_up, x_down = turn(x_far, 0, 1), turn(x_back, 0, -1)
+    x_pay, start = passed(x_one, x_up, start, start)
+    x_up = turn(x_pay, 0, 1)
+    grad_y, start = call(
+        join_kernel,
+        (first, x_own, x_up, x_down, start),
+        [array((owned, tgt_cols)), col_vector],
+        name="grad_y",
+    )
+    g_start_bar = start.reshape(tgt_cols)
     return (g_start_bar, grad_x, grad_y)
 
 

time: 279 us -> 248 us (0.89)
  Pallas kernels: 73.1 us -> 32 us
  waiting for transfers between devices: 34 us -> 57.6 us
  blocking collectives: 103 us -> 91.4 us
  local copies, waits for them, and re-layouts: 21.5 us -> 24.7 us
    pallas_call x29 -> x30, Pallas kernels: 73.1 us -> 32 us  [call(): pl.pallas_call(kernel, out_shape=[pltpu.VMEM(out.shape, out.dtype) if mat...]
    ppermute x16, waiting for transfers between devices: 23.1 us -> 42.2 us  [turn(): return lax.ppermute(value, ('rows', 'cols'), moves)]
    all_to_all x9 -> x8, blocking collectives: 103 us -> 91.4 us  [exchanged(): return lax.all_to_all(copies, axis, 0, 0, tiled=True)]
    all_to_all x3, waiting for transfers between devices: 10.9 us -> 15.4 us  [exchanged(): return lax.all_to_all(copies, axis, 0, 0, tiled=True)]
    unnamed x50 -> x36, local copies, waits for them, and re-layouts: 20.2 us -> 24.7 us
    all_to_all x3, starting transfers between devices: 16.3 us -> 12.4 us  [exchanged(): return lax.all_to_all(copies, axis, 0, 0, tiled=True)]
  transfers between devices with their start and end apart: 21 -> 21, of which waited for: 9 -> 9; matrix products, arithmetic and copies ran while one was open for 4% -> 0% of each run, Pallas kernels for 8% -> 4%
where the time goes in v1:
time: 248 us; the launch traced here: 247 us
  blocking collectives  91.4 us (37%)
  waiting for transfers between devices  57.6 us (23%)
  starting transfers between devices  40.3 us (16%)
  Pallas kernels  32 us (13%)
  local copies, waits for them, and re-layouts  24.7 us (10%)
    all_to_all x8, blocking collectives, exchanged(): return lax.all_to_all(copies, axis, 0, 0, tiled=True)  91.4 us
    ppermute x16, waiting for transfers between devices, turn(): return lax.ppermute(value, ('rows', 'cols'), moves)  42.2 us
    pallas_call x30, Pallas kernels, call(): pl.pallas_call(kernel, out_shape=[pltpu.VMEM(out.shape, out.dtype) if mat...  32 us
    unnamed x36, local copies, waits for them, and re-layouts  24.7 us
    ppermute x16, starting transfers between devices, turn(): return lax.ppermute(value, ('rows', 'cols'), moves)  21.2 us
    all_to_all x3, waiting for transfers between devices, exchanged(): return lax.all_to_all(copies, axis, 0, 0, tiled=True)  15.4 us
    all_to_all x3, starting transfers between devices, exchanged(): return lax.all_to_all(copies, axis, 0, 0, tiled=True)  12.4 us
    all_to_all x1, starting transfers between devices, body(): lax.all_to_all(first.reshape(z_count, owned, half), 'rows', 0, 0, tiled=T...  5.72 us
  transfers between devices with their start and end apart: 21, of which 9 were waited for; matrix products, arithmetic and copies ran while one was open for 0% of the time, Pallas kernels for 4%

profile of v1, /device:TPU:8, one launch (start us, length us, event | category | flops | bytes accessed | tf_op | source)
XLA Modules:
  0.0 247.1 jit_solution(1747586351769474619)
XLA Ops:
  0.6 4.9 %first_row_logs.1 = (f32[1024,1024]{1,0:T(8,128)S(1)}, f32[1024,1024]{1,0:T(8,128)S(1)}, f32[8,128]{1,0:T(8,128)S(1)}, f32[8,8,128]{2,1,0:T(8,128)S(1)}) custom-call(bf16[1024,1024]{1,0:T(8,128)(2,1)} %cost_hbm.1, s32[8,128]{1,0:T(8,128)} %bitcast.17, s32[8,128]{1,0:T(8,128)} %bitcast.18, s32[64,64]{1,0:T(8,128)} %mask_hbm.1, f32[8,128]{1,0:T(8,128)} %bitcast.19), custom_call_target="tpu_custom_call" | custom-call | tf_op jit(solution)/shard_map/first_row_logs/pallas_call | solution.py:629
  5.6 8.7 %all_to_all.60.parts_ref = f32[8,8,128]{2,1,0:T(8,128)S(1)} all-to-all(f32[8,8,128]{2,1,0:T(8,128)S(1)} %get-tuple-element.79), channel_id=1, replica_groups=mesh['rows'=32,'cols'=8] {'cols'}, dimensions={0} | all-to-all | bytes 65536 | tf_op jit(solution)/shard_map/all_to_all | solution.py:644
  14.3 0.6 col_logs.3
  14.9 21.4 %all_to_all.61.parts_ref = f32[32,8,128]{2,1,0:T(8,128)S(1)} all-to-all(f32[32,8,128]{2,1,0:T(8,128)S(1)} %get-tuple-element.83), channel_id=1, replica_groups=mesh['rows'=32,'cols'=8] {'rows'}, dimensions={0} | all-to-all | bytes 262144 | tf_op jit(solution)/shard_map/all_to_all | solution.py:644
  36.3 2.5 %second_row_logs.1 = (f32[1024,1024]{1,0:T(8,128)S(1)}, f32[8,128]{1,0:T(8,128)S(1)}, f32[8,128]{1,0:T(8,128)S(1)}, f32[8,8,128]{2,1,0:T(8,128)S(1)}) custom-call(f32[32,8,128]{2,1,0:T(8,128)S(1)} %all_to_all.61.parts_ref, f32[1024,1024]{1,0:T(8,128)S(1)} %get-tuple-element.82.score_ref), custom_call_target="tpu_custom_call" | custom-call | tf_op jit(solution)/shard_map/second_row_logs/pallas_call | solution.py:629
  38.8 10.0 %all_to_all.62.parts_ref = f32[8,8,128]{2,1,0:T(8,128)S(1)} all-to-all(f32[8,8,128]{2,1,0:T(8,128)S(1)} %get-tuple-element.84), channel_id=1, replica_groups=mesh['rows'=32,'cols'=8] {'cols'}, dimensions={0} | all-to-all | bytes 65536 | tf_op jit(solution)/shard_map/all_to_all | solution.py:644
  48.8 0.6 col_logs.4
  49.4 13.9 %all_to_all.63.parts_ref = f32[32,8,128]{2,1,0:T(8,128)S(1)} all-to-all(f32[32,8,128]{2,1,0:T(8,128)S(1)} %get-tuple-element.88), channel_id=1, replica_groups=mesh['rows'=32,'cols'=8] {'rows'}, dimensions={0} | all-to-all | bytes 262144 | tf_op jit(solution)/shard_map/all_to_all | solution.py:644
  63.2 0.6 third_row_logs.1
  63.8 7.8 %all_to_all.64.parts_ref = f32[8,8,128]{2,1,0:T(8,128)S(1)} all-to-all(f32[8,8,128]{2,1,0:T(8,128)S(1)} %get-tuple-element.89), channel_id=1, replica_groups=mesh['rows'=32,'cols'=8] {'cols'}, dimensions={0} | all-to-all | bytes 65536 | tf_op jit(solution)/shard_map/all_to_all | solution.py:644
  71.6 0.6 col_logs.5
  72.2 13.9 %all_to_all.65.parts_ref = f32[32,8,128]{2,1,0:T(8,128)S(1)} all-to-all(f32[32,8,128]{2,1,0:T(8,128)S(1)} %get-tuple-element.90), channel_id=1, replica_groups=mesh['rows'=32,'cols'=8] {'rows'}, dimensions={0} | all-to-all | bytes 262144 | tf_op jit(solution)/shard_map/all_to_all | solution.py:644
  86.0 0.6 row_plan.3
  86.6 7.8 %all_to_all.66.parts_ref = f32[8,8,128]{2,1,0:T(8,128)S(1)} all-to-all(f32[8,8,128]{2,1,0:T(8,128)S(1)} %get-tuple-element.93), channel_id=1, replica_groups=mesh['rows'=32,'cols'=8] {'cols'}, dimensions={0} | all-to-all | bytes 65536 | tf_op jit(solution)/shard_map/all_to_all | solution.py:644
  94.4 1.2 col_plan.2
  95.6 3.9 %all-to-all-start.7 = ((f32[32,8,128]{2,1,0:T(8,128)}), f32[32,8,128]{2,1,0:T(8,128)S(1)}, u32[]{:S(2)}, u32[]{:S(2)}) async-start(f32[32,8,128]{2,1,0:T(8,128)} %get-tuple-element.94.after_ref), calls=%async_computation.7 | async-start | bytes 262144 | tf_op jit(solution)/shard_map/all_to_all | solution.py:644
  99.5 2.1 turned.2.after_ref.src_ref
  101.6 8.4 %all-to-all-done.7.parts_ref = f32[32,8,128]{2,1,0:T(8,128)S(1)} async-done(((f32[32,8,128]{2,1,0:T(8,128)}), f32[32,8,128]{2,1,0:T(8,128)S(1)}, u32[]{:S(2)}, u32[]{:S(2)}) %all-to-all-start.7) | async-done | bytes 131104 | tf_op jit(solution)/shard_map/all_to_all | solution.py:644
  110.0 2.2 copy-done.1
  112.2 2.2 copy-done.6
  114.9 7.9 %all_to_all.67.parts_ref = f32[8,8,128]{2,1,0:T(8,128)S(1)} all-to-all(f32[8,8,128]{2,1,0:T(8,128)S(1)} %get-tuple-element.96), channel_id=1, replica_groups=mesh['rows'=32,'cols'=8] {'cols'}, dimensions={0} | all-to-all | bytes 65536 | tf_op jit(solution)/shard_map/all_to_all | solution.py:644
  122.8 1.4 col_plan.3
  124.2 3.9 %all-to-all-start.9 = ((f32[32,8,128]{2,1,0:T(8,128)}), f32[32,8,128]{2,1,0:T(8,128)S(1)}, u32[]{:S(2)}, u32[]{:S(2)}) async-start(f32[32,8,128]{2,1,0:T(8,128)} %get-tuple-element.97.after_ref), calls=%async_computation.9 | async-start | bytes 262144 | tf_op jit(solution)/shard_map/all_to_all | solution.py:644
  128.1 2.1 turned.3.after_ref.tgt_ref
  130.2 1.3 copy-done.11
  131.5 7.0 %all-to-all-done.9.parts_ref = f32[32,8,128]{2,1,0:T(8,128)S(1)} async-done(((f32[32,8,128]{2,1,0:T(8,128)}), f32[32,8,128]{2,1,0:T(8,128)S(1)}, u32[]{:S(2)}, u32[]{:S(2)}) %all-to-all-start.9) | async-done | bytes 131104 | tf_op jit(solution)/shard_map/all_to_all | solution.py:644
  138.5 2.2 copy-done.2
  140.7 2.2 copy-done.8
  142.9 1.6 copy-done.12
  144.5 1.2 row_plan.5
  145.7 4.7 %all-to-all-start.10 = ((f32[8,8,128]{2,1,0:T(8,128)}), f32[8,8,128]{2,1,0:T(8,128)S(1)}, u32[]{:S(2)}, u32[]{:S(2)}) async-start(f32[8,8,128]{2,1,0:T(8,128)} %get-tuple-element.99), calls=%async_computation.10 | async-start | bytes 65536 | tf_op jit(solution)/shard_map/all_to_all | solution.py:644
  150.5 2.2 copy-done.3
  152.7 2.2 copy-done.9
  154.8 2.2 most_cost_grad.1.most_ref
  157.0 2.1 copy-done.14
  159.1 2.2 copy-done.4
  161.3 2.2 copy-done.10
  163.5 2.2 copy-done.15
  165.7 2.1 cost_grad.1
  167.8 2.9 %grad_x_parts.1 = (f32[4,128,1024]{2,1,0:T(8,128)S(1)}, f32[4,128,1024]{2,1,0:T(8,128)S(1)}) custom-call(s32[4]{0:T(128)S(1)} %pad_add_fusion.place_ref, bf16[1024,1024]{1,0:T(8,128)(2,1)S(1)} %get-tuple-element.105.grad_ref, bf16[1024,1024]{1,0:T(8,128)(2,1)S(1)} %copy-done.13), custom_call_target="tpu_custom_call" | custom-call | tf_op jit(solution)/shard_map/grad_x_parts/pallas_call | solution.py:629
  170.7 1.0 collective-permute-start.3
  171.7 0.6 collective-permute-start
  172.4 2.5 grad_y_parts.1
  174.8 2.9 %collective-permute-start.1 = (f32[256,512]{1,0:T(8,128)S(1)}, f32[256,512]{1,0:T(8,128)S(1)}, u32[]{:S(2)}, u32[]{:S(2)}) collective-permute-start(f32[256,512]{1,0:T(8,128)S(1)} %get-tuple-element.111), channel_id=1, source_target_pairs={{0,192},{1,65},{8,200},{9,73},{16,208},{17,81},{24,216},{25,89},{3... | collective-permute-start | bytes 1572872 | tf_op jit(solution)/shard_map/ppermute | solution.py:823
  177.7 1.2 collective-permute-start.4
  179.0 2.0 collective-permute-start.2
  181.0 4.9 %collective-permute-done.4.arrived_ref = f32[136,512]{1,0:T(8,128)S(1)} collective-permute-done((f32[136,512]{1,0:T(8,128)S(1)}, f32[136,512]{1,0:T(8,128)S(1)}, u32[]{:S(2)}, u32[]{:S(2)}) %collective-permute-start.4) | collective-permute-done | bytes 278560 | tf_op jit(solution)/shard_map/ppermute | solution.py:823
  186.1 1.8 collective-permute-start.6
  188.4 0.7 collective-permute-start.5
  189.6 2.7 %collective-permute-start.8 = (f32[136,512]{1,0:T(8,128)S(1)}, f32[136,512]{1,0:T(8,128)S(1)}, u32[]{:S(2)}, u32[]{:S(2)}) collective-permute-start(f32[136,512]{1,0:T(8,128)S(1)} %get-tuple-element.127), channel_id=1, source_target_pairs={{0,56},{1,9},{8,0},{9,17},{16,8},{17,25},{24,16},{25,33},{32,24},{... | collective-permute-start | bytes 835592 | tf_op jit(solution)/shard_map/ppermute | solution.py:823
  192.3 5.9 %collective-permute-done.9.arrived_ref = f32[136,512]{1,0:T(8,128)S(1)} collective-permute-done((f32[136,512]{1,0:T(8,128)S(1)}, f32[136,512]{1,0:T(8,128)S(1)}, u32[]{:S(2)}, u32[]{:S(2)}) %collective-permute-start.9) | collective-permute-done | bytes 278560 | tf_op jit(solution)/shard_map/ppermute | solution.py:823
  198.9 0.9 added.2
  199.7 5.7 %all-to-all-start.11 = ((f32[8,32,512]{2,1,0:T(8,128)}), f32[8,32,512]{2,1,0:T(8,128)S(1)}, u32[]{:S(2)}, u32[]{:S(2)}) async-start(f32[8,32,512]{2,1,0:T(8,128)} %bitcast.9), calls=%async_computation.11 | async-start | bytes 1048576 | tf_op jit(solution)/shard_map/all_to_all | solution.py:883
  205.4 2.0 collective-permute-start.10
  207.5 1.6 collective-permute-start.13
  209.1 1.2 collective-permute-start.12
  210.3 16.1 %collective-permute-done.10.arrived_ref = f32[136,512]{1,0:T(8,128)S(1)} collective-permute-done((f32[136,512]{1,0:T(8,128)S(1)}, f32[136,512]{1,0:T(8,128)S(1)}, u32[]{:S(2)}, u32[]{:S(2)}) %collective-permute-start.10) | collective-permute-done | bytes 278560 | tf_op jit(solution)/shard_map/ppermute | solution.py:823
  226.6 0.9 added.3
  227.4 6.9 %collective-permute-done.11.up_ref = f32[136,512]{1,0:T(8,128)S(1)} collective-permute-done((f32[136,512]{1,0:T(8,128)S(1)}, f32[136,512]{1,0:T(8,128)S(1)}, u32[]{:S(2)}, u32[]{:S(2)}) %collective-permute-start.11) | collective-permute-done | bytes 278560 | tf_op jit(solution)/shard_map/ppermute | solution.py:823
  234.3 0.6 second_half.1
  235.0 3.2 %collective-permute-start.16 = (f32[40,512]{1,0:T(8,128)S(1)}, f32[40,512]{1,0:T(8,128)S(1)}, u32[]{:S(2)}, u32[]{:S(2)}) collective-permute-start(f32[40,512]{1,0:T(8,128)S(1)} %get-tuple-element.150), channel_id=1, source_target_pairs={{0,192},{1,65},{8,200},{9,73},{16,208},{17,81},{24,216},{25,89},{3... | collective-permute-start | bytes 245768 | tf_op jit(solution)/shard_map/ppermute | solution.py:823
  238.2 2.4 collective-permute-done.14.arrived_ref
  240.8 5.6 %collective-permute-done.15.up_ref = f32[40,512]{1,0:T(8,128)S(1)} collective-permute-done((f32[40,512]{1,0:T(8,128)S(1)}, f32[40,512]{1,0:T(8,128)S(1)}, u32[]{:S(2)}, u32[]{:S(2)}) %collective-permute-start.15) | collective-permute-done | bytes 81952 | tf_op jit(solution)/shard_map/ppermute | solution.py:823
  246.4 0.7 grad_y.1
  (54 shorter events, 2.7 us)
Async XLA Ops:
  5.6 88.9 %copy-start = (f32[1024,1024]{1,0:T(8,128)}, f32[1024,1024]{1,0:T(8,128)S(1)}, u32[]{:S(2)}) copy-start(f32[1024,1024]{1,0:T(8,128)S(1)} %get-tuple-element.82.score_ref) | copy-start | bytes 12582916
  38.7 55.7 %copy-start.5 = (f32[1024,1024]{1,0:T(8,128)}, f32[1024,1024]{1,0:T(8,128)S(1)}, u32[]{:S(2)}) copy-start(f32[1024,1024]{1,0:T(8,128)S(1)} %get-tuple-element.87.base_ref) | copy-start | bytes 12582916
  71.6 14.4 %copy-start.16 = (f32[1024]{0:T(1024)S(1)}, f32[1024]{0:T(1024)}, u32[]{:S(2)}) copy-start(f32[1024]{0:T(1024)} %param.15) | copy-start | bytes 12292
  86.0 8.4 %copy-start.17 = (f32[1024]{0:T(1024)S(1)}, f32[1024]{0:T(1024)}, u32[]{:S(2)}) copy-start(f32[1024]{0:T(1024)} %param.14) | copy-start | bytes 12292
  95.6 14.4 %all-to-all-start.7 = ((f32[32,8,128]{2,1,0:T(8,128)}), f32[32,8,128]{2,1,0:T(8,128)S(1)}, u32[]{:S(2)}, u32[]{:S(2)}) async-start(f32[32,8,128]{2,1,0:T(8,128)} %get-tuple-element.94.after_ref), calls=%async_computation.7 | async-start | bytes 262144 | tf_op jit(solution)/shard_map/all_to_all | solution.py:644
  110.0 2.2 copy-start.1
  112.2 2.2 copy-start.6
  114.4 8.5 %copy-start.7 = (f32[1024,1024]{1,0:T(8,128)S(1)}, f32[1024,1024]{1,0:T(8,128)}, u32[]{:S(2)}) copy-start(f32[1024,1024]{1,0:T(8,128)} %copy-done.5) | copy-start | bytes 12582916
  124.2 14.4 %all-to-all-start.9 = ((f32[32,8,128]{2,1,0:T(8,128)}), f32[32,8,128]{2,1,0:T(8,128)S(1)}, u32[]{:S(2)}, u32[]{:S(2)}) async-start(f32[32,8,128]{2,1,0:T(8,128)} %get-tuple-element.97.after_ref), calls=%async_computation.9 | async-start | bytes 262144 | tf_op jit(solution)/shard_map/all_to_all | solution.py:644
  130.2 1.3 copy-start.11
  138.5 2.2 copy-start.2
  140.7 2.2 copy-start.8
  142.9 1.6 copy-start.12
  145.7 13.4 %all-to-all-start.10 = ((f32[8,8,128]{2,1,0:T(8,128)}), f32[8,8,128]{2,1,0:T(8,128)S(1)}, u32[]{:S(2)}, u32[]{:S(2)}) async-start(f32[8,8,128]{2,1,0:T(8,128)} %get-tuple-element.99), calls=%async_computation.10 | async-start | bytes 65536 | tf_op jit(solution)/shard_map/all_to_all | solution.py:644
  150.5 2.2 copy-start.3
  152.6 2.2 copy-start.9
  157.0 2.1 copy-start.14
  159.1 2.2 copy-start.4
  161.3 2.2 copy-start.10
  163.5 2.2 copy-start.15
  165.7 2.2 copy-start.13
  170.7 15.2 %collective-permute-start.3 = (f32[4,128,1024]{2,1,0:T(8,128)S(1)}, f32[4,128,1024]{2,1,0:T(8,128)S(1)}, u32[]{:S(2)}, u32[]{:S(2)}) collective-permute-start(f32[4,128,1024]{2,1,0:T(8,128)S(1)} %get-tuple-element.114), channel_id=1, source_target_pairs={{0,1},{1,0},{2,3},{3,2},{4,5},{5,4},{6,7},{7,6},{8,9},{9,8},{10,11... | collective-permute-start | bytes 6291464 | tf_op jit(solution)/shard_map/ppermute | solution.py:848
  171.7 16.5 %collective-permute-start = (f32[256,512]{1,0:T(8,128)S(1)}, f32[256,512]{1,0:T(8,128)S(1)}, u32[]{:S(2)}, u32[]{:S(2)}) collective-permute-start(f32[256,512]{1,0:T(8,128)S(1)} %get-tuple-element.109), channel_id=1, source_target_pairs={{0,64},{1,193},{8,72},{9,201},{16,80},{17,209},{24,88},{25,217},{3... | collective-permute-start | bytes 1572872 | tf_op jit(solution)/shard_map/ppermute | solution.py:823
  174.8 13.4 %collective-permute-start.1 = (f32[256,512]{1,0:T(8,128)S(1)}, f32[256,512]{1,0:T(8,128)S(1)}, u32[]{:S(2)}, u32[]{:S(2)}) collective-permute-start(f32[256,512]{1,0:T(8,128)S(1)} %get-tuple-element.111), channel_id=1, source_target_pairs={{0,192},{1,65},{8,200},{9,73},{16,208},{17,81},{24,216},{25,89},{3... | collective-permute-start | bytes 1572872 | tf_op jit(solution)/shard_map/ppermute | solution.py:823
  177.7 8.1 %collective-permute-start.4 = (f32[136,512]{1,0:T(8,128)S(1)}, f32[136,512]{1,0:T(8,128)S(1)}, u32[]{:S(2)}, u32[]{:S(2)}) collective-permute-start(f32[136,512]{1,0:T(8,128)S(1)} %get-tuple-element.116), channel_id=1, source_target_pairs={{0,8},{1,57},{8,16},{9,1},{16,24},{17,9},{24,32},{25,17},{32,40},{... | collective-permute-start | bytes 835592 | tf_op jit(solution)/shard_map/ppermute | solution.py:823
  179.0 9.2 %collective-permute-start.2 = (f32[136,512]{1,0:T(8,128)S(1)}, f32[136,512]{1,0:T(8,128)S(1)}, u32[]{:S(2)}, u32[]{:S(2)}) collective-permute-start(f32[136,512]{1,0:T(8,128)S(1)} %get-tuple-element.113), channel_id=1, source_target_pairs={{0,56},{1,9},{8,0},{9,17},{16,8},{17,25},{24,16},{25,33},{32,24},{... | collective-permute-start | bytes 835592 | tf_op jit(solution)/shard_map/ppermute | solution.py:823
  186.1 12.2 %collective-permute-start.6 = (f32[128,1024]{1,0:T(8,128)S(1)}, f32[128,1024]{1,0:T(8,128)S(1)}, u32[]{:S(2)}, u32[]{:S(2)}) collective-permute-start(f32[128,1024]{1,0:T(8,128)S(1)} %get-tuple-element.123), channel_id=1, source_target_pairs={{0,2},{1,7},{8,10},{9,15},{16,18},{17,23},{24,26},{25,31},{32,34},... | collective-permute-start | bytes 1572872 | tf_op jit(solution)/shard_map/ppermute | solution.py:823
  187.9 10.4 %collective-permute-start.7 = (f32[128,1024]{1,0:T(8,128)S(1)}, f32[128,1024]{1,0:T(8,128)S(1)}, u32[]{:S(2)}, u32[]{:S(2)}) collective-permute-start(f32[128,1024]{1,0:T(8,128)S(1)} %get-tuple-element.125), channel_id=1, source_target_pairs={{0,6},{1,3},{8,14},{9,11},{16,22},{17,19},{24,30},{25,27},{32,38},... | collective-permute-start | bytes 1572872 | tf_op jit(solution)/shard_map/ppermute | solution.py:823
  188.4 10.5 %collective-permute-start.5 = (f32[256,512]{1,0:T(8,128)S(1)}, f32[256,512]{1,0:T(8,128)S(1)}, u32[]{:S(2)}, u32[]{:S(2)}) collective-permute-start(f32[256,512]{1,0:T(8,128)S(1)} %get-tuple-element.121), channel_id=1, source_target_pairs={{0,64},{1,193},{8,72},{9,201},{16,80},{17,209},{24,88},{25,217},{3... | collective-permute-start | bytes 1572872 | tf_op jit(solution)/shard_map/ppermute | solution.py:823
  189.1 9.1 %collective-permute-start.9 = (f32[136,512]{1,0:T(8,128)S(1)}, f32[136,512]{1,0:T(8,128)S(1)}, u32[]{:S(2)}, u32[]{:S(2)}) collective-permute-start(f32[136,512]{1,0:T(8,128)S(1)} %get-tuple-element.129), channel_id=1, source_target_pairs={{0,8},{1,57},{8,16},{9,1},{16,24},{17,9},{24,32},{25,17},{32,40},{... | collective-permute-start | bytes 835592 | tf_op jit(solution)/shard_map/ppermute | solution.py:823
  189.6 8.7 %collective-permute-start.8 = (f32[136,512]{1,0:T(8,128)S(1)}, f32[136,512]{1,0:T(8,128)S(1)}, u32[]{:S(2)}, u32[]{:S(2)}) collective-permute-start(f32[136,512]{1,0:T(8,128)S(1)} %get-tuple-element.127), channel_id=1, source_target_pairs={{0,56},{1,9},{8,0},{9,17},{16,8},{17,25},{24,16},{25,33},{32,24},{... | collective-permute-start | bytes 835592 | tf_op jit(solution)/shard_map/ppermute | solution.py:823
  199.7 46.7 %all-to-all-start.11 = ((f32[8,32,512]{2,1,0:T(8,128)}), f32[8,32,512]{2,1,0:T(8,128)S(1)}, u32[]{:S(2)}, u32[]{:S(2)}) async-start(f32[8,32,512]{2,1,0:T(8,128)} %bitcast.9), calls=%async_computation.11 | async-start | bytes 1048576 | tf_op jit(solution)/shard_map/all_to_all | solution.py:883
  205.4 21.0 %collective-permute-start.10 = (f32[136,512]{1,0:T(8,128)S(1)}, f32[136,512]{1,0:T(8,128)S(1)}, u32[]{:S(2)}, u32[]{:S(2)}) collective-permute-start(f32[136,512]{1,0:T(8,128)S(1)} %get-tuple-element.137), channel_id=1, source_target_pairs={{0,8},{1,57},{8,16},{9,1},{16,24},{17,9},{24,32},{25,17},{32,40},{... | collective-permute-start | bytes 835592 | tf_op jit(solution)/shard_map/ppermute | solution.py:823
  207.5 19.1 %collective-permute-start.13 = (f32[128,1024]{1,0:T(8,128)S(1)}, f32[128,1024]{1,0:T(8,128)S(1)}, u32[]{:S(2)}, u32[]{:S(2)}) collective-permute-start(f32[128,1024]{1,0:T(8,128)S(1)} %get-tuple-element.143), channel_id=1, source_target_pairs={{0,2},{1,7},{8,10},{9,15},{16,18},{17,23},{24,26},{25,31},{32,34},... | collective-permute-start | bytes 1572872 | tf_op jit(solution)/shard_map/ppermute | solution.py:823
  209.1 18.4 %collective-permute-start.12 = (f32[136,512]{1,0:T(8,128)S(1)}, f32[136,512]{1,0:T(8,128)S(1)}, u32[]{:S(2)}, u32[]{:S(2)}) collective-permute-start(f32[136,512]{1,0:T(8,128)S(1)} %get-tuple-element.140), channel_id=1, source_target_pairs={{0,56},{1,9},{8,0},{9,17},{16,8},{17,25},{24,16},{25,33},{32,24},{... | collective-permute-start | bytes 835592 | tf_op jit(solution)/shard_map/ppermute | solution.py:823
  226.5 7.8 %collective-permute-start.11 = (f32[136,512]{1,0:T(8,128)S(1)}, f32[136,512]{1,0:T(8,128)S(1)}, u32[]{:S(2)}, u32[]{:S(2)}) collective-permute-start(f32[136,512]{1,0:T(8,128)S(1)} %get-tuple-element.139), channel_id=1, source_target_pairs={{0,8},{1,57},{8,16},{9,1},{16,24},{17,9},{24,32},{25,17},{32,40},{... | collective-permute-start | bytes 835592 | tf_op jit(solution)/shard_map/ppermute | solution.py:823
  234.9 5.7 %collective-permute-start.14 = (f32[40,512]{1,0:T(8,128)S(1)}, f32[40,512]{1,0:T(8,128)S(1)}, u32[]{:S(2)}, u32[]{:S(2)}) collective-permute-start(f32[40,512]{1,0:T(8,128)S(1)} %get-tuple-element.147), channel_id=1, source_target_pairs={{0,64},{1,193},{8,72},{9,201},{16,80},{17,209},{24,88},{25,217},{3... | collective-permute-start | bytes 245768 | tf_op jit(solution)/shard_map/ppermute | solution.py:823
  235.0 5.7 %collective-permute-start.16 = (f32[40,512]{1,0:T(8,128)S(1)}, f32[40,512]{1,0:T(8,128)S(1)}, u32[]{:S(2)}, u32[]{:S(2)}) collective-permute-start(f32[40,512]{1,0:T(8,128)S(1)} %get-tuple-element.150), channel_id=1, source_target_pairs={{0,192},{1,65},{8,200},{9,73},{16,208},{17,81},{24,216},{25,89},{3... | collective-permute-start | bytes 245768 | tf_op jit(solution)/shard_map/ppermute | solution.py:823
  240.7 5.7 %collective-permute-start.15 = (f32[40,512]{1,0:T(8,128)S(1)}, f32[40,512]{1,0:T(8,128)S(1)}, u32[]{:S(2)}, u32[]{:S(2)}) collective-permute-start(f32[40,512]{1,0:T(8,128)S(1)} %get-tuple-element.149), channel_id=1, source_target_pairs={{0,64},{1,193},{8,72},{9,201},{16,80},{17,209},{24,88},{25,217},{3... | collective-permute-start | bytes 245768 | tf_op jit(solution)/shard_map/ppermute | solution.py:823

commit v2 on v1

--- a/solution.py
+++ b/solution.py
@@ -20,6 +20,7 @@
 FIRST_REACH = 75.0
 VMEM_BYTES = 16 * 2**20
 PINNED = 2**16
+BIG = 2**32
 F32 = jnp.float32
 
 
@@ -174,8 +175,9 @@
 
 
 def first_kernel(
-    cost_hbm, src_hbm, tgt_hbm, mask_hbm, dual_hbm, score_ref, base_ref, top_ref, copies_ref,
-    cost_ref, src_ref, tgt_ref, mask_ref, dual_ref, allowed_ref, log_ref, small_sem, cost_sem,
+    cost_hbm, src_hbm, tgt_hbm, mask_hbm, dual_hbm, emb_hbm, place_ref, score_ref, base_ref, top_ref,
+    copies_ref, turned_ref, cost_ref, src_ref, tgt_ref, mask_ref, dual_ref, emb_ref, allowed_ref,
+    log_ref, small_sem, cost_sem, emb_sem,
 ):
     small = [
         pltpu.make_async_copy(source, target, small_sem.at[at])
@@ -192,6 +194,11 @@
             pltpu.make_async_copy(cost_hbm.at[rows, :], cost_ref.at[rows, :], cost_sem.at[s])
         )
         blocks[-1].start()
+    embs = []
+    for s in range(emb_ref.shape[0] // LANES):
+        rows = pl.ds(s * LANES, LANES)
+        embs.append(pltpu.make_async_copy(emb_hbm.at[rows, :], emb_ref.at[rows, :], emb_sem.at[s]))
+        embs[-1].start()
     for copy in small:
         copy.wait()
     classes = mask_ref.shape[0]
@@ -227,6 +234,10 @@
         top_ref[s : s + 1, :] = to_row(jnp.concatenate(tops, axis=0))
         log_ref[s : s + 1, :] = to_row(jnp.concatenate(logs, axis=0))
     spread(copies_ref, log_ref[...])
+    for s, copy in enumerate(embs):
+        copy.wait()
+        rows = slice(s * LANES, (s + 1) * LANES)
+        turned_ref[:, rows] = emb_ref[rows, :].T
 
 
 def rebase_kernel(
@@ -295,7 +306,7 @@
 
 def row_plan_kernel(
     log_target, first, parts_ref, grad_ref, dual_in_ref, row_dual_ref, top_ref, base_dual_ref,
-    base_ref, score_ref, after_ref, out_ref, copies_ref, weight_ref, col_ref, sum_ref, tile_ref,
+    base_ref, score_ref, out_ref, copies_ref, weight_ref, col_ref, sum_ref, tile_ref,
 ):
     if first:
         dual = log_target - log_combined(parts_ref[...])
@@ -349,94 +360,6 @@
     spread(copies_ref, sum_ref[...])
 
 
-def turn_kernel(emb_hbm, after_ref, out_ref, emb_ref, sem):
-    strips = [slice(at, at + LANES) for at in range(0, emb_ref.shape[0], LANES)]
-    copies = [
-        pltpu.make_async_copy(
-            emb_hbm.at[pl.ds(at * LANES, LANES), :], emb_ref.at[pl.ds(at * LANES, LANES), :], sem.at[at]
-        )
-        for at in range(len(strips))
-    ]
-    for copy in copies:
-        copy.start()
-    for copy, strip in zip(copies, strips):
-        copy.wait()
-        out_ref[:, strip] = emb_ref[strip, :].T
-
-
-def is_near(dual_refs, row_refs, top_ref, base_dual_ref):
-    near = None
-    for ref in dual_refs:
-        test = jnp.max(jnp.abs(ref[...] - base_dual_ref[...])) <= REACH
-        near = test if near is None else jnp.logical_and(near, test)
-    for ref in row_refs:
-        near = jnp.logical_and(near, jnp.max(ref[...] + top_ref[...]) <= 60.0)
-    return near
-
-
-def most_grad_kernel(
-    log_source, log_target,
-    row1, row2, row3, col1, col2, col3, fbar2, fbar3, gbar1, gbar2, gbar3, top_ref, base_ref,
-    score_ref, out_ref, rows_ref, cols_ref, tile_ref,
-):
-    near = is_near((col2, col3), (row1, row2, row3), top_ref, col1)
-    count = groups_of(col1)
-
-    @pl.when(near)
-    def _():
-        for k, row in enumerate((row1, row2, row3)):
-            rows_ref[k] = -jnp.exp2(row[...] + top_ref[...])
-        rows_ref[3] = rows_ref[1] * fbar2[...]
-        rows_ref[4] = rows_ref[2] * fbar3[...]
-        leads = [jnp.zeros_like(col1), col2[...] - col1[...], col3[...] - col1[...]]
-        for k, grad in enumerate((gbar1, gbar2, gbar3)):
-            cols_ref[k] = jnp.exp2(leads[k] - log_target) * grad[...]
-        for k in range(2):
-            cols_ref[3 + k] = jnp.exp2(leads[k] - log_source)
-        for s in range(groups_of(row1)):
-            columns = [to_column(rows_ref[k, s : s + 1, :]) for k in range(5)]
-            for q in range(LANES // STRIP):
-                rows = slice(s * LANES + q * STRIP, s * LANES + (q + 1) * STRIP)
-                strips = [
-                    jnp.broadcast_to(part[q * STRIP : (q + 1) * STRIP], (STRIP, LANES))
-                    for part in columns
-                ]
-                for c in range(count):
-                    lanes = slice(c * LANES, (c + 1) * LANES)
-                    weight = strips[0] * cols_ref[0, c : c + 1, :]
-                    for k in range(1, 5):
-                        weight = weight + strips[k] * cols_ref[k, c : c + 1, :]
-                    out_ref[rows, lanes] = base_ref[rows, lanes] * weight
-
-    @pl.when(jnp.logical_not(near))
-    def _():
-        for k, row in enumerate((row1, row2, row3)):
-            rows_ref[k] = row[...]
-        rows_ref[3] = fbar2[...]
-        rows_ref[4] = fbar3[...]
-        for k, col in enumerate((col1, col2, col3)):
-            cols_ref[k] = col[...]
-        for k, grad in enumerate((gbar1, gbar2, gbar3)):
-            cols_ref[3 + k] = grad[...]
-
-        @pl.loop(0, groups_of(row1))
-        def _(group):
-            load_rows(score_ref, tile_ref, group)
-            columns = [to_column(rows_ref[k, pl.ds(group, 1), :]) for k in range(5)]
-            for c in range(count):
-                lanes = slice(c * LANES, (c + 1) * LANES)
-                value = jnp.zeros((LANES, LANES), F32)
-                for k in reversed(range(3)):
-                    scores = tile_ref[:, lanes] + columns[k]
-                    plan_q = jnp.exp2(scores + (cols_ref[k, c : c + 1, :] - log_target))
-                    value = value + plan_q * cols_ref[3 + k, c : c + 1, :]
-                    if k:
-                        plan_r = jnp.exp2(scores + (cols_ref[k - 1, c : c + 1, :] - log_source))
-                        value = value + plan_r * columns[2 + k]
-                start = pl.multiple_of(group * LANES, LANES)
-                out_ref[pl.ds(start, LANES), lanes] = -value
-
-
 def direction(place_ref):
     return 1 - 2 * place_ref[3]
 
@@ -468,51 +391,105 @@
     return jnp.dot(rows, grad_ref[:, :half], preferred_element_type=F32)
 
 
+def pieces(value):
+    first = value.astype(jnp.bfloat16).astype(F32)
+    second = (value - first).astype(jnp.bfloat16).astype(F32)
+    return first, second, value - first - second
+
+
 def grad_kernel(
-    log_source, counts, place_ref, parts_ref, row1, col1, top_ref, base_ref, most_ref, src_ref,
-    score_ref, out_ref, start_ref, z_far_ref, x_far_ref, rows_ref, cols_ref, tile_ref,
+    log_source, log_target, counts, place_ref, parts_ref, row1, row2, row3, col1, col2, col3,
+    fbar2, fbar3, gbar1, gbar2, gbar3, top_ref, base_ref, src_ref, score_ref,
+    out_ref, start_ref, z_far_ref, x_far_ref, z_back_ref, x_back_ref, rows_ref, cols_ref, tile_ref,
 ):
     fbar1 = -jnp.sum(parts_ref[...], axis=0)
-    row_lead = row1[...] + top_ref[...]
-    near = jnp.logical_and(jnp.max(jnp.abs(col1[...])) <= FIRST_REACH, jnp.max(row_lead) <= 60.0)
-    count = groups_of(col1)
+    leads = [ref[...] - col1[...] for ref in (col2, col3)]
+    row_leads = [ref[...] + top_ref[...] for ref in (row1, row2, row3)]
+    near = jnp.logical_and(
+        jnp.maximum(jnp.max(jnp.abs(leads[0])), jnp.max(jnp.abs(leads[1]))) <= REACH,
+        jnp.logical_and(
+            jnp.max(jnp.abs(col1[...])) <= FIRST_REACH,
+            jnp.max(jnp.maximum(jnp.maximum(row_leads[0], row_leads[1]), row_leads[2])) <= 60.0,
+        ),
+    )
+    count, groups = groups_of(col1), groups_of(row1)
 
     @pl.when(near)
     def _():
-        rows_ref[...] = -jnp.exp2(row_lead) * fbar1
-        cols_ref[...] = jnp.exp2(-col1[...] - log_source)
+        powers = [-jnp.exp2(lead) for lead in row_leads]
+        factors = [*powers, powers[1] * fbar2[...], powers[2] * fbar3[...], powers[0] * fbar1]
+        for k in range(8):
+            rows_ref[:, k, :] = factors[k] if k < 6 else jnp.zeros_like(fbar1)
+        column_factors = [
+            jnp.exp2(jnp.full_like(leads[0], -log_target)) * gbar1[...],
+            jnp.exp2(leads[0] - log_target) * gbar2[...],
+            jnp.exp2(leads[1] - log_target) * gbar3[...],
+            jnp.exp2(jnp.full_like(leads[0], -log_source)),
+            jnp.exp2(leads[0] - log_source),
+            jnp.exp2(-col1[...] - log_source),
+        ]
+        cols_ref[...] = jnp.zeros_like(cols_ref)
+        for k, factor in enumerate(column_factors):
+            for c in range(count):
+                cols_ref[k : k + 1, c * LANES : (c + 1) * LANES] = factor[c : c + 1, :]
+        b1, b2, b3 = pieces(cols_ref[...])
+        right = jnp.concatenate([b1, b2, b1, b2, b3, b1], axis=0).astype(jnp.bfloat16)
         held = [None] * count
-        for s in range(groups_of(row1)):
-            column = jnp.broadcast_to(to_column(rows_ref[s : s + 1, :]), (LANES, LANES))
+        for s in range(groups):
+            a1, a2, a3 = pieces(rows_ref[s])
+            left = jnp.concatenate([a1, a1, a2, a2, a1, a3], axis=0).astype(jnp.bfloat16)
+            tile_ref[...] = lax.dot_general(
+                left, right, (((0,), (0,)), ((), ())), preferred_element_type=F32
+            )
+            column = jnp.broadcast_to(to_column(rows_ref[s, 5:6, :]), (LANES, LANES))
             rows = slice(s * LANES, (s + 1) * LANES)
             for c in range(count):
                 lanes = slice(c * LANES, (c + 1) * LANES)
-                term = base_ref[rows, lanes] * column * cols_ref[c : c + 1, :]
-                out_ref[rows, lanes] = (most_ref[rows, lanes] + term).astype(jnp.bfloat16)
-                term = jnp.sum(term.reshape(LANES // 8, 8, LANES), axis=0)
+                base = base_ref[rows, lanes]
+                out_ref[rows, lanes] = (base * tile_ref[:, lanes]).astype(jnp.bfloat16)
+                term = jnp.sum((base * column).reshape(LANES // 8, 8, LANES), axis=0)
                 held[c] = term if held[c] is None else held[c] + term
         for c, term in enumerate(held):
-            start_ref[c : c + 1, :] = jnp.sum(term, axis=0, keepdims=True)
+            start_ref[c : c + 1, :] = (
+                jnp.sum(term, axis=0, keepdims=True) * column_factors[5][c : c + 1, :]
+            )
 
     @pl.when(jnp.logical_not(near))
     def _():
-        rows_ref[...] = -fbar1
+        zero = jnp.zeros_like(fbar1)
+        for k, value in enumerate(
+            (row1[...], row2[...], row3[...], fbar1, fbar2[...], fbar3[...], zero, zero)
+        ):
+            rows_ref[:, k, :] = value
         start_ref[...] = jnp.zeros_like(start_ref)
-
-        @pl.loop(0, groups_of(row1))
+        columns_of = (None, col1, col2, col3)
+        grads_of = (None, gbar1, gbar2, gbar3)
+
+        @pl.loop(0, groups)
         def _(group):
             load_rows(score_ref, tile_ref, group)
-            column = to_column(row1[pl.ds(group, 1), :]) - log_source
-            weight = to_column(rows_ref[pl.ds(group, 1), :])
+            taken = rows_ref[group]
+            columns = [to_column(taken[k : k + 1, :]) for k in range(6)]
             rows = pl.ds(pl.multiple_of(group * LANES, LANES), LANES)
             for c in range(count):
                 lanes = slice(c * LANES, (c + 1) * LANES)
-                term = jnp.exp2(tile_ref[:, lanes] + column) * weight
-                out_ref[rows, lanes] = (most_ref[rows, lanes] + term).astype(jnp.bfloat16)
-                start_ref[c : c + 1, :] += jnp.sum(term, axis=0, keepdims=True)
-
+                value = jnp.zeros((LANES, LANES), F32)
+                for k in reversed(range(3)):
+                    scores = tile_ref[:, lanes] + columns[k]
+                    plan_q = jnp.exp2(scores + (columns_of[k + 1][c : c + 1, :] - log_target))
+                    value = value + plan_q * grads_of[k + 1][c : c + 1, :]
+                    before = columns_of[k][c : c + 1, :] if k else jnp.zeros((1, LANES), F32)
+                    term = jnp.exp2(scores + (before - log_source)) * columns[3 + k]
+                    value = value + term
+                    if not k:
+                        start_ref[c : c + 1, :] -= jnp.sum(term, axis=0, keepdims=True)
+                out_ref[rows, lanes] = (-value).astype(jnp.bfloat16)
+
+    reach = counts[1] // 2
+    put(z_far_ref, z_block(place_ref, src_ref, out_ref, reach, counts), start_ref[...])
+    put(z_back_ref, z_block(place_ref, src_ref, out_ref, 1 - reach, counts), start_ref[...])
     x_far_ref[...] = x_block(place_ref, src_ref, out_ref, counts[0] // 2, counts)
-    put(z_far_ref, z_block(place_ref, src_ref, out_ref, counts[1] // 2, counts), start_ref[...])
+    x_back_ref[...] = x_block(place_ref, src_ref, out_ref, -1, counts)
 
 
 def put(out_ref, block, rider):
@@ -526,35 +503,27 @@
     return ref[ref.shape[0] - 8 :, :LANES]
 
 
-def x_part_kernel(y_count, place_ref, grad_ref, tgt_ref, sent_ref, kept_ref, order_ref):
-    block = tgt_ref.shape[0] // (2 * y_count)
+def x_part_kernel(y_count, place_ref, grad_ref, tgt_ref, after_ref, sent_ref, kept_ref, order_ref):
+    block = tgt_ref.shape[1] // (2 * y_count)
     core, turn = place_ref[3], direction(place_ref)
     for side, out_ref in ((0, sent_ref), (1, kept_ref)):
         for k, offset in enumerate((2, 1, -1, 0)):
             step = offset * (2 * side - 1)
             at = lax.rem(place_ref[1] + turn * step + y_count, y_count)
             owner = at * 2 + (core if side else 1 - core)
-            order_ref[k * block : (k + 1) * block, :] = tgt_ref[
-                pl.ds(pl.multiple_of(owner * block, block), block), :
+            order_ref[:, k * block : (k + 1) * block] = tgt_ref[
+                :, pl.ds(pl.multiple_of(owner * block, block), block)
             ]
-        product = lax.dot_general(
-            order_ref[...], grad_ref[...], (((1,), (1,)), ((), ())), preferred_element_type=F32
-        )
-        out_ref[...] = product.reshape(out_ref.shape)
-
-
-def y_parts_kernel(counts, place_ref, grad_ref, src_ref, start_ref, after_ref, *outs):
-    x_outs, z_outs = outs[:3], outs[3:]
-    for out_ref, offset in zip(x_outs, (-1, 1, 0)):
+        out_ref[...] = jnp.dot(grad_ref[...], order_ref[...], preferred_element_type=F32)
+
+
+def y_parts_kernel(counts, place_ref, grad_ref, src_ref, *outs):
+    reach = counts[1] // 2
+    offsets = [*range(reach - 1, 0, -1), *range(2 - reach, 1)]
+    for out_ref, offset in zip(outs, offsets):
+        out_ref[...] = z_block(place_ref, src_ref, grad_ref, offset, counts)
+    for out_ref, offset in zip(outs[len(offsets) :], (1, 0)):
         out_ref[...] = x_block(place_ref, src_ref, grad_ref, offset, counts)
-    reach = counts[1] // 2
-    offsets = [1 - reach, *range(reach - 1, 0, -1), *range(2 - reach, 1)]
-    for out_ref, offset in zip(z_outs, offsets):
-        block = z_block(place_ref, src_ref, grad_ref, offset, counts)
-        if offset == 1 - reach:
-            put(out_ref, block, start_ref[...])
-        else:
-            out_ref[...] = block
 
 
 def add_kernel(count, *refs):
@@ -566,6 +535,13 @@
     token_ref[...] = jnp.zeros_like(token_ref)
 
 
+def turn_kernel(sum_ref, up_ref, after_ref, out_ref, token_ref):
+    for s in range(sum_ref.shape[0] // LANES):
+        rows = slice(s * LANES, (s + 1) * LANES)
+        out_ref[:, rows] = (sum_ref[rows, :] + up_ref[rows, :]).T
+    token_ref[...] = jnp.zeros_like(token_ref)
+
+
 def pair_kernel(one_ref, up_ref, own_ref, down_ref, after_ref, pay_ref, sum_ref, token_ref):
     pay_ref[...] = one_ref[...] + up_ref[...]
     sum_ref[...] = own_ref[...] + down_ref[...]
@@ -580,8 +556,10 @@
 
 
 def chip_kernel(kept_ref, arrived_ref, after_ref, *outs):
+    block = outs[0].shape[1]
     for k, out_ref in enumerate(outs[:-1]):
-        out_ref[...] = kept_ref[k] + arrived_ref[k]
+        lanes = slice(k * block, (k + 1) * block)
+        out_ref[...] = kept_ref[:, lanes] + arrived_ref[:, lanes]
     outs[-1][...] = jnp.zeros_like(outs[-1])
 
 
@@ -611,7 +589,7 @@
 
 
 def call(
-    kernel, arguments, outs, scratch=(), in_hbm=(), loose=(), in_smem=(), last=False, name=None
+    kernel, arguments, outs, scratch=(), in_hbm=(), loose=(), in_smem=(), free=(), last=False, flops=1024, name=None
 ):
     spaces, values = [], []
     for at, value in enumerate(arguments):
@@ -622,7 +600,7 @@
             space = pl.ANY
         elif at in in_smem:
             space = pltpu.SMEM
-        if at in in_hbm or (space is pltpu.VMEM and value.size >= PINNED):
+        if at in in_hbm or (space is pltpu.VMEM and value.size >= PINNED and at not in free):
             value = pltpu.with_memory_space_constraint(value, space)
         spaces.append(space)
         values.append(value)
@@ -636,6 +614,7 @@
         out_specs=[pl.BlockSpec(memory_space=pltpu.VMEM)] * len(outs),
         scratch_shapes=list(scratch),
         compiler_params=pltpu.CompilerParams(vmem_limit_bytes=VMEM_BYTES),
+        cost_estimate=pl.CostEstimate(flops=flops, bytes_accessed=1024, transcendentals=0),
         name=name,
     )(*values)
 
@@ -648,13 +627,12 @@
     return jax.ShapeDtypeStruct((8, LANES), F32)
 
 
-def added(values, after, last=False):
+def added(values, after):
     return call(
         functools.partial(add_kernel, len(values)),
         (*values, after),
         [jax.ShapeDtypeStruct(values[0].shape, F32), token()],
         loose=(len(values),),
-        last=last,
         name="added",
     )
 
@@ -699,22 +677,32 @@
     row_held, col_held = pltpu.VMEM(row_shape, F32), pltpu.VMEM(col_shape, F32)
     slow = [pltpu.VMEM((LANES, tgt_cols), F32)]
 
-    score, start_base, start_top, copies = call(
+    x_count, z_count, y_count = 4, row_count // 4, col_count // 2
+    counts = (x_count, z_count)
+    owned = width // row_count
+    row_at, col_at = lax.axis_index("rows"), lax.axis_index("cols")
+    place = jnp.stack(
+        [row_at // z_count, col_at // 2, row_at % z_count, col_at % 2]
+    ).astype(jnp.int32)
+    score, start_base, start_top, copies, src_turned = call(
         first_kernel,
-        (cost, src_label, tgt_label, class_mask, g_start),
-        [matrix, matrix, row_vector, row_copies],
+        (cost, src_label, tgt_label, class_mask, g_start, src_emb, place),
+        [matrix, matrix, row_vector, row_copies, array(src_emb.shape[::-1], src_emb.dtype)],
         [
             pltpu.VMEM(cost.shape, cost.dtype),
             pltpu.VMEM(row_shape, jnp.int32),
             pltpu.VMEM(col_shape, jnp.int32),
             pltpu.VMEM(class_mask.shape, jnp.int32),
             col_held,
+            pltpu.VMEM(src_emb.shape, src_emb.dtype),
             pltpu.VMEM((LANES, tgt_cols), F32),
             row_held,
             pltpu.SemaphoreType.DMA((4,)),
             pltpu.SemaphoreType.DMA(row_shape[:1]),
+            pltpu.SemaphoreType.DMA(row_shape[:1]),
         ],
-        in_hbm=range(5),
+        in_hbm=range(6),
+        in_smem=(6,),
         name="first_row_logs",
     )
 
@@ -746,13 +734,12 @@
     )
     row3, copies = col_logs(exchanged(copies, "cols"), top, col1, base)
 
-    def row_plan(first, parts, grad, dual, row, after):
+    def row_plan(first, parts, grad, dual, row):
         return call(
             functools.partial(row_plan_kernel, log_target, first),
-            (parts, grad, dual, row, top, col1, base, score, after),
+            (parts, grad, dual, row, top, col1, base, score),
             [col_vector, row_copies],
             [col_held, col_held, row_held] + slow,
-            loose=(8,),
                 name="row_plan",
         )
 
@@ -766,42 +753,12 @@
         )
 
     none = jnp.zeros(row_shape, F32)
-
-    def turned(emb, after):
-        return call(
-            turn_kernel,
-            (emb, after),
-            [array(emb.shape[::-1], emb.dtype)],
-            [pltpu.VMEM(emb.shape, emb.dtype), pltpu.SemaphoreType.DMA((emb.shape[0] // LANES,))],
-            in_hbm=(0,),
-            loose=(1,),
-            name="turned",
-        )[0]
-
-    col3, copies = row_plan(True, exchanged(copies, "rows"), g_bar, col2, row3, g_bar)
+    col3, copies = row_plan(True, exchanged(copies, "rows"), g_bar, col2, row3)
     fbar3, copies = col_plan(exchanged(copies, "cols"), f_bar, col2, row3)
-    src_turned = turned(src_emb, copies)
-    gbar2, copies = row_plan(False, exchanged(copies, "rows"), g_bar, col2, row2, src_turned)
+    gbar2, copies = row_plan(False, exchanged(copies, "rows"), g_bar, col2, row2)
     fbar2, copies = col_plan(exchanged(copies, "cols"), none, col1, row2)
-    tgt_turned = turned(tgt_emb, copies)
-    gbar1, copies = row_plan(False, exchanged(copies, "rows"), g_bar, col1, row1, tgt_turned)
+    gbar1, copies = row_plan(False, exchanged(copies, "rows"), g_bar, col1, row1)
     parts = exchanged(copies, "cols")
-    (most,) = call(
-        functools.partial(most_grad_kernel, log_source, log_target),
-        (
-            row1, row2, row3, col1, col2, col3, fbar2, fbar3, gbar1, gbar2, g_bar, top, base, score,
-        ),
-        [matrix],
-        [pltpu.VMEM((5,) + row_shape, F32), pltpu.VMEM((6,) + col_shape, F32)] + slow,
-        name="most_cost_grad",
-    )
-    x_count, z_count, y_count = 4, row_count // 4, col_count // 2
-    counts = (x_count, z_count)
-    owned = width // row_count
-    row_at, col_at = lax.axis_index("rows"), lax.axis_index("cols")
-    place = jnp.stack(
-        [row_at // z_count, col_at // 2, row_at % z_count, col_at % 2]
-    ).astype(jnp.int32)
     devices = [
         (x, y, z, core)
         for x in range(x_count)
@@ -826,52 +783,55 @@
     z_rows, x_rows = x_count * owned, z_count * owned
     z_shape, z_riding = array((z_rows, half)), array((z_rows + 8, half))
     x_shape = array((x_rows, half))
-    rounded, start, z_far, x_far = call(
-        functools.partial(grad_kernel, log_source, counts),
-        (place, parts, row1, col1, top, base, most, src_turned, score),
-        [array(cost.shape, jnp.bfloat16), col_vector, z_riding, x_shape],
-        [row_held, col_held] + slow,
+    rounded, start, z_far, x_far, z_back, x_back = call(
+        functools.partial(grad_kernel, log_source, log_target, counts),
+        (
+            place, parts, row1, row2, row3, col1, col2, col3, fbar2, fbar3, gbar1, gbar2, g_bar,
+            top, base, src_turned, score,
+        ),
+        [array(cost.shape, jnp.bfloat16), col_vector, z_riding, x_shape, z_riding, x_shape],
+        [pltpu.VMEM((row_shape[0], 8, LANES), F32), pltpu.VMEM((8, tgt_cols), F32)] + slow,
         in_smem=(0,),
         name="cost_grad",
     )
-    z_up = turn(z_far, 2, 1)
-    x_up = turn(x_far, 0, 1)
-    chip_part = array((y_count, width // col_count, src_rows))
+    z_up, z_down = turn(z_far, 2, 1), turn(z_back, 2, -1)
+    x_up, x_down = turn(x_far, 0, 1), turn(x_back, 0, -1)
+    outs = call(
+        functools.partial(y_parts_kernel, counts),
+        (place, rounded, src_turned),
+        [z_shape] * (z_count - 2) + [x_shape] * 2,
+        in_smem=(0,),
+        flops=BIG,
+        name="grad_y_parts",
+    )
+    z_3, z_2, z_1, z_back2, z_back1, z_own, x_one, x_own = outs
+    z_pay, up_held = passed(z_3, z_up, start, start)
+    z_up = turn(z_pay, 2, 1)
+    chip_part = array((src_rows, width // 2))
     sent, kept = call(
         functools.partial(x_part_kernel, y_count),
-        (place, rounded, tgt_turned),
+        (place, rounded, tgt_emb, up_held),
         [chip_part, chip_part],
-        [pltpu.VMEM((width // 2, tgt_cols), jnp.bfloat16)],
+        [pltpu.VMEM((tgt_cols, width // 2), jnp.bfloat16)],
         in_smem=(0,),
+        loose=(3,),
+        free=(2,),
+        flops=BIG,
         name="grad_x_parts",
     )
     arrived = lax.ppermute(sent, "cols", [(at, at ^ 1) for at in range(col_count)])
-    outs = call(
-        functools.partial(y_parts_kernel, counts),
-        (place, rounded, src_turned, start, kept),
-        [x_shape] * 3 + [z_riding] + [z_shape] * (z_count - 2),
-        in_smem=(0,),
-        loose=(4,),
-        name="grad_y_parts",
-    )
-    x_back, x_one, x_own, z_back, z_3, z_2, z_1, z_back2, z_back1, z_own = outs
-    x_down = turn(x_back, 0, -1)
-    z_down = turn(z_back, 2, -1)
-    z_pay, up_held = passed(z_3, z_up, start, start)
-    z_up = turn(z_pay, 2, 1)
-    far, one, back, own = (array((width // col_count, src_rows)) for _ in range(4))
-    far, one, back, own, mark = call(
-        chip_kernel,
-        (kept, arrived, up_held),
-        [far, one, back, own, token()],
-        loose=(2,),
-        name="chip_sums",
-    )
-    y_up, y_down = turn(far, 1, 1), turn(back, 1, -1)
-    z_pay, down_held = passed(z_back2, z_down, jnp.zeros_like(start), mark)
+    z_pay, down_held = passed(z_back2, z_down, jnp.zeros_like(start), kept)
     z_down = turn(z_pay, 2, -1)
     x_pay, x_sum, mark = paired(x_one, x_up, x_own, x_down, down_held)
     x_up = turn(x_pay, 0, 1)
+    far, one, back, own, mark = call(
+        chip_kernel,
+        (kept, arrived, mark),
+        [array((src_rows, width // col_count))] * 4 + [token()],
+        loose=(2,),
+        name="chip_sums",
+    )
+    y_up, y_down = turn(far, 1, 1), turn(back, 1, -1)
     z_pay, up_held = passed(z_2, z_up, up_held, mark)
     z_up = turn(z_pay, 2, 1)
     z_pay, down_held = passed(z_back1, z_down, down_held, up_held)
@@ -885,7 +845,14 @@
     )
     z_pay, up_held = passed(z_1, z_up, up_held, mark)
     z_up = turn(z_pay, 2, 1)
-    grad_x, mark = added((y_sum, y_up), up_held, last=True)
+    grad_x, mark = call(
+        turn_kernel,
+        (y_sum, y_up, up_held),
+        [array((width // col_count, src_rows)), token()],
+        loose=(2,),
+        last=True,
+        name="grad_x",
+    )
     last, riding = array((owned, half)), array((owned + 8, half))
     x_far, x_back, x_one, x_own, start = call(
         functools.partial(split_kernel, x_count),

time: 248 us -> 240 us (0.968)
  blocking collectives: 91.4 us -> 125 us
  local copies, waits for them, and re-layouts: 24.7 us -> 0.01 us
  starting transfers between devices: 40.3 us -> 21.1 us
    all_to_all x8 -> x11, blocking collectives: 91.4 us -> 125 us  [exchanged(): return lax.all_to_all(copies, axis, 0, 0, tiled=True)]
    unnamed x36 -> x6, local copies, waits for them, and re-layouts: 24.7 us -> 0.01 us
    ppermute x16, waiting for transfers between devices: 42.2 us -> 58.1 us  [turn(): return lax.ppermute(value, ('rows', 'cols'), moves)]
    all_to_all x3 -> x0, waiting for transfers between devices: 15.4 us -> none  [exchanged(): return lax.all_to_all(copies, axis, 0, 0, tiled=True)]
    all_to_all x3 -> x0, starting transfers between devices: 12.4 us -> none  [exchanged(): return lax.all_to_all(copies, axis, 0, 0, tiled=True)]
    ppermute x16, starting transfers between devices: 21.2 us -> 17.5 us  [turn(): return lax.ppermute(value, ('rows', 'cols'), moves)]
    pallas_call x30 -> x27, Pallas kernels: 32 us -> 34.1 us  [call(): pl.pallas_call(kernel, out_shape=[pltpu.VMEM(out.shape, out.dtype) if mat...]
  transfers between devices with their start and end apart: 21 -> 18, of which waited for: 9 -> 9; matrix products, arithmetic and copies ran while one was open for 0% -> 0% of each run, Pallas kernels for 4% -> 2%
where the time goes in v2:
time: 240 us; the launch traced here: 239 us
  blocking collectives  125 us (52%)
  waiting for transfers between devices  58.1 us (24%)
  Pallas kernels  34.1 us (14%)
  starting transfers between devices  21.1 us (9%)
    all_to_all x11, blocking collectives, exchanged(): return lax.all_to_all(copies, axis, 0, 0, tiled=True)  125 us
    ppermute x16, waiting for transfers between devices, turn(): return lax.ppermute(value, ('rows', 'cols'), moves)  58.1 us
    pallas_call x27, Pallas kernels, call(): pl.pallas_call(kernel, out_shape=[pltpu.VMEM(out.shape, out.dtype) if mat...  34.1 us
    ppermute x16, starting transfers between devices, turn(): return lax.ppermute(value, ('rows', 'cols'), moves)  17.5 us
  transfers between devices with their start and end apart: 18, of which 9 were waited for; matrix products, arithmetic and copies ran while one was open for 0% of the time, Pallas kernels for 2%

profile of v2, /device:TPU:8, one launch (start us, length us, event | category | flops | bytes accessed | tf_op | source)
XLA Modules:
  0.0 238.9 jit_solution(14142332378454472041)
XLA Ops:
  0.7 0.1 pad_add_fusion.place_ref
  0.7 7.1 %first_row_logs.1 = (f32[1024,1024]{1,0:T(8,128)S(1)}, f32[1024,1024]{1,0:T(8,128)S(1)}, f32[8,128]{1,0:T(8,128)S(1)}, f32[8,8,128]{2,1,0:T(8,128)S(1)}, bf16[1024,1024]{1,0:T(8,128)(2,1)S(1)}) custom-call(bf16[1024,1024]{1,0:T(8,128)(2,1)} %cost_hbm.1, s32[8,128]{1,0:T(8,128)} %bitcast.16, s32[8,128]{1,0:T(8,128)} %bitcast.17, s32[64,64]{1,0:T(8,128)} %mask_hbm.1, ...), custom_call_target="tpu_custom_call" | custom-call | flops 1024 | bytes 1024 | tf_op jit(solution)/shard_map/first_row_logs/pallas_call | solution.py:607
  7.9 8.7 %all_to_all.60.parts_ref = f32[8,8,128]{2,1,0:T(8,128)S(1)} all-to-all(f32[8,8,128]{2,1,0:T(8,128)S(1)} %get-tuple-element.80), channel_id=1, replica_groups=mesh['rows'=32,'cols'=8] {'cols'}, dimensions={0} | all-to-all | bytes 65536 | tf_op jit(solution)/shard_map/all_to_all | solution.py:623
  16.6 2.9 %col_logs.3 = (f32[8,128]{1,0:T(8,128)S(1)}, f32[32,8,128]{2,1,0:T(8,128)S(1)}) custom-call(f32[8,8,128]{2,1,0:T(8,128)S(1)} %all_to_all.60.parts_ref, f32[8,128]{1,0:T(8,128)S(1)} %get-tuple-element.81.top_ref, f32[8,128]{1,0:T(8,128)S(1)} %broadcast_1_base_dual_ref_outer_ref_held_ref.2.base_dual_ref.outer_ref.held_ref, ...), custom_call_target="tpu_custom_call" | custom-call | flops 1024 | bytes 1024 | tf_op jit(solution)/shard_map/col_logs/pallas_call | solution.py:607
  19.5 21.5 %all_to_all.61.parts_ref = f32[32,8,128]{2,1,0:T(8,128)S(1)} all-to-all(f32[32,8,128]{2,1,0:T(8,128)S(1)} %get-tuple-element.84), channel_id=1, replica_groups=mesh['rows'=32,'cols'=8] {'rows'}, dimensions={0} | all-to-all | bytes 262144 | tf_op jit(solution)/shard_map/all_to_all | solution.py:623
  40.9 2.5 %second_row_logs.1 = (f32[1024,1024]{1,0:T(8,128)S(1)}, f32[8,128]{1,0:T(8,128)S(1)}, f32[8,128]{1,0:T(8,128)S(1)}, f32[8,8,128]{2,1,0:T(8,128)S(1)}) custom-call(f32[32,8,128]{2,1,0:T(8,128)S(1)} %all_to_all.61.parts_ref, f32[1024,1024]{1,0:T(8,128)S(1)} %get-tuple-element.83.score_ref), custom_call_target="tpu_custom_call" | custom-call | flops 1024 | bytes 1024 | tf_op jit(solution)/shard_map/second_row_logs/pallas_call | solution.py:607
  43.4 7.7 %all_to_all.62.parts_ref = f32[8,8,128]{2,1,0:T(8,128)S(1)} all-to-all(f32[8,8,128]{2,1,0:T(8,128)S(1)} %get-tuple-element.85), channel_id=1, replica_groups=mesh['rows'=32,'cols'=8] {'cols'}, dimensions={0} | all-to-all | bytes 65536 | tf_op jit(solution)/shard_map/all_to_all | solution.py:623
  51.1 0.6 col_logs.4
  51.8 13.9 %all_to_all.63.parts_ref = f32[32,8,128]{2,1,0:T(8,128)S(1)} all-to-all(f32[32,8,128]{2,1,0:T(8,128)S(1)} %get-tuple-element.89), channel_id=1, replica_groups=mesh['rows'=32,'cols'=8] {'rows'}, dimensions={0} | all-to-all | bytes 262144 | tf_op jit(solution)/shard_map/all_to_all | solution.py:623
  65.6 0.6 third_row_logs.1
  66.2 7.8 %all_to_all.64.parts_ref = f32[8,8,128]{2,1,0:T(8,128)S(1)} all-to-all(f32[8,8,128]{2,1,0:T(8,128)S(1)} %get-tuple-element.90), channel_id=1, replica_groups=mesh['rows'=32,'cols'=8] {'cols'}, dimensions={0} | all-to-all | bytes 65536 | tf_op jit(solution)/shard_map/all_to_all | solution.py:623
  74.0 0.6 col_logs.5
  74.7 13.9 %all_to_all.65.parts_ref = f32[32,8,128]{2,1,0:T(8,128)S(1)} all-to-all(f32[32,8,128]{2,1,0:T(8,128)S(1)} %get-tuple-element.91), channel_id=1, replica_groups=mesh['rows'=32,'cols'=8] {'rows'}, dimensions={0} | all-to-all | bytes 262144 | tf_op jit(solution)/shard_map/all_to_all | solution.py:623
  88.5 0.6 row_plan.3
  89.1 7.8 %all_to_all.66.parts_ref = f32[8,8,128]{2,1,0:T(8,128)S(1)} all-to-all(f32[8,8,128]{2,1,0:T(8,128)S(1)} %get-tuple-element.94), channel_id=1, replica_groups=mesh['rows'=32,'cols'=8] {'cols'}, dimensions={0} | all-to-all | bytes 65536 | tf_op jit(solution)/shard_map/all_to_all | solution.py:623
  97.0 0.5 col_plan.2
  97.5 13.9 %all_to_all.67.parts_ref = f32[32,8,128]{2,1,0:T(8,128)S(1)} all-to-all(f32[32,8,128]{2,1,0:T(8,128)S(1)} %get-tuple-element.95), channel_id=1, replica_groups=mesh['rows'=32,'cols'=8] {'rows'}, dimensions={0} | all-to-all | bytes 262144 | tf_op jit(solution)/shard_map/all_to_all | solution.py:623
  111.3 0.5 row_plan.4
  111.9 7.8 %all_to_all.68.parts_ref = f32[8,8,128]{2,1,0:T(8,128)S(1)} all-to-all(f32[8,8,128]{2,1,0:T(8,128)S(1)} %get-tuple-element.97), channel_id=1, replica_groups=mesh['rows'=32,'cols'=8] {'cols'}, dimensions={0} | all-to-all | bytes 65536 | tf_op jit(solution)/shard_map/all_to_all | solution.py:623
  119.7 0.7 col_plan.3
  120.4 13.9 %all_to_all.69.parts_ref = f32[32,8,128]{2,1,0:T(8,128)S(1)} all-to-all(f32[32,8,128]{2,1,0:T(8,128)S(1)} %get-tuple-element.98), channel_id=1, replica_groups=mesh['rows'=32,'cols'=8] {'rows'}, dimensions={0} | all-to-all | bytes 262144 | tf_op jit(solution)/shard_map/all_to_all | solution.py:623
  134.3 0.5 row_plan.5
  134.8 7.8 %all_to_all.70.parts_ref = f32[8,8,128]{2,1,0:T(8,128)S(1)} all-to-all(f32[8,8,128]{2,1,0:T(8,128)S(1)} %get-tuple-element.100), channel_id=1, replica_groups=mesh['rows'=32,'cols'=8] {'cols'}, dimensions={0} | all-to-all | bytes 65536 | tf_op jit(solution)/shard_map/all_to_all | solution.py:623
  142.6 7.5 %cost_grad.1 = (bf16[1024,1024]{1,0:T(8,128)(2,1)S(1)}, f32[8,128]{1,0:T(8,128)S(1)}, f32[136,512]{1,0:T(8,128)S(1)}, f32[256,512]{1,0:T(8,128)S(1)}, f32[136,512]{1,0:T(8,128)S(1)}, /*index=5*/f32[256,512]{1,0:T(8,128)S(1)}) custom-call(s32[4]{0:T(128)S(1)} %pad_add_fusion.place_ref, f32[8,8,128]{2,1,0:T(8,128)S(1)} %all_to_all.70.parts_ref, ...), custom_call_target="tpu_custom_call" | custom-call | flops 1024 | bytes 1024 | tf_op jit(solution)/shard_map/cost_grad/pallas_call | solution.py:607
  150.1 1.4 collective-permute-start.3
  151.5 2.1 grad_y_parts.1
  153.6 4.3 %collective-permute-done.3.arrived_ref = f32[136,512]{1,0:T(8,128)S(1)} collective-permute-done((f32[136,512]{1,0:T(8,128)S(1)}, f32[136,512]{1,0:T(8,128)S(1)}, u32[]{:S(2)}, u32[]{:S(2)}) %collective-permute-start.3) | collective-permute-done | bytes 278560 | tf_op jit(solution)/shard_map/ppermute | solution.py:780
  158.0 3.2 %grad_x_parts.1 = (f32[1024,512]{1,0:T(8,128)S(1)}, f32[1024,512]{1,0:T(8,128)S(1)}) custom-call(s32[4]{0:T(128)S(1)} %pad_add_fusion.place_ref, bf16[1024,1024]{1,0:T(8,128)(2,1)S(1)} %get-tuple-element.107.grad_ref, bf16[1024,1024]{1,0:T(8,128)(2,1)S(1)} %copy-done.2, f32[8,128]{1,0:T(8,128)S(1)} %get-tuple-element.117.after_ref.held_ref), custom_call_target="tpu_custom_call" | custom-call | flops 4294967296 | bytes 1024 | tf_op jit(solution)/shard_map/grad_x_parts/pallas_call | solution.py:607
  161.3 0.1 collective-permute-start.5
  161.4 0.7 collective-permute-start
  162.1 2.6 %collective-permute-start.1 = (f32[256,512]{1,0:T(8,128)S(1)}, f32[256,512]{1,0:T(8,128)S(1)}, u32[]{:S(2)}, u32[]{:S(2)}) collective-permute-start(f32[256,512]{1,0:T(8,128)S(1)} %get-tuple-element.111), channel_id=1, source_target_pairs={{0,192},{1,65},{8,200},{9,73},{16,208},{17,81},{24,216},{25,89},{3... | collective-permute-start | bytes 1572872 | tf_op jit(solution)/shard_map/ppermute | solution.py:780
  164.7 0.0 collective-permute-start.2
  164.7 6.5 %collective-permute-done.2.arrived_ref = f32[136,512]{1,0:T(8,128)S(1)} collective-permute-done((f32[136,512]{1,0:T(8,128)S(1)}, f32[136,512]{1,0:T(8,128)S(1)}, u32[]{:S(2)}, u32[]{:S(2)}) %collective-permute-start.2) | collective-permute-done | bytes 278560 | tf_op jit(solution)/shard_map/ppermute | solution.py:780
  171.3 5.8 %collective-permute-done.up_ref = f32[256,512]{1,0:T(8,128)S(1)} collective-permute-done((f32[256,512]{1,0:T(8,128)S(1)}, f32[256,512]{1,0:T(8,128)S(1)}, u32[]{:S(2)}, u32[]{:S(2)}) %collective-permute-start) | collective-permute-done | bytes 524320 | tf_op jit(solution)/shard_map/ppermute | solution.py:780
  177.1 0.0 collective-permute-done.1.down_ref
  177.1 0.1 paired.2
  177.2 0.0 collective-permute-done.5.arrived_ref
  177.2 0.5 chip_sums.1
  177.7 0.8 collective-permute-start.6
  178.5 1.5 collective-permute-start.7
  180.0 0.0 collective-permute-start.4
  180.0 0.1 collective-permute-start.9
  180.1 3.2 %collective-permute-start.8 = (f32[136,512]{1,0:T(8,128)S(1)}, f32[136,512]{1,0:T(8,128)S(1)}, u32[]{:S(2)}, u32[]{:S(2)}) collective-permute-start(f32[136,512]{1,0:T(8,128)S(1)} %get-tuple-element.129), channel_id=1, source_target_pairs={{0,56},{1,9},{8,0},{9,17},{16,8},{17,25},{24,16},{25,33},{32,24},{... | collective-permute-start | bytes 835592 | tf_op jit(solution)/shard_map/ppermute | solution.py:780
  183.3 6.1 %collective-permute-done.9.arrived_ref = f32[136,512]{1,0:T(8,128)S(1)} collective-permute-done((f32[136,512]{1,0:T(8,128)S(1)}, f32[136,512]{1,0:T(8,128)S(1)}, u32[]{:S(2)}, u32[]{:S(2)}) %collective-permute-start.9) | collective-permute-done | bytes 278560 | tf_op jit(solution)/shard_map/ppermute | solution.py:780
  189.5 0.0 collective-permute-done.8.arrived_ref
  189.5 3.0 %collective-permute-done.6.up_ref = f32[1024,128]{1,0:T(8,128)S(1)} collective-permute-done((f32[1024,128]{1,0:T(8,128)S(1)}, f32[1024,128]{1,0:T(8,128)S(1)}, u32[]{:S(2)}, u32[]{:S(2)}) %collective-permute-start.6) | collective-permute-done | bytes 524320 | tf_op jit(solution)/shard_map/ppermute | solution.py:780
  192.5 0.0 collective-permute-done.7.down_ref
  192.5 0.1 paired.3
  192.6 0.9 added.1
  193.5 3.5 %all-to-all-start.11 = ((f32[8,32,512]{2,1,0:T(8,128)}), f32[8,32,512]{2,1,0:T(8,128)S(1)}, u32[]{:S(2)}, u32[]{:S(2)}) async-start(f32[8,32,512]{2,1,0:T(8,128)} %bitcast.9), calls=%async_computation.11 | async-start | bytes 1048576 | tf_op jit(solution)/shard_map/all_to_all | solution.py:843
  197.0 1.9 collective-permute-start.10
  198.9 0.5 collective-permute-start.13
  199.4 1.4 collective-permute-start.12
  200.8 17.5 %collective-permute-done.10.arrived_ref = f32[136,512]{1,0:T(8,128)S(1)} collective-permute-done((f32[136,512]{1,0:T(8,128)S(1)}, f32[136,512]{1,0:T(8,128)S(1)}, u32[]{:S(2)}, u32[]{:S(2)}) %collective-permute-start.10) | collective-permute-done | bytes 278560 | tf_op jit(solution)/shard_map/ppermute | solution.py:780
  218.3 0.1 collective-permute-start.11
  218.4 1.0 grad_x.1
  219.4 6.7 %collective-permute-done.11.up_ref = f32[136,512]{1,0:T(8,128)S(1)} collective-permute-done((f32[136,512]{1,0:T(8,128)S(1)}, f32[136,512]{1,0:T(8,128)S(1)}, u32[]{:S(2)}, u32[]{:S(2)}) %collective-permute-start.11) | collective-permute-done | bytes 278560 | tf_op jit(solution)/shard_map/ppermute | solution.py:780
  226.1 0.6 second_half.1
  226.7 0.1 collective-permute-start.14
  226.8 3.2 %collective-permute-start.16 = (f32[40,512]{1,0:T(8,128)S(1)}, f32[40,512]{1,0:T(8,128)S(1)}, u32[]{:S(2)}, u32[]{:S(2)}) collective-permute-start(f32[40,512]{1,0:T(8,128)S(1)} %get-tuple-element.152), channel_id=1, source_target_pairs={{0,192},{1,65},{8,200},{9,73},{16,208},{17,81},{24,216},{25,89},{3... | collective-permute-start | bytes 245768 | tf_op jit(solution)/shard_map/ppermute | solution.py:780
  230.0 2.4 %collective-permute-done.14.arrived_ref = f32[40,512]{1,0:T(8,128)S(1)} collective-permute-done((f32[40,512]{1,0:T(8,128)S(1)}, f32[40,512]{1,0:T(8,128)S(1)}, u32[]{:S(2)}, u32[]{:S(2)}) %collective-permute-start.14) | collective-permute-done | bytes 81952 | tf_op jit(solution)/shard_map/ppermute | solution.py:780
  232.5 0.1 collective-permute-start.15
  232.6 5.6 %collective-permute-done.15.up_ref = f32[40,512]{1,0:T(8,128)S(1)} collective-permute-done((f32[40,512]{1,0:T(8,128)S(1)}, f32[40,512]{1,0:T(8,128)S(1)}, u32[]{:S(2)}, u32[]{:S(2)}) %collective-permute-start.15) | collective-permute-done | bytes 81952 | tf_op jit(solution)/shard_map/ppermute | solution.py:780
  238.2 0.7 grad_y.1
  (18 shorter events, 0.2 us)
Async XLA Ops:
  74.0 14.5 %copy-start = (f32[1024]{0:T(1024)S(1)}, f32[1024]{0:T(1024)}, u32[]{:S(2)}) copy-start(f32[1024]{0:T(1024)} %param.15) | copy-start | bytes 12292
  88.5 8.4 %copy-start.1 = (f32[1024]{0:T(1024)S(1)}, f32[1024]{0:T(1024)}, u32[]{:S(2)}) copy-start(f32[1024]{0:T(1024)} %param.14) | copy-start | bytes 12292
  150.1 7.8 %collective-permute-start.3 = (f32[136,512]{1,0:T(8,128)S(1)}, f32[136,512]{1,0:T(8,128)S(1)}, u32[]{:S(2)}, u32[]{:S(2)}) collective-permute-start(f32[136,512]{1,0:T(8,128)S(1)} %get-tuple-element.115), channel_id=1, source_target_pairs={{0,8},{1,57},{8,16},{9,1},{16,24},{17,9},{24,32},{25,17},{32,40},{... | collective-permute-start | bytes 835592 | tf_op jit(solution)/shard_map/ppermute | solution.py:780
  151.5 6.5 %copy-start.2 = (bf16[1024,1024]{1,0:T(8,128)(2,1)S(1)}, bf16[1024,1024]{1,0:T(8,128)(2,1)}, u32[]{:S(2)}) copy-start(bf16[1024,1024]{1,0:T(8,128)(2,1)} %tgt_ref.1) | copy-start | bytes 6291460
  161.3 16.0 %collective-permute-start.5 = (f32[1024,512]{1,0:T(8,128)S(1)}, f32[1024,512]{1,0:T(8,128)S(1)}, u32[]{:S(2)}, u32[]{:S(2)}) collective-permute-start(f32[1024,512]{1,0:T(8,128)S(1)} %get-tuple-element.122), channel_id=1, source_target_pairs={{0,1},{1,0},{2,3},{3,2},{4,5},{5,4},{6,7},{7,6},{8,9},{9,8},{10,11... | collective-permute-start | bytes 6291464 | tf_op jit(solution)/shard_map/ppermute | solution.py:822
  161.4 15.7 %collective-permute-start = (f32[256,512]{1,0:T(8,128)S(1)}, f32[256,512]{1,0:T(8,128)S(1)}, u32[]{:S(2)}, u32[]{:S(2)}) collective-permute-start(f32[256,512]{1,0:T(8,128)S(1)} %get-tuple-element.109), channel_id=1, source_target_pairs={{0,64},{1,193},{8,72},{9,201},{16,80},{17,209},{24,88},{25,217},{3... | collective-permute-start | bytes 1572872 | tf_op jit(solution)/shard_map/ppermute | solution.py:780
  162.1 15.0 %collective-permute-start.1 = (f32[256,512]{1,0:T(8,128)S(1)}, f32[256,512]{1,0:T(8,128)S(1)}, u32[]{:S(2)}, u32[]{:S(2)}) collective-permute-start(f32[256,512]{1,0:T(8,128)S(1)} %get-tuple-element.111), channel_id=1, source_target_pairs={{0,192},{1,65},{8,200},{9,73},{16,208},{17,81},{24,216},{25,89},{3... | collective-permute-start | bytes 1572872 | tf_op jit(solution)/shard_map/ppermute | solution.py:780
  164.7 6.5 %collective-permute-start.2 = (f32[136,512]{1,0:T(8,128)S(1)}, f32[136,512]{1,0:T(8,128)S(1)}, u32[]{:S(2)}, u32[]{:S(2)}) collective-permute-start(f32[136,512]{1,0:T(8,128)S(1)} %get-tuple-element.113), channel_id=1, source_target_pairs={{0,56},{1,9},{8,0},{9,17},{16,8},{17,25},{24,16},{25,33},{32,24},{... | collective-permute-start | bytes 835592 | tf_op jit(solution)/shard_map/ppermute | solution.py:780
  177.7 14.8 %collective-permute-start.6 = (f32[1024,128]{1,0:T(8,128)S(1)}, f32[1024,128]{1,0:T(8,128)S(1)}, u32[]{:S(2)}, u32[]{:S(2)}) collective-permute-start(f32[1024,128]{1,0:T(8,128)S(1)} %get-tuple-element.125), channel_id=1, source_target_pairs={{0,2},{1,7},{8,10},{9,15},{16,18},{17,23},{24,26},{25,31},{32,34},... | collective-permute-start | bytes 1572872 | tf_op jit(solution)/shard_map/ppermute | solution.py:780
  178.5 14.0 %collective-permute-start.7 = (f32[1024,128]{1,0:T(8,128)S(1)}, f32[1024,128]{1,0:T(8,128)S(1)}, u32[]{:S(2)}, u32[]{:S(2)}) collective-permute-start(f32[1024,128]{1,0:T(8,128)S(1)} %get-tuple-element.127), channel_id=1, source_target_pairs={{0,6},{1,3},{8,14},{9,11},{16,22},{17,19},{24,30},{25,27},{32,38},... | collective-permute-start | bytes 1572872 | tf_op jit(solution)/shard_map/ppermute | solution.py:780
  180.0 12.6 %collective-permute-start.4 = (f32[256,512]{1,0:T(8,128)S(1)}, f32[256,512]{1,0:T(8,128)S(1)}, u32[]{:S(2)}, u32[]{:S(2)}) collective-permute-start(f32[256,512]{1,0:T(8,128)S(1)} %get-tuple-element.121), channel_id=1, source_target_pairs={{0,64},{1,193},{8,72},{9,201},{16,80},{17,209},{24,88},{25,217},{3... | collective-permute-start | bytes 1572872 | tf_op jit(solution)/shard_map/ppermute | solution.py:780
  180.0 9.4 %collective-permute-start.9 = (f32[136,512]{1,0:T(8,128)S(1)}, f32[136,512]{1,0:T(8,128)S(1)}, u32[]{:S(2)}, u32[]{:S(2)}) collective-permute-start(f32[136,512]{1,0:T(8,128)S(1)} %get-tuple-element.131), channel_id=1, source_target_pairs={{0,8},{1,57},{8,16},{9,1},{16,24},{17,9},{24,32},{25,17},{32,40},{... | collective-permute-start | bytes 835592 | tf_op jit(solution)/shard_map/ppermute | solution.py:780
  180.1 9.3 %collective-permute-start.8 = (f32[136,512]{1,0:T(8,128)S(1)}, f32[136,512]{1,0:T(8,128)S(1)}, u32[]{:S(2)}, u32[]{:S(2)}) collective-permute-start(f32[136,512]{1,0:T(8,128)S(1)} %get-tuple-element.129), channel_id=1, source_target_pairs={{0,56},{1,9},{8,0},{9,17},{16,8},{17,25},{24,16},{25,33},{32,24},{... | collective-permute-start | bytes 835592 | tf_op jit(solution)/shard_map/ppermute | solution.py:780
  193.5 44.7 %all-to-all-start.11 = ((f32[8,32,512]{2,1,0:T(8,128)}), f32[8,32,512]{2,1,0:T(8,128)S(1)}, u32[]{:S(2)}, u32[]{:S(2)}) async-start(f32[8,32,512]{2,1,0:T(8,128)} %bitcast.9), calls=%async_computation.11 | async-start | bytes 1048576 | tf_op jit(solution)/shard_map/all_to_all | solution.py:843
  197.0 21.3 %collective-permute-start.10 = (f32[136,512]{1,0:T(8,128)S(1)}, f32[136,512]{1,0:T(8,128)S(1)}, u32[]{:S(2)}, u32[]{:S(2)}) collective-permute-start(f32[136,512]{1,0:T(8,128)S(1)} %get-tuple-element.139), channel_id=1, source_target_pairs={{0,8},{1,57},{8,16},{9,1},{16,24},{17,9},{24,32},{25,17},{32,40},{... | collective-permute-start | bytes 835592 | tf_op jit(solution)/shard_map/ppermute | solution.py:780
  198.9 19.5 %collective-permute-start.13 = (f32[1024,128]{1,0:T(8,128)S(1)}, f32[1024,128]{1,0:T(8,128)S(1)}, u32[]{:S(2)}, u32[]{:S(2)}) collective-permute-start(f32[1024,128]{1,0:T(8,128)S(1)} %get-tuple-element.145), channel_id=1, source_target_pairs={{0,2},{1,7},{8,10},{9,15},{16,18},{17,23},{24,26},{25,31},{32,34},... | collective-permute-start | bytes 1572872 | tf_op jit(solution)/shard_map/ppermute | solution.py:780
  199.4 20.0 %collective-permute-start.12 = (f32[136,512]{1,0:T(8,128)S(1)}, f32[136,512]{1,0:T(8,128)S(1)}, u32[]{:S(2)}, u32[]{:S(2)}) collective-permute-start(f32[136,512]{1,0:T(8,128)S(1)} %get-tuple-element.142), channel_id=1, source_target_pairs={{0,56},{1,9},{8,0},{9,17},{16,8},{17,25},{24,16},{25,33},{32,24},{... | collective-permute-start | bytes 835592 | tf_op jit(solution)/shard_map/ppermute | solution.py:780
  218.3 7.8 %collective-permute-start.11 = (f32[136,512]{1,0:T(8,128)S(1)}, f32[136,512]{1,0:T(8,128)S(1)}, u32[]{:S(2)}, u32[]{:S(2)}) collective-permute-start(f32[136,512]{1,0:T(8,128)S(1)} %get-tuple-element.141), channel_id=1, source_target_pairs={{0,8},{1,57},{8,16},{9,1},{16,24},{17,9},{24,32},{25,17},{32,40},{... | collective-permute-start | bytes 835592 | tf_op jit(solution)/shard_map/ppermute | solution.py:780
  226.7 5.7 %collective-permute-start.14 = (f32[40,512]{1,0:T(8,128)S(1)}, f32[40,512]{1,0:T(8,128)S(1)}, u32[]{:S(2)}, u32[]{:S(2)}) collective-permute-start(f32[40,512]{1,0:T(8,128)S(1)} %get-tuple-element.149), channel_id=1, source_target_pairs={{0,64},{1,193},{8,72},{9,201},{16,80},{17,209},{24,88},{25,217},{3... | collective-permute-start | bytes 245768 | tf_op jit(solution)/shard_map/ppermute | solution.py:780
  226.8 5.7 %collective-permute-start.16 = (f32[40,512]{1,0:T(8,128)S(1)}, f32[40,512]{1,0:T(8,128)S(1)}, u32[]{:S(2)}, u32[]{:S(2)}) collective-permute-start(f32[40,512]{1,0:T(8,128)S(1)} %get-tuple-element.152), channel_id=1, source_target_pairs={{0,192},{1,65},{8,200},{9,73},{16,208},{17,81},{24,216},{25,89},{3... | collective-permute-start | bytes 245768 | tf_op jit(solution)/shard_map/ppermute | solution.py:780
  232.5 5.7 %collective-permute-start.15 = (f32[40,512]{1,0:T(8,128)S(1)}, f32[40,512]{1,0:T(8,128)S(1)}, u32[]{:S(2)}, u32[]{:S(2)}) collective-permute-start(f32[40,512]{1,0:T(8,128)S(1)} %get-tuple-element.151), channel_id=1, source_target_pairs={{0,64},{1,193},{8,72},{9,201},{16,80},{17,209},{24,88},{25,217},{3... | collective-permute-start | bytes 245768 | tf_op jit(solution)/shard_map/ppermute | solution.py:780

commit v3 on v2

--- a/solution.py
+++ b/solution.py
@@ -219,6 +219,9 @@
         src_hot = jnp.where(label == lane_ids, 1.0, 0.0).astype(jnp.bfloat16)
         allowed_ref[...] = jnp.dot(src_hot, allowed_of, preferred_element_type=F32)
         blocks[s].wait()
+        embs[s].wait()
+        strip = slice(s * LANES, (s + 1) * LANES)
+        turned_ref[:, strip] = emb_ref[strip, :].T
         tops, logs = [], []
         for q in range(LANES // STRIP):
             rows = slice(s * LANES + q * STRIP, s * LANES + (q + 1) * STRIP)
@@ -234,10 +237,6 @@
         top_ref[s : s + 1, :] = to_row(jnp.concatenate(tops, axis=0))
         log_ref[s : s + 1, :] = to_row(jnp.concatenate(logs, axis=0))
     spread(copies_ref, log_ref[...])
-    for s, copy in enumerate(embs):
-        copy.wait()
-        rows = slice(s * LANES, (s + 1) * LANES)
-        turned_ref[:, rows] = emb_ref[rows, :].T
 
 
 def rebase_kernel(
@@ -503,7 +502,7 @@
     return ref[ref.shape[0] - 8 :, :LANES]
 
 
-def x_part_kernel(y_count, place_ref, grad_ref, tgt_ref, after_ref, sent_ref, kept_ref, order_ref):
+def x_part(y_count, place_ref, grad_ref, tgt_ref, sent_ref, kept_ref, order_ref):
     block = tgt_ref.shape[1] // (2 * y_count)
     core, turn = place_ref[3], direction(place_ref)
     for side, out_ref in ((0, sent_ref), (1, kept_ref)):
@@ -517,7 +516,11 @@
         out_ref[...] = jnp.dot(grad_ref[...], order_ref[...], preferred_element_type=F32)
 
 
-def y_parts_kernel(counts, place_ref, grad_ref, src_ref, *outs):
+def parts_kernel(
+    counts, y_count, place_ref, grad_ref, src_ref, tgt_ref, sent_ref, kept_ref, *outs
+):
+    *outs, order_ref = outs
+    x_part(y_count, place_ref, grad_ref, tgt_ref, sent_ref, kept_ref, order_ref)
     reach = counts[1] // 2
     offsets = [*range(reach - 1, 0, -1), *range(2 - reach, 1)]
     for out_ref, offset in zip(outs, offsets):
@@ -526,66 +529,82 @@
         out_ref[...] = x_block(place_ref, src_ref, grad_ref, offset, counts)
 
 
-def add_kernel(count, *refs):
-    value = refs[0][...]
-    for ref in refs[1:count]:
-        value = value + ref[...]
-    out_ref, token_ref = refs[-2:]
-    out_ref[...] = value
-    token_ref[...] = jnp.zeros_like(token_ref)
-
-
-def turn_kernel(sum_ref, up_ref, after_ref, out_ref, token_ref):
-    for s in range(sum_ref.shape[0] // LANES):
-        rows = slice(s * LANES, (s + 1) * LANES)
-        out_ref[:, rows] = (sum_ref[rows, :] + up_ref[rows, :]).T
-    token_ref[...] = jnp.zeros_like(token_ref)
-
-
-def pair_kernel(one_ref, up_ref, own_ref, down_ref, after_ref, pay_ref, sum_ref, token_ref):
-    pay_ref[...] = one_ref[...] + up_ref[...]
-    sum_ref[...] = own_ref[...] + down_ref[...]
-    token_ref[...] = jnp.zeros_like(token_ref)
-
-
-def pass_kernel(block_ref, arrived_ref, held_ref, after_ref, out_ref, sum_ref):
+def forward(out_ref, block_ref, arrived_ref):
     rows = block_ref.shape[0]
     out_ref[:rows, :] = block_ref[...] + arrived_ref[:rows, :]
     out_ref[rows:, :] = arrived_ref[rows:, :]
-    sum_ref[...] = held_ref[...] + rider(arrived_ref)
-
-
-def chip_kernel(kept_ref, arrived_ref, after_ref, *outs):
-    block = outs[0].shape[1]
-    for k, out_ref in enumerate(outs[:-1]):
+
+
+def second_kernel(
+    z_up_ref, z_down_ref, x_up_ref, z_3_ref, z_back2_ref, x_one_ref, start_ref, part_ref,
+    z_ref, z_back_ref, x_ref, held_ref, sent_ref,
+):
+    sent_ref[...] = part_ref[...]
+    forward(z_ref, z_3_ref, z_up_ref)
+    forward(z_back_ref, z_back2_ref, z_down_ref)
+    x_ref[...] = x_one_ref[...] + x_up_ref[...]
+    held_ref[...] = start_ref[...] + rider(z_up_ref) + rider(z_down_ref)
+
+
+def third_kernel(
+    z_up_ref, z_down_ref, x_up_ref, arrived_ref, z_2_ref, z_back1_ref, x_own_ref, kept_ref,
+    start_ref, z_ref, z_back_ref, x_ref, far_ref, one_ref, back_ref, own_ref, held_ref,
+):
+    forward(z_ref, z_2_ref, z_up_ref)
+    forward(z_back_ref, z_back1_ref, z_down_ref)
+    x_ref[...] = x_own_ref[...] + x_up_ref[...]
+    block = far_ref.shape[1]
+    for k, out_ref in enumerate((far_ref, one_ref, back_ref, own_ref)):
         lanes = slice(k * block, (k + 1) * block)
         out_ref[...] = kept_ref[:, lanes] + arrived_ref[:, lanes]
-    outs[-1][...] = jnp.zeros_like(outs[-1])
-
-
-def split_kernel(
-    x_count, place_ref, own_ref, up_ref, down_ref, held_up_ref, held_down_ref, after_ref, far_ref,
-    back_ref, one_ref, last_ref, start_ref,
-):
-    start_ref[...] = (
-        held_up_ref[...] + held_down_ref[...] + rider(up_ref) + rider(down_ref)
-    )
-    block = own_ref.shape[0] // x_count
+    held_ref[...] = start_ref[...] + rider(z_up_ref) + rider(z_down_ref)
+
+
+def fourth_kernel(
+    z_up_ref, z_down_ref, x_down_ref, y_up_ref, z_1_ref, z_own_ref, x_sum_ref, one_ref, start_ref,
+    z_ref, z_sum_ref, x_ref, y_ref, held_ref,
+):
+    forward(z_ref, z_1_ref, z_up_ref)
+    z_sum_ref[...] = z_own_ref[...] + z_down_ref[: z_own_ref.shape[0], :]
+    x_ref[...] = x_sum_ref[...] + x_down_ref[...]
+    y_ref[...] = one_ref[...] + y_up_ref[...]
+    held_ref[...] = start_ref[...] + rider(z_up_ref) + rider(z_down_ref)
+
+
+def fifth_kernel(
+    x_count, place_ref, z_up_ref, y_up_ref, z_sum_ref, own_ref, start_ref,
+    far_ref, back_ref, one_ref, last_ref, y_ref, held_ref,
+):
+    held_ref[...] = start_ref[...] + rider(z_up_ref)
+    block = z_sum_ref.shape[0] // x_count
     for out_ref, offset in ((far_ref, 2), (back_ref, -1), (one_ref, 1), (last_ref, 0)):
         at = ring_place(place_ref, 0, offset, x_count)
         rows = pl.ds(pl.multiple_of(at * block, block), block)
-        value = own_ref[rows, :] + up_ref[rows, :] + down_ref[rows, :]
+        value = z_sum_ref[rows, :] + z_up_ref[rows, :]
         if offset in (2, -1):
-            put(out_ref, value, start_ref[...])
+            put(out_ref, value, held_ref[...])
         else:
             out_ref[...] = value
-
-
-def join_kernel(parts_ref, own_ref, up_ref, down_ref, held_ref, out_ref, start_ref):
-    rows, half = own_ref.shape
+    y_ref[...] = own_ref[...] + y_up_ref[...]
+
+
+def sixth_kernel(
+    x_up_ref, x_down_ref, y_down_ref, x_one_ref, x_own_ref, y_sum_ref, start_ref,
+    x_ref, x_sum_ref, grad_x_ref, held_ref,
+):
+    forward(x_ref, x_one_ref, x_up_ref)
+    x_sum_ref[...] = x_own_ref[...] + x_down_ref[: x_own_ref.shape[0], :]
+    for s in range(y_sum_ref.shape[0] // LANES):
+        rows = slice(s * LANES, (s + 1) * LANES)
+        grad_x_ref[:, rows] = (y_sum_ref[rows, :] + y_down_ref[rows, :]).T
+    held_ref[...] = start_ref[...] + rider(x_up_ref) + rider(x_down_ref)
+
+
+def last_kernel(parts_ref, x_up_ref, x_sum_ref, start_ref, out_ref, held_ref):
+    rows, half = x_sum_ref.shape
     out_ref[:, :half] = jnp.sum(parts_ref[...], axis=0)
-    out_ref[:, half:] = own_ref[...] + up_ref[:rows, :] + down_ref[:rows, :]
-    start_ref[...] = held_ref[...] + rider(up_ref) + rider(down_ref)
+    out_ref[:, half:] = x_sum_ref[...] + x_up_ref[:rows, :]
+    held_ref[...] = start_ref[...] + rider(x_up_ref)
 
 
 def call(
@@ -621,37 +640,6 @@
 
 def exchanged(copies, axis):
     return lax.all_to_all(copies, axis, 0, 0, tiled=True)
-
-
-def token():
-    return jax.ShapeDtypeStruct((8, LANES), F32)
-
-
-def added(values, after):
-    return call(
-        functools.partial(add_kernel, len(values)),
-        (*values, after),
-        [jax.ShapeDtypeStruct(values[0].shape, F32), token()],
-        loose=(len(values),),
-        name="added",
-    )
-
-
-def paired(one, up, own, down, after):
-    shape = jax.ShapeDtypeStruct(one.shape, F32)
-    return call(
-        pair_kernel, (one, up, own, down, after), [shape, shape, token()], loose=(4,), name="paired"
-    )
-
-
-def passed(block, arrived, held, after):
-    return call(
-        pass_kernel,
-        (block, arrived, held, after),
-        [jax.ShapeDtypeStruct(arrived.shape, F32), token()],
-        loose=(3,),
-        name="passed",
-    )
 
 
 def body(cost, src_label, tgt_label, class_mask, g_start, f_bar, g_bar, src_emb, tgt_emb):
@@ -794,82 +782,68 @@
         in_smem=(0,),
         name="cost_grad",
     )
-    z_up, z_down = turn(z_far, 2, 1), turn(z_back, 2, -1)
-    x_up, x_down = turn(x_far, 0, 1), turn(x_back, 0, -1)
+    z_up, z_down, x_up = turn(z_far, 2, 1), turn(z_back, 2, -1), turn(x_far, 0, 1)
+    chip_part = array((src_rows, width // 2))
     outs = call(
-        functools.partial(y_parts_kernel, counts),
-        (place, rounded, src_turned),
-        [z_shape] * (z_count - 2) + [x_shape] * 2,
-        in_smem=(0,),
-        flops=BIG,
-        name="grad_y_parts",
-    )
-    z_3, z_2, z_1, z_back2, z_back1, z_own, x_one, x_own = outs
-    z_pay, up_held = passed(z_3, z_up, start, start)
-    z_up = turn(z_pay, 2, 1)
-    chip_part = array((src_rows, width // 2))
-    sent, kept = call(
-        functools.partial(x_part_kernel, y_count),
-        (place, rounded, tgt_emb, up_held),
-        [chip_part, chip_part],
+        functools.partial(parts_kernel, counts, y_count),
+        (place, rounded, src_turned, tgt_emb),
+        [chip_part] * 2 + [z_shape] * (z_count - 2) + [x_shape] * 2,
         [pltpu.VMEM((tgt_cols, width // 2), jnp.bfloat16)],
         in_smem=(0,),
-        loose=(3,),
-        free=(2,),
+        free=(3,),
         flops=BIG,
-        name="grad_x_parts",
-    )
+        name="grad_parts",
+    )
+    sent, kept, z_3, z_2, z_1, z_back2, z_back1, z_own, x_one, x_own = outs
+    z_pay, z_back, x_pay, start, sent = call(
+        second_kernel,
+        (z_up, z_down, x_up, z_3, z_back2, x_one, start, sent),
+        [z_riding, z_riding, x_shape, col_vector, chip_part],
+        name="second_step",
+    )
+    z_up, z_down, x_up = turn(z_pay, 2, 1), turn(z_back, 2, -1), turn(x_pay, 0, 1)
     arrived = lax.ppermute(sent, "cols", [(at, at ^ 1) for at in range(col_count)])
-    z_pay, down_held = passed(z_back2, z_down, jnp.zeros_like(start), kept)
-    z_down = turn(z_pay, 2, -1)
-    x_pay, x_sum, mark = paired(x_one, x_up, x_own, x_down, down_held)
-    x_up = turn(x_pay, 0, 1)
-    far, one, back, own, mark = call(
-        chip_kernel,
-        (kept, arrived, mark),
-        [array((src_rows, width // col_count))] * 4 + [token()],
-        loose=(2,),
-        name="chip_sums",
-    )
-    y_up, y_down = turn(far, 1, 1), turn(back, 1, -1)
-    z_pay, up_held = passed(z_2, z_up, up_held, mark)
-    z_up = turn(z_pay, 2, 1)
-    z_pay, down_held = passed(z_back1, z_down, down_held, up_held)
-    z_down = turn(z_pay, 2, -1)
-    y_pay, y_sum, mark = paired(one, y_up, own, y_down, down_held)
-    y_up = turn(y_pay, 1, 1)
-    first, mark = added((x_sum, x_up), mark)
+    y_shape = array((src_rows, width // col_count))
+    z_pay, z_back, x_sum, far, one, back, own, start = call(
+        third_kernel,
+        (z_up, z_down, x_up, arrived, z_2, z_back1, x_own, kept, start),
+        [z_riding, z_riding, x_shape] + [y_shape] * 4 + [col_vector],
+        name="third_step",
+    )
+    z_up, z_down = turn(z_pay, 2, 1), turn(z_back, 2, -1)
+    x_down, y_up = turn(x_back, 0, -1), turn(far, 1, 1)
+    z_pay, z_sum, first, y_pay, start = call(
+        fourth_kernel,
+        (z_up, z_down, x_down, y_up, z_1, z_own, x_sum, one, start),
+        [z_riding, z_shape, x_shape, y_shape, col_vector],
+        name="fourth_step",
+    )
+    z_up, y_up = turn(z_pay, 2, 1), turn(y_pay, 1, 1)
     along_z = [[x * z_count + z for z in range(z_count)] for x in range(x_count)]
     first = lax.all_to_all(
         first.reshape(z_count, owned, half), "rows", 0, 0, tiled=True, axis_index_groups=along_z
     )
-    z_pay, up_held = passed(z_1, z_up, up_held, mark)
-    z_up = turn(z_pay, 2, 1)
-    grad_x, mark = call(
-        turn_kernel,
-        (y_sum, y_up, up_held),
-        [array((width // col_count, src_rows)), token()],
-        loose=(2,),
+    last, riding = array((owned, half)), array((owned + 8, half))
+    x_far, x_back, x_one, x_own, y_sum, start = call(
+        functools.partial(fifth_kernel, x_count),
+        (place, z_up, y_up, z_sum, own, start),
+        [riding, riding, last, last, y_shape, col_vector],
+        in_smem=(0,),
+        name="fifth_step",
+    )
+    x_up, x_down, y_down = turn(x_far, 0, 1), turn(x_back, 0, -1), turn(back, 1, -1)
+    x_pay, x_sum, grad_x, start = call(
+        sixth_kernel,
+        (x_up, x_down, y_down, x_one, x_own, y_sum, start),
+        [riding, last, array((width // col_count, src_rows)), col_vector],
         last=True,
-        name="grad_x",
-    )
-    last, riding = array((owned, half)), array((owned + 8, half))
-    x_far, x_back, x_one, x_own, start = call(
-        functools.partial(split_kernel, x_count),
-        (place, z_own, z_up, z_down, up_held, down_held, mark),
-        [riding, riding, last, last, col_vector],
-        in_smem=(0,),
-        loose=(6,),
-        name="second_half",
-    )
-    x_up, x_down = turn(x_far, 0, 1), turn(x_back, 0, -1)
-    x_pay, start = passed(x_one, x_up, start, start)
-    x_up = turn(x_pay, 0, 1)
+        name="sixth_step",
+    )
     grad_y, start = call(
-        join_kernel,
-        (first, x_own, x_up, x_down, start),
+        last_kernel,
+        (first, turn(x_pay, 0, 1), x_sum, start),
         [array((owned, tgt_cols)), col_vector],
-        name="grad_y",
+        name="last_step",
     )
     g_start_bar = start.reshape(tgt_cols)
     return (g_start_bar, grad_x, grad_y)

time: 240 us -> 221 us (0.921)
  waiting for transfers between devices: 58.1 us -> 35.1 us
  starting transfers between devices: 21.1 us -> 31.6 us
  Pallas kernels: 34.1 us -> 25.9 us
  blocking collectives: 125 us -> 129 us
    ppermute x16, waiting for transfers between devices: 58.1 us -> 35.1 us  [turn(): return lax.ppermute(value, ('rows', 'cols'), moves)]
    ppermute x16, starting transfers between devices: 17.5 us -> 26.1 us  [turn(): return lax.ppermute(value, ('rows', 'cols'), moves)]
    pallas_call x27 -> x19, Pallas kernels: 34.1 us -> 25.9 us  [call(): pl.pallas_call(kernel, out_shape=[pltpu.VMEM(out.shape, out.dtype) if mat...]
    all_to_all x11, blocking collectives: 125 us -> 129 us  [exchanged(): return lax.all_to_all(copies, axis, 0, 0, tiled=True)]
  transfers between devices with their start and end apart: 18 -> 18, of which waited for: 9 -> 10; matrix products, arithmetic and copies ran while one was open for 0% -> 0% of each run, Pallas kernels for 2% -> 3%
where the time goes in v3:
time: 221 us; the launch traced here: 222 us
  blocking collectives  129 us (58%)
  waiting for transfers between devices  35.1 us (16%)
  starting transfers between devices  31.6 us (14%)
  Pallas kernels  25.9 us (12%)
    all_to_all x11, blocking collectives, exchanged(): return lax.all_to_all(copies, axis, 0, 0, tiled=True)  129 us
    ppermute x16, waiting for transfers between devices, turn(): return lax.ppermute(value, ('rows', 'cols'), moves)  35.1 us
    ppermute x16, starting transfers between devices, turn(): return lax.ppermute(value, ('rows', 'cols'), moves)  26.1 us
    pallas_call x19, Pallas kernels, call(): pl.pallas_call(kernel, out_shape=[pltpu.VMEM(out.shape, out.dtype) if mat...  25.9 us
  transfers between devices with their start and end apart: 18, of which 10 were waited for; matrix products, arithmetic and copies ran while one was open for 0% of the time, Pallas kernels for 3%

profile of v3, /device:TPU:8, one launch (start us, length us, event | category | flops | bytes accessed | tf_op | source)
XLA Modules:
  0.0 222.3 jit_solution(2036956238801807053)
XLA Ops:
  0.7 0.1 pad_add_fusion.place_ref
  0.7 6.2 %first_row_logs.1 = (f32[1024,1024]{1,0:T(8,128)S(1)}, f32[1024,1024]{1,0:T(8,128)S(1)}, f32[8,128]{1,0:T(8,128)S(1)}, f32[8,8,128]{2,1,0:T(8,128)S(1)}, bf16[1024,1024]{1,0:T(8,128)(2,1)S(1)}) custom-call(bf16[1024,1024]{1,0:T(8,128)(2,1)} %cost_hbm.1, s32[8,128]{1,0:T(8,128)} %bitcast.16, s32[8,128]{1,0:T(8,128)} %bitcast.17, s32[64,64]{1,0:T(8,128)} %mask_hbm.1, ...), custom_call_target="tpu_custom_call" | custom-call | flops 1024 | bytes 1024 | tf_op jit(solution)/shard_map/first_row_logs/pallas_call | solution.py:626
  7.0 8.7 %all_to_all.60.parts_ref = f32[8,8,128]{2,1,0:T(8,128)S(1)} all-to-all(f32[8,8,128]{2,1,0:T(8,128)S(1)} %get-tuple-element.76), channel_id=1, replica_groups=mesh['rows'=32,'cols'=8] {'cols'}, dimensions={0} | all-to-all | bytes 65536 | tf_op jit(solution)/shard_map/all_to_all | solution.py:642
  15.7 0.6 col_logs.3
  16.3 21.4 %all_to_all.61.parts_ref = f32[32,8,128]{2,1,0:T(8,128)S(1)} all-to-all(f32[32,8,128]{2,1,0:T(8,128)S(1)} %get-tuple-element.80), channel_id=1, replica_groups=mesh['rows'=32,'cols'=8] {'rows'}, dimensions={0} | all-to-all | bytes 262144 | tf_op jit(solution)/shard_map/all_to_all | solution.py:642
  37.7 2.5 %second_row_logs.1 = (f32[1024,1024]{1,0:T(8,128)S(1)}, f32[8,128]{1,0:T(8,128)S(1)}, f32[8,128]{1,0:T(8,128)S(1)}, f32[8,8,128]{2,1,0:T(8,128)S(1)}) custom-call(f32[32,8,128]{2,1,0:T(8,128)S(1)} %all_to_all.61.parts_ref, f32[1024,1024]{1,0:T(8,128)S(1)} %get-tuple-element.79.score_ref), custom_call_target="tpu_custom_call" | custom-call | flops 1024 | bytes 1024 | tf_op jit(solution)/shard_map/second_row_logs/pallas_call | solution.py:626
  40.2 10.0 %all_to_all.62.parts_ref = f32[8,8,128]{2,1,0:T(8,128)S(1)} all-to-all(f32[8,8,128]{2,1,0:T(8,128)S(1)} %get-tuple-element.81), channel_id=1, replica_groups=mesh['rows'=32,'cols'=8] {'cols'}, dimensions={0} | all-to-all | bytes 65536 | tf_op jit(solution)/shard_map/all_to_all | solution.py:642
  50.2 0.6 col_logs.4
  50.9 13.9 %all_to_all.63.parts_ref = f32[32,8,128]{2,1,0:T(8,128)S(1)} all-to-all(f32[32,8,128]{2,1,0:T(8,128)S(1)} %get-tuple-element.85), channel_id=1, replica_groups=mesh['rows'=32,'cols'=8] {'rows'}, dimensions={0} | all-to-all | bytes 262144 | tf_op jit(solution)/shard_map/all_to_all | solution.py:642
  64.7 0.6 third_row_logs.1
  65.3 7.8 %all_to_all.64.parts_ref = f32[8,8,128]{2,1,0:T(8,128)S(1)} all-to-all(f32[8,8,128]{2,1,0:T(8,128)S(1)} %get-tuple-element.86), channel_id=1, replica_groups=mesh['rows'=32,'cols'=8] {'cols'}, dimensions={0} | all-to-all | bytes 65536 | tf_op jit(solution)/shard_map/all_to_all | solution.py:642
  73.2 0.6 col_logs.5
  73.8 14.8 %all_to_all.65.parts_ref = f32[32,8,128]{2,1,0:T(8,128)S(1)} all-to-all(f32[32,8,128]{2,1,0:T(8,128)S(1)} %get-tuple-element.87), channel_id=1, replica_groups=mesh['rows'=32,'cols'=8] {'rows'}, dimensions={0} | all-to-all | bytes 262144 | tf_op jit(solution)/shard_map/all_to_all | solution.py:642
  88.6 0.6 row_plan.3
  89.2 7.8 %all_to_all.66.parts_ref = f32[8,8,128]{2,1,0:T(8,128)S(1)} all-to-all(f32[8,8,128]{2,1,0:T(8,128)S(1)} %get-tuple-element.90), channel_id=1, replica_groups=mesh['rows'=32,'cols'=8] {'cols'}, dimensions={0} | all-to-all | bytes 65536 | tf_op jit(solution)/shard_map/all_to_all | solution.py:642
  97.1 0.5 col_plan.2
  97.6 14.8 %all_to_all.67.parts_ref = f32[32,8,128]{2,1,0:T(8,128)S(1)} all-to-all(f32[32,8,128]{2,1,0:T(8,128)S(1)} %get-tuple-element.91), channel_id=1, replica_groups=mesh['rows'=32,'cols'=8] {'rows'}, dimensions={0} | all-to-all | bytes 262144 | tf_op jit(solution)/shard_map/all_to_all | solution.py:642
  112.4 0.5 row_plan.4
  113.0 7.8 %all_to_all.68.parts_ref = f32[8,8,128]{2,1,0:T(8,128)S(1)} all-to-all(f32[8,8,128]{2,1,0:T(8,128)S(1)} %get-tuple-element.93), channel_id=1, replica_groups=mesh['rows'=32,'cols'=8] {'cols'}, dimensions={0} | all-to-all | bytes 65536 | tf_op jit(solution)/shard_map/all_to_all | solution.py:642
  120.8 0.7 col_plan.3
  121.5 13.9 %all_to_all.69.parts_ref = f32[32,8,128]{2,1,0:T(8,128)S(1)} all-to-all(f32[32,8,128]{2,1,0:T(8,128)S(1)} %get-tuple-element.94), channel_id=1, replica_groups=mesh['rows'=32,'cols'=8] {'rows'}, dimensions={0} | all-to-all | bytes 262144 | tf_op jit(solution)/shard_map/all_to_all | solution.py:642
  135.3 0.5 row_plan.5
  135.9 7.8 %all_to_all.70.parts_ref = f32[8,8,128]{2,1,0:T(8,128)S(1)} all-to-all(f32[8,8,128]{2,1,0:T(8,128)S(1)} %get-tuple-element.96), channel_id=1, replica_groups=mesh['rows'=32,'cols'=8] {'cols'}, dimensions={0} | all-to-all | bytes 65536 | tf_op jit(solution)/shard_map/all_to_all | solution.py:642
  143.7 3.0 %cost_grad.1 = (bf16[1024,1024]{1,0:T(8,128)(2,1)S(1)}, f32[8,128]{1,0:T(8,128)S(1)}, f32[136,512]{1,0:T(8,128)S(1)}, f32[256,512]{1,0:T(8,128)S(1)}, f32[136,512]{1,0:T(8,128)S(1)}, /*index=5*/f32[256,512]{1,0:T(8,128)S(1)}) custom-call(s32[4]{0:T(128)S(1)} %pad_add_fusion.place_ref, f32[8,8,128]{2,1,0:T(8,128)S(1)} %all_to_all.70.parts_ref, ...), custom_call_target="tpu_custom_call" | custom-call | flops 1024 | bytes 1024 | tf_op jit(solution)/shard_map/cost_grad/pallas_call | solution.py:626
  146.7 0.7 collective-permute-start.2
  147.4 1.3 collective-permute-start
  148.7 2.0 collective-permute-start.1
  150.6 4.7 %grad_parts.1 = (f32[1024,512]{1,0:T(8,128)S(1)}, f32[1024,512]{1,0:T(8,128)S(1)}, f32[128,512]{1,0:T(8,128)S(1)}, f32[128,512]{1,0:T(8,128)S(1)}, f32[128,512]{...) custom-call(s32[4]{0:T(128)S(1)} %pad_add_fusion.place_ref, ...), custom_call_target="tpu_custom_call" | custom-call | flops 4294967296 | bytes 1024 | tf_op jit(solution)/shard_map/grad_parts/pallas_call | solution.py:626
  155.3 0.0 collective-permute-done.z_up_ref
  155.3 1.5 collective-permute-done.1.z_down_ref
  156.8 0.4 collective-permute-done.2.x_up_ref
  157.2 0.2 second_step.1
  157.4 2.0 collective-permute-start.6
  159.4 0.6 collective-permute-start.5
  160.0 1.3 collective-permute-start.3
  161.3 2.0 collective-permute-start.4
  163.3 2.6 %collective-permute-start.9 = (f32[256,512]{1,0:T(8,128)S(1)}, f32[256,512]{1,0:T(8,128)S(1)}, u32[]{:S(2)}, u32[]{:S(2)}) collective-permute-start(f32[256,512]{1,0:T(8,128)S(1)} %get-tuple-element.123), channel_id=1, source_target_pairs={{0,192},{1,65},{8,200},{9,73},{16,208},{17,81},{24,216},{25,89},{3... | collective-permute-start | bytes 1572872 | tf_op jit(solution)/shard_map/ppermute | solution.py:768
  165.9 2.5 %collective-permute-done.3.z_up_ref = f32[136,512]{1,0:T(8,128)S(1)} collective-permute-done((f32[136,512]{1,0:T(8,128)S(1)}, f32[136,512]{1,0:T(8,128)S(1)}, u32[]{:S(2)}, u32[]{:S(2)}) %collective-permute-start.3) | collective-permute-done | bytes 278560 | tf_op jit(solution)/shard_map/ppermute | solution.py:768
  168.4 1.8 collective-permute-done.4.z_down_ref
  170.2 2.2 collective-permute-done.5.x_up_ref
  172.4 0.0 collective-permute-done.6.arrived_ref
  172.4 0.6 third_step.1
  173.0 4.1 %collective-permute-start.10 = (f32[1024,128]{1,0:T(8,128)S(1)}, f32[1024,128]{1,0:T(8,128)S(1)}, u32[]{:S(2)}, u32[]{:S(2)}) collective-permute-start(f32[1024,128]{1,0:T(8,128)S(1)} %get-tuple-element.124), channel_id=1, source_target_pairs={{0,2},{1,7},{8,10},{9,15},{16,18},{17,23},{24,26},{25,31},{32,34},... | collective-permute-start | bytes 1572872 | tf_op jit(solution)/shard_map/ppermute | solution.py:768
  177.1 2.5 %collective-permute-start.7 = (f32[136,512]{1,0:T(8,128)S(1)}, f32[136,512]{1,0:T(8,128)S(1)}, u32[]{:S(2)}, u32[]{:S(2)}) collective-permute-start(f32[136,512]{1,0:T(8,128)S(1)} %get-tuple-element.121), channel_id=1, source_target_pairs={{0,8},{1,57},{8,16},{9,1},{16,24},{17,9},{24,32},{25,17},{32,40},{... | collective-permute-start | bytes 835592 | tf_op jit(solution)/shard_map/ppermute | solution.py:768
  179.6 0.7 collective-permute-start.8
  180.3 0.0 collective-permute-done.9.x_down_ref
  180.3 5.7 %collective-permute-done.7.z_up_ref = f32[136,512]{1,0:T(8,128)S(1)} collective-permute-done((f32[136,512]{1,0:T(8,128)S(1)}, f32[136,512]{1,0:T(8,128)S(1)}, u32[]{:S(2)}, u32[]{:S(2)}) %collective-permute-start.7) | collective-permute-done | bytes 278560 | tf_op jit(solution)/shard_map/ppermute | solution.py:768
  186.0 0.2 collective-permute-done.8.z_down_ref
  186.2 1.0 fourth_step.1
  187.2 3.5 %all-to-all-start.11 = ((f32[8,32,512]{2,1,0:T(8,128)}), f32[8,32,512]{2,1,0:T(8,128)S(1)}, u32[]{:S(2)}, u32[]{:S(2)}) async-start(f32[8,32,512]{2,1,0:T(8,128)} %bitcast.9), calls=%async_computation.11 | async-start | bytes 1048576 | tf_op jit(solution)/shard_map/all_to_all | solution.py:823
  190.7 1.6 collective-permute-start.12
  192.3 1.1 collective-permute-start.15
  193.3 2.3 %collective-permute-start.11 = (f32[136,512]{1,0:T(8,128)S(1)}, f32[136,512]{1,0:T(8,128)S(1)}, u32[]{:S(2)}, u32[]{:S(2)}) collective-permute-start(f32[136,512]{1,0:T(8,128)S(1)} %get-tuple-element.131), channel_id=1, source_target_pairs={{0,8},{1,57},{8,16},{9,1},{16,24},{17,9},{24,32},{25,17},{32,40},{... | collective-permute-start | bytes 835592 | tf_op jit(solution)/shard_map/ppermute | solution.py:768
  195.6 12.3 %collective-permute-done.11.z_up_ref = f32[136,512]{1,0:T(8,128)S(1)} collective-permute-done((f32[136,512]{1,0:T(8,128)S(1)}, f32[136,512]{1,0:T(8,128)S(1)}, u32[]{:S(2)}, u32[]{:S(2)}) %collective-permute-start.11) | collective-permute-done | bytes 278560 | tf_op jit(solution)/shard_map/ppermute | solution.py:768
  207.9 0.0 collective-permute-done.12.y_up_ref
  207.9 0.7 fifth_step.1
  208.5 0.9 collective-permute-start.13
  209.4 2.4 %collective-permute-start.14 = (f32[40,512]{1,0:T(8,128)S(1)}, f32[40,512]{1,0:T(8,128)S(1)}, u32[]{:S(2)}, u32[]{:S(2)}) collective-permute-start(f32[40,512]{1,0:T(8,128)S(1)} %get-tuple-element.137), channel_id=1, source_target_pairs={{0,192},{1,65},{8,200},{9,73},{16,208},{17,81},{24,216},{25,89},{3... | collective-permute-start | bytes 245768 | tf_op jit(solution)/shard_map/ppermute | solution.py:768
  211.8 0.0 collective-permute-done.15.y_down_ref
  211.8 3.1 %collective-permute-done.13.x_up_ref = f32[40,512]{1,0:T(8,128)S(1)} collective-permute-done((f32[40,512]{1,0:T(8,128)S(1)}, f32[40,512]{1,0:T(8,128)S(1)}, u32[]{:S(2)}, u32[]{:S(2)}) %collective-permute-start.13) | collective-permute-done | bytes 81952 | tf_op jit(solution)/shard_map/ppermute | solution.py:768
  214.9 1.0 sixth_step.1
  215.9 0.1 collective-permute-start.16
  216.0 5.6 %collective-permute-done.16.x_up_ref = f32[40,512]{1,0:T(8,128)S(1)} collective-permute-done((f32[40,512]{1,0:T(8,128)S(1)}, f32[40,512]{1,0:T(8,128)S(1)}, u32[]{:S(2)}, u32[]{:S(2)}) %collective-permute-start.16) | collective-permute-done | bytes 81952 | tf_op jit(solution)/shard_map/ppermute | solution.py:768
  221.6 0.7 last_step.1
  (10 shorter events, 0.0 us)
Async XLA Ops:
  73.2 15.5 %copy-start = (f32[1024]{0:T(1024)S(1)}, f32[1024]{0:T(1024)}, u32[]{:S(2)}) copy-start(f32[1024]{0:T(1024)} %param.15) | copy-start | bytes 12292
  88.6 8.4 %copy-start.1 = (f32[1024]{0:T(1024)S(1)}, f32[1024]{0:T(1024)}, u32[]{:S(2)}) copy-start(f32[1024]{0:T(1024)} %param.14) | copy-start | bytes 12292
  143.7 6.9 %copy-start.2 = (bf16[1024,1024]{1,0:T(8,128)(2,1)S(1)}, bf16[1024,1024]{1,0:T(8,128)(2,1)}, u32[]{:S(2)}) copy-start(bf16[1024,1024]{1,0:T(8,128)(2,1)} %tgt_ref.1) | copy-start | bytes 6291460
  146.7 10.5 %collective-permute-start.2 = (f32[256,512]{1,0:T(8,128)S(1)}, f32[256,512]{1,0:T(8,128)S(1)}, u32[]{:S(2)}, u32[]{:S(2)}) collective-permute-start(f32[256,512]{1,0:T(8,128)S(1)} %get-tuple-element.105), channel_id=1, source_target_pairs={{0,64},{1,193},{8,72},{9,201},{16,80},{17,209},{24,88},{25,217},{3... | collective-permute-start | bytes 1572872 | tf_op jit(solution)/shard_map/ppermute | solution.py:768
  147.4 7.9 %collective-permute-start = (f32[136,512]{1,0:T(8,128)S(1)}, f32[136,512]{1,0:T(8,128)S(1)}, u32[]{:S(2)}, u32[]{:S(2)}) collective-permute-start(f32[136,512]{1,0:T(8,128)S(1)} %get-tuple-element.103), channel_id=1, source_target_pairs={{0,8},{1,57},{8,16},{9,1},{16,24},{17,9},{24,32},{25,17},{32,40},{... | collective-permute-start | bytes 835592 | tf_op jit(solution)/shard_map/ppermute | solution.py:768
  148.7 8.1 %collective-permute-start.1 = (f32[136,512]{1,0:T(8,128)S(1)}, f32[136,512]{1,0:T(8,128)S(1)}, u32[]{:S(2)}, u32[]{:S(2)}) collective-permute-start(f32[136,512]{1,0:T(8,128)S(1)} %get-tuple-element.104), channel_id=1, source_target_pairs={{0,56},{1,9},{8,0},{9,17},{16,8},{17,25},{24,16},{25,33},{32,24},{... | collective-permute-start | bytes 835592 | tf_op jit(solution)/shard_map/ppermute | solution.py:768
  157.4 15.0 %collective-permute-start.6 = (f32[1024,512]{1,0:T(8,128)S(1)}, f32[1024,512]{1,0:T(8,128)S(1)}, u32[]{:S(2)}, u32[]{:S(2)}) collective-permute-start(f32[1024,512]{1,0:T(8,128)S(1)} %get-tuple-element.115), channel_id=1, source_target_pairs={{0,1},{1,0},{2,3},{3,2},{4,5},{5,4},{6,7},{7,6},{8,9},{9,8},{10,11... | collective-permute-start | bytes 6291464 | tf_op jit(solution)/shard_map/ppermute | solution.py:805
  159.4 13.0 %collective-permute-start.5 = (f32[256,512]{1,0:T(8,128)S(1)}, f32[256,512]{1,0:T(8,128)S(1)}, u32[]{:S(2)}, u32[]{:S(2)}) collective-permute-start(f32[256,512]{1,0:T(8,128)S(1)} %get-tuple-element.114), channel_id=1, source_target_pairs={{0,64},{1,193},{8,72},{9,201},{16,80},{17,209},{24,88},{25,217},{3... | collective-permute-start | bytes 1572872 | tf_op jit(solution)/shard_map/ppermute | solution.py:768
  160.0 8.3 %collective-permute-start.3 = (f32[136,512]{1,0:T(8,128)S(1)}, f32[136,512]{1,0:T(8,128)S(1)}, u32[]{:S(2)}, u32[]{:S(2)}) collective-permute-start(f32[136,512]{1,0:T(8,128)S(1)} %get-tuple-element.112), channel_id=1, source_target_pairs={{0,8},{1,57},{8,16},{9,1},{16,24},{17,9},{24,32},{25,17},{32,40},{... | collective-permute-start | bytes 835592 | tf_op jit(solution)/shard_map/ppermute | solution.py:768
  161.3 8.9 %collective-permute-start.4 = (f32[136,512]{1,0:T(8,128)S(1)}, f32[136,512]{1,0:T(8,128)S(1)}, u32[]{:S(2)}, u32[]{:S(2)}) collective-permute-start(f32[136,512]{1,0:T(8,128)S(1)} %get-tuple-element.113), channel_id=1, source_target_pairs={{0,56},{1,9},{8,0},{9,17},{16,8},{17,25},{24,16},{25,33},{32,24},{... | collective-permute-start | bytes 835592 | tf_op jit(solution)/shard_map/ppermute | solution.py:768
  163.3 17.0 %collective-permute-start.9 = (f32[256,512]{1,0:T(8,128)S(1)}, f32[256,512]{1,0:T(8,128)S(1)}, u32[]{:S(2)}, u32[]{:S(2)}) collective-permute-start(f32[256,512]{1,0:T(8,128)S(1)} %get-tuple-element.123), channel_id=1, source_target_pairs={{0,192},{1,65},{8,200},{9,73},{16,208},{17,81},{24,216},{25,89},{3... | collective-permute-start | bytes 1572872 | tf_op jit(solution)/shard_map/ppermute | solution.py:768
  173.0 13.2 %collective-permute-start.10 = (f32[1024,128]{1,0:T(8,128)S(1)}, f32[1024,128]{1,0:T(8,128)S(1)}, u32[]{:S(2)}, u32[]{:S(2)}) collective-permute-start(f32[1024,128]{1,0:T(8,128)S(1)} %get-tuple-element.124), channel_id=1, source_target_pairs={{0,2},{1,7},{8,10},{9,15},{16,18},{17,23},{24,26},{25,31},{32,34},... | collective-permute-start | bytes 1572872 | tf_op jit(solution)/shard_map/ppermute | solution.py:768
  177.1 8.9 %collective-permute-start.7 = (f32[136,512]{1,0:T(8,128)S(1)}, f32[136,512]{1,0:T(8,128)S(1)}, u32[]{:S(2)}, u32[]{:S(2)}) collective-permute-start(f32[136,512]{1,0:T(8,128)S(1)} %get-tuple-element.121), channel_id=1, source_target_pairs={{0,8},{1,57},{8,16},{9,1},{16,24},{17,9},{24,32},{25,17},{32,40},{... | collective-permute-start | bytes 835592 | tf_op jit(solution)/shard_map/ppermute | solution.py:768
  179.6 6.5 %collective-permute-start.8 = (f32[136,512]{1,0:T(8,128)S(1)}, f32[136,512]{1,0:T(8,128)S(1)}, u32[]{:S(2)}, u32[]{:S(2)}) collective-permute-start(f32[136,512]{1,0:T(8,128)S(1)} %get-tuple-element.122), channel_id=1, source_target_pairs={{0,56},{1,9},{8,0},{9,17},{16,8},{17,25},{24,16},{25,33},{32,24},{... | collective-permute-start | bytes 835592 | tf_op jit(solution)/shard_map/ppermute | solution.py:768
  187.2 34.4 %all-to-all-start.11 = ((f32[8,32,512]{2,1,0:T(8,128)}), f32[8,32,512]{2,1,0:T(8,128)S(1)}, u32[]{:S(2)}, u32[]{:S(2)}) async-start(f32[8,32,512]{2,1,0:T(8,128)} %bitcast.9), calls=%async_computation.11 | async-start | bytes 1048576 | tf_op jit(solution)/shard_map/all_to_all | solution.py:823
  190.7 17.2 %collective-permute-start.12 = (f32[1024,128]{1,0:T(8,128)S(1)}, f32[1024,128]{1,0:T(8,128)S(1)}, u32[]{:S(2)}, u32[]{:S(2)}) collective-permute-start(f32[1024,128]{1,0:T(8,128)S(1)} %get-tuple-element.132), channel_id=1, source_target_pairs={{0,2},{1,7},{8,10},{9,15},{16,18},{17,23},{24,26},{25,31},{32,34},... | collective-permute-start | bytes 1572872 | tf_op jit(solution)/shard_map/ppermute | solution.py:768
  192.3 19.6 %collective-permute-start.15 = (f32[1024,128]{1,0:T(8,128)S(1)}, f32[1024,128]{1,0:T(8,128)S(1)}, u32[]{:S(2)}, u32[]{:S(2)}) collective-permute-start(f32[1024,128]{1,0:T(8,128)S(1)} %get-tuple-element.138), channel_id=1, source_target_pairs={{0,6},{1,3},{8,14},{9,11},{16,22},{17,19},{24,30},{25,27},{32,38},... | collective-permute-start | bytes 1572872 | tf_op jit(solution)/shard_map/ppermute | solution.py:768
  193.3 14.5 %collective-permute-start.11 = (f32[136,512]{1,0:T(8,128)S(1)}, f32[136,512]{1,0:T(8,128)S(1)}, u32[]{:S(2)}, u32[]{:S(2)}) collective-permute-start(f32[136,512]{1,0:T(8,128)S(1)} %get-tuple-element.131), channel_id=1, source_target_pairs={{0,8},{1,57},{8,16},{9,1},{16,24},{17,9},{24,32},{25,17},{32,40},{... | collective-permute-start | bytes 835592 | tf_op jit(solution)/shard_map/ppermute | solution.py:768
  208.5 6.4 %collective-permute-start.13 = (f32[40,512]{1,0:T(8,128)S(1)}, f32[40,512]{1,0:T(8,128)S(1)}, u32[]{:S(2)}, u32[]{:S(2)}) collective-permute-start(f32[40,512]{1,0:T(8,128)S(1)} %get-tuple-element.136), channel_id=1, source_target_pairs={{0,64},{1,193},{8,72},{9,201},{16,80},{17,209},{24,88},{25,217},{3... | collective-permute-start | bytes 245768 | tf_op jit(solution)/shard_map/ppermute | solution.py:768
  209.4 5.5 %collective-permute-start.14 = (f32[40,512]{1,0:T(8,128)S(1)}, f32[40,512]{1,0:T(8,128)S(1)}, u32[]{:S(2)}, u32[]{:S(2)}) collective-permute-start(f32[40,512]{1,0:T(8,128)S(1)} %get-tuple-element.137), channel_id=1, source_target_pairs={{0,192},{1,65},{8,200},{9,73},{16,208},{17,81},{24,216},{25,89},{3... | collective-permute-start | bytes 245768 | tf_op jit(solution)/shard_map/ppermute | solution.py:768
  215.9 5.7 %collective-permute-start.16 = (f32[40,512]{1,0:T(8,128)S(1)}, f32[40,512]{1,0:T(8,128)S(1)}, u32[]{:S(2)}, u32[]{:S(2)}) collective-permute-start(f32[40,512]{1,0:T(8,128)S(1)} %get-tuple-element.143), channel_id=1, source_target_pairs={{0,64},{1,193},{8,72},{9,201},{16,80},{17,209},{24,88},{25,217},{3... | collective-permute-start | bytes 245768 | tf_op jit(solution)/shard_map/ppermute | solution.py:768

commit v4 on v3

--- a/solution.py
+++ b/solution.py
@@ -21,6 +21,7 @@
 VMEM_BYTES = 16 * 2**20
 PINNED = 2**16
 BIG = 2**32
+STEP = 2**33
 F32 = jnp.float32
 
 
@@ -535,45 +536,46 @@
     out_ref[rows:, :] = arrived_ref[rows:, :]
 
 
-def second_kernel(
-    z_up_ref, z_down_ref, x_up_ref, z_3_ref, z_back2_ref, x_one_ref, start_ref, part_ref,
-    z_ref, z_back_ref, x_ref, held_ref, sent_ref,
-):
-    sent_ref[...] = part_ref[...]
-    forward(z_ref, z_3_ref, z_up_ref)
-    forward(z_back_ref, z_back2_ref, z_down_ref)
-    x_ref[...] = x_one_ref[...] + x_up_ref[...]
-    held_ref[...] = start_ref[...] + rider(z_up_ref) + rider(z_down_ref)
-
-
-def third_kernel(
-    z_up_ref, z_down_ref, x_up_ref, arrived_ref, z_2_ref, z_back1_ref, x_own_ref, kept_ref,
-    start_ref, z_ref, z_back_ref, x_ref, far_ref, one_ref, back_ref, own_ref, held_ref,
-):
-    forward(z_ref, z_2_ref, z_up_ref)
-    forward(z_back_ref, z_back1_ref, z_down_ref)
-    x_ref[...] = x_own_ref[...] + x_up_ref[...]
-    block = far_ref.shape[1]
-    for k, out_ref in enumerate((far_ref, one_ref, back_ref, own_ref)):
+def token(ref):
+    ref[...] = jnp.zeros_like(ref)
+
+
+def z_kernel(up_ref, down_ref, ahead_ref, behind_ref, start_ref, after_ref, z_ref, back_ref, held_ref):
+    forward(z_ref, ahead_ref, up_ref)
+    forward(back_ref, behind_ref, down_ref)
+    held_ref[...] = start_ref[...] + rider(up_ref) + rider(down_ref)
+
+
+def x_kernel(up_ref, down_ref, one_ref, own_ref, after_ref, pay_ref, sum_ref, token_ref):
+    pay_ref[...] = one_ref[...] + up_ref[...]
+    sum_ref[...] = own_ref[...] + down_ref[...]
+    token(token_ref)
+
+
+def add_kernel(one_ref, other_ref, after_ref, sum_ref, token_ref):
+    sum_ref[...] = one_ref[...] + other_ref[...]
+    token(token_ref)
+
+
+def chip_kernel(arrived_ref, kept_ref, after_ref, *outs):
+    block = outs[0].shape[1]
+    for k, out_ref in enumerate(outs[:-1]):
         lanes = slice(k * block, (k + 1) * block)
         out_ref[...] = kept_ref[:, lanes] + arrived_ref[:, lanes]
-    held_ref[...] = start_ref[...] + rider(z_up_ref) + rider(z_down_ref)
-
-
-def fourth_kernel(
-    z_up_ref, z_down_ref, x_down_ref, y_up_ref, z_1_ref, z_own_ref, x_sum_ref, one_ref, start_ref,
-    z_ref, z_sum_ref, x_ref, y_ref, held_ref,
-):
-    forward(z_ref, z_1_ref, z_up_ref)
-    z_sum_ref[...] = z_own_ref[...] + z_down_ref[: z_own_ref.shape[0], :]
-    x_ref[...] = x_sum_ref[...] + x_down_ref[...]
-    y_ref[...] = one_ref[...] + y_up_ref[...]
-    held_ref[...] = start_ref[...] + rider(z_up_ref) + rider(z_down_ref)
-
-
-def fifth_kernel(
-    x_count, place_ref, z_up_ref, y_up_ref, z_sum_ref, own_ref, start_ref,
-    far_ref, back_ref, one_ref, last_ref, y_ref, held_ref,
+    token(outs[-1])
+
+
+def last_z_kernel(
+    up_ref, down_ref, ahead_ref, own_ref, start_ref, after_ref, z_ref, z_sum_ref, held_ref
+):
+    forward(z_ref, ahead_ref, up_ref)
+    z_sum_ref[...] = own_ref[...] + down_ref[: own_ref.shape[0], :]
+    held_ref[...] = start_ref[...] + rider(up_ref) + rider(down_ref)
+
+
+def split_kernel(
+    x_count, place_ref, z_up_ref, z_sum_ref, start_ref, after_ref,
+    far_ref, back_ref, one_ref, last_ref, held_ref,
 ):
     held_ref[...] = start_ref[...] + rider(z_up_ref)
     block = z_sum_ref.shape[0] // x_count
@@ -581,30 +583,28 @@
         at = ring_place(place_ref, 0, offset, x_count)
         rows = pl.ds(pl.multiple_of(at * block, block), block)
         value = z_sum_ref[rows, :] + z_up_ref[rows, :]
-        if offset in (2, -1):
+        if offset:
             put(out_ref, value, held_ref[...])
         else:
             out_ref[...] = value
-    y_ref[...] = own_ref[...] + y_up_ref[...]
-
-
-def sixth_kernel(
-    x_up_ref, x_down_ref, y_down_ref, x_one_ref, x_own_ref, y_sum_ref, start_ref,
-    x_ref, x_sum_ref, grad_x_ref, held_ref,
-):
-    forward(x_ref, x_one_ref, x_up_ref)
-    x_sum_ref[...] = x_own_ref[...] + x_down_ref[: x_own_ref.shape[0], :]
-    for s in range(y_sum_ref.shape[0] // LANES):
+
+
+def turn_kernel(sum_ref, up_ref, after_ref, out_ref, token_ref):
+    for s in range(sum_ref.shape[0] // LANES):
         rows = slice(s * LANES, (s + 1) * LANES)
-        grad_x_ref[:, rows] = (y_sum_ref[rows, :] + y_down_ref[rows, :]).T
-    held_ref[...] = start_ref[...] + rider(x_up_ref) + rider(x_down_ref)
-
-
-def last_kernel(parts_ref, x_up_ref, x_sum_ref, start_ref, out_ref, held_ref):
-    rows, half = x_sum_ref.shape
+        out_ref[:, rows] = (sum_ref[rows, :] + up_ref[rows, :]).T
+    token(token_ref)
+
+
+def last_kernel(parts_ref, far_ref, one_ref, back_ref, own_ref, start_ref, out_ref, held_ref):
+    rows, half = own_ref.shape
     out_ref[:, :half] = jnp.sum(parts_ref[...], axis=0)
-    out_ref[:, half:] = x_sum_ref[...] + x_up_ref[:rows, :]
-    held_ref[...] = start_ref[...] + rider(x_up_ref)
+    value, held = own_ref[...], start_ref[...]
+    for ref in (far_ref, one_ref, back_ref):
+        value = value + ref[:rows, :]
+        held = held + rider(ref)
+    out_ref[:, half:] = value
+    held_ref[...] = held
 
 
 def call(
@@ -782,7 +782,8 @@
         in_smem=(0,),
         name="cost_grad",
     )
-    z_up, z_down, x_up = turn(z_far, 2, 1), turn(z_back, 2, -1), turn(x_far, 0, 1)
+    z_up, z_down = turn(z_far, 2, 1), turn(z_back, 2, -1)
+    x_up, x_down = turn(x_far, 0, 1), turn(x_back, 0, -1)
     chip_part = array((src_rows, width // 2))
     outs = call(
         functools.partial(parts_kernel, counts, y_count),
@@ -795,53 +796,79 @@
         name="grad_parts",
     )
     sent, kept, z_3, z_2, z_1, z_back2, z_back1, z_own, x_one, x_own = outs
-    z_pay, z_back, x_pay, start, sent = call(
-        second_kernel,
-        (z_up, z_down, x_up, z_3, z_back2, x_one, start, sent),
-        [z_riding, z_riding, x_shape, col_vector, chip_part],
-        name="second_step",
-    )
-    z_up, z_down, x_up = turn(z_pay, 2, 1), turn(z_back, 2, -1), turn(x_pay, 0, 1)
+    small = array((8, LANES))
+
+    def step(kernel, arguments, outs, name, last=False, in_smem=()):
+        return call(
+            kernel,
+            arguments,
+            outs,
+            loose=(len(arguments) - 1,),
+            last=last,
+            in_smem=in_smem,
+            flops=STEP,
+            name=name,
+        )
+
+    z_pay, z_back, start = step(
+        z_kernel,
+        (z_up, z_down, z_3, z_back2, start, kept),
+        [z_riding, z_riding, small],
+        "z_second",
+    )
+    z_up, z_down = turn(z_pay, 2, 1), turn(z_back, 2, -1)
     arrived = lax.ppermute(sent, "cols", [(at, at ^ 1) for at in range(col_count)])
+    x_pay, x_sum, mark = step(
+        x_kernel, (x_up, x_down, x_one, x_own, start), [x_shape, x_shape, small], "x_second"
+    )
+    x_up = turn(x_pay, 0, 1)
+    z_pay, z_back, start = step(
+        z_kernel,
+        (z_up, z_down, z_2, z_back1, start, mark),
+        [z_riding, z_riding, small],
+        "z_third",
+    )
+    z_up, z_down = turn(z_pay, 2, 1), turn(z_back, 2, -1)
     y_shape = array((src_rows, width // col_count))
-    z_pay, z_back, x_sum, far, one, back, own, start = call(
-        third_kernel,
-        (z_up, z_down, x_up, arrived, z_2, z_back1, x_own, kept, start),
-        [z_riding, z_riding, x_shape] + [y_shape] * 4 + [col_vector],
-        name="third_step",
-    )
-    z_up, z_down = turn(z_pay, 2, 1), turn(z_back, 2, -1)
-    x_down, y_up = turn(x_back, 0, -1), turn(far, 1, 1)
-    z_pay, z_sum, first, y_pay, start = call(
-        fourth_kernel,
-        (z_up, z_down, x_down, y_up, z_1, z_own, x_sum, one, start),
-        [z_riding, z_shape, x_shape, y_shape, col_vector],
-        name="fourth_step",
-    )
-    z_up, y_up = turn(z_pay, 2, 1), turn(y_pay, 1, 1)
+    far, one, back, own, mark = step(
+        chip_kernel, (arrived, kept, start), [y_shape] * 4 + [small], "chip_sums"
+    )
+    y_up, y_down = turn(far, 1, 1), turn(back, 1, -1)
+    first, mark = step(add_kernel, (x_sum, x_up, mark), [x_shape, small], "x_last")
     along_z = [[x * z_count + z for z in range(z_count)] for x in range(x_count)]
     first = lax.all_to_all(
         first.reshape(z_count, owned, half), "rows", 0, 0, tiled=True, axis_index_groups=along_z
     )
+    z_pay, z_sum, start = step(
+        last_z_kernel,
+        (z_up, z_down, z_1, z_own, start, mark),
+        [z_riding, z_shape, small],
+        "z_fourth",
+    )
+    z_up = turn(z_pay, 2, 1)
+    y_pay, y_sum, mark = step(
+        x_kernel, (y_up, y_down, one, own, start), [y_shape, y_shape, small], "y_second"
+    )
+    y_up = turn(y_pay, 1, 1)
     last, riding = array((owned, half)), array((owned + 8, half))
-    x_far, x_back, x_one, x_own, y_sum, start = call(
-        functools.partial(fifth_kernel, x_count),
-        (place, z_up, y_up, z_sum, own, start),
-        [riding, riding, last, last, y_shape, col_vector],
+    x_far, x_back, x_one, x_own, start = step(
+        functools.partial(split_kernel, x_count),
+        (place, z_up, z_sum, start, mark),
+        [riding, riding, riding, last, small],
+        "x_blocks",
         in_smem=(0,),
-        name="fifth_step",
-    )
-    x_up, x_down, y_down = turn(x_far, 0, 1), turn(x_back, 0, -1), turn(back, 1, -1)
-    x_pay, x_sum, grad_x, start = call(
-        sixth_kernel,
-        (x_up, x_down, y_down, x_one, x_own, y_sum, start),
-        [riding, last, array((width // col_count, src_rows)), col_vector],
+    )
+    x_far, x_one, x_back = turn(x_far, 0, 2), turn(x_one, 0, 1), turn(x_back, 0, -1)
+    grad_x, mark = step(
+        turn_kernel,
+        (y_sum, y_up, start),
+        [array((width // col_count, src_rows)), small],
+        "grad_x",
         last=True,
-        name="sixth_step",
     )
     grad_y, start = call(
         last_kernel,
-        (first, turn(x_pay, 0, 1), x_sum, start),
+        (first, x_far, x_one, x_back, x_own, start),
         [array((owned, tgt_cols)), col_vector],
         name="last_step",
     )

time: 221 us -> 208 us (0.941); the launches traced: 222 us -> 206 us
  waiting for transfers between devices: 35.1 us -> 22.5 us
  Pallas kernels: 25.9 us -> 32.5 us
  starting transfers between devices: 31.6 us -> 25 us
  blocking collectives: 129 us -> 125 us
    ppermute x16, waiting for transfers between devices: 35.1 us -> 22.5 us  [turn(): return lax.ppermute(value, ('rows', 'cols'), moves)]
    pallas_call x19 -> x23, Pallas kernels: 25.9 us -> 32.5 us  [call(): pl.pallas_call(kernel, out_shape=[pltpu.VMEM(out.shape, out.dtype) if mat...]
    ppermute x16, starting transfers between devices: 26.1 us -> 21.5 us  [turn(): return lax.ppermute(value, ('rows', 'cols'), moves)]
    all_to_all x11, blocking collectives: 129 us -> 125 us  [exchanged(): return lax.all_to_all(copies, axis, 0, 0, tiled=True)]
  transfers between devices with their start and end apart: 18 -> 18, of which waited for: 10 -> 7; matrix products, arithmetic and copies ran while one was open for 0% -> 0% of each run, Pallas kernels for 3% -> 4%
where the time goes in v4:
time: 208 us; the launch traced here: 206 us
  blocking collectives  125 us (60%)
  Pallas kernels  32.5 us (16%)
  starting transfers between devices  25 us (12%)
  waiting for transfers between devices  22.5 us (11%)
    all_to_all x11, blocking collectives, exchanged(): return lax.all_to_all(copies, axis, 0, 0, tiled=True)  125 us
    pallas_call x23, Pallas kernels, call(): pl.pallas_call(kernel, out_shape=[pltpu.VMEM(out.shape, out.dtype) if mat...  32.5 us
    ppermute x16, waiting for transfers between devices, turn(): return lax.ppermute(value, ('rows', 'cols'), moves)  22.5 us
    ppermute x16, starting transfers between devices, turn(): return lax.ppermute(value, ('rows', 'cols'), moves)  21.5 us
  transfers between devices with their start and end apart: 18, of which 7 were waited for; matrix products, arithmetic and copies ran while one was open for 0% of the time, Pallas kernels for 4%

profile of v4, /device:TPU:8, one launch (start us, length us, event | category | flops | bytes accessed | tf_op | source)
XLA Modules:
  0.0 206.4 jit_solution(16999878084914614964)
XLA Ops:
  0.7 0.1 pad_add_fusion.place_ref
  0.7 6.2 %first_row_logs.1 = (f32[1024,1024]{1,0:T(8,128)S(1)}, f32[1024,1024]{1,0:T(8,128)S(1)}, f32[8,128]{1,0:T(8,128)S(1)}, f32[8,8,128]{2,1,0:T(8,128)S(1)}, bf16[1024,1024]{1,0:T(8,128)(2,1)S(1)}) custom-call(bf16[1024,1024]{1,0:T(8,128)(2,1)} %cost_hbm.1, s32[8,128]{1,0:T(8,128)} %bitcast.16, s32[8,128]{1,0:T(8,128)} %bitcast.17, s32[64,64]{1,0:T(8,128)} %mask_hbm.1, ...), custom_call_target="tpu_custom_call" | custom-call | flops 1024 | bytes 1024 | tf_op jit(solution)/shard_map/first_row_logs/pallas_call | solution.py:626
  7.0 8.7 %all_to_all.60.parts_ref = f32[8,8,128]{2,1,0:T(8,128)S(1)} all-to-all(f32[8,8,128]{2,1,0:T(8,128)S(1)} %get-tuple-element.76), channel_id=1, replica_groups=mesh['rows'=32,'cols'=8] {'cols'}, dimensions={0} | all-to-all | bytes 65536 | tf_op jit(solution)/shard_map/all_to_all | solution.py:642
  15.7 2.9 %col_logs.3 = (f32[8,128]{1,0:T(8,128)S(1)}, f32[32,8,128]{2,1,0:T(8,128)S(1)}) custom-call(f32[8,8,128]{2,1,0:T(8,128)S(1)} %all_to_all.60.parts_ref, f32[8,128]{1,0:T(8,128)S(1)} %get-tuple-element.77.top_ref, f32[8,128]{1,0:T(8,128)S(1)} %broadcast_1_base_dual_ref_outer_ref.2.base_dual_ref.outer_ref, f32[1024,1024]{1,0:T(8,128)S(1)} %get-tuple-element.78.base_ref, ...), custom_call_target="tpu_custom_call" | custom-call | flops 1024 | bytes 1024 | tf_op jit(solution)/shard_map/col_logs/pallas_call | solution.py:626
  18.5 21.4 %all_to_all.61.parts_ref = f32[32,8,128]{2,1,0:T(8,128)S(1)} all-to-all(f32[32,8,128]{2,1,0:T(8,128)S(1)} %get-tuple-element.80), channel_id=1, replica_groups=mesh['rows'=32,'cols'=8] {'rows'}, dimensions={0} | all-to-all | bytes 262144 | tf_op jit(solution)/shard_map/all_to_all | solution.py:642
  39.9 2.5 %second_row_logs.1 = (f32[1024,1024]{1,0:T(8,128)S(1)}, f32[8,128]{1,0:T(8,128)S(1)}, f32[8,128]{1,0:T(8,128)S(1)}, f32[8,8,128]{2,1,0:T(8,128)S(1)}) custom-call(f32[32,8,128]{2,1,0:T(8,128)S(1)} %all_to_all.61.parts_ref, f32[1024,1024]{1,0:T(8,128)S(1)} %get-tuple-element.79.score_ref), custom_call_target="tpu_custom_call" | custom-call | flops 1024 | bytes 1024 | tf_op jit(solution)/shard_map/second_row_logs/pallas_call | solution.py:626
  42.4 7.8 %all_to_all.62.parts_ref = f32[8,8,128]{2,1,0:T(8,128)S(1)} all-to-all(f32[8,8,128]{2,1,0:T(8,128)S(1)} %get-tuple-element.81), channel_id=1, replica_groups=mesh['rows'=32,'cols'=8] {'cols'}, dimensions={0} | all-to-all | bytes 65536 | tf_op jit(solution)/shard_map/all_to_all | solution.py:642
  50.2 0.6 col_logs.4
  50.9 13.9 %all_to_all.63.parts_ref = f32[32,8,128]{2,1,0:T(8,128)S(1)} all-to-all(f32[32,8,128]{2,1,0:T(8,128)S(1)} %get-tuple-element.85), channel_id=1, replica_groups=mesh['rows'=32,'cols'=8] {'rows'}, dimensions={0} | all-to-all | bytes 262144 | tf_op jit(solution)/shard_map/all_to_all | solution.py:642
  64.7 0.6 third_row_logs.1
  65.3 7.8 %all_to_all.64.parts_ref = f32[8,8,128]{2,1,0:T(8,128)S(1)} all-to-all(f32[8,8,128]{2,1,0:T(8,128)S(1)} %get-tuple-element.86), channel_id=1, replica_groups=mesh['rows'=32,'cols'=8] {'cols'}, dimensions={0} | all-to-all | bytes 65536 | tf_op jit(solution)/shard_map/all_to_all | solution.py:642
  73.1 0.6 col_logs.5
  73.8 13.9 %all_to_all.65.parts_ref = f32[32,8,128]{2,1,0:T(8,128)S(1)} all-to-all(f32[32,8,128]{2,1,0:T(8,128)S(1)} %get-tuple-element.87), channel_id=1, replica_groups=mesh['rows'=32,'cols'=8] {'rows'}, dimensions={0} | all-to-all | bytes 262144 | tf_op jit(solution)/shard_map/all_to_all | solution.py:642
  87.6 0.6 row_plan.3
  88.2 7.8 %all_to_all.66.parts_ref = f32[8,8,128]{2,1,0:T(8,128)S(1)} all-to-all(f32[8,8,128]{2,1,0:T(8,128)S(1)} %get-tuple-element.90), channel_id=1, replica_groups=mesh['rows'=32,'cols'=8] {'cols'}, dimensions={0} | all-to-all | bytes 65536 | tf_op jit(solution)/shard_map/all_to_all | solution.py:642
  96.0 0.5 col_plan.2
  96.6 13.9 %all_to_all.67.parts_ref = f32[32,8,128]{2,1,0:T(8,128)S(1)} all-to-all(f32[32,8,128]{2,1,0:T(8,128)S(1)} %get-tuple-element.91), channel_id=1, replica_groups=mesh['rows'=32,'cols'=8] {'rows'}, dimensions={0} | all-to-all | bytes 262144 | tf_op jit(solution)/shard_map/all_to_all | solution.py:642
  110.4 0.5 row_plan.4
  111.0 7.8 %all_to_all.68.parts_ref = f32[8,8,128]{2,1,0:T(8,128)S(1)} all-to-all(f32[8,8,128]{2,1,0:T(8,128)S(1)} %get-tuple-element.93), channel_id=1, replica_groups=mesh['rows'=32,'cols'=8] {'cols'}, dimensions={0} | all-to-all | bytes 65536 | tf_op jit(solution)/shard_map/all_to_all | solution.py:642
  118.8 0.7 col_plan.3
  119.5 13.9 %all_to_all.69.parts_ref = f32[32,8,128]{2,1,0:T(8,128)S(1)} all-to-all(f32[32,8,128]{2,1,0:T(8,128)S(1)} %get-tuple-element.94), channel_id=1, replica_groups=mesh['rows'=32,'cols'=8] {'rows'}, dimensions={0} | all-to-all | bytes 262144 | tf_op jit(solution)/shard_map/all_to_all | solution.py:642
  133.3 0.5 row_plan.5
  133.9 7.8 %all_to_all.70.parts_ref = f32[8,8,128]{2,1,0:T(8,128)S(1)} all-to-all(f32[8,8,128]{2,1,0:T(8,128)S(1)} %get-tuple-element.96), channel_id=1, replica_groups=mesh['rows'=32,'cols'=8] {'cols'}, dimensions={0} | all-to-all | bytes 65536 | tf_op jit(solution)/shard_map/all_to_all | solution.py:642
  141.7 7.5 %cost_grad.1 = (bf16[1024,1024]{1,0:T(8,128)(2,1)S(1)}, f32[8,128]{1,0:T(8,128)S(1)}, f32[136,512]{1,0:T(8,128)S(1)}, f32[256,512]{1,0:T(8,128)S(1)}, f32[136,512]{1,0:T(8,128)S(1)}, /*index=5*/f32[256,512]{1,0:T(8,128)S(1)}) custom-call(s32[4]{0:T(128)S(1)} %pad_add_fusion.place_ref, f32[8,8,128]{2,1,0:T(8,128)S(1)} %all_to_all.70.parts_ref, ...), custom_call_target="tpu_custom_call" | custom-call | flops 1024 | bytes 1024 | tf_op jit(solution)/shard_map/cost_grad/pallas_call | solution.py:626
  149.2 1.3 collective-permute-start.2
  150.5 2.0 collective-permute-start.3
  152.5 0.6 collective-permute-start
  153.1 2.6 %collective-permute-start.1 = (f32[256,512]{1,0:T(8,128)S(1)}, f32[256,512]{1,0:T(8,128)S(1)}, u32[]{:S(2)}, u32[]{:S(2)}) collective-permute-start(f32[256,512]{1,0:T(8,128)S(1)} %get-tuple-element.104), channel_id=1, source_target_pairs={{0,192},{1,65},{8,200},{9,73},{16,208},{17,81},{24,216},{25,89},{3... | collective-permute-start | bytes 1572872 | tf_op jit(solution)/shard_map/ppermute | solution.py:768
  155.7 4.7 %grad_parts.1 = (f32[1024,512]{1,0:T(8,128)S(1)}, f32[1024,512]{1,0:T(8,128)S(1)}, f32[128,512]{1,0:T(8,128)S(1)}, f32[128,512]{1,0:T(8,128)S(1)}, f32[128,512]{...) custom-call(s32[4]{0:T(128)S(1)} %pad_add_fusion.place_ref, ...), custom_call_target="tpu_custom_call" | custom-call | flops 4294967296 | bytes 1024 | tf_op jit(solution)/shard_map/grad_parts/pallas_call | solution.py:626
  160.4 0.1 collective-permute-start.5
  160.5 0.0 collective-permute-done.3.down_ref
  160.5 0.1 z_second.1
  160.6 0.1 collective-permute-start.6
  160.7 3.2 %collective-permute-start.7 = (f32[136,512]{1,0:T(8,128)S(1)}, f32[136,512]{1,0:T(8,128)S(1)}, u32[]{:S(2)}, u32[]{:S(2)}) collective-permute-start(f32[136,512]{1,0:T(8,128)S(1)} %get-tuple-element.119), channel_id=1, source_target_pairs={{0,56},{1,9},{8,0},{9,17},{16,8},{17,25},{24,16},{25,33},{32,24},{... | collective-permute-start | bytes 835592 | tf_op jit(solution)/shard_map/ppermute | solution.py:768
  163.9 2.5 %collective-permute-done.up_ref = f32[256,512]{1,0:T(8,128)S(1)} collective-permute-done((f32[256,512]{1,0:T(8,128)S(1)}, f32[256,512]{1,0:T(8,128)S(1)}, u32[]{:S(2)}, u32[]{:S(2)}) %collective-permute-start) | collective-permute-done | bytes 524320 | tf_op jit(solution)/shard_map/ppermute | solution.py:768
  166.4 0.1 x_second.1
  166.5 0.1 collective-permute-start.4
  166.6 4.6 %collective-permute-done.6.up_ref = f32[136,512]{1,0:T(8,128)S(1)} collective-permute-done((f32[136,512]{1,0:T(8,128)S(1)}, f32[136,512]{1,0:T(8,128)S(1)}, u32[]{:S(2)}, u32[]{:S(2)}) %collective-permute-start.6) | collective-permute-done | bytes 278560 | tf_op jit(solution)/shard_map/ppermute | solution.py:768
  171.2 0.1 z_third.1
  171.3 0.1 collective-permute-start.8
  171.4 3.2 %collective-permute-start.9 = (f32[136,512]{1,0:T(8,128)S(1)}, f32[136,512]{1,0:T(8,128)S(1)}, u32[]{:S(2)}, u32[]{:S(2)}) collective-permute-start(f32[136,512]{1,0:T(8,128)S(1)} %get-tuple-element.127), channel_id=1, source_target_pairs={{0,56},{1,9},{8,0},{9,17},{16,8},{17,25},{24,16},{25,33},{32,24},{... | collective-permute-start | bytes 835592 | tf_op jit(solution)/shard_map/ppermute | solution.py:768
  174.6 0.0 collective-permute-done.5.arrived_ref
  174.6 0.5 chip_sums.1
  175.1 0.8 copy-done.3
  175.9 1.1 collective-permute-done.4.other_ref
  177.0 0.8 x_last.1
  177.9 3.5 %all-to-all-start.11 = ((f32[8,32,512]{2,1,0:T(8,128)}), f32[8,32,512]{2,1,0:T(8,128)S(1)}, u32[]{:S(2)}, u32[]{:S(2)}) async-start(f32[8,32,512]{2,1,0:T(8,128)} %bitcast.9), calls=%async_computation.11 | async-start | bytes 1048576 | tf_op jit(solution)/shard_map/all_to_all | solution.py:839
  181.4 0.1 collective-permute-start.11
  181.5 2.0 collective-permute-start.12
  183.5 0.1 z_fourth.1
  183.6 1.9 collective-permute-start.10
  185.5 8.5 %collective-permute-done.11.up_ref = f32[1024,128]{1,0:T(8,128)S(1)} collective-permute-done((f32[1024,128]{1,0:T(8,128)S(1)}, f32[1024,128]{1,0:T(8,128)S(1)}, u32[]{:S(2)}, u32[]{:S(2)}) %collective-permute-start.11) | collective-permute-done | bytes 524320 | tf_op jit(solution)/shard_map/ppermute | solution.py:768
  194.0 0.1 y_second.1
  194.1 0.6 collective-permute-start.16
  194.8 2.4 %collective-permute-done.10.z_up_ref = f32[136,512]{1,0:T(8,128)S(1)} collective-permute-done((f32[136,512]{1,0:T(8,128)S(1)}, f32[136,512]{1,0:T(8,128)S(1)}, u32[]{:S(2)}, u32[]{:S(2)}) %collective-permute-start.10) | collective-permute-done | bytes 278560 | tf_op jit(solution)/shard_map/ppermute | solution.py:768
  197.2 0.6 x_blocks.1
  197.8 0.3 collective-permute-start.13
  198.1 2.1 %collective-permute-start.14 = (f32[40,512]{1,0:T(8,128)S(1)}, f32[40,512]{1,0:T(8,128)S(1)}, u32[]{:S(2)}, u32[]{:S(2)}) collective-permute-start(f32[40,512]{1,0:T(8,128)S(1)} %get-tuple-element.140), channel_id=1, source_target_pairs={{0,64},{1,193},{8,72},{9,201},{16,80},{17,209},{24,88},{25,217},{3... | collective-permute-start | bytes 245768 | tf_op jit(solution)/shard_map/ppermute | solution.py:768
  200.2 1.1 collective-permute-start.15
  201.3 2.6 %collective-permute-done.13.far_ref = f32[40,512]{1,0:T(8,128)S(1)} collective-permute-done((f32[40,512]{1,0:T(8,128)S(1)}, f32[40,512]{1,0:T(8,128)S(1)}, u32[]{:S(2)}, u32[]{:S(2)}) %collective-permute-start.13) | collective-permute-done | bytes 81952 | tf_op jit(solution)/shard_map/ppermute | solution.py:768
  203.9 0.7 collective-permute-done.14.one_ref
  204.6 0.0 collective-permute-done.15.back_ref
  204.7 0.7 last_step.1
  205.4 1.0 grad_x.1
  (22 shorter events, 0.0 us)
Async XLA Ops:
  73.1 14.5 %copy-start = (f32[1024]{0:T(1024)S(1)}, f32[1024]{0:T(1024)}, u32[]{:S(2)}) copy-start(f32[1024]{0:T(1024)} %param.15) | copy-start | bytes 12292
  87.6 8.4 %copy-start.1 = (f32[1024]{0:T(1024)S(1)}, f32[1024]{0:T(1024)}, u32[]{:S(2)}) copy-start(f32[1024]{0:T(1024)} %param.14) | copy-start | bytes 12292
  141.7 14.1 %copy-start.2 = (bf16[1024,1024]{1,0:T(8,128)(2,1)S(1)}, bf16[1024,1024]{1,0:T(8,128)(2,1)}, u32[]{:S(2)}) copy-start(bf16[1024,1024]{1,0:T(8,128)(2,1)} %tgt_ref.1) | copy-start | bytes 6291460
  149.2 11.3 %collective-permute-start.2 = (f32[136,512]{1,0:T(8,128)S(1)}, f32[136,512]{1,0:T(8,128)S(1)}, u32[]{:S(2)}, u32[]{:S(2)}) collective-permute-start(f32[136,512]{1,0:T(8,128)S(1)} %get-tuple-element.108), channel_id=1, source_target_pairs={{0,8},{1,57},{8,16},{9,1},{16,24},{17,9},{24,32},{25,17},{32,40},{... | collective-permute-start | bytes 835592 | tf_op jit(solution)/shard_map/ppermute | solution.py:768
  150.5 10.0 %collective-permute-start.3 = (f32[136,512]{1,0:T(8,128)S(1)}, f32[136,512]{1,0:T(8,128)S(1)}, u32[]{:S(2)}, u32[]{:S(2)}) collective-permute-start(f32[136,512]{1,0:T(8,128)S(1)} %get-tuple-element.109), channel_id=1, source_target_pairs={{0,56},{1,9},{8,0},{9,17},{16,8},{17,25},{24,16},{25,33},{32,24},{... | collective-permute-start | bytes 835592 | tf_op jit(solution)/shard_map/ppermute | solution.py:768
  152.5 13.9 %collective-permute-start = (f32[256,512]{1,0:T(8,128)S(1)}, f32[256,512]{1,0:T(8,128)S(1)}, u32[]{:S(2)}, u32[]{:S(2)}) collective-permute-start(f32[256,512]{1,0:T(8,128)S(1)} %get-tuple-element.103), channel_id=1, source_target_pairs={{0,64},{1,193},{8,72},{9,201},{16,80},{17,209},{24,88},{25,217},{3... | collective-permute-start | bytes 1572872 | tf_op jit(solution)/shard_map/ppermute | solution.py:768
  153.1 13.3 %collective-permute-start.1 = (f32[256,512]{1,0:T(8,128)S(1)}, f32[256,512]{1,0:T(8,128)S(1)}, u32[]{:S(2)}, u32[]{:S(2)}) collective-permute-start(f32[256,512]{1,0:T(8,128)S(1)} %get-tuple-element.104), channel_id=1, source_target_pairs={{0,192},{1,65},{8,200},{9,73},{16,208},{17,81},{24,216},{25,89},{3... | collective-permute-start | bytes 1572872 | tf_op jit(solution)/shard_map/ppermute | solution.py:768
  160.4 14.2 %collective-permute-start.5 = (f32[1024,512]{1,0:T(8,128)S(1)}, f32[1024,512]{1,0:T(8,128)S(1)}, u32[]{:S(2)}, u32[]{:S(2)}) collective-permute-start(f32[1024,512]{1,0:T(8,128)S(1)} %get-tuple-element.117), channel_id=1, source_target_pairs={{0,1},{1,0},{2,3},{3,2},{4,5},{5,4},{6,7},{7,6},{8,9},{9,8},{10,11... | collective-permute-start | bytes 6291464 | tf_op jit(solution)/shard_map/ppermute | solution.py:820
  160.6 10.6 %collective-permute-start.6 = (f32[136,512]{1,0:T(8,128)S(1)}, f32[136,512]{1,0:T(8,128)S(1)}, u32[]{:S(2)}, u32[]{:S(2)}) collective-permute-start(f32[136,512]{1,0:T(8,128)S(1)} %get-tuple-element.118), channel_id=1, source_target_pairs={{0,8},{1,57},{8,16},{9,1},{16,24},{17,9},{24,32},{25,17},{32,40},{... | collective-permute-start | bytes 835592 | tf_op jit(solution)/shard_map/ppermute | solution.py:768
  160.7 10.5 %collective-permute-start.7 = (f32[136,512]{1,0:T(8,128)S(1)}, f32[136,512]{1,0:T(8,128)S(1)}, u32[]{:S(2)}, u32[]{:S(2)}) collective-permute-start(f32[136,512]{1,0:T(8,128)S(1)} %get-tuple-element.119), channel_id=1, source_target_pairs={{0,56},{1,9},{8,0},{9,17},{16,8},{17,25},{24,16},{25,33},{32,24},{... | collective-permute-start | bytes 835592 | tf_op jit(solution)/shard_map/ppermute | solution.py:768
  166.5 10.5 %collective-permute-start.4 = (f32[256,512]{1,0:T(8,128)S(1)}, f32[256,512]{1,0:T(8,128)S(1)}, u32[]{:S(2)}, u32[]{:S(2)}) collective-permute-start(f32[256,512]{1,0:T(8,128)S(1)} %get-tuple-element.116), channel_id=1, source_target_pairs={{0,64},{1,193},{8,72},{9,201},{16,80},{17,209},{24,88},{25,217},{3... | collective-permute-start | bytes 1572872 | tf_op jit(solution)/shard_map/ppermute | solution.py:768
  171.3 12.2 %collective-permute-start.8 = (f32[136,512]{1,0:T(8,128)S(1)}, f32[136,512]{1,0:T(8,128)S(1)}, u32[]{:S(2)}, u32[]{:S(2)}) collective-permute-start(f32[136,512]{1,0:T(8,128)S(1)} %get-tuple-element.126), channel_id=1, source_target_pairs={{0,8},{1,57},{8,16},{9,1},{16,24},{17,9},{24,32},{25,17},{32,40},{... | collective-permute-start | bytes 835592 | tf_op jit(solution)/shard_map/ppermute | solution.py:768
  171.4 12.1 %collective-permute-start.9 = (f32[136,512]{1,0:T(8,128)S(1)}, f32[136,512]{1,0:T(8,128)S(1)}, u32[]{:S(2)}, u32[]{:S(2)}) collective-permute-start(f32[136,512]{1,0:T(8,128)S(1)} %get-tuple-element.127), channel_id=1, source_target_pairs={{0,56},{1,9},{8,0},{9,17},{16,8},{17,25},{24,16},{25,33},{32,24},{... | collective-permute-start | bytes 835592 | tf_op jit(solution)/shard_map/ppermute | solution.py:768
  175.1 0.8 copy-start.3
  175.9 1.9 copy-start.5
  177.9 26.8 %all-to-all-start.11 = ((f32[8,32,512]{2,1,0:T(8,128)}), f32[8,32,512]{2,1,0:T(8,128)S(1)}, u32[]{:S(2)}, u32[]{:S(2)}) async-start(f32[8,32,512]{2,1,0:T(8,128)} %bitcast.9), calls=%async_computation.11 | async-start | bytes 1048576 | tf_op jit(solution)/shard_map/all_to_all | solution.py:839
  181.4 12.6 %collective-permute-start.11 = (f32[1024,128]{1,0:T(8,128)S(1)}, f32[1024,128]{1,0:T(8,128)S(1)}, u32[]{:S(2)}, u32[]{:S(2)}) collective-permute-start(f32[1024,128]{1,0:T(8,128)S(1)} %get-tuple-element.134), channel_id=1, source_target_pairs={{0,2},{1,7},{8,10},{9,15},{16,18},{17,23},{24,26},{25,31},{32,34},... | collective-permute-start | bytes 1572872 | tf_op jit(solution)/shard_map/ppermute | solution.py:768
  181.5 12.5 %collective-permute-start.12 = (f32[1024,128]{1,0:T(8,128)S(1)}, f32[1024,128]{1,0:T(8,128)S(1)}, u32[]{:S(2)}, u32[]{:S(2)}) collective-permute-start(f32[1024,128]{1,0:T(8,128)S(1)} %get-tuple-element.135), channel_id=1, source_target_pairs={{0,6},{1,3},{8,14},{9,11},{16,22},{17,19},{24,30},{25,27},{32,38},... | collective-permute-start | bytes 1572872 | tf_op jit(solution)/shard_map/ppermute | solution.py:768
  183.5 10.5 %copy-start.4 = (f32[1024,128]{1,0:T(8,128)S(1)}, f32[1024,128]{1,0:T(8,128)}, u32[]{:S(2)}) copy-start(f32[1024,128]{1,0:T(8,128)} %copy-done.3) | copy-start | bytes 1572868
  183.5 10.5 %copy-start.6 = (f32[1024,128]{1,0:T(8,128)S(1)}, f32[1024,128]{1,0:T(8,128)}, u32[]{:S(2)}) copy-start(f32[1024,128]{1,0:T(8,128)} %copy-done.5) | copy-start | bytes 1572868
  183.6 13.6 %collective-permute-start.10 = (f32[136,512]{1,0:T(8,128)S(1)}, f32[136,512]{1,0:T(8,128)S(1)}, u32[]{:S(2)}, u32[]{:S(2)}) collective-permute-start(f32[136,512]{1,0:T(8,128)S(1)} %get-tuple-element.131), channel_id=1, source_target_pairs={{0,8},{1,57},{8,16},{9,1},{16,24},{17,9},{24,32},{25,17},{32,40},{... | collective-permute-start | bytes 835592 | tf_op jit(solution)/shard_map/ppermute | solution.py:768
  194.1 11.3 %collective-permute-start.16 = (f32[1024,128]{1,0:T(8,128)S(1)}, f32[1024,128]{1,0:T(8,128)S(1)}, u32[]{:S(2)}, u32[]{:S(2)}) collective-permute-start(f32[1024,128]{1,0:T(8,128)S(1)} %get-tuple-element.146), channel_id=1, source_target_pairs={{0,2},{1,7},{8,10},{9,15},{16,18},{17,23},{24,26},{25,31},{32,34},... | collective-permute-start | bytes 1572872 | tf_op jit(solution)/shard_map/ppermute | solution.py:768
  197.8 6.1 %collective-permute-start.13 = (f32[40,512]{1,0:T(8,128)S(1)}, f32[40,512]{1,0:T(8,128)S(1)}, u32[]{:S(2)}, u32[]{:S(2)}) collective-permute-start(f32[40,512]{1,0:T(8,128)S(1)} %get-tuple-element.139), channel_id=1, source_target_pairs={{0,128},{1,129},{8,136},{9,137},{16,144},{17,145},{24,152},{25,153... | collective-permute-start | bytes 245768 | tf_op jit(solution)/shard_map/ppermute | solution.py:768
  198.1 6.5 %collective-permute-start.14 = (f32[40,512]{1,0:T(8,128)S(1)}, f32[40,512]{1,0:T(8,128)S(1)}, u32[]{:S(2)}, u32[]{:S(2)}) collective-permute-start(f32[40,512]{1,0:T(8,128)S(1)} %get-tuple-element.140), channel_id=1, source_target_pairs={{0,64},{1,193},{8,72},{9,201},{16,80},{17,209},{24,88},{25,217},{3... | collective-permute-start | bytes 245768 | tf_op jit(solution)/shard_map/ppermute | solution.py:768
  200.2 4.4 %collective-permute-start.15 = (f32[40,512]{1,0:T(8,128)S(1)}, f32[40,512]{1,0:T(8,128)S(1)}, u32[]{:S(2)}, u32[]{:S(2)}) collective-permute-start(f32[40,512]{1,0:T(8,128)S(1)} %get-tuple-element.141), channel_id=1, source_target_pairs={{0,192},{1,65},{8,200},{9,73},{16,208},{17,81},{24,216},{25,89},{3... | collective-permute-start | bytes 245768 | tf_op jit(solution)/shard_map/ppermute | solution.py:768

commit v5 on v4

--- a/solution.py
+++ b/solution.py
@@ -176,9 +176,9 @@
 
 
 def first_kernel(
-    cost_hbm, src_hbm, tgt_hbm, mask_hbm, dual_hbm, emb_hbm, place_ref, score_ref, base_ref, top_ref,
-    copies_ref, turned_ref, cost_ref, src_ref, tgt_ref, mask_ref, dual_ref, emb_ref, allowed_ref,
-    log_ref, small_sem, cost_sem, emb_sem,
+    cost_hbm, src_hbm, tgt_hbm, mask_hbm, dual_hbm, place_ref, score_ref, base_ref, top_ref,
+    copies_ref, cost_ref, src_ref, tgt_ref, mask_ref, dual_ref, allowed_ref, log_ref, small_sem,
+    cost_sem,
 ):
     small = [
         pltpu.make_async_copy(source, target, small_sem.at[at])
@@ -195,11 +195,6 @@
             pltpu.make_async_copy(cost_hbm.at[rows, :], cost_ref.at[rows, :], cost_sem.at[s])
         )
         blocks[-1].start()
-    embs = []
-    for s in range(emb_ref.shape[0] // LANES):
-        rows = pl.ds(s * LANES, LANES)
-        embs.append(pltpu.make_async_copy(emb_hbm.at[rows, :], emb_ref.at[rows, :], emb_sem.at[s]))
-        embs[-1].start()
     for copy in small:
         copy.wait()
     classes = mask_ref.shape[0]
@@ -220,9 +215,6 @@
         src_hot = jnp.where(label == lane_ids, 1.0, 0.0).astype(jnp.bfloat16)
         allowed_ref[...] = jnp.dot(src_hot, allowed_of, preferred_element_type=F32)
         blocks[s].wait()
-        embs[s].wait()
-        strip = slice(s * LANES, (s + 1) * LANES)
-        turned_ref[:, strip] = emb_ref[strip, :].T
         tops, logs = [], []
         for q in range(LANES // STRIP):
             rows = slice(s * LANES + q * STRIP, s * LANES + (q + 1) * STRIP)
@@ -241,20 +233,45 @@
 
 
 def rebase_kernel(
-    log_target, parts_ref, score_ref, base_ref, top_ref, dual_ref, copies_ref, log_ref
+    log_target, parts_ref, start_top_ref, start_base_ref, score_ref,
+    base_ref, top_ref, dual_ref, copies_ref, log_ref,
 ):
     dual_ref[...] = log_target - log_combined(parts_ref[...])
-    dual = wide(dual_ref)
+    top_ref[...] = start_top_ref[...]
+    powers = jnp.exp2(dual_ref[...])
     for s in range(groups_of(log_ref)):
-        tops, logs = [], []
-        for q in range(LANES // STRIP):
-            rows = slice(s * LANES + q * STRIP, s * LANES + (q + 1) * STRIP)
-            highest, powers, log = strip_logs(score_ref[rows, :] + dual)
-            base_ref[rows, :] = powers
-            tops.append(highest)
-            logs.append(log)
-        top_ref[s : s + 1, :] = to_row(jnp.concatenate(tops, axis=0))
-        log_ref[s : s + 1, :] = to_row(jnp.concatenate(logs, axis=0))
+        rows = slice(s * LANES, (s + 1) * LANES)
+        held = None
+        for c in range(groups_of(dual_ref)):
+            lanes = slice(c * LANES, (c + 1) * LANES)
+            term = start_base_ref[rows, lanes] * powers[c : c + 1, :]
+            base_ref[rows, lanes] = term
+            held = term if held is None else held + term
+        log_ref[s : s + 1, :] = to_row(jnp.sum(held, axis=1, keepdims=True))
+    lowest = jnp.min(jnp.log2(jnp.maximum(log_ref[...], 1e-37)))
+    near = jnp.logical_and(
+        jnp.max(jnp.abs(dual_ref[...])) <= FIRST_REACH,
+        lowest >= jnp.maximum(jnp.max(dual_ref[...]), 0.0) - 92.0,
+    )
+
+    @pl.when(near)
+    def _():
+        log_ref[...] = top_ref[...] + jnp.log2(log_ref[...])
+
+    @pl.when(jnp.logical_not(near))
+    def _():
+        dual = wide(dual_ref)
+        for s in range(groups_of(log_ref)):
+            tops, logs = [], []
+            for q in range(LANES // STRIP):
+                rows = slice(s * LANES + q * STRIP, s * LANES + (q + 1) * STRIP)
+                highest, powers, log = strip_logs(score_ref[rows, :] + dual)
+                base_ref[rows, :] = powers
+                tops.append(highest)
+                logs.append(log)
+            top_ref[s : s + 1, :] = to_row(jnp.concatenate(tops, axis=0))
+            log_ref[s : s + 1, :] = to_row(jnp.concatenate(logs, axis=0))
+
     spread(copies_ref, log_ref[...])
 
 
@@ -264,12 +281,14 @@
 ):
     dual_ref[...] = log_target - log_combined(parts_ref[...])
     lead = dual_ref[...] - base_dual_ref[...]
-    near = jnp.max(jnp.abs(lead)) <= REACH
+    weight_ref[...] = jnp.exp2(jnp.minimum(lead, 100.0))
+    row_sums(base_ref, weight_ref, sum_ref)
+    lowest = jnp.min(jnp.log2(jnp.maximum(sum_ref[...], 1e-37)))
+    most = jnp.maximum(jnp.max(base_dual_ref[...]), 0.0) + jnp.maximum(jnp.max(lead), 0.0)
+    near = jnp.logical_and(jnp.max(jnp.abs(lead)) <= REACH, lowest >= most - 92.0)
 
     @pl.when(near)
     def _():
-        weight_ref[...] = jnp.exp2(lead)
-        row_sums(base_ref, weight_ref, sum_ref)
         sum_ref[...] = top_ref[...] + jnp.log2(sum_ref[...])
 
     @pl.when(jnp.logical_not(near))
@@ -290,7 +309,10 @@
     most = jnp.max(lead)
     near = jnp.logical_and(
         most <= 60.0,
-        jnp.min(jnp.log2(jnp.maximum(sum_ref[...], 1e-37))) >= jnp.maximum(most, -15.0) - 85.0,
+        jnp.min(
+            jnp.log2(jnp.maximum(sum_ref[...], 1e-37)) - jnp.maximum(base_dual_ref[...], 0.0)
+        )
+        >= jnp.maximum(most, -15.0) - 85.0,
     )
 
     @pl.when(near)
@@ -318,7 +340,10 @@
         out_ref[...] = grad
     lead = dual - base_dual_ref[...]
     row_lead = row_dual_ref[...] + top_ref[...]
-    near = jnp.logical_and(jnp.max(jnp.abs(lead)) <= REACH, jnp.max(row_lead) <= 60.0)
+    most = jnp.max(row_lead) + jnp.maximum(jnp.max(base_dual_ref[...]), 0.0)
+    near = jnp.logical_and(
+        jnp.max(jnp.abs(lead)) <= REACH, most + jnp.maximum(jnp.max(lead), 0.0) <= 70.0
+    )
 
     @pl.when(near)
     def _():
@@ -343,7 +368,10 @@
     out_ref[...] = grad
     lead = dual_ref[...] - base_dual_ref[...]
     row_lead = row_dual_ref[...] + top_ref[...]
-    near = jnp.logical_and(jnp.max(jnp.abs(lead)) <= REACH, jnp.max(row_lead) <= 60.0)
+    most = jnp.max(row_lead) + jnp.maximum(jnp.max(base_dual_ref[...]), 0.0)
+    near = jnp.logical_and(
+        jnp.max(jnp.abs(lead)) <= REACH, most + jnp.maximum(jnp.max(lead), 0.0) <= 70.0
+    )
 
     @pl.when(near)
     def _():
@@ -399,18 +427,18 @@
 
 def grad_kernel(
     log_source, log_target, counts, place_ref, parts_ref, row1, row2, row3, col1, col2, col3,
-    fbar2, fbar3, gbar1, gbar2, gbar3, top_ref, base_ref, src_ref, score_ref,
-    out_ref, start_ref, z_far_ref, x_far_ref, z_back_ref, x_back_ref, rows_ref, cols_ref, tile_ref,
+    fbar2, fbar3, gbar1, gbar2, gbar3, top_ref, base_ref, emb_ref, score_ref,
+    out_ref, src_ref, start_ref, z_far_ref, x_far_ref, z_back_ref, x_back_ref, rows_ref, cols_ref, tile_ref,
 ):
     fbar1 = -jnp.sum(parts_ref[...], axis=0)
     leads = [ref[...] - col1[...] for ref in (col2, col3)]
     row_leads = [ref[...] + top_ref[...] for ref in (row1, row2, row3)]
+    most = jnp.max(jnp.maximum(jnp.maximum(row_leads[0], row_leads[1]), row_leads[2]))
+    most = most + jnp.maximum(jnp.max(col1[...]), 0.0)
+    ahead = jnp.maximum(jnp.max(jnp.maximum(leads[0], leads[1])), 0.0)
     near = jnp.logical_and(
         jnp.maximum(jnp.max(jnp.abs(leads[0])), jnp.max(jnp.abs(leads[1]))) <= REACH,
-        jnp.logical_and(
-            jnp.max(jnp.abs(col1[...])) <= FIRST_REACH,
-            jnp.max(jnp.maximum(jnp.maximum(row_leads[0], row_leads[1]), row_leads[2])) <= 60.0,
-        ),
+        jnp.logical_and(jnp.max(jnp.abs(col1[...])) <= FIRST_REACH, most + ahead <= 70.0),
     )
     count, groups = groups_of(col1), groups_of(row1)
 
@@ -443,6 +471,7 @@
             )
             column = jnp.broadcast_to(to_column(rows_ref[s, 5:6, :]), (LANES, LANES))
             rows = slice(s * LANES, (s + 1) * LANES)
+            src_ref[:, rows] = emb_ref[rows, :].T
             for c in range(count):
                 lanes = slice(c * LANES, (c + 1) * LANES)
                 base = base_ref[rows, lanes]
@@ -462,6 +491,8 @@
         ):
             rows_ref[:, k, :] = value
         start_ref[...] = jnp.zeros_like(start_ref)
+        for s in range(groups):
+            src_ref[:, s * LANES : (s + 1) * LANES] = emb_ref[s * LANES : (s + 1) * LANES, :].T
         columns_of = (None, col1, col2, col3)
         grads_of = (None, gbar1, gbar2, gbar3)
 
@@ -672,25 +703,23 @@
     place = jnp.stack(
         [row_at // z_count, col_at // 2, row_at % z_count, col_at % 2]
     ).astype(jnp.int32)
-    score, start_base, start_top, copies, src_turned = call(
+    score, start_base, start_top, copies = call(
         first_kernel,
-        (cost, src_label, tgt_label, class_mask, g_start, src_emb, place),
-        [matrix, matrix, row_vector, row_copies, array(src_emb.shape[::-1], src_emb.dtype)],
+        (cost, src_label, tgt_label, class_mask, g_start, place),
+        [matrix, matrix, row_vector, row_copies],
         [
             pltpu.VMEM(cost.shape, cost.dtype),
             pltpu.VMEM(row_shape, jnp.int32),
             pltpu.VMEM(col_shape, jnp.int32),
             pltpu.VMEM(class_mask.shape, jnp.int32),
             col_held,
-            pltpu.VMEM(src_emb.shape, src_emb.dtype),
             pltpu.VMEM((LANES, tgt_cols), F32),
             row_held,
             pltpu.SemaphoreType.DMA((4,)),
             pltpu.SemaphoreType.DMA(row_shape[:1]),
-            pltpu.SemaphoreType.DMA(row_shape[:1]),
         ],
-        in_hbm=range(6),
-        in_smem=(6,),
+        in_hbm=range(5),
+        in_smem=(5,),
         name="first_row_logs",
     )
 
@@ -707,7 +736,7 @@
     row1, copies = col_logs(exchanged(copies, "cols"), start_top, zero, start_base)
     base, top, col1, copies = call(
         functools.partial(rebase_kernel, log_target),
-        (exchanged(copies, "rows"), score),
+        (exchanged(copies, "rows"), start_top, start_base, score),
         [matrix, row_vector, col_vector, row_copies],
         [row_held],
         name="second_row_logs",
@@ -771,14 +800,23 @@
     z_rows, x_rows = x_count * owned, z_count * owned
     z_shape, z_riding = array((z_rows, half)), array((z_rows + 8, half))
     x_shape = array((x_rows, half))
-    rounded, start, z_far, x_far, z_back, x_back = call(
+    rounded, src_turned, start, z_far, x_far, z_back, x_back = call(
         functools.partial(grad_kernel, log_source, log_target, counts),
         (
             place, parts, row1, row2, row3, col1, col2, col3, fbar2, fbar3, gbar1, gbar2, g_bar,
-            top, base, src_turned, score,
+            top, base, src_emb, score,
         ),
-        [array(cost.shape, jnp.bfloat16), col_vector, z_riding, x_shape, z_riding, x_shape],
+        [
+            array(cost.shape, jnp.bfloat16),
+            array(src_emb.shape[::-1], src_emb.dtype),
+            col_vector,
+            z_riding,
+            x_shape,
+            z_riding,
+            x_shape,
+        ],
         [pltpu.VMEM((row_shape[0], 8, LANES), F32), pltpu.VMEM((8, tgt_cols), F32)] + slow,
+        free=(15,),
         in_smem=(0,),
         name="cost_grad",
     )

time: 208 us -> 225 us (1.082)
  Pallas kernels: 32.5 us -> 49.9 us
    pallas_call x23, Pallas kernels: 32.5 us -> 49.9 us  [call(): pl.pallas_call(kernel, out_shape=[pltpu.VMEM(out.shape, out.dtype) if mat...]
  transfers between devices with their start and end apart: 18 -> 18, of which waited for: 7 -> 7; matrix products, arithmetic and copies ran while one was open for 0% -> 0% of each run, Pallas kernels for 4% -> 3%
where the time goes in v5:
time: 225 us; the launch traced here: 224 us
  blocking collectives  125 us (56%)
  Pallas kernels  49.9 us (22%)
  starting transfers between devices  25.3 us (11%)
  waiting for transfers between devices  22.5 us (10%)
    all_to_all x11, blocking collectives, exchanged(): return lax.all_to_all(copies, axis, 0, 0, tiled=True)  125 us
    pallas_call x23, Pallas kernels, call(): pl.pallas_call(kernel, out_shape=[pltpu.VMEM(out.shape, out.dtype) if mat...  49.9 us
    ppermute x16, waiting for transfers between devices, turn(): return lax.ppermute(value, ('rows', 'cols'), moves)  22.5 us
    ppermute x16, starting transfers between devices, turn(): return lax.ppermute(value, ('rows', 'cols'), moves)  21.7 us
  transfers between devices with their start and end apart: 18, of which 7 were waited for; matrix products, arithmetic and copies ran while one was open for 0% of the time, Pallas kernels for 3%

profile of v5, /device:TPU:8, one launch (start us, length us, event | category | flops | bytes accessed | tf_op | source)
XLA Modules:
  0.0 224.2 jit_solution(13941978320028134496)
XLA Ops:
  0.7 0.1 pad_add_fusion.place_ref
  0.7 5.5 %first_row_logs.1 = (f32[1024,1024]{1,0:T(8,128)S(1)}, f32[1024,1024]{1,0:T(8,128)S(1)}, f32[8,128]{1,0:T(8,128)S(1)}, f32[8,8,128]{2,1,0:T(8,128)S(1)}) custom-call(bf16[1024,1024]{1,0:T(8,128)(2,1)} %cost_hbm.1, s32[8,128]{1,0:T(8,128)} %bitcast.16, s32[8,128]{1,0:T(8,128)} %bitcast.17, s32[64,64]{1,0:T(8,128)} %mask_hbm.1, f32[8,128]{1,0:T(8,128)} %bitcast.18, ...), custom_call_target="tpu_custom_call" | custom-call | flops 1024 | bytes 1024 | tf_op jit(solution)/shard_map/first_row_logs/pallas_call | solution.py:657
  6.2 8.7 %all_to_all.60.parts_ref = f32[8,8,128]{2,1,0:T(8,128)S(1)} all-to-all(f32[8,8,128]{2,1,0:T(8,128)S(1)} %get-tuple-element.76), channel_id=1, replica_groups=mesh['rows'=32,'cols'=8] {'cols'}, dimensions={0} | all-to-all | bytes 65536 | tf_op jit(solution)/shard_map/all_to_all | solution.py:673
  14.9 2.9 %col_logs.3 = (f32[8,128]{1,0:T(8,128)S(1)}, f32[32,8,128]{2,1,0:T(8,128)S(1)}) custom-call(f32[8,8,128]{2,1,0:T(8,128)S(1)} %all_to_all.60.parts_ref, f32[8,128]{1,0:T(8,128)S(1)} %get-tuple-element.77.top_ref.start_top_ref, f32[8,128]{1,0:T(8,128)S(1)} %broadcast_1_base_dual_ref_outer_ref.2.base_dual_ref.outer_ref, ...), custom_call_target="tpu_custom_call" | custom-call | flops 1024 | bytes 1024 | tf_op jit(solution)/shard_map/col_logs/pallas_call | solution.py:657
  17.8 21.4 %all_to_all.61.parts_ref = f32[32,8,128]{2,1,0:T(8,128)S(1)} all-to-all(f32[32,8,128]{2,1,0:T(8,128)S(1)} %get-tuple-element.80), channel_id=1, replica_groups=mesh['rows'=32,'cols'=8] {'rows'}, dimensions={0} | all-to-all | bytes 262144 | tf_op jit(solution)/shard_map/all_to_all | solution.py:673
  39.2 3.4 %second_row_logs.1 = (f32[1024,1024]{1,0:T(8,128)S(1)}, f32[8,128]{1,0:T(8,128)S(1)}, f32[8,128]{1,0:T(8,128)S(1)}, f32[8,8,128]{2,1,0:T(8,128)S(1)}) custom-call(f32[32,8,128]{2,1,0:T(8,128)S(1)} %all_to_all.61.parts_ref, f32[8,128]{1,0:T(8,128)S(1)} %get-tuple-element.77.top_ref.start_top_ref, f32[1024,1024]{1,0:T(8,128)S(1)} %get-tuple-element.78.base_ref.start_base_ref, ...), custom_call_target="tpu_custom_call" | custom-call | flops 1024 | bytes 1024 | tf_op jit(solution)/shard_map/second_row_logs/pallas_call | solution.py:657
  42.6 7.8 %all_to_all.62.parts_ref = f32[8,8,128]{2,1,0:T(8,128)S(1)} all-to-all(f32[8,8,128]{2,1,0:T(8,128)S(1)} %get-tuple-element.81), channel_id=1, replica_groups=mesh['rows'=32,'cols'=8] {'cols'}, dimensions={0} | all-to-all | bytes 65536 | tf_op jit(solution)/shard_map/all_to_all | solution.py:673
  50.4 2.9 %col_logs.4 = (f32[8,128]{1,0:T(8,128)S(1)}, f32[32,8,128]{2,1,0:T(8,128)S(1)}) custom-call(f32[8,8,128]{2,1,0:T(8,128)S(1)} %all_to_all.62.parts_ref, f32[8,128]{1,0:T(8,128)S(1)} %get-tuple-element.82.top_ref, f32[8,128]{1,0:T(8,128)S(1)} %get-tuple-element.83.base_dual_ref.dual_ref.dual_in_ref.col1, f32[1024,1024]{1,0:T(8,128)S(1)} %get-tuple-element.84.base_ref, ...), custom_call_target="tpu_custom_call" | custom-call | flops 1024 | bytes 1024 | tf_op jit(solution)/shard_map/col_logs/pallas_call | solution.py:657
  53.3 13.9 %all_to_all.63.parts_ref = f32[32,8,128]{2,1,0:T(8,128)S(1)} all-to-all(f32[32,8,128]{2,1,0:T(8,128)S(1)} %get-tuple-element.85), channel_id=1, replica_groups=mesh['rows'=32,'cols'=8] {'rows'}, dimensions={0} | all-to-all | bytes 262144 | tf_op jit(solution)/shard_map/all_to_all | solution.py:673
  67.1 3.4 %third_row_logs.1 = (f32[8,128]{1,0:T(8,128)S(1)}, f32[8,8,128]{2,1,0:T(8,128)S(1)}) custom-call(f32[32,8,128]{2,1,0:T(8,128)S(1)} %all_to_all.63.parts_ref, f32[8,128]{1,0:T(8,128)S(1)} %get-tuple-element.82.top_ref, f32[8,128]{1,0:T(8,128)S(1)} %get-tuple-element.83.base_dual_ref.dual_ref.dual_in_ref.col1, f32[1024,1024]{1,0:T(8,128)S(1)} %get-tuple-element.84.base_ref, ...), custom_call_target="tpu_custom_call" | custom-call | flops 1024 | bytes 1024 | tf_op jit(solution)/shard_map/third_row_logs/pallas_call | solution.py:657
  70.5 7.8 %all_to_all.64.parts_ref = f32[8,8,128]{2,1,0:T(8,128)S(1)} all-to-all(f32[8,8,128]{2,1,0:T(8,128)S(1)} %get-tuple-element.86), channel_id=1, replica_groups=mesh['rows'=32,'cols'=8] {'cols'}, dimensions={0} | all-to-all | bytes 65536 | tf_op jit(solution)/shard_map/all_to_all | solution.py:673
  78.3 2.9 %col_logs.5 = (f32[8,128]{1,0:T(8,128)S(1)}, f32[32,8,128]{2,1,0:T(8,128)S(1)}) custom-call(f32[8,8,128]{2,1,0:T(8,128)S(1)} %all_to_all.64.parts_ref, f32[8,128]{1,0:T(8,128)S(1)} %get-tuple-element.82.top_ref, f32[8,128]{1,0:T(8,128)S(1)} %get-tuple-element.83.base_dual_ref.dual_ref.dual_in_ref.col1, f32[1024,1024]{1,0:T(8,128)S(1)} %get-tuple-element.84.base_ref, ...), custom_call_target="tpu_custom_call" | custom-call | flops 1024 | bytes 1024 | tf_op jit(solution)/shard_map/col_logs/pallas_call | solution.py:657
  81.2 13.9 %all_to_all.65.parts_ref = f32[32,8,128]{2,1,0:T(8,128)S(1)} all-to-all(f32[32,8,128]{2,1,0:T(8,128)S(1)} %get-tuple-element.87), channel_id=1, replica_groups=mesh['rows'=32,'cols'=8] {'rows'}, dimensions={0} | all-to-all | bytes 262144 | tf_op jit(solution)/shard_map/all_to_all | solution.py:673
  95.0 3.1 %row_plan.3 = (f32[8,128]{1,0:T(8,128)S(1)}, f32[8,8,128]{2,1,0:T(8,128)S(1)}) custom-call(f32[32,8,128]{2,1,0:T(8,128)S(1)} %all_to_all.65.parts_ref, f32[8,128]{1,0:T(8,128)S(1)} %bitcast.11, f32[8,128]{1,0:T(8,128)S(1)} %get-tuple-element.88.dual_in_ref.dual_ref.col2, f32[8,128]{1,0:T(8,128)S(1)} %get-tuple-element.89.row_dual_ref.row3, ...), custom_call_target="tpu_custom_call" | custom-call | flops 1024 | bytes 1024 | tf_op jit(solution)/shard_map/row_plan/pallas_call | solution.py:657
  98.1 7.8 %all_to_all.66.parts_ref = f32[8,8,128]{2,1,0:T(8,128)S(1)} all-to-all(f32[8,8,128]{2,1,0:T(8,128)S(1)} %get-tuple-element.90), channel_id=1, replica_groups=mesh['rows'=32,'cols'=8] {'cols'}, dimensions={0} | all-to-all | bytes 65536 | tf_op jit(solution)/shard_map/all_to_all | solution.py:673
  105.9 1.6 col_plan.2
  107.5 13.9 %all_to_all.67.parts_ref = f32[32,8,128]{2,1,0:T(8,128)S(1)} all-to-all(f32[32,8,128]{2,1,0:T(8,128)S(1)} %get-tuple-element.91), channel_id=1, replica_groups=mesh['rows'=32,'cols'=8] {'rows'}, dimensions={0} | all-to-all | bytes 262144 | tf_op jit(solution)/shard_map/all_to_all | solution.py:673
  121.4 3.0 %row_plan.4 = (f32[8,128]{1,0:T(8,128)S(1)}, f32[8,8,128]{2,1,0:T(8,128)S(1)}) custom-call(f32[32,8,128]{2,1,0:T(8,128)S(1)} %all_to_all.67.parts_ref, f32[8,128]{1,0:T(8,128)S(1)} %bitcast.12, f32[8,128]{1,0:T(8,128)S(1)} %get-tuple-element.88.dual_in_ref.dual_ref.col2, f32[8,128]{1,0:T(8,128)S(1)} %get-tuple-element.92.row_dual_ref.row2, ...), custom_call_target="tpu_custom_call" | custom-call | flops 1024 | bytes 1024 | tf_op jit(solution)/shard_map/row_plan/pallas_call | solution.py:657
  124.4 7.8 %all_to_all.68.parts_ref = f32[8,8,128]{2,1,0:T(8,128)S(1)} all-to-all(f32[8,8,128]{2,1,0:T(8,128)S(1)} %get-tuple-element.93), channel_id=1, replica_groups=mesh['rows'=32,'cols'=8] {'cols'}, dimensions={0} | all-to-all | bytes 65536 | tf_op jit(solution)/shard_map/all_to_all | solution.py:673
  132.2 1.6 col_plan.3
  133.7 14.0 %all_to_all.69.parts_ref = f32[32,8,128]{2,1,0:T(8,128)S(1)} all-to-all(f32[32,8,128]{2,1,0:T(8,128)S(1)} %get-tuple-element.94), channel_id=1, replica_groups=mesh['rows'=32,'cols'=8] {'rows'}, dimensions={0} | all-to-all | bytes 262144 | tf_op jit(solution)/shard_map/all_to_all | solution.py:673
  147.8 3.0 %row_plan.5 = (f32[8,128]{1,0:T(8,128)S(1)}, f32[8,8,128]{2,1,0:T(8,128)S(1)}) custom-call(f32[32,8,128]{2,1,0:T(8,128)S(1)} %all_to_all.69.parts_ref, f32[8,128]{1,0:T(8,128)S(1)} %bitcast.13, f32[8,128]{1,0:T(8,128)S(1)} %get-tuple-element.83.base_dual_ref.dual_ref.dual_in_ref.col1, f32[8,128]{1,0:T(8,128)S(1)} %get-tuple-element.95.row_dual_ref.row1, ...), custom_call_target="tpu_custom_call" | custom-call | flops 1024 | bytes 1024 | tf_op jit(solution)/shard_map/row_plan/pallas_call | solution.py:657
  150.8 7.8 %all_to_all.70.parts_ref = f32[8,8,128]{2,1,0:T(8,128)S(1)} all-to-all(f32[8,8,128]{2,1,0:T(8,128)S(1)} %get-tuple-element.96), channel_id=1, replica_groups=mesh['rows'=32,'cols'=8] {'cols'}, dimensions={0} | all-to-all | bytes 65536 | tf_op jit(solution)/shard_map/all_to_all | solution.py:673
  158.6 8.2 %cost_grad.1 = (bf16[1024,1024]{1,0:T(8,128)(2,1)S(1)}, bf16[1024,1024]{1,0:T(8,128)(2,1)S(1)}, f32[8,128]{1,0:T(8,128)S(1)}, f32[136,512]{1,0:T(8,128)S(1)}, f3...) custom-call(s32[4]{0:T(128)S(1)} %pad_add_fusion.place_ref, ...), custom_call_target="tpu_custom_call" | custom-call | flops 1024 | bytes 1024 | tf_op jit(solution)/shard_map/cost_grad/pallas_call | solution.py:657
  166.8 1.4 collective-permute-start.2
  168.2 2.0 collective-permute-start.3
  170.1 0.6 collective-permute-start
  170.7 2.6 %collective-permute-start.1 = (f32[256,512]{1,0:T(8,128)S(1)}, f32[256,512]{1,0:T(8,128)S(1)}, u32[]{:S(2)}, u32[]{:S(2)}) collective-permute-start(f32[256,512]{1,0:T(8,128)S(1)} %get-tuple-element.103), channel_id=1, source_target_pairs={{0,192},{1,65},{8,200},{9,73},{16,208},{17,81},{24,216},{25,89},{3... | collective-permute-start | bytes 1572872 | tf_op jit(solution)/shard_map/ppermute | solution.py:797
  173.4 4.6 %grad_parts.1 = (f32[1024,512]{1,0:T(8,128)S(1)}, f32[1024,512]{1,0:T(8,128)S(1)}, f32[128,512]{1,0:T(8,128)S(1)}, f32[128,512]{1,0:T(8,128)S(1)}, f32[128,512]{...) custom-call(s32[4]{0:T(128)S(1)} %pad_add_fusion.place_ref, ...), custom_call_target="tpu_custom_call" | custom-call | flops 4294967296 | bytes 1024 | tf_op jit(solution)/shard_map/grad_parts/pallas_call | solution.py:657
  178.0 0.1 collective-permute-start.5
  178.1 0.0 collective-permute-done.2.up_ref
  178.1 0.0 collective-permute-done.3.down_ref
  178.1 0.1 z_second.1
  178.2 0.4 collective-permute-start.6
  178.5 3.2 %collective-permute-start.7 = (f32[136,512]{1,0:T(8,128)S(1)}, f32[136,512]{1,0:T(8,128)S(1)}, u32[]{:S(2)}, u32[]{:S(2)}) collective-permute-start(f32[136,512]{1,0:T(8,128)S(1)} %get-tuple-element.119), channel_id=1, source_target_pairs={{0,56},{1,9},{8,0},{9,17},{16,8},{17,25},{24,16},{25,33},{32,24},{... | collective-permute-start | bytes 835592 | tf_op jit(solution)/shard_map/ppermute | solution.py:797
  181.7 2.4 %collective-permute-done.up_ref = f32[256,512]{1,0:T(8,128)S(1)} collective-permute-done((f32[256,512]{1,0:T(8,128)S(1)}, f32[256,512]{1,0:T(8,128)S(1)}, u32[]{:S(2)}, u32[]{:S(2)}) %collective-permute-start) | collective-permute-done | bytes 524320 | tf_op jit(solution)/shard_map/ppermute | solution.py:797
  184.1 0.0 collective-permute-done.1.down_ref
  184.1 0.1 x_second.1
  184.2 0.1 collective-permute-start.4
  184.3 4.5 %collective-permute-done.6.up_ref = f32[136,512]{1,0:T(8,128)S(1)} collective-permute-done((f32[136,512]{1,0:T(8,128)S(1)}, f32[136,512]{1,0:T(8,128)S(1)}, u32[]{:S(2)}, u32[]{:S(2)}) %collective-permute-start.6) | collective-permute-done | bytes 278560 | tf_op jit(solution)/shard_map/ppermute | solution.py:797
  188.8 0.1 z_third.1
  188.9 0.1 collective-permute-start.8
  189.0 3.2 %collective-permute-start.9 = (f32[136,512]{1,0:T(8,128)S(1)}, f32[136,512]{1,0:T(8,128)S(1)}, u32[]{:S(2)}, u32[]{:S(2)}) collective-permute-start(f32[136,512]{1,0:T(8,128)S(1)} %get-tuple-element.127), channel_id=1, source_target_pairs={{0,56},{1,9},{8,0},{9,17},{16,8},{17,25},{24,16},{25,33},{32,24},{... | collective-permute-start | bytes 835592 | tf_op jit(solution)/shard_map/ppermute | solution.py:797
  192.2 0.5 chip_sums.1
  192.7 0.8 copy-done.4
  193.5 1.2 collective-permute-done.4.other_ref
  194.7 0.8 x_last.1
  195.5 3.5 %all-to-all-start.11 = ((f32[8,32,512]{2,1,0:T(8,128)}), f32[8,32,512]{2,1,0:T(8,128)S(1)}, u32[]{:S(2)}, u32[]{:S(2)}) async-start(f32[8,32,512]{2,1,0:T(8,128)} %bitcast.9), calls=%async_computation.11 | async-start | bytes 1048576 | tf_op jit(solution)/shard_map/all_to_all | solution.py:877
  199.0 0.6 collective-permute-start.11
  199.6 1.6 collective-permute-start.12
  201.1 0.1 z_fourth.1
  201.2 1.9 collective-permute-start.10
  203.1 8.5 %collective-permute-done.11.up_ref = f32[1024,128]{1,0:T(8,128)S(1)} collective-permute-done((f32[1024,128]{1,0:T(8,128)S(1)}, f32[1024,128]{1,0:T(8,128)S(1)}, u32[]{:S(2)}, u32[]{:S(2)}) %collective-permute-start.11) | collective-permute-done | bytes 524320 | tf_op jit(solution)/shard_map/ppermute | solution.py:797
  211.6 0.1 y_second.1
  211.8 0.6 collective-permute-start.16
  212.4 2.4 %collective-permute-done.10.z_up_ref = f32[136,512]{1,0:T(8,128)S(1)} collective-permute-done((f32[136,512]{1,0:T(8,128)S(1)}, f32[136,512]{1,0:T(8,128)S(1)}, u32[]{:S(2)}, u32[]{:S(2)}) %collective-permute-start.10) | collective-permute-done | bytes 278560 | tf_op jit(solution)/shard_map/ppermute | solution.py:797
  214.8 0.6 x_blocks.1
  215.4 0.3 collective-permute-start.13
  215.7 2.1 collective-permute-start.14
  217.9 1.1 collective-permute-start.15
  219.0 2.6 %collective-permute-done.13.far_ref = f32[40,512]{1,0:T(8,128)S(1)} collective-permute-done((f32[40,512]{1,0:T(8,128)S(1)}, f32[40,512]{1,0:T(8,128)S(1)}, u32[]{:S(2)}, u32[]{:S(2)}) %collective-permute-start.13) | collective-permute-done | bytes 81952 | tf_op jit(solution)/shard_map/ppermute | solution.py:797
  221.6 0.9 collective-permute-done.14.one_ref
  222.5 0.7 last_step.1
  223.2 1.0 grad_x.1
  (24 shorter events, 0.1 us)
Async XLA Ops:
  78.3 16.7 %copy-start.1 = (f32[1024]{0:T(1024)S(1)}, f32[1024]{0:T(1024)}, u32[]{:S(2)}) copy-start(f32[1024]{0:T(1024)} %param.15) | copy-start | bytes 12292
  95.0 10.9 %copy-start.2 = (f32[1024]{0:T(1024)S(1)}, f32[1024]{0:T(1024)}, u32[]{:S(2)}) copy-start(f32[1024]{0:T(1024)} %param.14) | copy-start | bytes 12292
  147.8 10.8 %copy-start = (bf16[1024,1024]{1,0:T(8,128)(2,1)S(1)}, bf16[1024,1024]{1,0:T(8,128)(2,1)}, u32[]{:S(2)}) copy-start(bf16[1024,1024]{1,0:T(8,128)(2,1)} %emb_ref.1) | copy-start | bytes 6291460
  158.6 14.7 %copy-start.3 = (bf16[1024,1024]{1,0:T(8,128)(2,1)S(1)}, bf16[1024,1024]{1,0:T(8,128)(2,1)}, u32[]{:S(2)}) copy-start(bf16[1024,1024]{1,0:T(8,128)(2,1)} %tgt_ref.1) | copy-start | bytes 6291460
  166.8 11.3 %collective-permute-start.2 = (f32[136,512]{1,0:T(8,128)S(1)}, f32[136,512]{1,0:T(8,128)S(1)}, u32[]{:S(2)}, u32[]{:S(2)}) collective-permute-start(f32[136,512]{1,0:T(8,128)S(1)} %get-tuple-element.108), channel_id=1, source_target_pairs={{0,8},{1,57},{8,16},{9,1},{16,24},{17,9},{24,32},{25,17},{32,40},{... | collective-permute-start | bytes 835592 | tf_op jit(solution)/shard_map/ppermute | solution.py:797
  168.2 9.9 %collective-permute-start.3 = (f32[136,512]{1,0:T(8,128)S(1)}, f32[136,512]{1,0:T(8,128)S(1)}, u32[]{:S(2)}, u32[]{:S(2)}) collective-permute-start(f32[136,512]{1,0:T(8,128)S(1)} %get-tuple-element.109), channel_id=1, source_target_pairs={{0,56},{1,9},{8,0},{9,17},{16,8},{17,25},{24,16},{25,33},{32,24},{... | collective-permute-start | bytes 835592 | tf_op jit(solution)/shard_map/ppermute | solution.py:797
  170.1 13.9 %collective-permute-start = (f32[256,512]{1,0:T(8,128)S(1)}, f32[256,512]{1,0:T(8,128)S(1)}, u32[]{:S(2)}, u32[]{:S(2)}) collective-permute-start(f32[256,512]{1,0:T(8,128)S(1)} %get-tuple-element.102), channel_id=1, source_target_pairs={{0,64},{1,193},{8,72},{9,201},{16,80},{17,209},{24,88},{25,217},{3... | collective-permute-start | bytes 1572872 | tf_op jit(solution)/shard_map/ppermute | solution.py:797
  170.7 13.3 %collective-permute-start.1 = (f32[256,512]{1,0:T(8,128)S(1)}, f32[256,512]{1,0:T(8,128)S(1)}, u32[]{:S(2)}, u32[]{:S(2)}) collective-permute-start(f32[256,512]{1,0:T(8,128)S(1)} %get-tuple-element.103), channel_id=1, source_target_pairs={{0,192},{1,65},{8,200},{9,73},{16,208},{17,81},{24,216},{25,89},{3... | collective-permute-start | bytes 1572872 | tf_op jit(solution)/shard_map/ppermute | solution.py:797
  178.0 14.2 %collective-permute-start.5 = (f32[1024,512]{1,0:T(8,128)S(1)}, f32[1024,512]{1,0:T(8,128)S(1)}, u32[]{:S(2)}, u32[]{:S(2)}) collective-permute-start(f32[1024,512]{1,0:T(8,128)S(1)} %get-tuple-element.117), channel_id=1, source_target_pairs={{0,1},{1,0},{2,3},{3,2},{4,5},{5,4},{6,7},{7,6},{8,9},{9,8},{10,11... | collective-permute-start | bytes 6291464 | tf_op jit(solution)/shard_map/ppermute | solution.py:858
  178.2 10.6 %collective-permute-start.6 = (f32[136,512]{1,0:T(8,128)S(1)}, f32[136,512]{1,0:T(8,128)S(1)}, u32[]{:S(2)}, u32[]{:S(2)}) collective-permute-start(f32[136,512]{1,0:T(8,128)S(1)} %get-tuple-element.118), channel_id=1, source_target_pairs={{0,8},{1,57},{8,16},{9,1},{16,24},{17,9},{24,32},{25,17},{32,40},{... | collective-permute-start | bytes 835592 | tf_op jit(solution)/shard_map/ppermute | solution.py:797
  178.5 10.3 %collective-permute-start.7 = (f32[136,512]{1,0:T(8,128)S(1)}, f32[136,512]{1,0:T(8,128)S(1)}, u32[]{:S(2)}, u32[]{:S(2)}) collective-permute-start(f32[136,512]{1,0:T(8,128)S(1)} %get-tuple-element.119), channel_id=1, source_target_pairs={{0,56},{1,9},{8,0},{9,17},{16,8},{17,25},{24,16},{25,33},{32,24},{... | collective-permute-start | bytes 835592 | tf_op jit(solution)/shard_map/ppermute | solution.py:797
  184.2 10.5 %collective-permute-start.4 = (f32[256,512]{1,0:T(8,128)S(1)}, f32[256,512]{1,0:T(8,128)S(1)}, u32[]{:S(2)}, u32[]{:S(2)}) collective-permute-start(f32[256,512]{1,0:T(8,128)S(1)} %get-tuple-element.116), channel_id=1, source_target_pairs={{0,64},{1,193},{8,72},{9,201},{16,80},{17,209},{24,88},{25,217},{3... | collective-permute-start | bytes 1572872 | tf_op jit(solution)/shard_map/ppermute | solution.py:797
  188.9 12.2 %collective-permute-start.8 = (f32[136,512]{1,0:T(8,128)S(1)}, f32[136,512]{1,0:T(8,128)S(1)}, u32[]{:S(2)}, u32[]{:S(2)}) collective-permute-start(f32[136,512]{1,0:T(8,128)S(1)} %get-tuple-element.126), channel_id=1, source_target_pairs={{0,8},{1,57},{8,16},{9,1},{16,24},{17,9},{24,32},{25,17},{32,40},{... | collective-permute-start | bytes 835592 | tf_op jit(solution)/shard_map/ppermute | solution.py:797
  189.0 12.2 %collective-permute-start.9 = (f32[136,512]{1,0:T(8,128)S(1)}, f32[136,512]{1,0:T(8,128)S(1)}, u32[]{:S(2)}, u32[]{:S(2)}) collective-permute-start(f32[136,512]{1,0:T(8,128)S(1)} %get-tuple-element.127), channel_id=1, source_target_pairs={{0,56},{1,9},{8,0},{9,17},{16,8},{17,25},{24,16},{25,33},{32,24},{... | collective-permute-start | bytes 835592 | tf_op jit(solution)/shard_map/ppermute | solution.py:797
  192.7 0.8 copy-start.4
  193.5 2.0 copy-start.6
  195.5 26.9 %all-to-all-start.11 = ((f32[8,32,512]{2,1,0:T(8,128)}), f32[8,32,512]{2,1,0:T(8,128)S(1)}, u32[]{:S(2)}, u32[]{:S(2)}) async-start(f32[8,32,512]{2,1,0:T(8,128)} %bitcast.9), calls=%async_computation.11 | async-start | bytes 1048576 | tf_op jit(solution)/shard_map/all_to_all | solution.py:877
  199.0 12.6 %collective-permute-start.11 = (f32[1024,128]{1,0:T(8,128)S(1)}, f32[1024,128]{1,0:T(8,128)S(1)}, u32[]{:S(2)}, u32[]{:S(2)}) collective-permute-start(f32[1024,128]{1,0:T(8,128)S(1)} %get-tuple-element.134), channel_id=1, source_target_pairs={{0,2},{1,7},{8,10},{9,15},{16,18},{17,23},{24,26},{25,31},{32,34},... | collective-permute-start | bytes 1572872 | tf_op jit(solution)/shard_map/ppermute | solution.py:797
  199.6 12.0 %collective-permute-start.12 = (f32[1024,128]{1,0:T(8,128)S(1)}, f32[1024,128]{1,0:T(8,128)S(1)}, u32[]{:S(2)}, u32[]{:S(2)}) collective-permute-start(f32[1024,128]{1,0:T(8,128)S(1)} %get-tuple-element.135), channel_id=1, source_target_pairs={{0,6},{1,3},{8,14},{9,11},{16,22},{17,19},{24,30},{25,27},{32,38},... | collective-permute-start | bytes 1572872 | tf_op jit(solution)/shard_map/ppermute | solution.py:797
  201.1 10.5 %copy-start.5 = (f32[1024,128]{1,0:T(8,128)S(1)}, f32[1024,128]{1,0:T(8,128)}, u32[]{:S(2)}) copy-start(f32[1024,128]{1,0:T(8,128)} %copy-done.4) | copy-start | bytes 1572868
  201.1 10.5 %copy-start.7 = (f32[1024,128]{1,0:T(8,128)S(1)}, f32[1024,128]{1,0:T(8,128)}, u32[]{:S(2)}) copy-start(f32[1024,128]{1,0:T(8,128)} %copy-done.6) | copy-start | bytes 1572868
  201.2 13.6 %collective-permute-start.10 = (f32[136,512]{1,0:T(8,128)S(1)}, f32[136,512]{1,0:T(8,128)S(1)}, u32[]{:S(2)}, u32[]{:S(2)}) collective-permute-start(f32[136,512]{1,0:T(8,128)S(1)} %get-tuple-element.131), channel_id=1, source_target_pairs={{0,8},{1,57},{8,16},{9,1},{16,24},{17,9},{24,32},{25,17},{32,40},{... | collective-permute-start | bytes 835592 | tf_op jit(solution)/shard_map/ppermute | solution.py:797
  211.8 11.4 %collective-permute-start.16 = (f32[1024,128]{1,0:T(8,128)S(1)}, f32[1024,128]{1,0:T(8,128)S(1)}, u32[]{:S(2)}, u32[]{:S(2)}) collective-permute-start(f32[1024,128]{1,0:T(8,128)S(1)} %get-tuple-element.146), channel_id=1, source_target_pairs={{0,2},{1,7},{8,10},{9,15},{16,18},{17,23},{24,26},{25,31},{32,34},... | collective-permute-start | bytes 1572872 | tf_op jit(solution)/shard_map/ppermute | solution.py:797
  215.4 6.1 %collective-permute-start.13 = (f32[40,512]{1,0:T(8,128)S(1)}, f32[40,512]{1,0:T(8,128)S(1)}, u32[]{:S(2)}, u32[]{:S(2)}) collective-permute-start(f32[40,512]{1,0:T(8,128)S(1)} %get-tuple-element.139), channel_id=1, source_target_pairs={{0,128},{1,129},{8,136},{9,137},{16,144},{17,145},{24,152},{25,153... | collective-permute-start | bytes 245768 | tf_op jit(solution)/shard_map/ppermute | solution.py:797
  215.7 6.7 %collective-permute-start.14 = (f32[40,512]{1,0:T(8,128)S(1)}, f32[40,512]{1,0:T(8,128)S(1)}, u32[]{:S(2)}, u32[]{:S(2)}) collective-permute-start(f32[40,512]{1,0:T(8,128)S(1)} %get-tuple-element.140), channel_id=1, source_target_pairs={{0,64},{1,193},{8,72},{9,201},{16,80},{17,209},{24,88},{25,217},{3... | collective-permute-start | bytes 245768 | tf_op jit(solution)/shard_map/ppermute | solution.py:797
  217.9 4.6 %collective-permute-start.15 = (f32[40,512]{1,0:T(8,128)S(1)}, f32[40,512]{1,0:T(8,128)S(1)}, u32[]{:S(2)}, u32[]{:S(2)}) collective-permute-start(f32[40,512]{1,0:T(8,128)S(1)} %get-tuple-element.141), channel_id=1, source_target_pairs={{0,192},{1,65},{8,200},{9,73},{16,208},{17,81},{24,216},{25,89},{3... | collective-permute-start | bytes 245768 | tf_op jit(solution)/shard_map/ppermute | solution.py:797

commit v6 on v5

--- a/solution.py
+++ b/solution.py
@@ -176,7 +176,7 @@
 
 
 def first_kernel(
-    cost_hbm, src_hbm, tgt_hbm, mask_hbm, dual_hbm, place_ref, score_ref, base_ref, top_ref,
+    cost_hbm, src_hbm, tgt_hbm, mask_hbm, dual_hbm, score_ref, base_ref, top_ref,
     copies_ref, cost_ref, src_ref, tgt_ref, mask_ref, dual_ref, allowed_ref, log_ref, small_sem,
     cost_sem,
 ):
@@ -345,11 +345,9 @@
         jnp.max(jnp.abs(lead)) <= REACH, most + jnp.maximum(jnp.max(lead), 0.0) <= 70.0
     )
 
-    @pl.when(near)
-    def _():
-        weight_ref[...] = jnp.exp2(lead - log_target) * grad
-        row_sums(base_ref, weight_ref, sum_ref)
-        sum_ref[...] = sum_ref[...] * jnp.exp2(row_lead)
+    weight_ref[...] = jnp.exp2(lead - log_target) * grad
+    row_sums(base_ref, weight_ref, sum_ref)
+    sum_ref[...] = sum_ref[...] * jnp.exp2(row_lead)
 
     @pl.when(jnp.logical_not(near))
     def _():
@@ -373,11 +371,9 @@
         jnp.max(jnp.abs(lead)) <= REACH, most + jnp.maximum(jnp.max(lead), 0.0) <= 70.0
     )
 
-    @pl.when(near)
-    def _():
-        weight_ref[...] = jnp.exp2(row_lead) * grad
-        col_sums(base_ref, weight_ref, sum_ref)
-        sum_ref[...] = sum_ref[...] * jnp.exp2(lead - log_source)
+    weight_ref[...] = jnp.exp2(row_lead) * grad
+    col_sums(base_ref, weight_ref, sum_ref)
+    sum_ref[...] = sum_ref[...] * jnp.exp2(lead - log_source)
 
     @pl.when(jnp.logical_not(near))
     def _():
@@ -386,6 +382,11 @@
         slow_col_weighted(score_ref, tile_ref, row_dual_ref, col_ref, weight_ref, sum_ref)
 
     spread(copies_ref, sum_ref[...])
+
+
+def place_of(counts):
+    row_at, col_at = lax.axis_index("rows"), lax.axis_index("cols")
+    return row_at // counts[1], col_at // 2, row_at % counts[1], col_at % 2
 
 
 def direction(place_ref):
@@ -426,10 +427,11 @@
 
 
 def grad_kernel(
-    log_source, log_target, counts, place_ref, parts_ref, row1, row2, row3, col1, col2, col3,
+    log_source, log_target, counts, parts_ref, row1, row2, row3, col1, col2, col3,
     fbar2, fbar3, gbar1, gbar2, gbar3, top_ref, base_ref, emb_ref, score_ref,
     out_ref, src_ref, start_ref, z_far_ref, x_far_ref, z_back_ref, x_back_ref, rows_ref, cols_ref, tile_ref,
 ):
+    place_ref = place_of(counts)
     fbar1 = -jnp.sum(parts_ref[...], axis=0)
     leads = [ref[...] - col1[...] for ref in (col2, col3)]
     row_leads = [ref[...] + top_ref[...] for ref in (row1, row2, row3)]
@@ -549,8 +551,9 @@
 
 
 def parts_kernel(
-    counts, y_count, place_ref, grad_ref, src_ref, tgt_ref, sent_ref, kept_ref, *outs
-):
+    counts, y_count, grad_ref, src_ref, tgt_ref, sent_ref, kept_ref, *outs
+):
+    place_ref = place_of(counts)
     *outs, order_ref = outs
     x_part(y_count, place_ref, grad_ref, tgt_ref, sent_ref, kept_ref, order_ref)
     reach = counts[1] // 2
@@ -583,9 +586,12 @@
     token(token_ref)
 
 
-def add_kernel(one_ref, other_ref, after_ref, sum_ref, token_ref):
-    sum_ref[...] = one_ref[...] + other_ref[...]
-    token(token_ref)
+def y_kernel(
+    up_ref, down_ref, one_ref, own_ref, x_up_ref, x_sum_ref, after_ref, pay_ref, sum_ref, x_ref,
+    token_ref,
+):
+    x_kernel(up_ref, down_ref, one_ref, own_ref, after_ref, pay_ref, sum_ref, token_ref)
+    x_ref[...] = x_sum_ref[...] + x_up_ref[...]
 
 
 def chip_kernel(arrived_ref, kept_ref, after_ref, *outs):
@@ -605,9 +611,10 @@
 
 
 def split_kernel(
-    x_count, place_ref, z_up_ref, z_sum_ref, start_ref, after_ref,
+    counts, z_up_ref, z_sum_ref, start_ref, after_ref,
     far_ref, back_ref, one_ref, last_ref, held_ref,
 ):
+    x_count, place_ref = counts[0], place_of(counts)
     held_ref[...] = start_ref[...] + rider(z_up_ref)
     block = z_sum_ref.shape[0] // x_count
     for out_ref, offset in ((far_ref, 2), (back_ref, -1), (one_ref, 1), (last_ref, 0)):
@@ -639,7 +646,7 @@
 
 
 def call(
-    kernel, arguments, outs, scratch=(), in_hbm=(), loose=(), in_smem=(), free=(), last=False, flops=1024, name=None
+    kernel, arguments, outs, scratch=(), in_hbm=(), loose=(), free=(), last=False, flops=1024, name=None
 ):
     spaces, values = [], []
     for at, value in enumerate(arguments):
@@ -648,8 +655,6 @@
             space = pltpu.HBM
         elif at in loose:
             space = pl.ANY
-        elif at in in_smem:
-            space = pltpu.SMEM
         if at in in_hbm or (space is pltpu.VMEM and value.size >= PINNED and at not in free):
             value = pltpu.with_memory_space_constraint(value, space)
         spaces.append(space)
@@ -699,13 +704,9 @@
     x_count, z_count, y_count = 4, row_count // 4, col_count // 2
     counts = (x_count, z_count)
     owned = width // row_count
-    row_at, col_at = lax.axis_index("rows"), lax.axis_index("cols")
-    place = jnp.stack(
-        [row_at // z_count, col_at // 2, row_at % z_count, col_at % 2]
-    ).astype(jnp.int32)
     score, start_base, start_top, copies = call(
         first_kernel,
-        (cost, src_label, tgt_label, class_mask, g_start, place),
+        (cost, src_label, tgt_label, class_mask, g_start),
         [matrix, matrix, row_vector, row_copies],
         [
             pltpu.VMEM(cost.shape, cost.dtype),
@@ -719,7 +720,6 @@
             pltpu.SemaphoreType.DMA(row_shape[:1]),
         ],
         in_hbm=range(5),
-        in_smem=(5,),
         name="first_row_logs",
     )
 
@@ -803,7 +803,7 @@
     rounded, src_turned, start, z_far, x_far, z_back, x_back = call(
         functools.partial(grad_kernel, log_source, log_target, counts),
         (
-            place, parts, row1, row2, row3, col1, col2, col3, fbar2, fbar3, gbar1, gbar2, g_bar,
+            parts, row1, row2, row3, col1, col2, col3, fbar2, fbar3, gbar1, gbar2, g_bar,
             top, base, src_emb, score,
         ),
         [
@@ -816,8 +816,7 @@
             x_shape,
         ],
         [pltpu.VMEM((row_shape[0], 8, LANES), F32), pltpu.VMEM((8, tgt_cols), F32)] + slow,
-        free=(15,),
-        in_smem=(0,),
+        free=(14,),
         name="cost_grad",
     )
     z_up, z_down = turn(z_far, 2, 1), turn(z_back, 2, -1)
@@ -825,26 +824,24 @@
     chip_part = array((src_rows, width // 2))
     outs = call(
         functools.partial(parts_kernel, counts, y_count),
-        (place, rounded, src_turned, tgt_emb),
+        (rounded, src_turned, tgt_emb),
         [chip_part] * 2 + [z_shape] * (z_count - 2) + [x_shape] * 2,
         [pltpu.VMEM((tgt_cols, width // 2), jnp.bfloat16)],
-        in_smem=(0,),
-        free=(3,),
+        free=(2,),
         flops=BIG,
         name="grad_parts",
     )
     sent, kept, z_3, z_2, z_1, z_back2, z_back1, z_own, x_one, x_own = outs
     small = array((8, LANES))
 
-    def step(kernel, arguments, outs, name, last=False, in_smem=()):
+    def step(kernel, arguments, outs, name, last=False, flops=STEP):
         return call(
             kernel,
             arguments,
             outs,
             loose=(len(arguments) - 1,),
             last=last,
-            in_smem=in_smem,
-            flops=STEP,
+            flops=flops,
             name=name,
         )
 
@@ -857,44 +854,48 @@
     z_up, z_down = turn(z_pay, 2, 1), turn(z_back, 2, -1)
     arrived = lax.ppermute(sent, "cols", [(at, at ^ 1) for at in range(col_count)])
     x_pay, x_sum, mark = step(
-        x_kernel, (x_up, x_down, x_one, x_own, start), [x_shape, x_shape, small], "x_second"
+        x_kernel, (x_up, x_down, x_one, x_own, start), [x_shape, x_shape, small], "x_second",
+        flops=2**34
     )
     x_up = turn(x_pay, 0, 1)
+    y_shape = array((src_rows, width // col_count))
+    far, one, back, own, mark = step(
+        chip_kernel, (arrived, kept, mark), [y_shape] * 4 + [small], "chip_sums"
+    )
+    y_up, y_down = turn(far, 1, 1), turn(back, 1, -1)
     z_pay, z_back, start = step(
         z_kernel,
         (z_up, z_down, z_2, z_back1, start, mark),
         [z_riding, z_riding, small],
         "z_third",
+        flops=2**31,
     )
     z_up, z_down = turn(z_pay, 2, 1), turn(z_back, 2, -1)
-    y_shape = array((src_rows, width // col_count))
-    far, one, back, own, mark = step(
-        chip_kernel, (arrived, kept, start), [y_shape] * 4 + [small], "chip_sums"
-    )
-    y_up, y_down = turn(far, 1, 1), turn(back, 1, -1)
-    first, mark = step(add_kernel, (x_sum, x_up, mark), [x_shape, small], "x_last")
+    z_pay, z_sum, start = step(
+        last_z_kernel,
+        (z_up, z_down, z_1, z_own, start, start),
+        [z_riding, z_shape, small],
+        "z_fourth",
+        flops=2**31,
+    )
+    z_up = turn(z_pay, 2, 1)
+    y_pay, y_sum, first, mark = step(
+        y_kernel,
+        (y_up, y_down, one, own, x_up, x_sum, start),
+        [y_shape, y_shape, x_shape, small],
+        "y_second",
+    )
     along_z = [[x * z_count + z for z in range(z_count)] for x in range(x_count)]
     first = lax.all_to_all(
         first.reshape(z_count, owned, half), "rows", 0, 0, tiled=True, axis_index_groups=along_z
     )
-    z_pay, z_sum, start = step(
-        last_z_kernel,
-        (z_up, z_down, z_1, z_own, start, mark),
-        [z_riding, z_shape, small],
-        "z_fourth",
-    )
-    z_up = turn(z_pay, 2, 1)
-    y_pay, y_sum, mark = step(
-        x_kernel, (y_up, y_down, one, own, start), [y_shape, y_shape, small], "y_second"
-    )
     y_up = turn(y_pay, 1, 1)
     last, riding = array((owned, half)), array((owned + 8, half))
     x_far, x_back, x_one, x_own, start = step(
-        functools.partial(split_kernel, x_count),
-        (place, z_up, z_sum, start, mark),
+        functools.partial(split_kernel, counts),
+        (z_up, z_sum, start, mark),
         [riding, riding, riding, last, small],
         "x_blocks",
-        in_smem=(0,),
     )
     x_far, x_one, x_back = turn(x_far, 0, 2), turn(x_one, 0, 1), turn(x_back, 0, -1)
     grad_x, mark = step(

time: 225 us -> 225 us (level)
    ppermute x16, waiting for transfers between devices: 22.5 us -> 15.1 us  [turn(): return lax.ppermute(value, ('rows', 'cols'), moves)]
    all_to_all x1, waiting for transfers between devices: 0.01 us -> 7.2 us  [body(): lax.all_to_all(first.reshape(z_count, owned, half), 'rows', 0, 0, tiled=T...]
    pallas_call x23 -> x22, Pallas kernels: 49.9 us -> 48.9 us  [call(): pl.pallas_call(kernel, out_shape=[pltpu.VMEM(out.shape, out.dtype) if mat...]
where the time goes in v6:
time: 225 us; the launch traced here: 222 us
  blocking collectives  125 us (56%)
  Pallas kernels  48.9 us (22%)
  starting transfers between devices  25.3 us (11%)
  waiting for transfers between devices  22.3 us (10%)
    all_to_all x11, blocking collectives, exchanged(): return lax.all_to_all(copies, axis, 0, 0, tiled=True)  125 us
    pallas_call x22, Pallas kernels, call(): pl.pallas_call(kernel, out_shape=[pltpu.VMEM(out.shape, out.dtype) if mat...  48.9 us
    ppermute x16, starting transfers between devices, turn(): return lax.ppermute(value, ('rows', 'cols'), moves)  20.8 us
    ppermute x16, waiting for transfers between devices, turn(): return lax.ppermute(value, ('rows', 'cols'), moves)  15.1 us
    all_to_all x1, waiting for transfers between devices, body(): lax.all_to_all(first.reshape(z_count, owned, half), 'rows', 0, 0, tiled=T...  7.2 us
  transfers between devices with their start and end apart: 18, of which 7 were waited for; matrix products, arithmetic and copies ran while one was open for 0% of the time, Pallas kernels for 3%

profile of v6, /device:TPU:8, one launch (start us, length us, event | category | flops | bytes accessed | tf_op | source)
XLA Modules:
  0.0 221.9 jit_solution(8662068231472186823)
XLA Ops:
  0.6 4.9 %first_row_logs.1 = (f32[1024,1024]{1,0:T(8,128)S(1)}, f32[1024,1024]{1,0:T(8,128)S(1)}, f32[8,128]{1,0:T(8,128)S(1)}, f32[8,8,128]{2,1,0:T(8,128)S(1)}) custom-call(bf16[1024,1024]{1,0:T(8,128)(2,1)} %cost_hbm.1, s32[8,128]{1,0:T(8,128)} %bitcast.12, s32[8,128]{1,0:T(8,128)} %bitcast.13, s32[64,64]{1,0:T(8,128)} %mask_hbm.1, f32[8,128]{1,0:T(8,128)} %bitcast.14), custom_call_target="tpu_custom_call" | custom-call | flops 1024 | bytes 1024 | tf_op jit(solution)/shard_map/first_row_logs/pallas_call | solution.py:662
  5.6 8.7 %all_to_all.60.parts_ref = f32[8,8,128]{2,1,0:T(8,128)S(1)} all-to-all(f32[8,8,128]{2,1,0:T(8,128)S(1)} %get-tuple-element.75), channel_id=1, replica_groups=mesh['rows'=32,'cols'=8] {'cols'}, dimensions={0} | all-to-all | bytes 65536 | tf_op jit(solution)/shard_map/all_to_all | solution.py:678
  14.3 2.9 %col_logs.3 = (f32[8,128]{1,0:T(8,128)S(1)}, f32[32,8,128]{2,1,0:T(8,128)S(1)}) custom-call(f32[8,8,128]{2,1,0:T(8,128)S(1)} %all_to_all.60.parts_ref, f32[8,128]{1,0:T(8,128)S(1)} %get-tuple-element.76.top_ref.start_top_ref, f32[8,128]{1,0:T(8,128)S(1)} %broadcast_1_base_dual_ref_outer_ref.2.base_dual_ref.outer_ref, ...), custom_call_target="tpu_custom_call" | custom-call | flops 1024 | bytes 1024 | tf_op jit(solution)/shard_map/col_logs/pallas_call | solution.py:662
  17.2 21.4 %all_to_all.61.parts_ref = f32[32,8,128]{2,1,0:T(8,128)S(1)} all-to-all(f32[32,8,128]{2,1,0:T(8,128)S(1)} %get-tuple-element.79), channel_id=1, replica_groups=mesh['rows'=32,'cols'=8] {'rows'}, dimensions={0} | all-to-all | bytes 262144 | tf_op jit(solution)/shard_map/all_to_all | solution.py:678
  38.5 3.4 %second_row_logs.1 = (f32[1024,1024]{1,0:T(8,128)S(1)}, f32[8,128]{1,0:T(8,128)S(1)}, f32[8,128]{1,0:T(8,128)S(1)}, f32[8,8,128]{2,1,0:T(8,128)S(1)}) custom-call(f32[32,8,128]{2,1,0:T(8,128)S(1)} %all_to_all.61.parts_ref, f32[8,128]{1,0:T(8,128)S(1)} %get-tuple-element.76.top_ref.start_top_ref, f32[1024,1024]{1,0:T(8,128)S(1)} %get-tuple-element.77.base_ref.start_base_ref, ...), custom_call_target="tpu_custom_call" | custom-call | flops 1024 | bytes 1024 | tf_op jit(solution)/shard_map/second_row_logs/pallas_call | solution.py:662
  41.9 7.8 %all_to_all.62.parts_ref = f32[8,8,128]{2,1,0:T(8,128)S(1)} all-to-all(f32[8,8,128]{2,1,0:T(8,128)S(1)} %get-tuple-element.80), channel_id=1, replica_groups=mesh['rows'=32,'cols'=8] {'cols'}, dimensions={0} | all-to-all | bytes 65536 | tf_op jit(solution)/shard_map/all_to_all | solution.py:678
  49.7 2.8 %col_logs.4 = (f32[8,128]{1,0:T(8,128)S(1)}, f32[32,8,128]{2,1,0:T(8,128)S(1)}) custom-call(f32[8,8,128]{2,1,0:T(8,128)S(1)} %all_to_all.62.parts_ref, f32[8,128]{1,0:T(8,128)S(1)} %get-tuple-element.81.top_ref, f32[8,128]{1,0:T(8,128)S(1)} %get-tuple-element.82.base_dual_ref.dual_ref.dual_in_ref.col1, f32[1024,1024]{1,0:T(8,128)S(1)} %get-tuple-element.83.base_ref, ...), custom_call_target="tpu_custom_call" | custom-call | flops 1024 | bytes 1024 | tf_op jit(solution)/shard_map/col_logs/pallas_call | solution.py:662
  52.6 13.9 %all_to_all.63.parts_ref = f32[32,8,128]{2,1,0:T(8,128)S(1)} all-to-all(f32[32,8,128]{2,1,0:T(8,128)S(1)} %get-tuple-element.84), channel_id=1, replica_groups=mesh['rows'=32,'cols'=8] {'rows'}, dimensions={0} | all-to-all | bytes 262144 | tf_op jit(solution)/shard_map/all_to_all | solution.py:678
  66.4 3.3 %third_row_logs.1 = (f32[8,128]{1,0:T(8,128)S(1)}, f32[8,8,128]{2,1,0:T(8,128)S(1)}) custom-call(f32[32,8,128]{2,1,0:T(8,128)S(1)} %all_to_all.63.parts_ref, f32[8,128]{1,0:T(8,128)S(1)} %get-tuple-element.81.top_ref, f32[8,128]{1,0:T(8,128)S(1)} %get-tuple-element.82.base_dual_ref.dual_ref.dual_in_ref.col1, f32[1024,1024]{1,0:T(8,128)S(1)} %get-tuple-element.83.base_ref, ...), custom_call_target="tpu_custom_call" | custom-call | flops 1024 | bytes 1024 | tf_op jit(solution)/shard_map/third_row_logs/pallas_call | solution.py:662
  69.8 7.8 %all_to_all.64.parts_ref = f32[8,8,128]{2,1,0:T(8,128)S(1)} all-to-all(f32[8,8,128]{2,1,0:T(8,128)S(1)} %get-tuple-element.85), channel_id=1, replica_groups=mesh['rows'=32,'cols'=8] {'cols'}, dimensions={0} | all-to-all | bytes 65536 | tf_op jit(solution)/shard_map/all_to_all | solution.py:678
  77.6 2.8 %col_logs.5 = (f32[8,128]{1,0:T(8,128)S(1)}, f32[32,8,128]{2,1,0:T(8,128)S(1)}) custom-call(f32[8,8,128]{2,1,0:T(8,128)S(1)} %all_to_all.64.parts_ref, f32[8,128]{1,0:T(8,128)S(1)} %get-tuple-element.81.top_ref, f32[8,128]{1,0:T(8,128)S(1)} %get-tuple-element.82.base_dual_ref.dual_ref.dual_in_ref.col1, f32[1024,1024]{1,0:T(8,128)S(1)} %get-tuple-element.83.base_ref, ...), custom_call_target="tpu_custom_call" | custom-call | flops 1024 | bytes 1024 | tf_op jit(solution)/shard_map/col_logs/pallas_call | solution.py:662
  80.4 13.9 %all_to_all.65.parts_ref = f32[32,8,128]{2,1,0:T(8,128)S(1)} all-to-all(f32[32,8,128]{2,1,0:T(8,128)S(1)} %get-tuple-element.86), channel_id=1, replica_groups=mesh['rows'=32,'cols'=8] {'rows'}, dimensions={0} | all-to-all | bytes 262144 | tf_op jit(solution)/shard_map/all_to_all | solution.py:678
  94.2 3.4 %row_plan.3 = (f32[8,128]{1,0:T(8,128)S(1)}, f32[8,8,128]{2,1,0:T(8,128)S(1)}) custom-call(f32[32,8,128]{2,1,0:T(8,128)S(1)} %all_to_all.65.parts_ref, f32[8,128]{1,0:T(8,128)S(1)} %bitcast.7, f32[8,128]{1,0:T(8,128)S(1)} %get-tuple-element.87.dual_in_ref.dual_ref.col2, f32[8,128]{1,0:T(8,128)S(1)} %get-tuple-element.88.row_dual_ref.row3, ...), custom_call_target="tpu_custom_call" | custom-call | flops 1024 | bytes 1024 | tf_op jit(solution)/shard_map/row_plan/pallas_call | solution.py:662
  97.6 7.8 %all_to_all.66.parts_ref = f32[8,8,128]{2,1,0:T(8,128)S(1)} all-to-all(f32[8,8,128]{2,1,0:T(8,128)S(1)} %get-tuple-element.89), channel_id=1, replica_groups=mesh['rows'=32,'cols'=8] {'cols'}, dimensions={0} | all-to-all | bytes 65536 | tf_op jit(solution)/shard_map/all_to_all | solution.py:678
  105.4 1.8 col_plan.2
  107.2 13.9 %all_to_all.67.parts_ref = f32[32,8,128]{2,1,0:T(8,128)S(1)} all-to-all(f32[32,8,128]{2,1,0:T(8,128)S(1)} %get-tuple-element.90), channel_id=1, replica_groups=mesh['rows'=32,'cols'=8] {'rows'}, dimensions={0} | all-to-all | bytes 262144 | tf_op jit(solution)/shard_map/all_to_all | solution.py:678
  121.1 3.3 %row_plan.4 = (f32[8,128]{1,0:T(8,128)S(1)}, f32[8,8,128]{2,1,0:T(8,128)S(1)}) custom-call(f32[32,8,128]{2,1,0:T(8,128)S(1)} %all_to_all.67.parts_ref, f32[8,128]{1,0:T(8,128)S(1)} %bitcast.8, f32[8,128]{1,0:T(8,128)S(1)} %get-tuple-element.87.dual_in_ref.dual_ref.col2, f32[8,128]{1,0:T(8,128)S(1)} %get-tuple-element.91.row_dual_ref.row2, ...), custom_call_target="tpu_custom_call" | custom-call | flops 1024 | bytes 1024 | tf_op jit(solution)/shard_map/row_plan/pallas_call | solution.py:662
  124.4 7.8 %all_to_all.68.parts_ref = f32[8,8,128]{2,1,0:T(8,128)S(1)} all-to-all(f32[8,8,128]{2,1,0:T(8,128)S(1)} %get-tuple-element.92), channel_id=1, replica_groups=mesh['rows'=32,'cols'=8] {'cols'}, dimensions={0} | all-to-all | bytes 65536 | tf_op jit(solution)/shard_map/all_to_all | solution.py:678
  132.2 1.8 col_plan.3
  134.0 13.9 %all_to_all.69.parts_ref = f32[32,8,128]{2,1,0:T(8,128)S(1)} all-to-all(f32[32,8,128]{2,1,0:T(8,128)S(1)} %get-tuple-element.93), channel_id=1, replica_groups=mesh['rows'=32,'cols'=8] {'rows'}, dimensions={0} | all-to-all | bytes 262144 | tf_op jit(solution)/shard_map/all_to_all | solution.py:678
  147.8 3.3 %row_plan.5 = (f32[8,128]{1,0:T(8,128)S(1)}, f32[8,8,128]{2,1,0:T(8,128)S(1)}) custom-call(f32[32,8,128]{2,1,0:T(8,128)S(1)} %all_to_all.69.parts_ref, f32[8,128]{1,0:T(8,128)S(1)} %bitcast.9, f32[8,128]{1,0:T(8,128)S(1)} %get-tuple-element.82.base_dual_ref.dual_ref.dual_in_ref.col1, f32[8,128]{1,0:T(8,128)S(1)} %get-tuple-element.94.row_dual_ref.row1, ...), custom_call_target="tpu_custom_call" | custom-call | flops 1024 | bytes 1024 | tf_op jit(solution)/shard_map/row_plan/pallas_call | solution.py:662
  151.2 7.8 %all_to_all.70.parts_ref = f32[8,8,128]{2,1,0:T(8,128)S(1)} all-to-all(f32[8,8,128]{2,1,0:T(8,128)S(1)} %get-tuple-element.95), channel_id=1, replica_groups=mesh['rows'=32,'cols'=8] {'cols'}, dimensions={0} | all-to-all | bytes 65536 | tf_op jit(solution)/shard_map/all_to_all | solution.py:678
  159.0 7.6 %cost_grad.1 = (bf16[1024,1024]{1,0:T(8,128)(2,1)S(1)}, bf16[1024,1024]{1,0:T(8,128)(2,1)S(1)}, f32[8,128]{1,0:T(8,128)S(1)}, f32[136,512]{1,0:T(8,128)S(1)}, f3...) custom-call(f32[8,8,128]{2,1,0:T(8,128)S(1)} %all_to_all.70.parts_ref, ...), custom_call_target="tpu_custom_call" | custom-call | flops 1024 | bytes 1024 | tf_op jit(solution)/shard_map/cost_grad/pallas_call | solution.py:662
  166.6 1.4 collective-permute-start.3
  168.0 2.0 collective-permute-start.4
  169.9 0.6 collective-permute-start.1
  170.6 2.6 %collective-permute-start.2 = (f32[256,512]{1,0:T(8,128)S(1)}, f32[256,512]{1,0:T(8,128)S(1)}, u32[]{:S(2)}, u32[]{:S(2)}) collective-permute-start(f32[256,512]{1,0:T(8,128)S(1)} %get-tuple-element.106), channel_id=1, source_target_pairs={{0,192},{1,65},{8,200},{9,73},{16,208},{17,81},{24,216},{25,89},{3... | collective-permute-start | bytes 1572872 | tf_op jit(solution)/shard_map/ppermute | solution.py:797
  173.2 4.0 %grad_parts.1 = (f32[1024,512]{1,0:T(8,128)S(1)}, f32[1024,512]{1,0:T(8,128)S(1)}, f32[128,512]{1,0:T(8,128)S(1)}, f32[128,512]{1,0:T(8,128)S(1)}, f32[128,512]{...) custom-call(bf16[1024,1024]{1,0:T(8,128)(2,1)S(1)} %get-tuple-elemen, ...), custom_call_target="tpu_custom_call" | custom-call | flops 4294967296 | bytes 1024 | tf_op jit(solution)/shard_map/grad_parts/pallas_call | solution.py:662
  177.2 0.1 collective-permute-start
  177.3 0.0 collective-permute-done.3.up_ref
  177.3 0.0 collective-permute-done.4.down_ref
  177.3 0.1 z_second.1
  177.4 0.4 collective-permute-start.8
  177.7 3.2 %collective-permute-start.9 = (f32[136,512]{1,0:T(8,128)S(1)}, f32[136,512]{1,0:T(8,128)S(1)}, u32[]{:S(2)}, u32[]{:S(2)}) collective-permute-start(f32[136,512]{1,0:T(8,128)S(1)} %get-tuple-element.123), channel_id=1, source_target_pairs={{0,56},{1,9},{8,0},{9,17},{16,8},{17,25},{24,16},{25,33},{32,24},{... | collective-permute-start | bytes 835592 | tf_op jit(solution)/shard_map/ppermute | solution.py:797
  180.9 3.0 %collective-permute-done.1.up_ref = f32[256,512]{1,0:T(8,128)S(1)} collective-permute-done((f32[256,512]{1,0:T(8,128)S(1)}, f32[256,512]{1,0:T(8,128)S(1)}, u32[]{:S(2)}, u32[]{:S(2)}) %collective-permute-start.1) | collective-permute-done | bytes 524320 | tf_op jit(solution)/shard_map/ppermute | solution.py:797
  183.9 0.0 collective-permute-done.2.down_ref
  183.9 0.1 x_second.1
  184.0 0.1 collective-permute-start.7
  184.1 0.5 chip_sums.1
  184.6 0.6 collective-permute-start.5
  185.1 1.6 collective-permute-start.6
  186.7 1.3 collective-permute-done.8.up_ref
  188.0 0.1 z_third.1
  188.1 0.1 collective-permute-start.10
  188.2 3.2 %collective-permute-start.11 = (f32[136,512]{1,0:T(8,128)S(1)}, f32[136,512]{1,0:T(8,128)S(1)}, u32[]{:S(2)}, u32[]{:S(2)}) collective-permute-start(f32[136,512]{1,0:T(8,128)S(1)} %get-tuple-element.128), channel_id=1, source_target_pairs={{0,56},{1,9},{8,0},{9,17},{16,8},{17,25},{24,16},{25,33},{32,24},{... | collective-permute-start | bytes 835592 | tf_op jit(solution)/shard_map/ppermute | solution.py:797
  191.4 6.4 %collective-permute-done.10.up_ref = f32[136,512]{1,0:T(8,128)S(1)} collective-permute-done((f32[136,512]{1,0:T(8,128)S(1)}, f32[136,512]{1,0:T(8,128)S(1)}, u32[]{:S(2)}, u32[]{:S(2)}) %collective-permute-start.10) | collective-permute-done | bytes 278560 | tf_op jit(solution)/shard_map/ppermute | solution.py:797
  197.8 0.1 z_fourth.1
  197.9 0.1 collective-permute-start.12
  198.0 0.0 collective-permute-done.7.x_up_ref
  198.0 0.0 collective-permute-done.6.down_ref
  198.0 1.0 y_second.1
  199.0 4.5 %all-to-all-start.11 = ((f32[8,32,512]{2,1,0:T(8,128)}), f32[8,32,512]{2,1,0:T(8,128)S(1)}, u32[]{:S(2)}, u32[]{:S(2)}) async-start(f32[8,32,512]{2,1,0:T(8,128)} %bitcast.5), calls=%async_computation.11 | async-start | bytes 1048576 | tf_op jit(solution)/shard_map/all_to_all | solution.py:889
  203.5 0.5 collective-permute-start.16
  203.9 1.8 collective-permute-done.12.z_up_ref
  205.8 1.4 collective-permute-start.13
  207.2 2.4 %collective-permute-start.14 = (f32[40,512]{1,0:T(8,128)S(1)}, f32[40,512]{1,0:T(8,128)S(1)}, u32[]{:S(2)}, u32[]{:S(2)}) collective-permute-start(f32[40,512]{1,0:T(8,128)S(1)} %get-tuple-element.138), channel_id=1, source_target_pairs={{0,64},{1,193},{8,72},{9,201},{16,80},{17,209},{24,88},{25,217},{3... | collective-permute-start | bytes 245768 | tf_op jit(solution)/shard_map/ppermute | solution.py:797
  209.6 0.8 collective-permute-start.15
  210.4 2.4 %collective-permute-done.16.up_ref = f32[1024,128]{1,0:T(8,128)S(1)} collective-permute-done((f32[1024,128]{1,0:T(8,128)S(1)}, f32[1024,128]{1,0:T(8,128)S(1)}, u32[]{:S(2)}, u32[]{:S(2)}) %collective-permute-start.16) | collective-permute-done | bytes 524320 | tf_op jit(solution)/shard_map/ppermute | solution.py:797
  212.9 1.0 grad_x.1
  213.9 0.0 collective-permute-done.13.far_ref
  213.9 0.1 collective-permute-done.14.one_ref
  214.0 0.0 collective-permute-done.15.back_ref
  214.0 7.2 %all-to-all-done.11.parts_ref = f32[8,32,512]{2,1,0:T(8,128)S(1)} async-done(((f32[8,32,512]{2,1,0:T(8,128)}), f32[8,32,512]{2,1,0:T(8,128)S(1)}, u32[]{:S(2)}, u32[]{:S(2)}) %all-to-all-start.11) | async-done | bytes 524320 | tf_op jit(solution)/shard_map/all_to_all | solution.py:889
  221.2 0.7 last_step.1
  (14 shorter events, 0.1 us)
Async XLA Ops:
  77.6 16.7 %copy-start.1 = (f32[1024]{0:T(1024)S(1)}, f32[1024]{0:T(1024)}, u32[]{:S(2)}) copy-start(f32[1024]{0:T(1024)} %param.15) | copy-start | bytes 12292
  94.2 11.2 %copy-start.2 = (f32[1024]{0:T(1024)S(1)}, f32[1024]{0:T(1024)}, u32[]{:S(2)}) copy-start(f32[1024]{0:T(1024)} %param.14) | copy-start | bytes 12292
  147.8 11.1 %copy-start = (bf16[1024,1024]{1,0:T(8,128)(2,1)S(1)}, bf16[1024,1024]{1,0:T(8,128)(2,1)}, u32[]{:S(2)}) copy-start(bf16[1024,1024]{1,0:T(8,128)(2,1)} %emb_ref.1) | copy-start | bytes 6291460
  159.0 14.2 %copy-start.3 = (bf16[1024,1024]{1,0:T(8,128)(2,1)S(1)}, bf16[1024,1024]{1,0:T(8,128)(2,1)}, u32[]{:S(2)}) copy-start(bf16[1024,1024]{1,0:T(8,128)(2,1)} %tgt_ref.1) | copy-start | bytes 6291460
  166.6 10.6 %collective-permute-start.3 = (f32[136,512]{1,0:T(8,128)S(1)}, f32[136,512]{1,0:T(8,128)S(1)}, u32[]{:S(2)}, u32[]{:S(2)}) collective-permute-start(f32[136,512]{1,0:T(8,128)S(1)} %get-tuple-element.109), channel_id=1, source_target_pairs={{0,8},{1,57},{8,16},{9,1},{16,24},{17,9},{24,32},{25,17},{32,40},{... | collective-permute-start | bytes 835592 | tf_op jit(solution)/shard_map/ppermute | solution.py:797
  168.0 9.3 %collective-permute-start.4 = (f32[136,512]{1,0:T(8,128)S(1)}, f32[136,512]{1,0:T(8,128)S(1)}, u32[]{:S(2)}, u32[]{:S(2)}) collective-permute-start(f32[136,512]{1,0:T(8,128)S(1)} %get-tuple-element.110), channel_id=1, source_target_pairs={{0,56},{1,9},{8,0},{9,17},{16,8},{17,25},{24,16},{25,33},{32,24},{... | collective-permute-start | bytes 835592 | tf_op jit(solution)/shard_map/ppermute | solution.py:797
  169.9 13.9 %collective-permute-start.1 = (f32[256,512]{1,0:T(8,128)S(1)}, f32[256,512]{1,0:T(8,128)S(1)}, u32[]{:S(2)}, u32[]{:S(2)}) collective-permute-start(f32[256,512]{1,0:T(8,128)S(1)} %get-tuple-element.105), channel_id=1, source_target_pairs={{0,64},{1,193},{8,72},{9,201},{16,80},{17,209},{24,88},{25,217},{3... | collective-permute-start | bytes 1572872 | tf_op jit(solution)/shard_map/ppermute | solution.py:797
  170.6 13.3 %collective-permute-start.2 = (f32[256,512]{1,0:T(8,128)S(1)}, f32[256,512]{1,0:T(8,128)S(1)}, u32[]{:S(2)}, u32[]{:S(2)}) collective-permute-start(f32[256,512]{1,0:T(8,128)S(1)} %get-tuple-element.106), channel_id=1, source_target_pairs={{0,192},{1,65},{8,200},{9,73},{16,208},{17,81},{24,216},{25,89},{3... | collective-permute-start | bytes 1572872 | tf_op jit(solution)/shard_map/ppermute | solution.py:797
  177.2 6.9 %collective-permute-start = (f32[1024,512]{1,0:T(8,128)S(1)}, f32[1024,512]{1,0:T(8,128)S(1)}, u32[]{:S(2)}, u32[]{:S(2)}) collective-permute-start(f32[1024,512]{1,0:T(8,128)S(1)} %get-tuple-element.103), channel_id=1, source_target_pairs={{0,1},{1,0},{2,3},{3,2},{4,5},{5,4},{6,7},{7,6},{8,9},{9,8},{10,11... | collective-permute-start | bytes 6291464 | tf_op jit(solution)/shard_map/ppermute | solution.py:855
  177.4 10.6 %collective-permute-start.8 = (f32[136,512]{1,0:T(8,128)S(1)}, f32[136,512]{1,0:T(8,128)S(1)}, u32[]{:S(2)}, u32[]{:S(2)}) collective-permute-start(f32[136,512]{1,0:T(8,128)S(1)} %get-tuple-element.122), channel_id=1, source_target_pairs={{0,8},{1,57},{8,16},{9,1},{16,24},{17,9},{24,32},{25,17},{32,40},{... | collective-permute-start | bytes 835592 | tf_op jit(solution)/shard_map/ppermute | solution.py:797
  177.7 10.3 %collective-permute-start.9 = (f32[136,512]{1,0:T(8,128)S(1)}, f32[136,512]{1,0:T(8,128)S(1)}, u32[]{:S(2)}, u32[]{:S(2)}) collective-permute-start(f32[136,512]{1,0:T(8,128)S(1)} %get-tuple-element.123), channel_id=1, source_target_pairs={{0,56},{1,9},{8,0},{9,17},{16,8},{17,25},{24,16},{25,33},{32,24},{... | collective-permute-start | bytes 835592 | tf_op jit(solution)/shard_map/ppermute | solution.py:797
  184.0 14.0 %collective-permute-start.7 = (f32[256,512]{1,0:T(8,128)S(1)}, f32[256,512]{1,0:T(8,128)S(1)}, u32[]{:S(2)}, u32[]{:S(2)}) collective-permute-start(f32[256,512]{1,0:T(8,128)S(1)} %get-tuple-element.120), channel_id=1, source_target_pairs={{0,64},{1,193},{8,72},{9,201},{16,80},{17,209},{24,88},{25,217},{3... | collective-permute-start | bytes 1572872 | tf_op jit(solution)/shard_map/ppermute | solution.py:797
  184.6 13.4 %collective-permute-start.5 = (f32[1024,128]{1,0:T(8,128)S(1)}, f32[1024,128]{1,0:T(8,128)S(1)}, u32[]{:S(2)}, u32[]{:S(2)}) collective-permute-start(f32[1024,128]{1,0:T(8,128)S(1)} %get-tuple-element.116), channel_id=1, source_target_pairs={{0,2},{1,7},{8,10},{9,15},{16,18},{17,23},{24,26},{25,31},{32,34},... | collective-permute-start | bytes 1572872 | tf_op jit(solution)/shard_map/ppermute | solution.py:797
  185.1 12.9 %collective-permute-start.6 = (f32[1024,128]{1,0:T(8,128)S(1)}, f32[1024,128]{1,0:T(8,128)S(1)}, u32[]{:S(2)}, u32[]{:S(2)}) collective-permute-start(f32[1024,128]{1,0:T(8,128)S(1)} %get-tuple-element.117), channel_id=1, source_target_pairs={{0,6},{1,3},{8,14},{9,11},{16,22},{17,19},{24,30},{25,27},{32,38},... | collective-permute-start | bytes 1572872 | tf_op jit(solution)/shard_map/ppermute | solution.py:797
  188.1 9.7 %collective-permute-start.10 = (f32[136,512]{1,0:T(8,128)S(1)}, f32[136,512]{1,0:T(8,128)S(1)}, u32[]{:S(2)}, u32[]{:S(2)}) collective-permute-start(f32[136,512]{1,0:T(8,128)S(1)} %get-tuple-element.127), channel_id=1, source_target_pairs={{0,8},{1,57},{8,16},{9,1},{16,24},{17,9},{24,32},{25,17},{32,40},{... | collective-permute-start | bytes 835592 | tf_op jit(solution)/shard_map/ppermute | solution.py:797
  188.2 9.6 %collective-permute-start.11 = (f32[136,512]{1,0:T(8,128)S(1)}, f32[136,512]{1,0:T(8,128)S(1)}, u32[]{:S(2)}, u32[]{:S(2)}) collective-permute-start(f32[136,512]{1,0:T(8,128)S(1)} %get-tuple-element.128), channel_id=1, source_target_pairs={{0,56},{1,9},{8,0},{9,17},{16,8},{17,25},{24,16},{25,33},{32,24},{... | collective-permute-start | bytes 835592 | tf_op jit(solution)/shard_map/ppermute | solution.py:797
  197.9 7.8 %collective-permute-start.12 = (f32[136,512]{1,0:T(8,128)S(1)}, f32[136,512]{1,0:T(8,128)S(1)}, u32[]{:S(2)}, u32[]{:S(2)}) collective-permute-start(f32[136,512]{1,0:T(8,128)S(1)} %get-tuple-element.134), channel_id=1, source_target_pairs={{0,8},{1,57},{8,16},{9,1},{16,24},{17,9},{24,32},{25,17},{32,40},{... | collective-permute-start | bytes 835592 | tf_op jit(solution)/shard_map/ppermute | solution.py:797
  199.0 22.2 %all-to-all-start.11 = ((f32[8,32,512]{2,1,0:T(8,128)}), f32[8,32,512]{2,1,0:T(8,128)S(1)}, u32[]{:S(2)}, u32[]{:S(2)}) async-start(f32[8,32,512]{2,1,0:T(8,128)} %bitcast.5), calls=%async_computation.11 | async-start | bytes 1048576 | tf_op jit(solution)/shard_map/all_to_all | solution.py:889
  203.5 9.4 %collective-permute-start.16 = (f32[1024,128]{1,0:T(8,128)S(1)}, f32[1024,128]{1,0:T(8,128)S(1)}, u32[]{:S(2)}, u32[]{:S(2)}) collective-permute-start(f32[1024,128]{1,0:T(8,128)S(1)} %get-tuple-element.144), channel_id=1, source_target_pairs={{0,2},{1,7},{8,10},{9,15},{16,18},{17,23},{24,26},{25,31},{32,34},... | collective-permute-start | bytes 1572872 | tf_op jit(solution)/shard_map/ppermute | solution.py:797
  205.8 8.1 %collective-permute-start.13 = (f32[40,512]{1,0:T(8,128)S(1)}, f32[40,512]{1,0:T(8,128)S(1)}, u32[]{:S(2)}, u32[]{:S(2)}) collective-permute-start(f32[40,512]{1,0:T(8,128)S(1)} %get-tuple-element.137), channel_id=1, source_target_pairs={{0,128},{1,129},{8,136},{9,137},{16,144},{17,145},{24,152},{25,153... | collective-permute-start | bytes 245768 | tf_op jit(solution)/shard_map/ppermute | solution.py:797
  207.2 6.8 %collective-permute-start.14 = (f32[40,512]{1,0:T(8,128)S(1)}, f32[40,512]{1,0:T(8,128)S(1)}, u32[]{:S(2)}, u32[]{:S(2)}) collective-permute-start(f32[40,512]{1,0:T(8,128)S(1)} %get-tuple-element.138), channel_id=1, source_target_pairs={{0,64},{1,193},{8,72},{9,201},{16,80},{17,209},{24,88},{25,217},{3... | collective-permute-start | bytes 245768 | tf_op jit(solution)/shard_map/ppermute | solution.py:797
  209.6 4.4 %collective-permute-start.15 = (f32[40,512]{1,0:T(8,128)S(1)}, f32[40,512]{1,0:T(8,128)S(1)}, u32[]{:S(2)}, u32[]{:S(2)}) collective-permute-start(f32[40,512]{1,0:T(8,128)S(1)} %get-tuple-element.139), channel_id=1, source_target_pairs={{0,192},{1,65},{8,200},{9,73},{16,208},{17,81},{24,216},{25,89},{3... | collective-permute-start | bytes 245768 | tf_op jit(solution)/shard_map/ppermute | solution.py:797

commit v7 on v6

--- a/solution.py
+++ b/solution.py
@@ -536,32 +536,37 @@
     return ref[ref.shape[0] - 8 :, :LANES]
 
 
-def x_part(y_count, place_ref, grad_ref, tgt_ref, sent_ref, kept_ref, order_ref):
+def x_part(y_count, place_ref, grad_ref, tgt_ref, side, out_ref, order_ref):
     block = tgt_ref.shape[1] // (2 * y_count)
     core, turn = place_ref[3], direction(place_ref)
-    for side, out_ref in ((0, sent_ref), (1, kept_ref)):
-        for k, offset in enumerate((2, 1, -1, 0)):
-            step = offset * (2 * side - 1)
-            at = lax.rem(place_ref[1] + turn * step + y_count, y_count)
-            owner = at * 2 + (core if side else 1 - core)
-            order_ref[:, k * block : (k + 1) * block] = tgt_ref[
-                :, pl.ds(pl.multiple_of(owner * block, block), block)
-            ]
-        out_ref[...] = jnp.dot(grad_ref[...], order_ref[...], preferred_element_type=F32)
-
-
-def parts_kernel(
-    counts, y_count, grad_ref, src_ref, tgt_ref, sent_ref, kept_ref, *outs
-):
+    for k, offset in enumerate((2, 1, -1, 0)):
+        step = offset * (2 * side - 1)
+        at = lax.rem(place_ref[1] + turn * step + y_count, y_count)
+        owner = at * 2 + (core if side else 1 - core)
+        order_ref[:, k * block : (k + 1) * block] = tgt_ref[
+            :, pl.ds(pl.multiple_of(owner * block, block), block)
+        ]
+    out_ref[...] = jnp.dot(grad_ref[...], order_ref[...], preferred_element_type=F32)
+
+
+def first_parts_kernel(counts, y_count, grad_ref, src_ref, tgt_ref, *outs):
+    sent_ref, z_ref, z_back_ref, one_ref, own_ref, order_ref = outs
     place_ref = place_of(counts)
+    reach = counts[1] // 2
+    z_ref[...] = z_block(place_ref, src_ref, grad_ref, reach - 1, counts)
+    z_back_ref[...] = z_block(place_ref, src_ref, grad_ref, 2 - reach, counts)
+    for out_ref, offset in ((one_ref, 1), (own_ref, 0)):
+        out_ref[...] = x_block(place_ref, src_ref, grad_ref, offset, counts)
+    x_part(y_count, place_ref, grad_ref, tgt_ref, 0, sent_ref, order_ref)
+
+
+def other_parts_kernel(counts, y_count, grad_ref, src_ref, tgt_ref, after_ref, kept_ref, *outs):
     *outs, order_ref = outs
-    x_part(y_count, place_ref, grad_ref, tgt_ref, sent_ref, kept_ref, order_ref)
+    place_ref = place_of(counts)
+    x_part(y_count, place_ref, grad_ref, tgt_ref, 1, kept_ref, order_ref)
     reach = counts[1] // 2
-    offsets = [*range(reach - 1, 0, -1), *range(2 - reach, 1)]
-    for out_ref, offset in zip(outs, offsets):
+    for out_ref, offset in zip(outs, [*range(reach - 2, 0, -1), *range(3 - reach, 1)]):
         out_ref[...] = z_block(place_ref, src_ref, grad_ref, offset, counts)
-    for out_ref, offset in zip(outs[len(offsets) :], (1, 0)):
-        out_ref[...] = x_block(place_ref, src_ref, grad_ref, offset, counts)
 
 
 def forward(out_ref, block_ref, arrived_ref):
@@ -822,16 +827,16 @@
     z_up, z_down = turn(z_far, 2, 1), turn(z_back, 2, -1)
     x_up, x_down = turn(x_far, 0, 1), turn(x_back, 0, -1)
     chip_part = array((src_rows, width // 2))
-    outs = call(
-        functools.partial(parts_kernel, counts, y_count),
+    order = [pltpu.VMEM((tgt_cols, width // 2), jnp.bfloat16)]
+    sent, z_3, z_back2, x_one, x_own = call(
+        functools.partial(first_parts_kernel, counts, y_count),
         (rounded, src_turned, tgt_emb),
-        [chip_part] * 2 + [z_shape] * (z_count - 2) + [x_shape] * 2,
-        [pltpu.VMEM((tgt_cols, width // 2), jnp.bfloat16)],
+        [chip_part, z_shape, z_shape, x_shape, x_shape],
+        order,
         free=(2,),
         flops=BIG,
-        name="grad_parts",
-    )
-    sent, kept, z_3, z_2, z_1, z_back2, z_back1, z_own, x_one, x_own = outs
+        name="first_parts",
+    )
     small = array((8, LANES))
 
     def step(kernel, arguments, outs, name, last=False, flops=STEP):
@@ -847,14 +852,24 @@
 
     z_pay, z_back, start = step(
         z_kernel,
-        (z_up, z_down, z_3, z_back2, start, kept),
+        (z_up, z_down, z_3, z_back2, start, sent),
         [z_riding, z_riding, small],
         "z_second",
     )
     z_up, z_down = turn(z_pay, 2, 1), turn(z_back, 2, -1)
     arrived = lax.ppermute(sent, "cols", [(at, at ^ 1) for at in range(col_count)])
+    kept, z_2, z_1, z_back1, z_own = call(
+        functools.partial(other_parts_kernel, counts, y_count),
+        (rounded, src_turned, tgt_emb, start),
+        [chip_part] + [z_shape] * 4,
+        order,
+        free=(2,),
+        loose=(3,),
+        flops=BIG,
+        name="other_parts",
+    )
     x_pay, x_sum, mark = step(
-        x_kernel, (x_up, x_down, x_one, x_own, start), [x_shape, x_shape, small], "x_second",
+        x_kernel, (x_up, x_down, x_one, x_own, z_own), [x_shape, x_shape, small], "x_second",
         flops=2**34
     )
     x_up = turn(x_pay, 0, 1)

time: 225 us -> 225 us (level)
  waiting for transfers between devices: 22.3 us -> 19.4 us
  starting transfers between devices: 25.3 us -> 28.2 us
    all_to_all x1, waiting for transfers between devices: 7.2 us -> 4.15 us  [body(): lax.all_to_all(first.reshape(z_count, owned, half), 'rows', 0, 0, tiled=T...]
    ppermute x16, starting transfers between devices: 20.8 us -> 23.2 us  [turn(): return lax.ppermute(value, ('rows', 'cols'), moves)]
    pallas_call x22 -> x23, Pallas kernels: 48.9 us -> 49 us  [call(): pl.pallas_call(kernel, out_shape=[pltpu.VMEM(out.shape, out.dtype) if mat...]
  transfers between devices with their start and end apart: 18 -> 18, of which waited for: 7 -> 9; matrix products, arithmetic and copies ran while one was open for 0% -> 0% of each run, Pallas kernels for 3% -> 3%
where the time goes in v7:
time: 225 us; the launch traced here: 222 us
  blocking collectives  125 us (56%)
  Pallas kernels  49 us (22%)
  starting transfers between devices  28.2 us (13%)
  waiting for transfers between devices  19.4 us (9%)
    all_to_all x11, blocking collectives, exchanged(): return lax.all_to_all(copies, axis, 0, 0, tiled=True)  125 us
    pallas_call x23, Pallas kernels, call(): pl.pallas_call(kernel, out_shape=[pltpu.VMEM(out.shape, out.dtype) if mat...  49 us
    ppermute x16, starting transfers between devices, turn(): return lax.ppermute(value, ('rows', 'cols'), moves)  23.2 us
    ppermute x16, waiting for transfers between devices, turn(): return lax.ppermute(value, ('rows', 'cols'), moves)  15.2 us
    all_to_all x1, starting transfers between devices, body(): lax.all_to_all(first.reshape(z_count, owned, half), 'rows', 0, 0, tiled=T...  4.83 us
  transfers between devices with their start and end apart: 18, of which 9 were waited for; matrix products, arithmetic and copies ran while one was open for 0% of the time, Pallas kernels for 3%

profile of v7, /device:TPU:8, one launch (start us, length us, event | category | flops | bytes accessed | tf_op | source)
XLA Modules:
  0.0 221.9 jit_solution(8392103997972368180)
XLA Ops:
  0.6 4.9 %first_row_logs.1 = (f32[1024,1024]{1,0:T(8,128)S(1)}, f32[1024,1024]{1,0:T(8,128)S(1)}, f32[8,128]{1,0:T(8,128)S(1)}, f32[8,8,128]{2,1,0:T(8,128)S(1)}) custom-call(bf16[1024,1024]{1,0:T(8,128)(2,1)} %cost_hbm.1, s32[8,128]{1,0:T(8,128)} %bitcast.12, s32[8,128]{1,0:T(8,128)} %bitcast.13, s32[64,64]{1,0:T(8,128)} %mask_hbm.1, f32[8,128]{1,0:T(8,128)} %bitcast.14), custom_call_target="tpu_custom_call" | custom-call | flops 1024 | bytes 1024 | tf_op jit(solution)/shard_map/first_row_logs/pallas_call | solution.py:667
  5.6 8.7 %all_to_all.60.parts_ref = f32[8,8,128]{2,1,0:T(8,128)S(1)} all-to-all(f32[8,8,128]{2,1,0:T(8,128)S(1)} %get-tuple-element.75), channel_id=1, replica_groups=mesh['rows'=32,'cols'=8] {'cols'}, dimensions={0} | all-to-all | bytes 65536 | tf_op jit(solution)/shard_map/all_to_all | solution.py:683
  14.3 2.9 %col_logs.3 = (f32[8,128]{1,0:T(8,128)S(1)}, f32[32,8,128]{2,1,0:T(8,128)S(1)}) custom-call(f32[8,8,128]{2,1,0:T(8,128)S(1)} %all_to_all.60.parts_ref, f32[8,128]{1,0:T(8,128)S(1)} %get-tuple-element.76.top_ref.start_top_ref, f32[8,128]{1,0:T(8,128)S(1)} %broadcast_1_base_dual_ref_outer_ref.2.base_dual_ref.outer_ref, ...), custom_call_target="tpu_custom_call" | custom-call | flops 1024 | bytes 1024 | tf_op jit(solution)/shard_map/col_logs/pallas_call | solution.py:667
  17.2 21.4 %all_to_all.61.parts_ref = f32[32,8,128]{2,1,0:T(8,128)S(1)} all-to-all(f32[32,8,128]{2,1,0:T(8,128)S(1)} %get-tuple-element.79), channel_id=1, replica_groups=mesh['rows'=32,'cols'=8] {'rows'}, dimensions={0} | all-to-all | bytes 262144 | tf_op jit(solution)/shard_map/all_to_all | solution.py:683
  38.5 3.4 %second_row_logs.1 = (f32[1024,1024]{1,0:T(8,128)S(1)}, f32[8,128]{1,0:T(8,128)S(1)}, f32[8,128]{1,0:T(8,128)S(1)}, f32[8,8,128]{2,1,0:T(8,128)S(1)}) custom-call(f32[32,8,128]{2,1,0:T(8,128)S(1)} %all_to_all.61.parts_ref, f32[8,128]{1,0:T(8,128)S(1)} %get-tuple-element.76.top_ref.start_top_ref, f32[1024,1024]{1,0:T(8,128)S(1)} %get-tuple-element.77.base_ref.start_base_ref, ...), custom_call_target="tpu_custom_call" | custom-call | flops 1024 | bytes 1024 | tf_op jit(solution)/shard_map/second_row_logs/pallas_call | solution.py:667
  41.9 7.8 %all_to_all.62.parts_ref = f32[8,8,128]{2,1,0:T(8,128)S(1)} all-to-all(f32[8,8,128]{2,1,0:T(8,128)S(1)} %get-tuple-element.80), channel_id=1, replica_groups=mesh['rows'=32,'cols'=8] {'cols'}, dimensions={0} | all-to-all | bytes 65536 | tf_op jit(solution)/shard_map/all_to_all | solution.py:683
  49.7 2.8 %col_logs.4 = (f32[8,128]{1,0:T(8,128)S(1)}, f32[32,8,128]{2,1,0:T(8,128)S(1)}) custom-call(f32[8,8,128]{2,1,0:T(8,128)S(1)} %all_to_all.62.parts_ref, f32[8,128]{1,0:T(8,128)S(1)} %get-tuple-element.81.top_ref, f32[8,128]{1,0:T(8,128)S(1)} %get-tuple-element.82.base_dual_ref.dual_ref.dual_in_ref.col1, f32[1024,1024]{1,0:T(8,128)S(1)} %get-tuple-element.83.base_ref, ...), custom_call_target="tpu_custom_call" | custom-call | flops 1024 | bytes 1024 | tf_op jit(solution)/shard_map/col_logs/pallas_call | solution.py:667
  52.6 13.9 %all_to_all.63.parts_ref = f32[32,8,128]{2,1,0:T(8,128)S(1)} all-to-all(f32[32,8,128]{2,1,0:T(8,128)S(1)} %get-tuple-element.84), channel_id=1, replica_groups=mesh['rows'=32,'cols'=8] {'rows'}, dimensions={0} | all-to-all | bytes 262144 | tf_op jit(solution)/shard_map/all_to_all | solution.py:683
  66.4 3.3 %third_row_logs.1 = (f32[8,128]{1,0:T(8,128)S(1)}, f32[8,8,128]{2,1,0:T(8,128)S(1)}) custom-call(f32[32,8,128]{2,1,0:T(8,128)S(1)} %all_to_all.63.parts_ref, f32[8,128]{1,0:T(8,128)S(1)} %get-tuple-element.81.top_ref, f32[8,128]{1,0:T(8,128)S(1)} %get-tuple-element.82.base_dual_ref.dual_ref.dual_in_ref.col1, f32[1024,1024]{1,0:T(8,128)S(1)} %get-tuple-element.83.base_ref, ...), custom_call_target="tpu_custom_call" | custom-call | flops 1024 | bytes 1024 | tf_op jit(solution)/shard_map/third_row_logs/pallas_call | solution.py:667
  69.8 7.8 %all_to_all.64.parts_ref = f32[8,8,128]{2,1,0:T(8,128)S(1)} all-to-all(f32[8,8,128]{2,1,0:T(8,128)S(1)} %get-tuple-element.85), channel_id=1, replica_groups=mesh['rows'=32,'cols'=8] {'cols'}, dimensions={0} | all-to-all | bytes 65536 | tf_op jit(solution)/shard_map/all_to_all | solution.py:683
  77.6 2.8 %col_logs.5 = (f32[8,128]{1,0:T(8,128)S(1)}, f32[32,8,128]{2,1,0:T(8,128)S(1)}) custom-call(f32[8,8,128]{2,1,0:T(8,128)S(1)} %all_to_all.64.parts_ref, f32[8,128]{1,0:T(8,128)S(1)} %get-tuple-element.81.top_ref, f32[8,128]{1,0:T(8,128)S(1)} %get-tuple-element.82.base_dual_ref.dual_ref.dual_in_ref.col1, f32[1024,1024]{1,0:T(8,128)S(1)} %get-tuple-element.83.base_ref, ...), custom_call_target="tpu_custom_call" | custom-call | flops 1024 | bytes 1024 | tf_op jit(solution)/shard_map/col_logs/pallas_call | solution.py:667
  80.4 13.9 %all_to_all.65.parts_ref = f32[32,8,128]{2,1,0:T(8,128)S(1)} all-to-all(f32[32,8,128]{2,1,0:T(8,128)S(1)} %get-tuple-element.86), channel_id=1, replica_groups=mesh['rows'=32,'cols'=8] {'rows'}, dimensions={0} | all-to-all | bytes 262144 | tf_op jit(solution)/shard_map/all_to_all | solution.py:683
  94.2 3.4 %row_plan.3 = (f32[8,128]{1,0:T(8,128)S(1)}, f32[8,8,128]{2,1,0:T(8,128)S(1)}) custom-call(f32[32,8,128]{2,1,0:T(8,128)S(1)} %all_to_all.65.parts_ref, f32[8,128]{1,0:T(8,128)S(1)} %bitcast.7, f32[8,128]{1,0:T(8,128)S(1)} %get-tuple-element.87.dual_in_ref.dual_ref.col2, f32[8,128]{1,0:T(8,128)S(1)} %get-tuple-element.88.row_dual_ref.row3, ...), custom_call_target="tpu_custom_call" | custom-call | flops 1024 | bytes 1024 | tf_op jit(solution)/shard_map/row_plan/pallas_call | solution.py:667
  97.6 7.8 %all_to_all.66.parts_ref = f32[8,8,128]{2,1,0:T(8,128)S(1)} all-to-all(f32[8,8,128]{2,1,0:T(8,128)S(1)} %get-tuple-element.89), channel_id=1, replica_groups=mesh['rows'=32,'cols'=8] {'cols'}, dimensions={0} | all-to-all | bytes 65536 | tf_op jit(solution)/shard_map/all_to_all | solution.py:683
  105.4 1.8 col_plan.2
  107.2 13.9 %all_to_all.67.parts_ref = f32[32,8,128]{2,1,0:T(8,128)S(1)} all-to-all(f32[32,8,128]{2,1,0:T(8,128)S(1)} %get-tuple-element.90), channel_id=1, replica_groups=mesh['rows'=32,'cols'=8] {'rows'}, dimensions={0} | all-to-all | bytes 262144 | tf_op jit(solution)/shard_map/all_to_all | solution.py:683
  121.1 3.3 %row_plan.4 = (f32[8,128]{1,0:T(8,128)S(1)}, f32[8,8,128]{2,1,0:T(8,128)S(1)}) custom-call(f32[32,8,128]{2,1,0:T(8,128)S(1)} %all_to_all.67.parts_ref, f32[8,128]{1,0:T(8,128)S(1)} %bitcast.8, f32[8,128]{1,0:T(8,128)S(1)} %get-tuple-element.87.dual_in_ref.dual_ref.col2, f32[8,128]{1,0:T(8,128)S(1)} %get-tuple-element.91.row_dual_ref.row2, ...), custom_call_target="tpu_custom_call" | custom-call | flops 1024 | bytes 1024 | tf_op jit(solution)/shard_map/row_plan/pallas_call | solution.py:667
  124.4 7.8 %all_to_all.68.parts_ref = f32[8,8,128]{2,1,0:T(8,128)S(1)} all-to-all(f32[8,8,128]{2,1,0:T(8,128)S(1)} %get-tuple-element.92), channel_id=1, replica_groups=mesh['rows'=32,'cols'=8] {'cols'}, dimensions={0} | all-to-all | bytes 65536 | tf_op jit(solution)/shard_map/all_to_all | solution.py:683
  132.2 1.8 col_plan.3
  134.0 13.9 %all_to_all.69.parts_ref = f32[32,8,128]{2,1,0:T(8,128)S(1)} all-to-all(f32[32,8,128]{2,1,0:T(8,128)S(1)} %get-tuple-element.93), channel_id=1, replica_groups=mesh['rows'=32,'cols'=8] {'rows'}, dimensions={0} | all-to-all | bytes 262144 | tf_op jit(solution)/shard_map/all_to_all | solution.py:683
  147.8 3.3 %row_plan.5 = (f32[8,128]{1,0:T(8,128)S(1)}, f32[8,8,128]{2,1,0:T(8,128)S(1)}) custom-call(f32[32,8,128]{2,1,0:T(8,128)S(1)} %all_to_all.69.parts_ref, f32[8,128]{1,0:T(8,128)S(1)} %bitcast.9, f32[8,128]{1,0:T(8,128)S(1)} %get-tuple-element.82.base_dual_ref.dual_ref.dual_in_ref.col1, f32[8,128]{1,0:T(8,128)S(1)} %get-tuple-element.94.row_dual_ref.row1, ...), custom_call_target="tpu_custom_call" | custom-call | flops 1024 | bytes 1024 | tf_op jit(solution)/shard_map/row_plan/pallas_call | solution.py:667
  151.2 7.8 %all_to_all.70.parts_ref = f32[8,8,128]{2,1,0:T(8,128)S(1)} all-to-all(f32[8,8,128]{2,1,0:T(8,128)S(1)} %get-tuple-element.95), channel_id=1, replica_groups=mesh['rows'=32,'cols'=8] {'cols'}, dimensions={0} | all-to-all | bytes 65536 | tf_op jit(solution)/shard_map/all_to_all | solution.py:683
  159.0 7.6 %cost_grad.1 = (bf16[1024,1024]{1,0:T(8,128)(2,1)S(1)}, bf16[1024,1024]{1,0:T(8,128)(2,1)S(1)}, f32[8,128]{1,0:T(8,128)S(1)}, f32[136,512]{1,0:T(8,128)S(1)}, f3...) custom-call(f32[8,8,128]{2,1,0:T(8,128)S(1)} %all_to_all.70.parts_ref, ...), custom_call_target="tpu_custom_call" | custom-call | flops 1024 | bytes 1024 | tf_op jit(solution)/shard_map/cost_grad/pallas_call | solution.py:667
  166.6 1.4 collective-permute-start.1
  168.0 2.0 collective-permute-start.2
  169.9 0.6 collective-permute-start.3
  170.6 2.6 %collective-permute-start.4 = (f32[256,512]{1,0:T(8,128)S(1)}, f32[256,512]{1,0:T(8,128)S(1)}, u32[]{:S(2)}, u32[]{:S(2)}) collective-permute-start(f32[256,512]{1,0:T(8,128)S(1)} %get-tuple-element.112), channel_id=1, source_target_pairs={{0,192},{1,65},{8,200},{9,73},{16,208},{17,81},{24,216},{25,89},{3... | collective-permute-start | bytes 1572872 | tf_op jit(solution)/shard_map/ppermute | solution.py:802
  173.2 2.2 first_parts.1
  175.4 0.1 collective-permute-start
  175.5 0.9 collective-permute-done.1.up_ref
  176.4 0.0 collective-permute-done.2.down_ref
  176.4 0.1 z_second.1
  176.5 0.5 collective-permute-start.8
  176.9 2.9 %collective-permute-start.9 = (f32[136,512]{1,0:T(8,128)S(1)}, f32[136,512]{1,0:T(8,128)S(1)}, u32[]{:S(2)}, u32[]{:S(2)}) collective-permute-start(f32[136,512]{1,0:T(8,128)S(1)} %get-tuple-element.124), channel_id=1, source_target_pairs={{0,56},{1,9},{8,0},{9,17},{16,8},{17,25},{24,16},{25,33},{32,24},{... | collective-permute-start | bytes 835592 | tf_op jit(solution)/shard_map/ppermute | solution.py:802
  179.8 2.0 other_parts.1
  181.7 2.1 collective-permute-done.3.up_ref
  183.9 0.1 x_second.1
  184.0 0.1 collective-permute-start.7
  184.1 0.0 collective-permute-done.arrived_ref
  184.1 0.5 chip_sums.1
  184.6 0.6 collective-permute-start.5
  185.1 1.5 collective-permute-start.6
  186.7 0.0 collective-permute-done.8.up_ref
  186.7 0.1 z_third.1
  186.7 1.3 collective-permute-start.10
  188.1 2.0 collective-permute-start.11
  190.1 7.2 %collective-permute-done.10.up_ref = f32[136,512]{1,0:T(8,128)S(1)} collective-permute-done((f32[136,512]{1,0:T(8,128)S(1)}, f32[136,512]{1,0:T(8,128)S(1)}, u32[]{:S(2)}, u32[]{:S(2)}) %collective-permute-start.10) | collective-permute-done | bytes 278560 | tf_op jit(solution)/shard_map/ppermute | solution.py:802
  197.3 0.0 collective-permute-done.11.down_ref
  197.3 0.1 z_fourth.1
  197.4 0.1 collective-permute-start.12
  197.5 0.2 collective-permute-done.5.up_ref
  197.6 0.0 collective-permute-done.6.down_ref
  197.6 1.0 y_second.1
  198.6 4.8 %all-to-all-start.11 = ((f32[8,32,512]{2,1,0:T(8,128)}), f32[8,32,512]{2,1,0:T(8,128)S(1)}, u32[]{:S(2)}, u32[]{:S(2)}) async-start(f32[8,32,512]{2,1,0:T(8,128)} %bitcast.5), calls=%async_computation.11 | async-start | bytes 1048576 | tf_op jit(solution)/shard_map/all_to_all | solution.py:904
  203.4 0.4 collective-permute-start.16
  203.8 1.3 collective-permute-done.12.z_up_ref
  205.2 1.5 collective-permute-start.13
  206.8 5.8 %collective-permute-start.14 = (f32[40,512]{1,0:T(8,128)S(1)}, f32[40,512]{1,0:T(8,128)S(1)}, u32[]{:S(2)}, u32[]{:S(2)}) collective-permute-start(f32[40,512]{1,0:T(8,128)S(1)} %get-tuple-element.138), channel_id=1, source_target_pairs={{0,64},{1,193},{8,72},{9,201},{16,80},{17,209},{24,88},{25,217},{3... | collective-permute-start | bytes 245768 | tf_op jit(solution)/shard_map/ppermute | solution.py:802
  212.6 0.4 collective-permute-done.16.up_ref
  213.0 1.0 grad_x.1
  214.0 0.6 collective-permute-done.14.one_ref
  214.7 2.4 %collective-permute-done.15.back_ref = f32[40,512]{1,0:T(8,128)S(1)} collective-permute-done((f32[40,512]{1,0:T(8,128)S(1)}, f32[40,512]{1,0:T(8,128)S(1)}, u32[]{:S(2)}, u32[]{:S(2)}) %collective-permute-start.15) | collective-permute-done | bytes 81952 | tf_op jit(solution)/shard_map/ppermute | solution.py:802
  217.0 4.1 %all-to-all-done.11.parts_ref = f32[8,32,512]{2,1,0:T(8,128)S(1)} async-done(((f32[8,32,512]{2,1,0:T(8,128)}), f32[8,32,512]{2,1,0:T(8,128)S(1)}, u32[]{:S(2)}, u32[]{:S(2)}) %all-to-all-start.11) | async-done | bytes 524320 | tf_op jit(solution)/shard_map/all_to_all | solution.py:904
  221.2 0.7 last_step.1
  (15 shorter events, 0.1 us)
Async XLA Ops:
  77.6 16.7 %copy-start.1 = (f32[1024]{0:T(1024)S(1)}, f32[1024]{0:T(1024)}, u32[]{:S(2)}) copy-start(f32[1024]{0:T(1024)} %param.15) | copy-start | bytes 12292
  94.2 11.2 %copy-start.2 = (f32[1024]{0:T(1024)S(1)}, f32[1024]{0:T(1024)}, u32[]{:S(2)}) copy-start(f32[1024]{0:T(1024)} %param.14) | copy-start | bytes 12292
  147.8 11.1 %copy-start = (bf16[1024,1024]{1,0:T(8,128)(2,1)S(1)}, bf16[1024,1024]{1,0:T(8,128)(2,1)}, u32[]{:S(2)}) copy-start(bf16[1024,1024]{1,0:T(8,128)(2,1)} %emb_ref.1) | copy-start | bytes 6291460
  159.0 14.2 %copy-start.3 = (bf16[1024,1024]{1,0:T(8,128)(2,1)S(1)}, bf16[1024,1024]{1,0:T(8,128)(2,1)}, u32[]{:S(2)}) copy-start(bf16[1024,1024]{1,0:T(8,128)(2,1)} %tgt_ref.3) | copy-start | bytes 6291460
  166.6 9.8 %collective-permute-start.1 = (f32[136,512]{1,0:T(8,128)S(1)}, f32[136,512]{1,0:T(8,128)S(1)}, u32[]{:S(2)}, u32[]{:S(2)}) collective-permute-start(f32[136,512]{1,0:T(8,128)S(1)} %get-tuple-element.104), channel_id=1, source_target_pairs={{0,8},{1,57},{8,16},{9,1},{16,24},{17,9},{24,32},{25,17},{32,40},{... | collective-permute-start | bytes 835592 | tf_op jit(solution)/shard_map/ppermute | solution.py:802
  168.0 8.4 %collective-permute-start.2 = (f32[136,512]{1,0:T(8,128)S(1)}, f32[136,512]{1,0:T(8,128)S(1)}, u32[]{:S(2)}, u32[]{:S(2)}) collective-permute-start(f32[136,512]{1,0:T(8,128)S(1)} %get-tuple-element.105), channel_id=1, source_target_pairs={{0,56},{1,9},{8,0},{9,17},{16,8},{17,25},{24,16},{25,33},{32,24},{... | collective-permute-start | bytes 835592 | tf_op jit(solution)/shard_map/ppermute | solution.py:802
  169.9 13.9 %collective-permute-start.3 = (f32[256,512]{1,0:T(8,128)S(1)}, f32[256,512]{1,0:T(8,128)S(1)}, u32[]{:S(2)}, u32[]{:S(2)}) collective-permute-start(f32[256,512]{1,0:T(8,128)S(1)} %get-tuple-element.111), channel_id=1, source_target_pairs={{0,64},{1,193},{8,72},{9,201},{16,80},{17,209},{24,88},{25,217},{3... | collective-permute-start | bytes 1572872 | tf_op jit(solution)/shard_map/ppermute | solution.py:802
  170.6 13.3 %collective-permute-start.4 = (f32[256,512]{1,0:T(8,128)S(1)}, f32[256,512]{1,0:T(8,128)S(1)}, u32[]{:S(2)}, u32[]{:S(2)}) collective-permute-start(f32[256,512]{1,0:T(8,128)S(1)} %get-tuple-element.112), channel_id=1, source_target_pairs={{0,192},{1,65},{8,200},{9,73},{16,208},{17,81},{24,216},{25,89},{3... | collective-permute-start | bytes 1572872 | tf_op jit(solution)/shard_map/ppermute | solution.py:802
  175.4 8.7 %collective-permute-start = (f32[1024,512]{1,0:T(8,128)S(1)}, f32[1024,512]{1,0:T(8,128)S(1)}, u32[]{:S(2)}, u32[]{:S(2)}) collective-permute-start(f32[1024,512]{1,0:T(8,128)S(1)} %get-tuple-element.103.after_ref), channel_id=1, source_target_pairs={{0,1},{1,0},{2,3},{3,2},{4,5},{5,4},{6,7},{7,6},{8,9},{9,8},{10,11... | collective-permute-start | bytes 6291464 | tf_op jit(solution)/shard_map/ppermute | solution.py:860
  176.5 10.2 %collective-permute-start.8 = (f32[136,512]{1,0:T(8,128)S(1)}, f32[136,512]{1,0:T(8,128)S(1)}, u32[]{:S(2)}, u32[]{:S(2)}) collective-permute-start(f32[136,512]{1,0:T(8,128)S(1)} %get-tuple-element.123), channel_id=1, source_target_pairs={{0,8},{1,57},{8,16},{9,1},{16,24},{17,9},{24,32},{25,17},{32,40},{... | collective-permute-start | bytes 835592 | tf_op jit(solution)/shard_map/ppermute | solution.py:802
  176.9 9.7 %collective-permute-start.9 = (f32[136,512]{1,0:T(8,128)S(1)}, f32[136,512]{1,0:T(8,128)S(1)}, u32[]{:S(2)}, u32[]{:S(2)}) collective-permute-start(f32[136,512]{1,0:T(8,128)S(1)} %get-tuple-element.124), channel_id=1, source_target_pairs={{0,56},{1,9},{8,0},{9,17},{16,8},{17,25},{24,16},{25,33},{32,24},{... | collective-permute-start | bytes 835592 | tf_op jit(solution)/shard_map/ppermute | solution.py:802
  184.0 13.5 %collective-permute-start.7 = (f32[256,512]{1,0:T(8,128)S(1)}, f32[256,512]{1,0:T(8,128)S(1)}, u32[]{:S(2)}, u32[]{:S(2)}) collective-permute-start(f32[256,512]{1,0:T(8,128)S(1)} %get-tuple-element.121), channel_id=1, source_target_pairs={{0,64},{1,193},{8,72},{9,201},{16,80},{17,209},{24,88},{25,217},{3... | collective-permute-start | bytes 1572872 | tf_op jit(solution)/shard_map/ppermute | solution.py:802
  184.6 13.1 %collective-permute-start.5 = (f32[1024,128]{1,0:T(8,128)S(1)}, f32[1024,128]{1,0:T(8,128)S(1)}, u32[]{:S(2)}, u32[]{:S(2)}) collective-permute-start(f32[1024,128]{1,0:T(8,128)S(1)} %get-tuple-element.117), channel_id=1, source_target_pairs={{0,2},{1,7},{8,10},{9,15},{16,18},{17,23},{24,26},{25,31},{32,34},... | collective-permute-start | bytes 1572872 | tf_op jit(solution)/shard_map/ppermute | solution.py:802
  185.1 12.5 %collective-permute-start.6 = (f32[1024,128]{1,0:T(8,128)S(1)}, f32[1024,128]{1,0:T(8,128)S(1)}, u32[]{:S(2)}, u32[]{:S(2)}) collective-permute-start(f32[1024,128]{1,0:T(8,128)S(1)} %get-tuple-element.118), channel_id=1, source_target_pairs={{0,6},{1,3},{8,14},{9,11},{16,22},{17,19},{24,30},{25,27},{32,38},... | collective-permute-start | bytes 1572872 | tf_op jit(solution)/shard_map/ppermute | solution.py:802
  186.7 10.5 %collective-permute-start.10 = (f32[136,512]{1,0:T(8,128)S(1)}, f32[136,512]{1,0:T(8,128)S(1)}, u32[]{:S(2)}, u32[]{:S(2)}) collective-permute-start(f32[136,512]{1,0:T(8,128)S(1)} %get-tuple-element.128), channel_id=1, source_target_pairs={{0,8},{1,57},{8,16},{9,1},{16,24},{17,9},{24,32},{25,17},{32,40},{... | collective-permute-start | bytes 835592 | tf_op jit(solution)/shard_map/ppermute | solution.py:802
  188.1 9.2 %collective-permute-start.11 = (f32[136,512]{1,0:T(8,128)S(1)}, f32[136,512]{1,0:T(8,128)S(1)}, u32[]{:S(2)}, u32[]{:S(2)}) collective-permute-start(f32[136,512]{1,0:T(8,128)S(1)} %get-tuple-element.129), channel_id=1, source_target_pairs={{0,56},{1,9},{8,0},{9,17},{16,8},{17,25},{24,16},{25,33},{32,24},{... | collective-permute-start | bytes 835592 | tf_op jit(solution)/shard_map/ppermute | solution.py:802
  197.4 7.8 %collective-permute-start.12 = (f32[136,512]{1,0:T(8,128)S(1)}, f32[136,512]{1,0:T(8,128)S(1)}, u32[]{:S(2)}, u32[]{:S(2)}) collective-permute-start(f32[136,512]{1,0:T(8,128)S(1)} %get-tuple-element.134), channel_id=1, source_target_pairs={{0,8},{1,57},{8,16},{9,1},{16,24},{17,9},{24,32},{25,17},{32,40},{... | collective-permute-start | bytes 835592 | tf_op jit(solution)/shard_map/ppermute | solution.py:802
  198.6 22.6 %all-to-all-start.11 = ((f32[8,32,512]{2,1,0:T(8,128)}), f32[8,32,512]{2,1,0:T(8,128)S(1)}, u32[]{:S(2)}, u32[]{:S(2)}) async-start(f32[8,32,512]{2,1,0:T(8,128)} %bitcast.5), calls=%async_computation.11 | async-start | bytes 1048576 | tf_op jit(solution)/shard_map/all_to_all | solution.py:904
  203.4 9.6 %collective-permute-start.16 = (f32[1024,128]{1,0:T(8,128)S(1)}, f32[1024,128]{1,0:T(8,128)S(1)}, u32[]{:S(2)}, u32[]{:S(2)}) collective-permute-start(f32[1024,128]{1,0:T(8,128)S(1)} %get-tuple-element.144), channel_id=1, source_target_pairs={{0,2},{1,7},{8,10},{9,15},{16,18},{17,23},{24,26},{25,31},{32,34},... | collective-permute-start | bytes 1572872 | tf_op jit(solution)/shard_map/ppermute | solution.py:802
  205.2 8.8 %collective-permute-start.13 = (f32[40,512]{1,0:T(8,128)S(1)}, f32[40,512]{1,0:T(8,128)S(1)}, u32[]{:S(2)}, u32[]{:S(2)}) collective-permute-start(f32[40,512]{1,0:T(8,128)S(1)} %get-tuple-element.137), channel_id=1, source_target_pairs={{0,128},{1,129},{8,136},{9,137},{16,144},{17,145},{24,152},{25,153... | collective-permute-start | bytes 245768 | tf_op jit(solution)/shard_map/ppermute | solution.py:802
  206.8 7.9 %collective-permute-start.14 = (f32[40,512]{1,0:T(8,128)S(1)}, f32[40,512]{1,0:T(8,128)S(1)}, u32[]{:S(2)}, u32[]{:S(2)}) collective-permute-start(f32[40,512]{1,0:T(8,128)S(1)} %get-tuple-element.138), channel_id=1, source_target_pairs={{0,64},{1,193},{8,72},{9,201},{16,80},{17,209},{24,88},{25,217},{3... | collective-permute-start | bytes 245768 | tf_op jit(solution)/shard_map/ppermute | solution.py:802
  212.6 4.4 %collective-permute-start.15 = (f32[40,512]{1,0:T(8,128)S(1)}, f32[40,512]{1,0:T(8,128)S(1)}, u32[]{:S(2)}, u32[]{:S(2)}) collective-permute-start(f32[40,512]{1,0:T(8,128)S(1)} %get-tuple-element.139), channel_id=1, source_target_pairs={{0,192},{1,65},{8,200},{9,73},{16,208},{17,81},{24,216},{25,89},{3... | collective-permute-start | bytes 245768 | tf_op jit(solution)/shard_map/ppermute | solution.py:802
